TPU v7x, 512 devices: a whole 4x8x8 slice. The times are simulated.
512 devices in a mesh: blk: 32 (over x, z_hi, core), uly: 16 (over y, z_lo).
Axes of the slice: x: 4, y: 8, z: 8 (z_hi: 4, z_lo: 2; z = z_hi * 2 + z_lo), core: 2. Of those that a mesh axis runs over, the one named last changes fastest.
Arguments:
- queries: bfloat16 [32768, 1536], P(('blk', 'uly')), may hold values from -6 to 6, as said below
- keys: bfloat16 [32768, 1536], P(('blk', 'uly')), may hold values from -6 to 6, as said below
- values: bfloat16 [32768, 1536], P(('blk', 'uly')), may hold values from -6 to 6
- block_mask: int32 [12, 256, 256], P(None, 'blk'), may hold values from 0 to 1, as said below
Outputs:
- attended: bfloat16 [32768, 1536], P(('blk', 'uly'))
Inputs may be any that keep to these rules, and one draw needn't show every extreme that they name: `queries`: drawn like normal activations; a few rows may point along a common direction. `keys`: drawn like normal activations; a few rows may point along a common direction. `block_mask`: for every head and query block, each aligned group of 8 key blocks holds exactly one 1; every diagonal block is 1.
All inputs are finite; a program needn't handle non-finite values.
Results may differ from a plain program's by a relative error of at most 0.0095.
Values may be sent and summed in bfloat16 or wider, within the bound.
No kernel may reach another device: no remote copies, remote signals or barrier semaphores. Data moves between devices by JAX's collectives and lax.ppermute only.
A program may use at most 64 MiB of HBM per device.

v0:
```python
import math

import jax
import jax.numpy as jnp
from jax import lax
from jax.sharding import PartitionSpec as P


def from_behind(shard, axis, by):
    length = lax.axis_size(axis)
    return lax.ppermute(shard, axis, [(i, (i + by) % length) for i in range(length)])


def shards(queries, keys, values, block_mask):
    n_uly = lax.axis_size("uly")
    n_blk = lax.axis_size("blk")
    here_uly = lax.axis_index("uly")
    here_blk = lax.axis_index("blk")
    tok = queries.shape[0]
    heads = block_mask.shape[0]
    head_size = queries.shape[1] // heads
    block_len = tok * n_uly // block_mask.shape[1]
    cap = (heads + n_uly - 1) // n_uly
    slots = n_uly * cap
    span = tok * n_uly
    segb = span // block_len
    scale = 1.0 / math.sqrt(head_size)
    head_ids = jnp.arange(heads, dtype=jnp.int32)
    place = head_ids % n_uly * cap + head_ids // n_uly
    slot_ids = jnp.arange(slots, dtype=jnp.int32)
    onehot = place[None, :] == slot_ids[:, None]
    slot_head = jnp.sum(jnp.where(onehot, head_ids[None, :], 0), axis=1)
    mine = lax.dynamic_slice_in_dim(slot_head, here_uly * cap, cap, 0)
    select = onehot.astype(jnp.bfloat16)

    def spread(field):
        field = field.reshape(tok, heads, head_size)
        moved = jnp.einsum("thd,sh->tsd", field, select, preferred_element_type=jnp.float32)
        return moved.astype(jnp.bfloat16)

    q_all, k_all, v_all = (
        lax.all_to_all(spread(queries), "uly", split_axis=1, concat_axis=0, tiled=True),
        lax.all_to_all(spread(keys), "uly", split_axis=1, concat_axis=0, tiled=True),
        lax.all_to_all(spread(values), "uly", split_axis=1, concat_axis=0, tiled=True),
    )
    q_rows = q_all.reshape(segb, block_len, cap, head_size)
    own_mask = block_mask[mine].astype(jnp.bfloat16)

    def attend_one(carry, key_piece, value_piece, key_start):
        source = key_start // span
        picker = lax.dynamic_slice_in_dim(own_mask, source * segb, segb, 2)
        key_blocks = key_piece.reshape(segb, block_len, cap, head_size)
        value_blocks = value_piece.reshape(segb, block_len, cap, head_size)
        chosen_k = jnp.einsum(
            "cqs,sbch->cqbh", picker, key_blocks, preferred_element_type=jnp.float32
        ).astype(jnp.bfloat16)
        chosen_v = jnp.einsum(
            "cqs,sbch->cqbh", picker, value_blocks, preferred_element_type=jnp.float32
        ).astype(jnp.bfloat16)
        peak_old, total_old, acc_old = carry
        scores = (
            jnp.einsum("qach,cqbh->cqab", q_rows, chosen_k, preferred_element_type=jnp.float32)
            * scale
        )
        peak_new = jnp.maximum(peak_old, jnp.max(scores, axis=3))
        weights = jnp.exp(scores - peak_new[..., None])
        factor = jnp.exp(peak_old - peak_new)
        total_new = total_old * factor + jnp.sum(weights, axis=3)
        update = jnp.einsum(
            "cqab,cqbh->cqah",
            weights.astype(jnp.bfloat16),
            chosen_v,
            preferred_element_type=jnp.float32,
        )
        return (peak_new, total_new, acc_old * factor[..., None] + update)

    def attend(carry, key_piece, value_piece, key_start):
        pieces = key_piece.shape[0] // span

        def inner(index, state):
            return attend_one(state, key_piece, value_piece, key_start + index * span)

        return lax.fori_loop(0, pieces, inner, carry)

    start = (
        jnp.full((cap, segb, block_len), -1e30, jnp.float32),
        jnp.zeros((cap, segb, block_len), jnp.float32),
        jnp.zeros((cap, segb, block_len, head_size), jnp.float32),
    )
    first = attend(start, k_all, v_all, here_blk * span)

    def cycle_step(step, state):
        carry, key_now, value_now = state
        key_now, value_now = from_behind((key_now, value_now), "blk", 1)
        source = (here_blk - step) % n_blk
        return (attend(carry, key_now, value_now, source * span), key_now, value_now)

    final = lax.fori_loop(1, n_blk, cycle_step, (first, k_all, v_all))[0]
    peak_fin, total_fin, acc_fin = final
    result = (acc_fin / total_fin[..., None]).astype(jnp.bfloat16)
    result = jnp.transpose(result, (1, 2, 0, 3)).reshape(span, cap * head_size)
    back = lax.all_to_all(result, "uly", split_axis=0, concat_axis=1, tiled=True)
    back = back.reshape(tok, slots, head_size)
    gathered = jnp.einsum("tsd,sh->thd", back, select, preferred_element_type=jnp.float32)
    return gathered.astype(jnp.bfloat16).reshape(tok, heads * head_size)


def solution(mesh):
    placed = (
        P(("blk", "uly"), None),
        P(("blk", "uly"), None),
        P(("blk", "uly"), None),
        P(None, "blk", None),
    )
    return jax.shard_map(
        shards, mesh=mesh, in_specs=placed, out_specs=P(("blk", "uly"), None), check_vma=False
    )
```

profile of v0, /device:TPU:8, one launch (start us, length us, event | category | flops | bytes accessed | tf_op | source)
XLA Modules:
  0.0 658.8 jit_solution(3904722171160673093)
XLA Ops:
  2.2 9.5 %all-to-all-start.1 = ((bf16[64,16,128]{2,0,1:T(8,128)(2,1)}), bf16[64,16,128]{2,0,1:T(8,128)(2,1)S(1)}, u32[]{:S(2)}, u32[]{:S(2)}) async-start(bf16[64,16,128]{2,0,1:T(8,128)(2,1)} %copy.30), calls=%async_computation.1 | async-start | bytes 524288 | tf_op jit(solution)/shard_map/all_to_all | solution.py:43
  13.0 9.3 %all-to-all-done.1 = bf16[64,16,128]{2,0,1:T(8,128)(2,1)S(1)} async-done(((bf16[64,16,128]{2,0,1:T(8,128)(2,1)}), bf16[64,16,128]{2,0,1:T(8,128)(2,1)S(1)}, u32[]{:S(2)}, u32[]{:S(2)}) %all-to-all-start.1) | async-done | bytes 262176 | tf_op jit(solution)/shard_map/all_to_all | solution.py:43
  42.2 8.7 %all-to-all-done.2 = bf16[64,16,128]{2,0,1:T(8,128)(2,1)S(1)} async-done(((bf16[64,16,128]{2,0,1:T(8,128)(2,1)}), bf16[64,16,128]{2,0,1:T(8,128)(2,1)S(1)}, u32[]{:S(2)}, u32[]{:S(2)}) %all-to-all-start.2) | async-done | bytes 262176 | tf_op jit(solution)/shard_map/all_to_all | solution.py:44
  51.7 586.9 %while.46 = (s32[]{:T(128)}, f32[1,8,128]{2,1,0:T(8,128)S(1)}, f32[1,8,128]{2,1,0:T(8,128)S(1)}, f32[1,8,128,128]{3,2,1,0:T(8,128)S(1)}, bf16[1024,1,128]{2,0,1:...) while((s32[]{:T(128)}, f32[1,8,128]{2,1,0:T(8,128)S(1)}, ...), condition=%wide.region_6.7_spmd, body=%wide.region_3.6_spmd.sunk | while | flops 72616992 | bytes 7672398 | solution.py:98
  92.2 12.7 %collective-permute-done = bf16[1024,1,128]{2,0,1:T(8,128)(2,1)S(1)} collective-permute-done((bf16[1024,1,128]{2,0,1:T(8,128)(2,1)S(1)}, bf16[1024,1,128]{2,0,1:T(8,128)(2,1)S(1)}, u32[]{:S(2)}, u32[]{:S(2)}) %collective-permute-start) | collective-permute-done | bytes 262176 | tf_op jit(solution)/shard_map/while/body/eval_jaxpr/ppermute | solution.py:11
  112.9 8.1 %collective-permute-done = bf16[1024,1,128]{2,0,1:T(8,128)(2,1)S(1)} collective-permute-done((bf16[1024,1,128]{2,0,1:T(8,128)(2,1)S(1)}, bf16[1024,1,128]{2,0,1:T(8,128)(2,1)S(1)}, u32[]{:S(2)}, u32[]{:S(2)}) %collective-permute-start) | collective-permute-done | bytes 262176 | tf_op jit(solution)/shard_map/while/body/eval_jaxpr/ppermute | solution.py:11
  131.7 12.1 %collective-permute-done = bf16[1024,1,128]{2,0,1:T(8,128)(2,1)S(1)} collective-permute-done((bf16[1024,1,128]{2,0,1:T(8,128)(2,1)S(1)}, bf16[1024,1,128]{2,0,1:T(8,128)(2,1)S(1)}, u32[]{:S(2)}, u32[]{:S(2)}) %collective-permute-start) | collective-permute-done | bytes 262176 | tf_op jit(solution)/shard_map/while/body/eval_jaxpr/ppermute | solution.py:11
  151.8 10.9 %collective-permute-done = bf16[1024,1,128]{2,0,1:T(8,128)(2,1)S(1)} collective-permute-done((bf16[1024,1,128]{2,0,1:T(8,128)(2,1)S(1)}, bf16[1024,1,128]{2,0,1:T(8,128)(2,1)S(1)}, u32[]{:S(2)}, u32[]{:S(2)}) %collective-permute-start) | collective-permute-done | bytes 262176 | tf_op jit(solution)/shard_map/while/body/eval_jaxpr/ppermute | solution.py:11
  170.7 11.0 %collective-permute-done = bf16[1024,1,128]{2,0,1:T(8,128)(2,1)S(1)} collective-permute-done((bf16[1024,1,128]{2,0,1:T(8,128)(2,1)S(1)}, bf16[1024,1,128]{2,0,1:T(8,128)(2,1)S(1)}, u32[]{:S(2)}, u32[]{:S(2)}) %collective-permute-start) | collective-permute-done | bytes 262176 | tf_op jit(solution)/shard_map/while/body/eval_jaxpr/ppermute | solution.py:11
  189.6 8.0 %collective-permute-done = bf16[1024,1,128]{2,0,1:T(8,128)(2,1)S(1)} collective-permute-done((bf16[1024,1,128]{2,0,1:T(8,128)(2,1)S(1)}, bf16[1024,1,128]{2,0,1:T(8,128)(2,1)S(1)}, u32[]{:S(2)}, u32[]{:S(2)}) %collective-permute-start) | collective-permute-done | bytes 262176 | tf_op jit(solution)/shard_map/while/body/eval_jaxpr/ppermute | solution.py:11
  208.5 10.8 %collective-permute-done = bf16[1024,1,128]{2,0,1:T(8,128)(2,1)S(1)} collective-permute-done((bf16[1024,1,128]{2,0,1:T(8,128)(2,1)S(1)}, bf16[1024,1,128]{2,0,1:T(8,128)(2,1)S(1)}, u32[]{:S(2)}, u32[]{:S(2)}) %collective-permute-start) | collective-permute-done | bytes 262176 | tf_op jit(solution)/shard_map/while/body/eval_jaxpr/ppermute | solution.py:11
  227.3 10.8 %collective-permute-done = bf16[1024,1,128]{2,0,1:T(8,128)(2,1)S(1)} collective-permute-done((bf16[1024,1,128]{2,0,1:T(8,128)(2,1)S(1)}, bf16[1024,1,128]{2,0,1:T(8,128)(2,1)S(1)}, u32[]{:S(2)}, u32[]{:S(2)}) %collective-permute-start) | collective-permute-done | bytes 262176 | tf_op jit(solution)/shard_map/while/body/eval_jaxpr/ppermute | solution.py:11
  246.2 8.0 %collective-permute-done = bf16[1024,1,128]{2,0,1:T(8,128)(2,1)S(1)} collective-permute-done((bf16[1024,1,128]{2,0,1:T(8,128)(2,1)S(1)}, bf16[1024,1,128]{2,0,1:T(8,128)(2,1)S(1)}, u32[]{:S(2)}, u32[]{:S(2)}) %collective-permute-start) | collective-permute-done | bytes 262176 | tf_op jit(solution)/shard_map/while/body/eval_jaxpr/ppermute | solution.py:11
  265.1 10.9 %collective-permute-done = bf16[1024,1,128]{2,0,1:T(8,128)(2,1)S(1)} collective-permute-done((bf16[1024,1,128]{2,0,1:T(8,128)(2,1)S(1)}, bf16[1024,1,128]{2,0,1:T(8,128)(2,1)S(1)}, u32[]{:S(2)}, u32[]{:S(2)}) %collective-permute-start) | collective-permute-done | bytes 262176 | tf_op jit(solution)/shard_map/while/body/eval_jaxpr/ppermute | solution.py:11
  284.0 10.8 %collective-permute-done = bf16[1024,1,128]{2,0,1:T(8,128)(2,1)S(1)} collective-permute-done((bf16[1024,1,128]{2,0,1:T(8,128)(2,1)S(1)}, bf16[1024,1,128]{2,0,1:T(8,128)(2,1)S(1)}, u32[]{:S(2)}, u32[]{:S(2)}) %collective-permute-start) | collective-permute-done | bytes 262176 | tf_op jit(solution)/shard_map/while/body/eval_jaxpr/ppermute | solution.py:11
  302.8 8.0 %collective-permute-done = bf16[1024,1,128]{2,0,1:T(8,128)(2,1)S(1)} collective-permute-done((bf16[1024,1,128]{2,0,1:T(8,128)(2,1)S(1)}, bf16[1024,1,128]{2,0,1:T(8,128)(2,1)S(1)}, u32[]{:S(2)}, u32[]{:S(2)}) %collective-permute-start) | collective-permute-done | bytes 262176 | tf_op jit(solution)/shard_map/while/body/eval_jaxpr/ppermute | solution.py:11
  340.6 8.1 %collective-permute-done = bf16[1024,1,128]{2,0,1:T(8,128)(2,1)S(1)} collective-permute-done((bf16[1024,1,128]{2,0,1:T(8,128)(2,1)S(1)}, bf16[1024,1,128]{2,0,1:T(8,128)(2,1)S(1)}, u32[]{:S(2)}, u32[]{:S(2)}) %collective-permute-start) | collective-permute-done | bytes 262176 | tf_op jit(solution)/shard_map/while/body/eval_jaxpr/ppermute | solution.py:11
  359.4 8.1 %collective-permute-done = bf16[1024,1,128]{2,0,1:T(8,128)(2,1)S(1)} collective-permute-done((bf16[1024,1,128]{2,0,1:T(8,128)(2,1)S(1)}, bf16[1024,1,128]{2,0,1:T(8,128)(2,1)S(1)}, u32[]{:S(2)}, u32[]{:S(2)}) %collective-permute-start) | collective-permute-done | bytes 262176 | tf_op jit(solution)/shard_map/while/body/eval_jaxpr/ppermute | solution.py:11
  378.3 10.9 %collective-permute-done = bf16[1024,1,128]{2,0,1:T(8,128)(2,1)S(1)} collective-permute-done((bf16[1024,1,128]{2,0,1:T(8,128)(2,1)S(1)}, bf16[1024,1,128]{2,0,1:T(8,128)(2,1)S(1)}, u32[]{:S(2)}, u32[]{:S(2)}) %collective-permute-start) | collective-permute-done | bytes 262176 | tf_op jit(solution)/shard_map/while/body/eval_jaxpr/ppermute | solution.py:11
  397.2 10.9 %collective-permute-done = bf16[1024,1,128]{2,0,1:T(8,128)(2,1)S(1)} collective-permute-done((bf16[1024,1,128]{2,0,1:T(8,128)(2,1)S(1)}, bf16[1024,1,128]{2,0,1:T(8,128)(2,1)S(1)}, u32[]{:S(2)}, u32[]{:S(2)}) %collective-permute-start) | collective-permute-done | bytes 262176 | tf_op jit(solution)/shard_map/while/body/eval_jaxpr/ppermute | solution.py:11
  416.1 10.9 %collective-permute-done = bf16[1024,1,128]{2,0,1:T(8,128)(2,1)S(1)} collective-permute-done((bf16[1024,1,128]{2,0,1:T(8,128)(2,1)S(1)}, bf16[1024,1,128]{2,0,1:T(8,128)(2,1)S(1)}, u32[]{:S(2)}, u32[]{:S(2)}) %collective-permute-start) | collective-permute-done | bytes 262176 | tf_op jit(solution)/shard_map/while/body/eval_jaxpr/ppermute | solution.py:11
  434.9 10.9 %collective-permute-done = bf16[1024,1,128]{2,0,1:T(8,128)(2,1)S(1)} collective-permute-done((bf16[1024,1,128]{2,0,1:T(8,128)(2,1)S(1)}, bf16[1024,1,128]{2,0,1:T(8,128)(2,1)S(1)}, u32[]{:S(2)}, u32[]{:S(2)}) %collective-permute-start) | collective-permute-done | bytes 262176 | tf_op jit(solution)/shard_map/while/body/eval_jaxpr/ppermute | solution.py:11
  453.8 8.0 %collective-permute-done = bf16[1024,1,128]{2,0,1:T(8,128)(2,1)S(1)} collective-permute-done((bf16[1024,1,128]{2,0,1:T(8,128)(2,1)S(1)}, bf16[1024,1,128]{2,0,1:T(8,128)(2,1)S(1)}, u32[]{:S(2)}, u32[]{:S(2)}) %collective-permute-start) | collective-permute-done | bytes 262176 | tf_op jit(solution)/shard_map/while/body/eval_jaxpr/ppermute | solution.py:11
  472.7 10.8 %collective-permute-done = bf16[1024,1,128]{2,0,1:T(8,128)(2,1)S(1)} collective-permute-done((bf16[1024,1,128]{2,0,1:T(8,128)(2,1)S(1)}, bf16[1024,1,128]{2,0,1:T(8,128)(2,1)S(1)}, u32[]{:S(2)}, u32[]{:S(2)}) %collective-permute-start) | collective-permute-done | bytes 262176 | tf_op jit(solution)/shard_map/while/body/eval_jaxpr/ppermute | solution.py:11
  491.5 10.8 %collective-permute-done = bf16[1024,1,128]{2,0,1:T(8,128)(2,1)S(1)} collective-permute-done((bf16[1024,1,128]{2,0,1:T(8,128)(2,1)S(1)}, bf16[1024,1,128]{2,0,1:T(8,128)(2,1)S(1)}, u32[]{:S(2)}, u32[]{:S(2)}) %collective-permute-start) | collective-permute-done | bytes 262176 | tf_op jit(solution)/shard_map/while/body/eval_jaxpr/ppermute | solution.py:11
  510.4 8.0 %collective-permute-done = bf16[1024,1,128]{2,0,1:T(8,128)(2,1)S(1)} collective-permute-done((bf16[1024,1,128]{2,0,1:T(8,128)(2,1)S(1)}, bf16[1024,1,128]{2,0,1:T(8,128)(2,1)S(1)}, u32[]{:S(2)}, u32[]{:S(2)}) %collective-permute-start) | collective-permute-done | bytes 262176 | tf_op jit(solution)/shard_map/while/body/eval_jaxpr/ppermute | solution.py:11
  529.3 8.0 %collective-permute-done = bf16[1024,1,128]{2,0,1:T(8,128)(2,1)S(1)} collective-permute-done((bf16[1024,1,128]{2,0,1:T(8,128)(2,1)S(1)}, bf16[1024,1,128]{2,0,1:T(8,128)(2,1)S(1)}, u32[]{:S(2)}, u32[]{:S(2)}) %collective-permute-start) | collective-permute-done | bytes 262176 | tf_op jit(solution)/shard_map/while/body/eval_jaxpr/ppermute | solution.py:11
  548.2 8.0 %collective-permute-done = bf16[1024,1,128]{2,0,1:T(8,128)(2,1)S(1)} collective-permute-done((bf16[1024,1,128]{2,0,1:T(8,128)(2,1)S(1)}, bf16[1024,1,128]{2,0,1:T(8,128)(2,1)S(1)}, u32[]{:S(2)}, u32[]{:S(2)}) %collective-permute-start) | collective-permute-done | bytes 262176 | tf_op jit(solution)/shard_map/while/body/eval_jaxpr/ppermute | solution.py:11
  567.0 8.0 %collective-permute-done = bf16[1024,1,128]{2,0,1:T(8,128)(2,1)S(1)} collective-permute-done((bf16[1024,1,128]{2,0,1:T(8,128)(2,1)S(1)}, bf16[1024,1,128]{2,0,1:T(8,128)(2,1)S(1)}, u32[]{:S(2)}, u32[]{:S(2)}) %collective-permute-start) | collective-permute-done | bytes 262176 | tf_op jit(solution)/shard_map/while/body/eval_jaxpr/ppermute | solution.py:11
  585.9 8.0 %collective-permute-done = bf16[1024,1,128]{2,0,1:T(8,128)(2,1)S(1)} collective-permute-done((bf16[1024,1,128]{2,0,1:T(8,128)(2,1)S(1)}, bf16[1024,1,128]{2,0,1:T(8,128)(2,1)S(1)}, u32[]{:S(2)}, u32[]{:S(2)}) %collective-permute-start) | collective-permute-done | bytes 262176 | tf_op jit(solution)/shard_map/while/body/eval_jaxpr/ppermute | solution.py:11
  604.8 8.0 %collective-permute-done = bf16[1024,1,128]{2,0,1:T(8,128)(2,1)S(1)} collective-permute-done((bf16[1024,1,128]{2,0,1:T(8,128)(2,1)S(1)}, bf16[1024,1,128]{2,0,1:T(8,128)(2,1)S(1)}, u32[]{:S(2)}, u32[]{:S(2)}) %collective-permute-start) | collective-permute-done | bytes 262176 | tf_op jit(solution)/shard_map/while/body/eval_jaxpr/ppermute | solution.py:11
  638.8 18.9 %all_to_all.67 = bf16[16,64,128]{2,1,0:T(8,128)(2,1)S(1)} all-to-all(bf16[16,64,128]{2,1,0:T(8,128)(2,1)S(1)} %bitcast.115), channel_id=1, replica_groups=mesh['blk'=32,'uly'=16] {'uly'}, dimensions={0} | all-to-all | bytes 524288 | tf_op jit(solution)/shard_map/all_to_all | solution.py:102
  (437 shorter events, 346.0 us)
Async XLA Ops:
  2.2 20.1 %all-to-all-start.1 = ((bf16[64,16,128]{2,0,1:T(8,128)(2,1)}), bf16[64,16,128]{2,0,1:T(8,128)(2,1)S(1)}, u32[]{:S(2)}, u32[]{:S(2)}) async-start(bf16[64,16,128]{2,0,1:T(8,128)(2,1)} %copy.30), calls=%async_computation.1 | async-start | bytes 524288 | tf_op jit(solution)/shard_map/all_to_all | solution.py:43
  70.7 16.4 %collective-permute-start.1 = (bf16[1024,1,128]{2,0,1:T(8,128)(2,1)S(1)}, bf16[1024,1,128]{2,0,1:T(8,128)(2,1)S(1)}, u32[]{:S(2)}, u32[]{:S(2)}) collective-permute-start(bf16[1024,1,128]{2,0,1:T(8,128)(2,1)S(1)} %get-tuple-element.436), channel_id=1, source_target_pairs={{0,16},{16,32},{32,48},{48,64},{64,80},{80,96},{96,112},{112,128},... | collective-permute-start | bytes 786440 | tf_op jit(solution)/shard_map/while/body/eval_jaxpr/ppermute | solution.py:11
  88.3 16.6 %collective-permute-start = (bf16[1024,1,128]{2,0,1:T(8,128)(2,1)S(1)}, bf16[1024,1,128]{2,0,1:T(8,128)(2,1)S(1)}, u32[]{:S(2)}, u32[]{:S(2)}) collective-permute-start(bf16[1024,1,128]{2,0,1:T(8,128)(2,1)S(1)} %get-tuple-element.435), channel_id=1, source_target_pairs={{0,16},{16,32},{32,48},{48,64},{64,80},{80,96},{96,112},{112,128},... | collective-permute-start | bytes 786440 | tf_op jit(solution)/shard_map/while/body/eval_jaxpr/ppermute | solution.py:11
  90.2 17.5 %collective-permute-start.1 = (bf16[1024,1,128]{2,0,1:T(8,128)(2,1)S(1)}, bf16[1024,1,128]{2,0,1:T(8,128)(2,1)S(1)}, u32[]{:S(2)}, u32[]{:S(2)}) collective-permute-start(bf16[1024,1,128]{2,0,1:T(8,128)(2,1)S(1)} %get-tuple-element.436), channel_id=1, source_target_pairs={{0,16},{16,32},{32,48},{48,64},{64,80},{80,96},{96,112},{112,128},... | collective-permute-start | bytes 786440 | tf_op jit(solution)/shard_map/while/body/eval_jaxpr/ppermute | solution.py:11
  110.9 15.7 %collective-permute-start.1 = (bf16[1024,1,128]{2,0,1:T(8,128)(2,1)S(1)}, bf16[1024,1,128]{2,0,1:T(8,128)(2,1)S(1)}, u32[]{:S(2)}, u32[]{:S(2)}) collective-permute-start(bf16[1024,1,128]{2,0,1:T(8,128)(2,1)S(1)} %get-tuple-element.436), channel_id=1, source_target_pairs={{0,16},{16,32},{32,48},{48,64},{64,80},{80,96},{96,112},{112,128},... | collective-permute-start | bytes 786440 | tf_op jit(solution)/shard_map/while/body/eval_jaxpr/ppermute | solution.py:11
  127.8 16.0 %collective-permute-start = (bf16[1024,1,128]{2,0,1:T(8,128)(2,1)S(1)}, bf16[1024,1,128]{2,0,1:T(8,128)(2,1)S(1)}, u32[]{:S(2)}, u32[]{:S(2)}) collective-permute-start(bf16[1024,1,128]{2,0,1:T(8,128)(2,1)S(1)} %get-tuple-element.435), channel_id=1, source_target_pairs={{0,16},{16,32},{32,48},{48,64},{64,80},{80,96},{96,112},{112,128},... | collective-permute-start | bytes 786440 | tf_op jit(solution)/shard_map/while/body/eval_jaxpr/ppermute | solution.py:11
  129.8 16.9 %collective-permute-start.1 = (bf16[1024,1,128]{2,0,1:T(8,128)(2,1)S(1)}, bf16[1024,1,128]{2,0,1:T(8,128)(2,1)S(1)}, u32[]{:S(2)}, u32[]{:S(2)}) collective-permute-start(bf16[1024,1,128]{2,0,1:T(8,128)(2,1)S(1)} %get-tuple-element.436), channel_id=1, source_target_pairs={{0,16},{16,32},{32,48},{48,64},{64,80},{80,96},{96,112},{112,128},... | collective-permute-start | bytes 786440 | tf_op jit(solution)/shard_map/while/body/eval_jaxpr/ppermute | solution.py:11
  149.8 15.7 %collective-permute-start.1 = (bf16[1024,1,128]{2,0,1:T(8,128)(2,1)S(1)}, bf16[1024,1,128]{2,0,1:T(8,128)(2,1)S(1)}, u32[]{:S(2)}, u32[]{:S(2)}) collective-permute-start(bf16[1024,1,128]{2,0,1:T(8,128)(2,1)S(1)} %get-tuple-element.436), channel_id=1, source_target_pairs={{0,16},{16,32},{32,48},{48,64},{64,80},{80,96},{96,112},{112,128},... | collective-permute-start | bytes 786440 | tf_op jit(solution)/shard_map/while/body/eval_jaxpr/ppermute | solution.py:11
  168.7 15.8 %collective-permute-start.1 = (bf16[1024,1,128]{2,0,1:T(8,128)(2,1)S(1)}, bf16[1024,1,128]{2,0,1:T(8,128)(2,1)S(1)}, u32[]{:S(2)}, u32[]{:S(2)}) collective-permute-start(bf16[1024,1,128]{2,0,1:T(8,128)(2,1)S(1)} %get-tuple-element.436), channel_id=1, source_target_pairs={{0,16},{16,32},{32,48},{48,64},{64,80},{80,96},{96,112},{112,128},... | collective-permute-start | bytes 786440 | tf_op jit(solution)/shard_map/while/body/eval_jaxpr/ppermute | solution.py:11
  187.6 15.7 %collective-permute-start.1 = (bf16[1024,1,128]{2,0,1:T(8,128)(2,1)S(1)}, bf16[1024,1,128]{2,0,1:T(8,128)(2,1)S(1)}, u32[]{:S(2)}, u32[]{:S(2)}) collective-permute-start(bf16[1024,1,128]{2,0,1:T(8,128)(2,1)S(1)} %get-tuple-element.436), channel_id=1, source_target_pairs={{0,16},{16,32},{32,48},{48,64},{64,80},{80,96},{96,112},{112,128},... | collective-permute-start | bytes 786440 | tf_op jit(solution)/shard_map/while/body/eval_jaxpr/ppermute | solution.py:11
  206.5 15.7 %collective-permute-start.1 = (bf16[1024,1,128]{2,0,1:T(8,128)(2,1)S(1)}, bf16[1024,1,128]{2,0,1:T(8,128)(2,1)S(1)}, u32[]{:S(2)}, u32[]{:S(2)}) collective-permute-start(bf16[1024,1,128]{2,0,1:T(8,128)(2,1)S(1)} %get-tuple-element.436), channel_id=1, source_target_pairs={{0,16},{16,32},{32,48},{48,64},{64,80},{80,96},{96,112},{112,128},... | collective-permute-start | bytes 786440 | tf_op jit(solution)/shard_map/while/body/eval_jaxpr/ppermute | solution.py:11
  225.4 15.7 %collective-permute-start.1 = (bf16[1024,1,128]{2,0,1:T(8,128)(2,1)S(1)}, bf16[1024,1,128]{2,0,1:T(8,128)(2,1)S(1)}, u32[]{:S(2)}, u32[]{:S(2)}) collective-permute-start(bf16[1024,1,128]{2,0,1:T(8,128)(2,1)S(1)} %get-tuple-element.436), channel_id=1, source_target_pairs={{0,16},{16,32},{32,48},{48,64},{64,80},{80,96},{96,112},{112,128},... | collective-permute-start | bytes 786440 | tf_op jit(solution)/shard_map/while/body/eval_jaxpr/ppermute | solution.py:11
  244.2 15.7 %collective-permute-start.1 = (bf16[1024,1,128]{2,0,1:T(8,128)(2,1)S(1)}, bf16[1024,1,128]{2,0,1:T(8,128)(2,1)S(1)}, u32[]{:S(2)}, u32[]{:S(2)}) collective-permute-start(bf16[1024,1,128]{2,0,1:T(8,128)(2,1)S(1)} %get-tuple-element.436), channel_id=1, source_target_pairs={{0,16},{16,32},{32,48},{48,64},{64,80},{80,96},{96,112},{112,128},... | collective-permute-start | bytes 786440 | tf_op jit(solution)/shard_map/while/body/eval_jaxpr/ppermute | solution.py:11
  263.1 15.7 %collective-permute-start.1 = (bf16[1024,1,128]{2,0,1:T(8,128)(2,1)S(1)}, bf16[1024,1,128]{2,0,1:T(8,128)(2,1)S(1)}, u32[]{:S(2)}, u32[]{:S(2)}) collective-permute-start(bf16[1024,1,128]{2,0,1:T(8,128)(2,1)S(1)} %get-tuple-element.436), channel_id=1, source_target_pairs={{0,16},{16,32},{32,48},{48,64},{64,80},{80,96},{96,112},{112,128},... | collective-permute-start | bytes 786440 | tf_op jit(solution)/shard_map/while/body/eval_jaxpr/ppermute | solution.py:11
  282.0 15.7 %collective-permute-start.1 = (bf16[1024,1,128]{2,0,1:T(8,128)(2,1)S(1)}, bf16[1024,1,128]{2,0,1:T(8,128)(2,1)S(1)}, u32[]{:S(2)}, u32[]{:S(2)}) collective-permute-start(bf16[1024,1,128]{2,0,1:T(8,128)(2,1)S(1)} %get-tuple-element.436), channel_id=1, source_target_pairs={{0,16},{16,32},{32,48},{48,64},{64,80},{80,96},{96,112},{112,128},... | collective-permute-start | bytes 786440 | tf_op jit(solution)/shard_map/while/body/eval_jaxpr/ppermute | solution.py:11
  300.9 15.7 %collective-permute-start.1 = (bf16[1024,1,128]{2,0,1:T(8,128)(2,1)S(1)}, bf16[1024,1,128]{2,0,1:T(8,128)(2,1)S(1)}, u32[]{:S(2)}, u32[]{:S(2)}) collective-permute-start(bf16[1024,1,128]{2,0,1:T(8,128)(2,1)S(1)} %get-tuple-element.436), channel_id=1, source_target_pairs={{0,16},{16,32},{32,48},{48,64},{64,80},{80,96},{96,112},{112,128},... | collective-permute-start | bytes 786440 | tf_op jit(solution)/shard_map/while/body/eval_jaxpr/ppermute | solution.py:11
  319.7 15.7 %collective-permute-start.1 = (bf16[1024,1,128]{2,0,1:T(8,128)(2,1)S(1)}, bf16[1024,1,128]{2,0,1:T(8,128)(2,1)S(1)}, u32[]{:S(2)}, u32[]{:S(2)}) collective-permute-start(bf16[1024,1,128]{2,0,1:T(8,128)(2,1)S(1)} %get-tuple-element.436), channel_id=1, source_target_pairs={{0,16},{16,32},{32,48},{48,64},{64,80},{80,96},{96,112},{112,128},... | collective-permute-start | bytes 786440 | tf_op jit(solution)/shard_map/while/body/eval_jaxpr/ppermute | solution.py:11
  338.6 15.7 %collective-permute-start.1 = (bf16[1024,1,128]{2,0,1:T(8,128)(2,1)S(1)}, bf16[1024,1,128]{2,0,1:T(8,128)(2,1)S(1)}, u32[]{:S(2)}, u32[]{:S(2)}) collective-permute-start(bf16[1024,1,128]{2,0,1:T(8,128)(2,1)S(1)} %get-tuple-element.436), channel_id=1, source_target_pairs={{0,16},{16,32},{32,48},{48,64},{64,80},{80,96},{96,112},{112,128},... | collective-permute-start | bytes 786440 | tf_op jit(solution)/shard_map/while/body/eval_jaxpr/ppermute | solution.py:11
  357.5 15.7 %collective-permute-start.1 = (bf16[1024,1,128]{2,0,1:T(8,128)(2,1)S(1)}, bf16[1024,1,128]{2,0,1:T(8,128)(2,1)S(1)}, u32[]{:S(2)}, u32[]{:S(2)}) collective-permute-start(bf16[1024,1,128]{2,0,1:T(8,128)(2,1)S(1)} %get-tuple-element.436), channel_id=1, source_target_pairs={{0,16},{16,32},{32,48},{48,64},{64,80},{80,96},{96,112},{112,128},... | collective-permute-start | bytes 786440 | tf_op jit(solution)/shard_map/while/body/eval_jaxpr/ppermute | solution.py:11
  376.3 15.7 %collective-permute-start.1 = (bf16[1024,1,128]{2,0,1:T(8,128)(2,1)S(1)}, bf16[1024,1,128]{2,0,1:T(8,128)(2,1)S(1)}, u32[]{:S(2)}, u32[]{:S(2)}) collective-permute-start(bf16[1024,1,128]{2,0,1:T(8,128)(2,1)S(1)} %get-tuple-element.436), channel_id=1, source_target_pairs={{0,16},{16,32},{32,48},{48,64},{64,80},{80,96},{96,112},{112,128},... | collective-permute-start | bytes 786440 | tf_op jit(solution)/shard_map/while/body/eval_jaxpr/ppermute | solution.py:11
  395.2 15.7 %collective-permute-start.1 = (bf16[1024,1,128]{2,0,1:T(8,128)(2,1)S(1)}, bf16[1024,1,128]{2,0,1:T(8,128)(2,1)S(1)}, u32[]{:S(2)}, u32[]{:S(2)}) collective-permute-start(bf16[1024,1,128]{2,0,1:T(8,128)(2,1)S(1)} %get-tuple-element.436), channel_id=1, source_target_pairs={{0,16},{16,32},{32,48},{48,64},{64,80},{80,96},{96,112},{112,128},... | collective-permute-start | bytes 786440 | tf_op jit(solution)/shard_map/while/body/eval_jaxpr/ppermute | solution.py:11
  414.1 15.7 %collective-permute-start.1 = (bf16[1024,1,128]{2,0,1:T(8,128)(2,1)S(1)}, bf16[1024,1,128]{2,0,1:T(8,128)(2,1)S(1)}, u32[]{:S(2)}, u32[]{:S(2)}) collective-permute-start(bf16[1024,1,128]{2,0,1:T(8,128)(2,1)S(1)} %get-tuple-element.436), channel_id=1, source_target_pairs={{0,16},{16,32},{32,48},{48,64},{64,80},{80,96},{96,112},{112,128},... | collective-permute-start | bytes 786440 | tf_op jit(solution)/shard_map/while/body/eval_jaxpr/ppermute | solution.py:11
  433.0 15.7 %collective-permute-start.1 = (bf16[1024,1,128]{2,0,1:T(8,128)(2,1)S(1)}, bf16[1024,1,128]{2,0,1:T(8,128)(2,1)S(1)}, u32[]{:S(2)}, u32[]{:S(2)}) collective-permute-start(bf16[1024,1,128]{2,0,1:T(8,128)(2,1)S(1)} %get-tuple-element.436), channel_id=1, source_target_pairs={{0,16},{16,32},{32,48},{48,64},{64,80},{80,96},{96,112},{112,128},... | collective-permute-start | bytes 786440 | tf_op jit(solution)/shard_map/while/body/eval_jaxpr/ppermute | solution.py:11
  451.8 15.7 %collective-permute-start.1 = (bf16[1024,1,128]{2,0,1:T(8,128)(2,1)S(1)}, bf16[1024,1,128]{2,0,1:T(8,128)(2,1)S(1)}, u32[]{:S(2)}, u32[]{:S(2)}) collective-permute-start(bf16[1024,1,128]{2,0,1:T(8,128)(2,1)S(1)} %get-tuple-element.436), channel_id=1, source_target_pairs={{0,16},{16,32},{32,48},{48,64},{64,80},{80,96},{96,112},{112,128},... | collective-permute-start | bytes 786440 | tf_op jit(solution)/shard_map/while/body/eval_jaxpr/ppermute | solution.py:11
  470.7 15.7 %collective-permute-start.1 = (bf16[1024,1,128]{2,0,1:T(8,128)(2,1)S(1)}, bf16[1024,1,128]{2,0,1:T(8,128)(2,1)S(1)}, u32[]{:S(2)}, u32[]{:S(2)}) collective-permute-start(bf16[1024,1,128]{2,0,1:T(8,128)(2,1)S(1)} %get-tuple-element.436), channel_id=1, source_target_pairs={{0,16},{16,32},{32,48},{48,64},{64,80},{80,96},{96,112},{112,128},... | collective-permute-start | bytes 786440 | tf_op jit(solution)/shard_map/while/body/eval_jaxpr/ppermute | solution.py:11
  489.6 15.7 %collective-permute-start.1 = (bf16[1024,1,128]{2,0,1:T(8,128)(2,1)S(1)}, bf16[1024,1,128]{2,0,1:T(8,128)(2,1)S(1)}, u32[]{:S(2)}, u32[]{:S(2)}) collective-permute-start(bf16[1024,1,128]{2,0,1:T(8,128)(2,1)S(1)} %get-tuple-element.436), channel_id=1, source_target_pairs={{0,16},{16,32},{32,48},{48,64},{64,80},{80,96},{96,112},{112,128},... | collective-permute-start | bytes 786440 | tf_op jit(solution)/shard_map/while/body/eval_jaxpr/ppermute | solution.py:11
  508.4 15.7 %collective-permute-start.1 = (bf16[1024,1,128]{2,0,1:T(8,128)(2,1)S(1)}, bf16[1024,1,128]{2,0,1:T(8,128)(2,1)S(1)}, u32[]{:S(2)}, u32[]{:S(2)}) collective-permute-start(bf16[1024,1,128]{2,0,1:T(8,128)(2,1)S(1)} %get-tuple-element.436), channel_id=1, source_target_pairs={{0,16},{16,32},{32,48},{48,64},{64,80},{80,96},{96,112},{112,128},... | collective-permute-start | bytes 786440 | tf_op jit(solution)/shard_map/while/body/eval_jaxpr/ppermute | solution.py:11
  527.3 15.7 %collective-permute-start.1 = (bf16[1024,1,128]{2,0,1:T(8,128)(2,1)S(1)}, bf16[1024,1,128]{2,0,1:T(8,128)(2,1)S(1)}, u32[]{:S(2)}, u32[]{:S(2)}) collective-permute-start(bf16[1024,1,128]{2,0,1:T(8,128)(2,1)S(1)} %get-tuple-element.436), channel_id=1, source_target_pairs={{0,16},{16,32},{32,48},{48,64},{64,80},{80,96},{96,112},{112,128},... | collective-permute-start | bytes 786440 | tf_op jit(solution)/shard_map/while/body/eval_jaxpr/ppermute | solution.py:11
  546.2 15.7 %collective-permute-start.1 = (bf16[1024,1,128]{2,0,1:T(8,128)(2,1)S(1)}, bf16[1024,1,128]{2,0,1:T(8,128)(2,1)S(1)}, u32[]{:S(2)}, u32[]{:S(2)}) collective-permute-start(bf16[1024,1,128]{2,0,1:T(8,128)(2,1)S(1)} %get-tuple-element.436), channel_id=1, source_target_pairs={{0,16},{16,32},{32,48},{48,64},{64,80},{80,96},{96,112},{112,128},... | collective-permute-start | bytes 786440 | tf_op jit(solution)/shard_map/while/body/eval_jaxpr/ppermute | solution.py:11
  565.1 15.7 %collective-permute-start.1 = (bf16[1024,1,128]{2,0,1:T(8,128)(2,1)S(1)}, bf16[1024,1,128]{2,0,1:T(8,128)(2,1)S(1)}, u32[]{:S(2)}, u32[]{:S(2)}) collective-permute-start(bf16[1024,1,128]{2,0,1:T(8,128)(2,1)S(1)} %get-tuple-element.436), channel_id=1, source_target_pairs={{0,16},{16,32},{32,48},{48,64},{64,80},{80,96},{96,112},{112,128},... | collective-permute-start | bytes 786440 | tf_op jit(solution)/shard_map/while/body/eval_jaxpr/ppermute | solution.py:11
  583.9 15.7 %collective-permute-start.1 = (bf16[1024,1,128]{2,0,1:T(8,128)(2,1)S(1)}, bf16[1024,1,128]{2,0,1:T(8,128)(2,1)S(1)}, u32[]{:S(2)}, u32[]{:S(2)}) collective-permute-start(bf16[1024,1,128]{2,0,1:T(8,128)(2,1)S(1)} %get-tuple-element.436), channel_id=1, source_target_pairs={{0,16},{16,32},{32,48},{48,64},{64,80},{80,96},{96,112},{112,128},... | collective-permute-start | bytes 786440 | tf_op jit(solution)/shard_map/while/body/eval_jaxpr/ppermute | solution.py:11
  602.8 15.7 %collective-permute-start.1 = (bf16[1024,1,128]{2,0,1:T(8,128)(2,1)S(1)}, bf16[1024,1,128]{2,0,1:T(8,128)(2,1)S(1)}, u32[]{:S(2)}, u32[]{:S(2)}) collective-permute-start(bf16[1024,1,128]{2,0,1:T(8,128)(2,1)S(1)} %get-tuple-element.436), channel_id=1, source_target_pairs={{0,16},{16,32},{32,48},{48,64},{64,80},{80,96},{96,112},{112,128},... | collective-permute-start | bytes 786440 | tf_op jit(solution)/shard_map/while/body/eval_jaxpr/ppermute | solution.py:11
  (35 other events, 464.3 us)
where the time goes:
time: 661 us; the launch traced here: 659 us
  waiting for transfers between devices  434 us (66%)
  starting transfers between devices  145 us (22%)
  matrix products  43.4 us (7%)
  blocking collectives  18.9 us (3%)
    ppermute x62, waiting for transfers between devices, from_behind(): lax.ppermute(shard, axis, [(i, (i + by) % length) for i in range(length)])  411 us
    ppermute x62, starting transfers between devices, from_behind(): lax.ppermute(shard, axis, [(i, (i + by) % length) for i in range(length)])  126 us
    all_to_all x1, blocking collectives, shards(): lax.all_to_all(result, 'uly', split_axis=0, concat_axis=1, tiled=True)  18.9 us
    dot_general x32, matrix products, attend_one(): jnp.einsum('cqab,cqbh->cqah', weights.astype(jnp.bfloat16), chosen_v, pre...  13.5 us
  transfers between devices with their start and end apart: 65, of which 65 were waited for; matrix products, arithmetic and copies ran while one was open for 2% of the time, Pallas kernels for 0%

commit v1 on v0

v1 whole, which is shorter than its diff:
```python
import functools
import math

import jax
import jax.numpy as jnp
from jax import lax
from jax.experimental import pallas as pl
from jax.experimental.pallas import tpu as pltpu
from jax.sharding import PartitionSpec as P

BF = jnp.bfloat16
F32 = jnp.float32
NX, NZ, NC, NU = 4, 4, 2, 16
HEADS, HD, BS, TOK = 12, 128, 128, 64
SEGB = 8
EXTRA = 16
LSE = 32
VMEM = pl.BlockSpec(memory_space=pltpu.VMEM)
SMEM = pl.BlockSpec(memory_space=pltpu.SMEM)


def blk_perm(dx, dz, dc):
    pairs = []
    for x in range(NX):
        for z in range(NZ):
            for c in range(NC):
                to = ((x + dx) % NX * NZ + (z + dz) % NZ) * NC + (c ^ dc)
                pairs.append(((x * NZ + z) * NC + c, to))
    return pairs


def shift(field, dx, dz, dc):
    return lax.ppermute(field, "blk", blk_perm(dx, dz, dc))


def pack_kernel(head_ref, q_ref, k_ref, v_ref, mask_ref, out_ref, picks_ref):
    for h in range(HEADS):
        lanes = slice(h * HD, (h + 1) * HD)
        out_ref[h, 0:TOK, :] = q_ref[:, lanes]
        out_ref[h, TOK : 2 * TOK, :] = k_ref[:, lanes]
        out_ref[h, 2 * TOK : 3 * TOK, :] = v_ref[:, lanes]
    for s in range(HEADS, NU):
        out_ref[s] = jnp.zeros((3 * TOK, HD), BF)
    live = mask_ref[head_ref[0]].astype(F32).astype(BF)
    rows, cols = live.shape
    i = lax.broadcasted_iota(jnp.int32, (cols, HD), 0)
    g = lax.broadcasted_iota(jnp.int32, (cols, HD), 1)
    weight = jnp.where(i // SEGB == g, i % SEGB, 0).astype(F32).astype(BF)
    picks = jnp.dot(live, weight, preferred_element_type=F32)
    picks_ref[...] = jnp.concatenate([picks, jnp.zeros((EXTRA - rows, HD), F32)], axis=0).astype(BF)


def attend_kernel(columns_ref, picks_ref, *refs):
    q_refs, kv_refs, out_ref = refs[:NZ], refs[NZ : NZ + NX * NC], refs[-1]
    scale = 1.0 / math.sqrt(HD)
    for z in range(NZ):
        q_ref = q_refs[z]

        def one(qb, carry):
            q = q_ref[pl.ds(pl.multiple_of(qb * BS, BS), BS), :]
            keys, values = [], []
            for c, kv_ref in enumerate(kv_refs):
                j = picks_ref[z * SEGB + qb, columns_ref[c]]
                both = kv_ref[pl.ds(2 * j, 2)]
                keys.append(both[:, :TOK, :].reshape(BS, HD))
                values.append(both[:, TOK:, :].reshape(BS, HD))
            k = jnp.concatenate(keys, axis=0)
            v = jnp.concatenate(values, axis=0)
            s = lax.dot_general(q, k, (((1,), (1,)), ((), ())), preferred_element_type=F32)
            peak = jnp.max(s, axis=1, keepdims=True)
            w = jnp.exp((s - peak) * scale)
            total = jnp.sum(w, axis=1, keepdims=True)
            o = jnp.dot(w.astype(BF), v, preferred_element_type=F32) / total
            out_ref[z, pl.ds(pl.multiple_of(qb * BS, BS), BS), :] = o.astype(BF)
            lse = peak * scale + jnp.log(total)
            lse = jnp.transpose(jnp.broadcast_to(lse, (BS, HD)))[0:1, :]
            row = lax.broadcasted_iota(jnp.int32, (SEGB, HD), 0)
            return jnp.where(row == qb, jnp.broadcast_to(lse, (SEGB, HD)), carry)

        lse = lax.fori_loop(0, SEGB, one, jnp.zeros((SEGB, HD), F32))
        hi = lse.astype(BF).astype(F32)
        mid = (lse - hi).astype(BF).astype(F32)
        low = lse - hi - mid
        out_ref[z, SEGB * BS :, :] = jnp.concatenate([hi, mid, low, jnp.zeros_like(hi)], axis=0).astype(BF)


def merge_kernel(a_ref, b_ref, c_ref, d_ref, out_ref):
    refs = (a_ref, b_ref, c_ref, d_ref)
    lses = []
    for r in refs:
        rows = r[SEGB * BS :, :].astype(F32)
        lses.append(rows[0:SEGB] + rows[SEGB : 2 * SEGB] + rows[2 * SEGB : 3 * SEGB])
    top = functools.reduce(jnp.maximum, lses)
    parts = [jnp.exp(s - top) for s in lses]
    total = functools.reduce(jnp.add, parts)
    parts = [p / total for p in parts]
    for qb in range(SEGB):
        acc = jnp.zeros((BS, HD), F32)
        for r, p in zip(refs, parts):
            w = jnp.transpose(jnp.broadcast_to(p[qb : qb + 1, :], (BS, HD)))
            acc = acc + w * r[qb * BS : (qb + 1) * BS, :].astype(F32)
        out_ref[qb * BS : (qb + 1) * BS, :] = acc.astype(BF)


def unpack_kernel(in_ref, out_ref):
    for h in range(HEADS):
        out_ref[:, h * HD : (h + 1) * HD] = in_ref[h]


def call(kernel, outs, specs, *args, flops=0, moved=1 << 20):
    return pl.pallas_call(
        kernel,
        out_shape=outs,
        in_specs=specs,
        out_specs=jax.tree.map(lambda _: VMEM, outs),
        compiler_params=pltpu.CompilerParams(vmem_limit_bytes=48 << 20),
        cost_estimate=pl.CostEstimate(flops=flops, bytes_accessed=moved, transcendentals=0),
    )(*args)


def shards(queries, keys, values, block_mask):
    here_blk = lax.axis_index("blk")
    here_uly = lax.axis_index("uly")
    x, z, c = here_blk // (NZ * NC), here_blk // NC % NZ, here_blk % NC
    head = jnp.minimum(here_uly, HEADS - 1).reshape(1).astype(jnp.int32)
    packed, picks = call(
        pack_kernel,
        (jax.ShapeDtypeStruct((NU, 3 * TOK, HD), BF), jax.ShapeDtypeStruct((EXTRA, HD), BF)),
        [SMEM, VMEM, VMEM, VMEM, VMEM],
        head, queries, keys, values, block_mask,
    )
    got = lax.all_to_all(packed, "uly", split_axis=0, concat_axis=0, tiled=True)
    q_own = jnp.concatenate([got[:, :TOK].reshape(NU * TOK, HD), picks], axis=0)
    kv_own = got[:, TOK:]

    kvs, columns = [], []
    for dx in range(NX):
        near = kv_own if dx == 0 else shift(kv_own, dx, 0, 0)
        for dc in range(NC):
            kvs.append(near if dc == 0 else shift(near, 0, 0, 1))
            columns.append(((x - dx) % NX * NZ + z) * NC + (c ^ dc))
    qs = [q_own if dz == 0 else shift(q_own, 0, dz, 0) for dz in range(NZ)]
    picks_all = jnp.concatenate([q[NU * TOK : NU * TOK + SEGB] for q in qs], axis=0).astype(jnp.int32)
    parts = call(
        attend_kernel,
        jax.ShapeDtypeStruct((NZ, NU * TOK + LSE, HD), BF),
        [SMEM, SMEM] + [VMEM] * (NZ + NX * NC),
        jnp.stack(columns).astype(jnp.int32), picks_all, *qs, *kvs,
        flops=1 << 31, moved=6 << 20,
    )
    backs = [parts[0]] + [shift(parts[dz], 0, -dz, 0) for dz in range(1, NZ)]
    merged = call(merge_kernel, jax.ShapeDtypeStruct((NU * TOK, HD), BF), [VMEM] * NZ, *backs)
    home = lax.all_to_all(merged.reshape(NU, TOK, HD), "uly", split_axis=0, concat_axis=0, tiled=True)
    return call(unpack_kernel, jax.ShapeDtypeStruct((TOK, HEADS * HD), BF), [VMEM], home)


def solution(mesh):
    placed = (
        P(("blk", "uly"), None),
        P(("blk", "uly"), None),
        P(("blk", "uly"), None),
        P(None, "blk", None),
    )
    return jax.shard_map(
        shards, mesh=mesh, in_specs=placed, out_specs=P(("blk", "uly"), None), check_vma=False
    )
```

time: 661 us -> 168 us (0.25)
  the two profiles are of different devices: /device:TPU:8 before, /device:TPU:6 now
where the time goes in v1:
time: 168 us; the launch traced here: 166 us
  blocking collectives  49.1 us (29%)
  waiting for transfers between devices  47.6 us (28%)
  starting transfers between devices  42.6 us (25%)
  Pallas kernels  21.5 us (13%)
  local copies, waits for them, and re-layouts  5.09 us (3%)
    ppermute x13, waiting for transfers between devices, shift(): return lax.ppermute(field, 'blk', blk_perm(dx, dz, dc))  47.6 us
    ppermute x13, starting transfers between devices, shift(): return lax.ppermute(field, 'blk', blk_perm(dx, dz, dc))  42.6 us
    all_to_all x1, blocking collectives, shards(): got = lax.all_to_all(packed, 'uly', split_axis=0, concat_axis=0, tiled=True)  32.2 us
    pallas_call x4, Pallas kernels, call(): pl.pallas_call(kernel, out_shape=outs, in_specs=specs, out_specs=jax.tree...  21.5 us
    all_to_all x1, blocking collectives, shards(): lax.all_to_all(merged.reshape(NU, TOK, HD), 'uly', split_axis=0, concat_a...  16.9 us
    unnamed x8, local copies, waits for them, and re-layouts  3.67 us
  transfers between devices with their start and end apart: 13, of which 5 were waited for; matrix products, arithmetic and copies ran while one was open for 0% of the time, Pallas kernels for 0%

profile of v1, /device:TPU:6, one launch (start us, length us, event | category | flops | bytes accessed | tf_op | source)
XLA Modules:
  0.0 166.2 jit_solution(17304393305158676933)
XLA Ops:
  0.0 0.9 copy-done
  0.9 0.9 copy-done.1
  1.9 0.9 copy-done.2
  2.8 0.9 copy-done.3
  3.7 0.3 shard_map.46
  3.9 32.2 %all_to_all.10 = bf16[16,192,128]{2,1,0:T(8,128)(2,1)S(1)} all-to-all(bf16[16,192,128]{2,1,0:T(8,128)(2,1)S(1)} %get-tuple-element.8), channel_id=1, replica_groups=mesh['blk'=32,'uly'=16] {'uly'}, dimensions={0} | all-to-all | bytes 1572864 | tf_op jit(solution)/shard_map/all_to_all | solution.py:132
  36.1 2.7 %collective-permute-start.8 = (bf16[16,128,128]{2,1,0:T(8,128)(2,1)S(1)}, bf16[16,128,128]{2,1,0:T(8,128)(2,1)S(1)}, u32[]{:S(2)}, u32[]{:S(2)}) collective-permute-start(bf16[16,128,128]{2,1,0:T(8,128)(2,1)S(1)} %slice.44.refs_4_), channel_id=1, source_target_pairs={{0,384},{16,400},{32,416},{48,432},{64,448},{80,464},{96,480},{112... | collective-permute-start | bytes 1572872 | tf_op jit(solution)/shard_map/ppermute | solution.py:33
  38.9 3.0 %collective-permute-start.6 = (bf16[16,128,128]{2,1,0:T(8,128)(2,1)S(1)}, bf16[16,128,128]{2,1,0:T(8,128)(2,1)S(1)}, u32[]{:S(2)}, u32[]{:S(2)}) collective-permute-start(bf16[16,128,128]{2,1,0:T(8,128)(2,1)S(1)} %slice.44.refs_4_), channel_id=1, source_target_pairs={{0,256},{16,272},{32,288},{48,304},{64,320},{80,336},{96,352},{112... | collective-permute-start | bytes 1572872 | tf_op jit(solution)/shard_map/ppermute | solution.py:33
  41.9 4.0 %collective-permute-start.4 = (bf16[16,128,128]{2,1,0:T(8,128)(2,1)S(1)}, bf16[16,128,128]{2,1,0:T(8,128)(2,1)S(1)}, u32[]{:S(2)}, u32[]{:S(2)}) collective-permute-start(bf16[16,128,128]{2,1,0:T(8,128)(2,1)S(1)} %slice.44.refs_4_), channel_id=1, source_target_pairs={{0,128},{16,144},{32,160},{48,176},{64,192},{80,208},{96,224},{112... | collective-permute-start | bytes 1572872 | tf_op jit(solution)/shard_map/ppermute | solution.py:33
  46.0 10.0 %collective-permute-start.2 = (bf16[1040,128]{1,0:T(8,128)(2,1)S(1)}, bf16[1040,128]{1,0:T(8,128)(2,1)S(1)}, u32[]{:S(2)}, u32[]{:S(2)}) collective-permute-start(bf16[1040,128]{1,0:T(8,128)(2,1)S(1)} %pad_maximum_fusion.refs_0_), channel_id=1, source_target_pairs={{0,96},{16,112},{32,0},{48,16},{64,32},{80,48},{96,64},{112,80},{1... | collective-permute-start | bytes 798728 | tf_op jit(solution)/shard_map/ppermute | solution.py:33
  56.0 1.9 %collective-permute-start.1 = (bf16[1040,128]{1,0:T(8,128)(2,1)S(1)}, bf16[1040,128]{1,0:T(8,128)(2,1)S(1)}, u32[]{:S(2)}, u32[]{:S(2)}) collective-permute-start(bf16[1040,128]{1,0:T(8,128)(2,1)S(1)} %pad_maximum_fusion.refs_0_), channel_id=1, source_target_pairs={{0,64},{16,80},{32,96},{48,112},{64,0},{80,16},{96,32},{112,48},{1... | collective-permute-start | bytes 798728 | tf_op jit(solution)/shard_map/ppermute | solution.py:33
  58.0 18.0 %collective-permute-done.2.refs_3_ = bf16[1040,128]{1,0:T(8,128)(2,1)S(1)} collective-permute-done((bf16[1040,128]{1,0:T(8,128)(2,1)S(1)}, bf16[1040,128]{1,0:T(8,128)(2,1)S(1)}, u32[]{:S(2)}, u32[]{:S(2)}) %collective-permute-start.2) | collective-permute-done | bytes 266272 | tf_op jit(solution)/shard_map/ppermute | solution.py:33
  76.0 1.9 %collective-permute-start.3 = (bf16[16,128,128]{2,1,0:T(8,128)(2,1)S(1)}, bf16[16,128,128]{2,1,0:T(8,128)(2,1)}, u32[]{:S(2)}, u32[]{:S(2)}) collective-permute-start(bf16[16,128,128]{2,1,0:T(8,128)(2,1)S(1)} %slice.44.refs_4_), channel_id=1, source_target_pairs={{0,16},{16,0},{32,48},{48,32},{64,80},{80,64},{96,112},{112,96},{1... | collective-permute-start | bytes 1572872 | tf_op jit(solution)/shard_map/ppermute | solution.py:33
  77.9 0.0 collective-permute-done.8.refs_10_
  77.9 2.4 %collective-permute-start.9 = (bf16[16,128,128]{2,1,0:T(8,128)(2,1)S(1)}, bf16[16,128,128]{2,1,0:T(8,128)(2,1)}, u32[]{:S(2)}, u32[]{:S(2)}) collective-permute-start(bf16[16,128,128]{2,1,0:T(8,128)(2,1)S(1)} %collective-permute-done.8.refs_10_), channel_id=1, source_target_pairs={{0,16},{16,0},{32,48},{48,32},{64,80},{80,64},{96,112},{112,96},{1... | collective-permute-start | bytes 1572872 | tf_op jit(solution)/shard_map/ppermute | solution.py:33
  80.3 0.0 collective-permute-done.6.refs_8_
  80.3 1.9 %collective-permute-start.7 = (bf16[16,128,128]{2,1,0:T(8,128)(2,1)S(1)}, bf16[16,128,128]{2,1,0:T(8,128)(2,1)}, u32[]{:S(2)}, u32[]{:S(2)}) collective-permute-start(bf16[16,128,128]{2,1,0:T(8,128)(2,1)S(1)} %collective-permute-done.6.refs_8_), channel_id=1, source_target_pairs={{0,16},{16,0},{32,48},{48,32},{64,80},{80,64},{96,112},{112,96},{1... | collective-permute-start | bytes 1572872 | tf_op jit(solution)/shard_map/ppermute | solution.py:33
  82.3 2.4 %collective-permute-start.5 = (bf16[16,128,128]{2,1,0:T(8,128)(2,1)S(1)}, bf16[16,128,128]{2,1,0:T(8,128)(2,1)}, u32[]{:S(2)}, u32[]{:S(2)}) collective-permute-start(bf16[16,128,128]{2,1,0:T(8,128)(2,1)S(1)} %collective-permute-done.4.refs_6_), channel_id=1, source_target_pairs={{0,16},{16,0},{32,48},{48,32},{64,80},{80,64},{96,112},{112,96},{1... | collective-permute-start | bytes 1572872 | tf_op jit(solution)/shard_map/ppermute | solution.py:33
  84.7 1.9 %collective-permute-start = (bf16[1040,128]{1,0:T(8,128)(2,1)S(1)}, bf16[1040,128]{1,0:T(8,128)(2,1)S(1)}, u32[]{:S(2)}, u32[]{:S(2)}) collective-permute-start(bf16[1040,128]{1,0:T(8,128)(2,1)S(1)} %pad_maximum_fusion.refs_0_), channel_id=1, source_target_pairs={{0,32},{16,48},{32,64},{48,80},{64,96},{80,112},{96,0},{112,16},{1... | collective-permute-start | bytes 798728 | tf_op jit(solution)/shard_map/ppermute | solution.py:33
  86.7 0.1 stack.35.columns_ref
  86.8 13.0 %collective-permute-done.refs_1_ = bf16[1040,128]{1,0:T(8,128)(2,1)S(1)} collective-permute-done((bf16[1040,128]{1,0:T(8,128)(2,1)S(1)}, bf16[1040,128]{1,0:T(8,128)(2,1)S(1)}, u32[]{:S(2)}, u32[]{:S(2)}) %collective-permute-start) | collective-permute-done | bytes 266272 | tf_op jit(solution)/shard_map/ppermute | solution.py:33
  99.9 19.9 %shard_map.47 = bf16[4,1056,128]{2,1,0:T(8,128)(2,1)} custom-call(s32[8]{0:T(128)S(1)} %stack.35.columns_ref, s32[32,128]{1,0:T(8,128)S(1)} %maximum_convert_fusion.picks_ref, bf16[1040,128]{1,0:T(8,128)(2,1)S(1)} %pad_maximum_fusion.refs_0_, bf16[1040,128]{1,0:T(8,128)(2,1)S(1)} %collective-permute-done.refs_1_, ...), custom_call_target="tpu_custom_call" | custom-call | flops 2147483648 | bytes 6291456 | tf_op jit(solution)/shard_map/pallas_call | solution.py:111
  119.8 1.3 slice_bitcast_fusion
  121.1 2.9 %collective-permute-start.12 = (bf16[1056,128]{1,0:T(8,128)(2,1)S(1)}, bf16[1056,128]{1,0:T(8,128)(2,1)S(1)}, u32[]{:S(2)}, u32[]{:S(2)}) collective-permute-start(bf16[1056,128]{1,0:T(8,128)(2,1)S(1)} %get-tuple-element.9), channel_id=1, source_target_pairs={{0,32},{16,48},{32,64},{48,80},{64,96},{80,112},{96,0},{112,16},{1... | collective-permute-start | bytes 811016 | tf_op jit(solution)/shard_map/ppermute | solution.py:33
  124.0 3.9 %collective-permute-start.11 = (bf16[1056,128]{1,0:T(8,128)(2,1)S(1)}, bf16[1056,128]{1,0:T(8,128)(2,1)S(1)}, u32[]{:S(2)}, u32[]{:S(2)}) collective-permute-start(bf16[1056,128]{1,0:T(8,128)(2,1)S(1)} %get-tuple-element.10), channel_id=1, source_target_pairs={{0,64},{16,80},{32,96},{48,112},{64,0},{80,16},{96,32},{112,48},{1... | collective-permute-start | bytes 811016 | tf_op jit(solution)/shard_map/ppermute | solution.py:33
  127.9 3.5 %collective-permute-start.10 = (bf16[1056,128]{1,0:T(8,128)(2,1)S(1)}, bf16[1056,128]{1,0:T(8,128)(2,1)S(1)}, u32[]{:S(2)}, u32[]{:S(2)}) collective-permute-start(bf16[1056,128]{1,0:T(8,128)(2,1)S(1)} %get-tuple-element.11), channel_id=1, source_target_pairs={{0,96},{16,112},{32,0},{48,16},{64,32},{80,48},{96,64},{112,80},{1... | collective-permute-start | bytes 811016 | tf_op jit(solution)/shard_map/ppermute | solution.py:33
  131.4 6.6 %collective-permute-done.12.d_ref = bf16[1056,128]{1,0:T(8,128)(2,1)S(1)} collective-permute-done((bf16[1056,128]{1,0:T(8,128)(2,1)S(1)}, bf16[1056,128]{1,0:T(8,128)(2,1)S(1)}, u32[]{:S(2)}, u32[]{:S(2)}) %collective-permute-start.12) | collective-permute-done | bytes 270368 | tf_op jit(solution)/shard_map/ppermute | solution.py:33
  137.9 6.9 %collective-permute-done.11.c_ref = bf16[1056,128]{1,0:T(8,128)(2,1)S(1)} collective-permute-done((bf16[1056,128]{1,0:T(8,128)(2,1)S(1)}, bf16[1056,128]{1,0:T(8,128)(2,1)S(1)}, u32[]{:S(2)}, u32[]{:S(2)}) %collective-permute-start.11) | collective-permute-done | bytes 270368 | tf_op jit(solution)/shard_map/ppermute | solution.py:33
  144.9 3.1 %collective-permute-done.10.b_ref = bf16[1056,128]{1,0:T(8,128)(2,1)S(1)} collective-permute-done((bf16[1056,128]{1,0:T(8,128)(2,1)S(1)}, bf16[1056,128]{1,0:T(8,128)(2,1)S(1)}, u32[]{:S(2)}, u32[]{:S(2)}) %collective-permute-start.10) | collective-permute-done | bytes 270368 | tf_op jit(solution)/shard_map/ppermute | solution.py:33
  148.0 0.6 shard_map.48
  148.6 16.9 %all_to_all.11.in_ref = bf16[16,64,128]{2,1,0:T(8,128)(2,1)S(1)} all-to-all(bf16[16,64,128]{2,1,0:T(8,128)(2,1)S(1)} %bitcast.19), channel_id=1, replica_groups=mesh['blk'=32,'uly'=16] {'uly'}, dimensions={0} | all-to-all | bytes 524288 | tf_op jit(solution)/shard_map/all_to_all | solution.py:153
  165.5 0.7 shard_map.49
  (18 shorter events, 0.1 us)
Async XLA Ops:
  0.0 0.9 copy-start
  0.9 0.9 copy-start.1
  1.9 0.9 copy-start.2
  2.8 0.9 copy-start.3
  36.1 41.7 %collective-permute-start.8 = (bf16[16,128,128]{2,1,0:T(8,128)(2,1)S(1)}, bf16[16,128,128]{2,1,0:T(8,128)(2,1)S(1)}, u32[]{:S(2)}, u32[]{:S(2)}) collective-permute-start(bf16[16,128,128]{2,1,0:T(8,128)(2,1)S(1)} %slice.44.refs_4_), channel_id=1, source_target_pairs={{0,384},{16,400},{32,416},{48,432},{64,448},{80,464},{96,480},{112... | collective-permute-start | bytes 1572872 | tf_op jit(solution)/shard_map/ppermute | solution.py:33
  38.9 41.4 %collective-permute-start.6 = (bf16[16,128,128]{2,1,0:T(8,128)(2,1)S(1)}, bf16[16,128,128]{2,1,0:T(8,128)(2,1)S(1)}, u32[]{:S(2)}, u32[]{:S(2)}) collective-permute-start(bf16[16,128,128]{2,1,0:T(8,128)(2,1)S(1)} %slice.44.refs_4_), channel_id=1, source_target_pairs={{0,256},{16,272},{32,288},{48,304},{64,320},{80,336},{96,352},{112... | collective-permute-start | bytes 1572872 | tf_op jit(solution)/shard_map/ppermute | solution.py:33
  41.9 40.3 %collective-permute-start.4 = (bf16[16,128,128]{2,1,0:T(8,128)(2,1)S(1)}, bf16[16,128,128]{2,1,0:T(8,128)(2,1)S(1)}, u32[]{:S(2)}, u32[]{:S(2)}) collective-permute-start(bf16[16,128,128]{2,1,0:T(8,128)(2,1)S(1)} %slice.44.refs_4_), channel_id=1, source_target_pairs={{0,128},{16,144},{32,160},{48,176},{64,192},{80,208},{96,224},{112... | collective-permute-start | bytes 1572872 | tf_op jit(solution)/shard_map/ppermute | solution.py:33
  46.0 30.0 %collective-permute-start.2 = (bf16[1040,128]{1,0:T(8,128)(2,1)S(1)}, bf16[1040,128]{1,0:T(8,128)(2,1)S(1)}, u32[]{:S(2)}, u32[]{:S(2)}) collective-permute-start(bf16[1040,128]{1,0:T(8,128)(2,1)S(1)} %pad_maximum_fusion.refs_0_), channel_id=1, source_target_pairs={{0,96},{16,112},{32,0},{48,16},{64,32},{80,48},{96,64},{112,80},{1... | collective-permute-start | bytes 798728 | tf_op jit(solution)/shard_map/ppermute | solution.py:33
  56.0 28.6 %collective-permute-start.1 = (bf16[1040,128]{1,0:T(8,128)(2,1)S(1)}, bf16[1040,128]{1,0:T(8,128)(2,1)S(1)}, u32[]{:S(2)}, u32[]{:S(2)}) collective-permute-start(bf16[1040,128]{1,0:T(8,128)(2,1)S(1)} %pad_maximum_fusion.refs_0_), channel_id=1, source_target_pairs={{0,64},{16,80},{32,96},{48,112},{64,0},{80,16},{96,32},{112,48},{1... | collective-permute-start | bytes 798728 | tf_op jit(solution)/shard_map/ppermute | solution.py:33
  76.0 23.9 %collective-permute-start.3 = (bf16[16,128,128]{2,1,0:T(8,128)(2,1)S(1)}, bf16[16,128,128]{2,1,0:T(8,128)(2,1)}, u32[]{:S(2)}, u32[]{:S(2)}) collective-permute-start(bf16[16,128,128]{2,1,0:T(8,128)(2,1)S(1)} %slice.44.refs_4_), channel_id=1, source_target_pairs={{0,16},{16,0},{32,48},{48,32},{64,80},{80,64},{96,112},{112,96},{1... | collective-permute-start | bytes 1572872 | tf_op jit(solution)/shard_map/ppermute | solution.py:33
  77.9 22.0 %collective-permute-start.9 = (bf16[16,128,128]{2,1,0:T(8,128)(2,1)S(1)}, bf16[16,128,128]{2,1,0:T(8,128)(2,1)}, u32[]{:S(2)}, u32[]{:S(2)}) collective-permute-start(bf16[16,128,128]{2,1,0:T(8,128)(2,1)S(1)} %collective-permute-done.8.refs_10_), channel_id=1, source_target_pairs={{0,16},{16,0},{32,48},{48,32},{64,80},{80,64},{96,112},{112,96},{1... | collective-permute-start | bytes 1572872 | tf_op jit(solution)/shard_map/ppermute | solution.py:33
  80.3 19.6 %collective-permute-start.7 = (bf16[16,128,128]{2,1,0:T(8,128)(2,1)S(1)}, bf16[16,128,128]{2,1,0:T(8,128)(2,1)}, u32[]{:S(2)}, u32[]{:S(2)}) collective-permute-start(bf16[16,128,128]{2,1,0:T(8,128)(2,1)S(1)} %collective-permute-done.6.refs_8_), channel_id=1, source_target_pairs={{0,16},{16,0},{32,48},{48,32},{64,80},{80,64},{96,112},{112,96},{1... | collective-permute-start | bytes 1572872 | tf_op jit(solution)/shard_map/ppermute | solution.py:33
  82.3 17.6 %collective-permute-start.5 = (bf16[16,128,128]{2,1,0:T(8,128)(2,1)S(1)}, bf16[16,128,128]{2,1,0:T(8,128)(2,1)}, u32[]{:S(2)}, u32[]{:S(2)}) collective-permute-start(bf16[16,128,128]{2,1,0:T(8,128)(2,1)S(1)} %collective-permute-done.4.refs_6_), channel_id=1, source_target_pairs={{0,16},{16,0},{32,48},{48,32},{64,80},{80,64},{96,112},{112,96},{1... | collective-permute-start | bytes 1572872 | tf_op jit(solution)/shard_map/ppermute | solution.py:33
  84.7 15.2 %collective-permute-start = (bf16[1040,128]{1,0:T(8,128)(2,1)S(1)}, bf16[1040,128]{1,0:T(8,128)(2,1)S(1)}, u32[]{:S(2)}, u32[]{:S(2)}) collective-permute-start(bf16[1040,128]{1,0:T(8,128)(2,1)S(1)} %pad_maximum_fusion.refs_0_), channel_id=1, source_target_pairs={{0,32},{16,48},{32,64},{48,80},{64,96},{80,112},{96,0},{112,16},{1... | collective-permute-start | bytes 798728 | tf_op jit(solution)/shard_map/ppermute | solution.py:33
  121.1 16.9 %collective-permute-start.12 = (bf16[1056,128]{1,0:T(8,128)(2,1)S(1)}, bf16[1056,128]{1,0:T(8,128)(2,1)S(1)}, u32[]{:S(2)}, u32[]{:S(2)}) collective-permute-start(bf16[1056,128]{1,0:T(8,128)(2,1)S(1)} %get-tuple-element.9), channel_id=1, source_target_pairs={{0,32},{16,48},{32,64},{48,80},{64,96},{80,112},{96,0},{112,16},{1... | collective-permute-start | bytes 811016 | tf_op jit(solution)/shard_map/ppermute | solution.py:33
  124.0 20.9 %collective-permute-start.11 = (bf16[1056,128]{1,0:T(8,128)(2,1)S(1)}, bf16[1056,128]{1,0:T(8,128)(2,1)S(1)}, u32[]{:S(2)}, u32[]{:S(2)}) collective-permute-start(bf16[1056,128]{1,0:T(8,128)(2,1)S(1)} %get-tuple-element.10), channel_id=1, source_target_pairs={{0,64},{16,80},{32,96},{48,112},{64,0},{80,16},{96,32},{112,48},{1... | collective-permute-start | bytes 811016 | tf_op jit(solution)/shard_map/ppermute | solution.py:33
  127.9 20.1 %collective-permute-start.10 = (bf16[1056,128]{1,0:T(8,128)(2,1)S(1)}, bf16[1056,128]{1,0:T(8,128)(2,1)S(1)}, u32[]{:S(2)}, u32[]{:S(2)}) collective-permute-start(bf16[1056,128]{1,0:T(8,128)(2,1)S(1)} %get-tuple-element.11), channel_id=1, source_target_pairs={{0,96},{16,112},{32,0},{48,16},{64,32},{80,48},{96,64},{112,80},{1... | collective-permute-start | bytes 811016 | tf_op jit(solution)/shard_map/ppermute | solution.py:33

commit v2 on v1

v2 whole, which is shorter than its diff:
```python
import functools
import math

import jax
import jax.numpy as jnp
from jax import lax
from jax.experimental import pallas as pl
from jax.experimental.pallas import tpu as pltpu
from jax.sharding import Mesh, PartitionSpec as P

BF = jnp.bfloat16
F32 = jnp.float32
NX, NZ, NC, NU = 4, 4, 2, 16
HEADS, HD, BS, TOK = 12, 128, 128, 64
SEGB = 8
GROUPS = NX * NC
HALF = 4
ROWS = HALF * BS
EXTRA = 16
EXP2 = math.log2(math.e) / math.sqrt(HD)
AXES = ("x", "zh", "core", "y", "zl")
VMEM = pl.BlockSpec(memory_space=pltpu.VMEM)
SMEM = pl.BlockSpec(memory_space=pltpu.SMEM)
ANY = pl.BlockSpec(memory_space=pl.ANY)


def shift(field, axis, by):
    n = lax.axis_size(axis)
    return lax.ppermute(field, axis, [(i, (i + by) % n) for i in range(n)])


def pack_kernel(head_ref, q_hbm, k_hbm, v_hbm, mask_hbm, out_ref, picks_ref, q_ref, k_ref, v_ref, mask_ref, sems):
    pairs = ((mask_hbm.at[head_ref[0]], mask_ref), (q_hbm, q_ref), (k_hbm, k_ref), (v_hbm, v_ref))
    copies = [pltpu.make_async_copy(src, dst, sems.at[i]) for i, (src, dst) in enumerate(pairs)]
    for copy in copies:
        copy.start()
    for s in range(HEADS, NU):
        out_ref[s] = jnp.zeros((3 * TOK, HD), BF)
    copies[0].wait()
    live = mask_ref[...].astype(F32).astype(BF)
    cols = live.shape[1]
    i = lax.broadcasted_iota(jnp.int32, (cols, HD), 0)
    g = lax.broadcasted_iota(jnp.int32, (cols, HD), 1)
    weight = jnp.where(i // SEGB == g, i % SEGB, 0).astype(F32).astype(BF)
    picks = jnp.dot(live, weight, preferred_element_type=F32)
    pad = jnp.zeros((EXTRA - HALF, HD), F32)
    for half in range(2):
        picks_ref[half] = jnp.concatenate([picks[half * HALF : (half + 1) * HALF], pad], axis=0).astype(BF)
    for n, ref in enumerate((q_ref, k_ref, v_ref)):
        copies[n + 1].wait()
        for h in range(HEADS):
            out_ref[h, n * TOK : (n + 1) * TOK, :] = ref[:, h * HD : (h + 1) * HD]


def split3(lse):
    hi = lse.astype(BF).astype(F32)
    mid = (lse - hi).astype(BF).astype(F32)
    return jnp.concatenate([hi, mid, lse - hi - mid, jnp.zeros_like(hi)], axis=0).astype(BF)


def join3(rows):
    rows = rows.astype(F32)
    return rows[0:HALF] + rows[HALF : 2 * HALF] + rows[2 * HALF : 3 * HALF]


def attend_kernel(halves, n_kv, columns_ref, picks_ref, *refs):
    n_q = len(set(ref for ref, _ in halves))
    q_refs, kv_refs, out_refs = refs[:n_q], refs[n_q : n_q + n_kv], refs[n_q + n_kv :]
    groups = kv_refs if n_kv == GROUPS else [kv_refs[0].at[g] for g in range(GROUPS)]
    columns = [columns_ref[g] for g in range(GROUPS)]
    blocks = [(h, b) for h in range(len(halves)) for b in range(HALF)]
    n = len(blocks)
    fetched, scores, weights, peaks, totals = {}, {}, {}, {}, {}
    lses = [[] for _ in halves]
    for t in range(n + 2):
        ahead, here, last = t, t - 1, t - 2
        if ahead < n:
            h, b = blocks[ahead]
            ref, part = halves[h]
            q = (q_refs[ref] if part is None else q_refs[ref].at[part])[b * BS : (b + 1) * BS, :]
            keys, values = [], []
            for g in range(GROUPS):
                j = picks_ref[h * HALF + b, columns[g]]
                both = groups[g][pl.ds(2 * j, 2)]
                keys.append(both[:, :TOK, :].reshape(BS, HD))
                values.append(both[:, TOK:, :].reshape(BS, HD))
            fetched[ahead], scores[ahead] = (q, keys, values), []
        if 0 <= here < n:
            weights[here], peaks[here], totals[here] = [], [], []
        acc = None
        for step in range(4):
            if ahead < n:
                q, keys, _ = fetched[ahead]
                pair = jnp.concatenate(keys[2 * step : 2 * step + 2], axis=0)
                scores[ahead].append(
                    lax.dot_general(q, pair, (((1,), (1,)), ((), ())), preferred_element_type=F32)
                )
            if 0 <= here < n:
                rows = slice(step * BS // 4, (step + 1) * BS // 4)
                part = [s[rows] for s in scores[here]]
                peak = jnp.max(functools.reduce(jnp.maximum, part), axis=1, keepdims=True)
                w = [jnp.exp2((s - peak) * EXP2) for s in part]
                totals[here].append(jnp.sum(functools.reduce(jnp.add, w), axis=1, keepdims=True))
                peaks[here].append(peak)
                weights[here].append([p.astype(BF) for p in w])
            if 0 <= last < n:
                w = jnp.concatenate([p[step] for p in weights[last]], axis=0)
                pair = jnp.concatenate(fetched[last][2][2 * step : 2 * step + 2], axis=0)
                product = jnp.dot(w, pair, preferred_element_type=F32)
                acc = product if acc is None else acc + product
        if 0 <= last < n:
            h, b = blocks[last]
            peak, total = jnp.concatenate(peaks[last], axis=0), jnp.concatenate(totals[last], axis=0)
            out_refs[h][b * BS : (b + 1) * BS, :] = (acc * (1.0 / total)).astype(BF)
            lse = peak * EXP2 + jnp.log2(total)
            lses[h].append(jnp.transpose(jnp.broadcast_to(lse, (BS, HD)))[0:1, :])
            if b == HALF - 1:
                out_refs[h][ROWS:, :] = split3(jnp.concatenate(lses[h], axis=0))
            fetched[last] = scores[last] = weights[last] = None


def merge_kernel(keep, pairs, *refs):
    n_in = len(refs) - len(pairs)
    for n, members in enumerate(pairs):
        ins, out_ref = [refs[m] for m in members], refs[n_in + n]
        lses = [join3(r[ROWS:, :]) for r in ins]
        top = functools.reduce(jnp.maximum, lses)
        parts = [jnp.exp2(s - top) for s in lses]
        total = functools.reduce(jnp.add, parts)
        parts = [p / total for p in parts]
        for b in range(HALF):
            rows = slice(b * BS, (b + 1) * BS)
            acc = jnp.zeros((BS, HD), F32)
            for r, p in zip(ins, parts):
                acc = acc + jnp.transpose(jnp.broadcast_to(p[b : b + 1, :], (BS, HD))) * r[rows, :].astype(F32)
            out_ref[rows, :] = acc.astype(BF)
        if keep:
            out_ref[ROWS:, :] = split3(top + jnp.log2(total))


def unpack_kernel(in_ref, out_ref):
    for h in range(HEADS):
        out_ref[:, h * HD : (h + 1) * HD] = in_ref[h]


def call(kernel, outs, specs, *args, scratch=(), flops=0, moved=1 << 18):
    return pl.pallas_call(
        kernel,
        out_shape=outs,
        in_specs=specs,
        out_specs=jax.tree.map(lambda _: VMEM, outs),
        scratch_shapes=list(scratch),
        compiler_params=pltpu.CompilerParams(vmem_limit_bytes=24 << 20),
        cost_estimate=pl.CostEstimate(flops=flops, bytes_accessed=moved, transcendentals=0),
    )(*args)


def half_shape(rows=ROWS + EXTRA):
    return jax.ShapeDtypeStruct((rows, HD), BF)


def attend(columns, picks, queries, halves, kvs):
    return call(
        functools.partial(attend_kernel, halves, len(kvs)),
        [half_shape() for _ in halves],
        [SMEM, SMEM] + [VMEM] * (len(queries) + len(kvs)),
        columns, picks, *queries, *kvs,
        flops=len(halves) * (1 << 28), moved=4 << 20,
    )


def merge(keep, pairs, *ins):
    outs = [half_shape() if keep else half_shape(ROWS) for _ in pairs]
    return call(functools.partial(merge_kernel, keep, pairs), outs, [VMEM] * len(ins), *ins)


def picks_of(*halves):
    return jnp.concatenate([h[ROWS : ROWS + HALF] for h in halves], axis=0).astype(jnp.int32)


def shards(queries, keys, values, block_mask):
    x, z, c = lax.axis_index("x"), lax.axis_index("zh"), lax.axis_index("core")
    here_uly = lax.axis_index(("y", "zl"))
    head = jnp.minimum(here_uly, HEADS - 1).reshape(1).astype(jnp.int32)
    packed, picks = call(
        pack_kernel,
        (jax.ShapeDtypeStruct((NU, 3 * TOK, HD), BF), jax.ShapeDtypeStruct((2, EXTRA, HD), BF)),
        [SMEM, ANY, ANY, ANY, ANY],
        head, queries, keys, values, block_mask,
        scratch=[pltpu.VMEM(queries.shape, BF)] * 3
        + [pltpu.VMEM(block_mask.shape[1:], jnp.int32), pltpu.SemaphoreType.DMA((4,))],
    )
    got = lax.all_to_all(packed, ("y", "zl"), split_axis=0, concat_axis=0, tiled=True)
    kv_own = got[:, TOK:]
    q0 = jnp.concatenate([got[:, :TOK].reshape(2, ROWS, HD), picks], axis=1)

    kvs = [lax.all_gather(kv_own, ("x", "core"), axis=0, tiled=False)]
    columns = [(i // NC * NZ + z) * NC + i % NC for i in range(GROUPS)]
    columns = jnp.stack(columns).astype(jnp.int32)
    q1, q3 = shift(q0, "zh", 1), shift(q0, "zh", -1)
    q2a, q2b = shift(q1[0], "zh", 1), shift(q3[1], "zh", -1)

    o2a, o2b = attend(columns, picks_of(q2a, q2b), [q2a, q2b], ((0, None), (1, None)), kvs)
    via_a, via_b = shift(o2a, "zh", 1), shift(o2b, "zh", -1)
    o0a, o0b, o1a, o1b, o3a, o3b = attend(
        columns, picks_of(q0[0], q0[1], q1[0], q1[1], q3[0], q3[1]), [q0, q1, q3],
        ((0, 0), (0, 1), (1, 0), (1, 1), (2, 0), (2, 1)), kvs,
    )
    m1b, m3a = merge(True, ((0, 1), (2, 3)), o1b, via_b, o3a, via_a)
    back1 = shift(jnp.stack([o1a, m1b]), "zh", -1)
    back3 = shift(jnp.stack([m3a, o3b]), "zh", 1)
    whole = merge(False, ((0, 2, 4), (1, 3, 5)), o0a, o0b, back1[0], back1[1], back3[0], back3[1])
    whole = jnp.concatenate(whole, axis=0).reshape(NU, TOK, HD)
    home = lax.all_to_all(whole, ("y", "zl"), split_axis=0, concat_axis=0, tiled=True)
    return call(unpack_kernel, jax.ShapeDtypeStruct((TOK, HEADS * HD), BF), [VMEM], home)


def solution(mesh):
    fine = Mesh(mesh.devices.reshape(NX, NZ, NC, NU // 2, 2), AXES)
    tokens = P(AXES, None)
    placed = (tokens, tokens, tokens, P(None, AXES[:3], None))
    return jax.shard_map(shards, mesh=fine, in_specs=placed, out_specs=tokens, check_vma=False)
```

time: 168 us -> 151 us (0.90)
  waiting for transfers between devices: 47.6 us -> 28.4 us
  between operations: 0.33 us -> 13.6 us
  Pallas kernels: 21.5 us -> 11.4 us
  starting transfers between devices: 42.6 us -> 38.1 us
  local copies, waits for them, and re-layouts: 5.09 us -> 6.96 us
  blocking collectives: 49.1 us -> 50.8 us
    ppermute x13 -> x8, waiting for transfers between devices: 47.6 us -> 28.3 us  [shift(): return lax.ppermute(field, axis, [(i, (i + by) % n) for i in range(n)])]
    pallas_call x4 -> x6, Pallas kernels: 21.5 us -> 11.4 us  [call(): pl.pallas_call(kernel, out_shape=outs, in_specs=specs, out_specs=jax.tree...]
    ppermute x13 -> x8, starting transfers between devices: 42.6 us -> 38.1 us  [shift(): return lax.ppermute(field, axis, [(i, (i + by) % n) for i in range(n)])]
    unnamed x8 -> x12, local copies, waits for them, and re-layouts: 3.67 us -> 5.86 us
    all_to_all x2, blocking collectives: 49.1 us -> 50.8 us  [the longest x1 32.2 us: shards(): lax.all_to_all(packed, ('y', 'zl'), split_axis=0, concat_axis=0, tiled=True)]
  transfers between devices with their start and end apart: 13 -> 9, of which waited for: 5 -> 6; matrix products, arithmetic and copies ran while one was open for 0% -> 0% of each run, Pallas kernels for 0% -> 4%
where the time goes in v2:
time: 151 us; the launch traced here: 149 us
  blocking collectives  50.8 us (34%)
  starting transfers between devices  38.1 us (25%)
  waiting for transfers between devices  28.4 us (19%)
  between operations  13.6 us (9%)
  Pallas kernels  11.4 us (8%)
  local copies, waits for them, and re-layouts  6.96 us (5%)
    ppermute x8, starting transfers between devices, shift(): return lax.ppermute(field, axis, [(i, (i + by) % n) for i in range(n)])  38.1 us
    all_to_all x1, blocking collectives, shards(): lax.all_to_all(packed, ('y', 'zl'), split_axis=0, concat_axis=0, tiled=True)  32.2 us
    ppermute x8, waiting for transfers between devices, shift(): return lax.ppermute(field, axis, [(i, (i + by) % n) for i in range(n)])  28.3 us
    all_to_all x1, blocking collectives, shards(): lax.all_to_all(whole, ('y', 'zl'), split_axis=0, concat_axis=0, tiled=True)  18.6 us
    pallas_call x6, Pallas kernels, call(): pl.pallas_call(kernel, out_shape=outs, in_specs=specs, out_specs=jax.tree...  11.4 us
    unnamed x12, local copies, waits for them, and re-layouts  5.86 us
  transfers between devices with their start and end apart: 9, of which 6 were waited for; matrix products, arithmetic and copies ran while one was open for 0% of the time, Pallas kernels for 4%

profile of v2, /device:TPU:6, one launch (start us, length us, event | category | flops | bytes accessed | tf_op | source)
XLA Modules:
  0.0 149.4 jit_solution(5120222180321784883)
XLA Ops:
  6.5 0.9 copy-done.2
  7.5 0.9 copy-done.3
  8.4 0.9 copy-done.4
  9.3 0.9 copy-done.5
  10.2 1.1 shard_map.46
  11.3 32.2 %all_to_all.10 = bf16[16,192,128]{2,1,0:T(8,128)(2,1)S(1)} all-to-all(bf16[16,192,128]{2,1,0:T(8,128)(2,1)S(1)} %get-tuple-element.20), channel_id=1, replica_groups=mesh['x'=4,'zh'=4,'core'=2,'y'=8,'zl'=2] {'y','zl'}, dimensions={0} | all-to-all | bytes 1572864 | tf_op jit(solution)/shard_map/all_to_all | solution.py:193
  43.4 0.8 slice.107
  44.3 0.0 all-gather.3.cloned.1.call-update
  44.4 10.0 %collective-permute-start.1 = (bf16[2,528,128]{2,1,0:T(8,128)(2,1)S(1)}, bf16[2,528,128]{2,1,0:T(8,128)(2,1)S(1)}, u32[]{:S(2)}, u32[]{:S(2)}) collective-permute-start(bf16[2,528,128]{2,1,0:T(8,128)(2,1)S(1)} %pad_maximum_fusion.refs_0_), channel_id=1, source_target_pairs={{0,96},{32,0},{64,32},{96,64},{1,97},{33,1},{65,33},{97,65},{2,98}... | collective-permute-start | bytes 811016 | tf_op jit(solution)/shard_map/ppermute | solution.py:29
  54.4 1.9 %collective-permute-start = (bf16[2,528,128]{2,1,0:T(8,128)(2,1)S(1)}, bf16[2,528,128]{2,1,0:T(8,128)(2,1)S(1)}, u32[]{:S(2)}, u32[]{:S(2)}) collective-permute-start(bf16[2,528,128]{2,1,0:T(8,128)(2,1)S(1)} %pad_maximum_fusion.refs_0_), channel_id=1, source_target_pairs={{0,32},{32,64},{64,96},{96,0},{1,33},{33,65},{65,97},{97,1},{2,34}... | collective-permute-start | bytes 811016 | tf_op jit(solution)/shard_map/ppermute | solution.py:29
  56.4 0.1 stack.53.columns_ref
  56.5 4.4 %collective-permute-done.1.refs_2_ = bf16[2,528,128]{2,1,0:T(8,128)(2,1)S(1)} collective-permute-done((bf16[2,528,128]{2,1,0:T(8,128)(2,1)S(1)}, bf16[2,528,128]{2,1,0:T(8,128)(2,1)S(1)}, u32[]{:S(2)}, u32[]{:S(2)}) %collective-permute-start.1) | collective-permute-done | bytes 270368 | tf_op jit(solution)/shard_map/ppermute | solution.py:29
  60.8 9.6 %collective-permute-start.3 = (bf16[528,128]{1,0:T(8,128)(2,1)S(1)}, bf16[528,128]{1,0:T(8,128)(2,1)S(1)}, u32[]{:S(2)}, u32[]{:S(2)}) collective-permute-start(bf16[528,128]{1,0:T(8,128)(2,1)S(1)} %slice_bitcast_fusion.4), channel_id=1, source_target_pairs={{0,96},{32,0},{64,32},{96,64},{1,97},{33,1},{65,33},{97,65},{2,98}... | collective-permute-start | bytes 405512 | tf_op jit(solution)/shard_map/ppermute | solution.py:29
  70.5 1.9 %collective-permute-start.2 = (bf16[528,128]{1,0:T(8,128)(2,1)S(1)}, bf16[528,128]{1,0:T(8,128)(2,1)S(1)}, u32[]{:S(2)}, u32[]{:S(2)}) collective-permute-start(bf16[528,128]{1,0:T(8,128)(2,1)S(1)} %slice_bitcast_fusion.5), channel_id=1, source_target_pairs={{0,32},{32,64},{64,96},{96,0},{1,33},{33,65},{65,97},{97,1},{2,34}... | collective-permute-start | bytes 405512 | tf_op jit(solution)/shard_map/ppermute | solution.py:29
  72.5 0.1 concatenate.13
  72.6 2.1 %collective-permute-done.3.refs_1_ = bf16[528,128]{1,0:T(8,128)(2,1)S(1)} collective-permute-done((bf16[528,128]{1,0:T(8,128)(2,1)S(1)}, bf16[528,128]{1,0:T(8,128)(2,1)S(1)}, u32[]{:S(2)}, u32[]{:S(2)}) %collective-permute-start.3) | collective-permute-done | bytes 135200 | tf_op jit(solution)/shard_map/ppermute | solution.py:29
  74.6 5.0 %collective-permute-done.2.refs_0_ = bf16[528,128]{1,0:T(8,128)(2,1)S(1)} collective-permute-done((bf16[528,128]{1,0:T(8,128)(2,1)S(1)}, bf16[528,128]{1,0:T(8,128)(2,1)S(1)}, u32[]{:S(2)}, u32[]{:S(2)}) %collective-permute-start.2) | collective-permute-done | bytes 135200 | tf_op jit(solution)/shard_map/ppermute | solution.py:29
  79.6 0.0 all-gather.3.cloned.1.call-done
  79.7 2.2 %copy-done = bf16[128,128,128]{2,1,0:T(8,128)(2,1)S(1)} copy-done((bf16[128,128,128]{2,1,0:T(8,128)(2,1)S(1)}, bf16[128,128,128]{2,1,0:T(8,128)(2,1)}, u32[]{:S(2)}) %copy-start) | copy-done | bytes 4194328
  81.9 2.7 %shard_map.48 = (bf16[528,128]{1,0:T(8,128)(2,1)S(1)}, bf16[528,128]{1,0:T(8,128)(2,1)S(1)}) custom-call(s32[8]{0:T(128)S(1)} %stack.53.columns_ref, s32[8,128]{1,0:T(8,128)S(1)} %maximum_convert_fusion.picks_ref, bf16[528,128]{1,0:T(8,128)(2,1)S(1)} %collective-permute-done.2.refs_0_, bf16[528,128]{1,0:T(8,128)(2,1)S(1)} %collective-permute-done.3.refs_1_, ...), custom_call_target="tpu_custom_call" | custom-call | flops 536870912 | bytes 4194304 | tf_op jit(solution)/shard_map/pallas_call | solution.py:147
  84.6 5.9 %collective-permute-start.4 = (bf16[528,128]{1,0:T(8,128)(2,1)S(1)}, bf16[528,128]{1,0:T(8,128)(2,1)S(1)}, u32[]{:S(2)}, u32[]{:S(2)}) collective-permute-start(bf16[528,128]{1,0:T(8,128)(2,1)S(1)} %get-tuple-element.25), channel_id=1, source_target_pairs={{0,96},{32,0},{64,32},{96,64},{1,97},{33,1},{65,33},{97,65},{2,98}... | collective-permute-start | bytes 405512 | tf_op jit(solution)/shard_map/ppermute | solution.py:29
  90.6 1.9 %collective-permute-start.5 = (bf16[528,128]{1,0:T(8,128)(2,1)S(1)}, bf16[528,128]{1,0:T(8,128)(2,1)S(1)}, u32[]{:S(2)}, u32[]{:S(2)}) collective-permute-start(bf16[528,128]{1,0:T(8,128)(2,1)S(1)} %get-tuple-element.27), channel_id=1, source_target_pairs={{0,32},{32,64},{64,96},{96,0},{1,33},{33,65},{65,97},{97,1},{2,34}... | collective-permute-start | bytes 405512 | tf_op jit(solution)/shard_map/ppermute | solution.py:29
  92.5 6.1 %shard_map.47 = (bf16[528,128]{1,0:T(8,128)(2,1)S(1)}, bf16[528,128]{1,0:T(8,128)(2,1)S(1)}, bf16[528,128]{1,0:T(8,128)(2,1)S(1)}, bf16[528,128]{1,0:T(8,128)(2,...) custom-call(s32[8]{0:T(128)S(1)} %stack.53.columns_ref, s32[24,128]{1,0:T(8,128)S(1)} %convert_element_type.6.picks_ref, ...), custom_call_target="tpu_custom_call" | custom-call | flops 1610612736 | bytes 4194304 | tf_op jit(solution)/shard_map/pallas_call | solution.py:147
  98.6 2.3 %collective-permute-done.5.refs_3_ = bf16[528,128]{1,0:T(8,128)(2,1)S(1)} collective-permute-done((bf16[528,128]{1,0:T(8,128)(2,1)S(1)}, bf16[528,128]{1,0:T(8,128)(2,1)S(1)}, u32[]{:S(2)}, u32[]{:S(2)}) %collective-permute-start.5) | collective-permute-done | bytes 135200 | tf_op jit(solution)/shard_map/ppermute | solution.py:29
  100.8 0.4 shard_map.49
  101.2 3.8 %collective-permute-start.6 = (bf16[2,528,128]{2,1,0:T(8,128)(2,1)S(1)}, bf16[2,528,128]{2,1,0:T(8,128)(2,1)S(1)}, u32[]{:S(2)}, u32[]{:S(2)}) collective-permute-start(bf16[2,528,128]{2,1,0:T(8,128)(2,1)S(1)} %pad_maximum_fusion.1), channel_id=1, source_target_pairs={{0,96},{32,0},{64,32},{96,64},{1,97},{33,1},{65,33},{97,65},{2,98}... | collective-permute-start | bytes 811016 | tf_op jit(solution)/shard_map/ppermute | solution.py:29
  105.1 2.9 %collective-permute-start.7 = (bf16[2,528,128]{2,1,0:T(8,128)(2,1)S(1)}, bf16[2,528,128]{2,1,0:T(8,128)(2,1)S(1)}, u32[]{:S(2)}, u32[]{:S(2)}) collective-permute-start(bf16[2,528,128]{2,1,0:T(8,128)(2,1)S(1)} %pad_maximum_fusion.2), channel_id=1, source_target_pairs={{0,32},{32,64},{64,96},{96,0},{1,33},{33,65},{65,97},{97,1},{2,34}... | collective-permute-start | bytes 811016 | tf_op jit(solution)/shard_map/ppermute | solution.py:29
  108.0 4.1 %collective-permute-done.6 = bf16[2,528,128]{2,1,0:T(8,128)(2,1)S(1)} collective-permute-done((bf16[2,528,128]{2,1,0:T(8,128)(2,1)S(1)}, bf16[2,528,128]{2,1,0:T(8,128)(2,1)S(1)}, u32[]{:S(2)}, u32[]{:S(2)}) %collective-permute-start.6) | collective-permute-done | bytes 270368 | tf_op jit(solution)/shard_map/ppermute | solution.py:29
  112.1 10.6 %collective-permute-done.7 = bf16[2,528,128]{2,1,0:T(8,128)(2,1)S(1)} collective-permute-done((bf16[2,528,128]{2,1,0:T(8,128)(2,1)S(1)}, bf16[2,528,128]{2,1,0:T(8,128)(2,1)S(1)}, u32[]{:S(2)}, u32[]{:S(2)}) %collective-permute-start.7) | collective-permute-done | bytes 270368 | tf_op jit(solution)/shard_map/ppermute | solution.py:29
  122.7 0.5 shard_map.50
  123.2 18.6 %all_to_all.11.in_ref = bf16[16,64,128]{2,1,0:T(8,128)(2,1)S(1)} all-to-all(bf16[16,64,128]{2,1,0:T(8,128)(2,1)S(1)} %bitcast.47), channel_id=1, replica_groups=mesh['x'=4,'zh'=4,'core'=2,'y'=8,'zl'=2] {'y','zl'}, dimensions={0} | all-to-all | bytes 524288 | tf_op jit(solution)/shard_map/all_to_all | solution.py:214
  141.9 0.7 shard_map.51
  (26 shorter events, 0.2 us)
Async XLA Ops:
  6.5 73.1 %all-gather.3.cloned.1.call-start = ((), (), s32[]{:S(2)}) async-start(), calls=%async_computation.2 | async-start | bytes 4718592 | tf_op jit(solution)/shard_map/all_gather | solution.py:197
  6.5 0.9 copy-start.2
  7.5 0.9 copy-start.3
  8.4 0.9 copy-start.4
  9.3 0.9 copy-start.5
  44.4 16.4 %collective-permute-start.1 = (bf16[2,528,128]{2,1,0:T(8,128)(2,1)S(1)}, bf16[2,528,128]{2,1,0:T(8,128)(2,1)S(1)}, u32[]{:S(2)}, u32[]{:S(2)}) collective-permute-start(bf16[2,528,128]{2,1,0:T(8,128)(2,1)S(1)} %pad_maximum_fusion.refs_0_), channel_id=1, source_target_pairs={{0,96},{32,0},{64,32},{96,64},{1,97},{33,1},{65,33},{97,65},{2,98}... | collective-permute-start | bytes 811016 | tf_op jit(solution)/shard_map/ppermute | solution.py:29
  54.4 16.1 %collective-permute-start = (bf16[2,528,128]{2,1,0:T(8,128)(2,1)S(1)}, bf16[2,528,128]{2,1,0:T(8,128)(2,1)S(1)}, u32[]{:S(2)}, u32[]{:S(2)}) collective-permute-start(bf16[2,528,128]{2,1,0:T(8,128)(2,1)S(1)} %pad_maximum_fusion.refs_0_), channel_id=1, source_target_pairs={{0,32},{32,64},{64,96},{96,0},{1,33},{33,65},{65,97},{97,1},{2,34}... | collective-permute-start | bytes 811016 | tf_op jit(solution)/shard_map/ppermute | solution.py:29
  60.8 13.8 %collective-permute-start.3 = (bf16[528,128]{1,0:T(8,128)(2,1)S(1)}, bf16[528,128]{1,0:T(8,128)(2,1)S(1)}, u32[]{:S(2)}, u32[]{:S(2)}) collective-permute-start(bf16[528,128]{1,0:T(8,128)(2,1)S(1)} %slice_bitcast_fusion.4), channel_id=1, source_target_pairs={{0,96},{32,0},{64,32},{96,64},{1,97},{33,1},{65,33},{97,65},{2,98}... | collective-permute-start | bytes 405512 | tf_op jit(solution)/shard_map/ppermute | solution.py:29
  70.5 9.1 %collective-permute-start.2 = (bf16[528,128]{1,0:T(8,128)(2,1)S(1)}, bf16[528,128]{1,0:T(8,128)(2,1)S(1)}, u32[]{:S(2)}, u32[]{:S(2)}) collective-permute-start(bf16[528,128]{1,0:T(8,128)(2,1)S(1)} %slice_bitcast_fusion.5), channel_id=1, source_target_pairs={{0,32},{32,64},{64,96},{96,0},{1,33},{33,65},{65,97},{97,1},{2,34}... | collective-permute-start | bytes 405512 | tf_op jit(solution)/shard_map/ppermute | solution.py:29
  79.7 2.2 %copy-start = (bf16[128,128,128]{2,1,0:T(8,128)(2,1)S(1)}, bf16[128,128,128]{2,1,0:T(8,128)(2,1)}, u32[]{:S(2)}) copy-start(bf16[128,128,128]{2,1,0:T(8,128)(2,1)} %all-gather.3.cloned.1.call-done) | copy-start | bytes 12582916
  81.9 10.6 %copy-start.1 = (bf16[128,128,128]{2,1,0:T(8,128)(2,1)S(1)}, bf16[128,128,128]{2,1,0:T(8,128)(2,1)}, u32[]{:S(2)}) copy-start(bf16[128,128,128]{2,1,0:T(8,128)(2,1)} %all-gather.3.cloned.1.call-done) | copy-start | bytes 12582916
  84.6 14.0 %collective-permute-start.4 = (bf16[528,128]{1,0:T(8,128)(2,1)S(1)}, bf16[528,128]{1,0:T(8,128)(2,1)S(1)}, u32[]{:S(2)}, u32[]{:S(2)}) collective-permute-start(bf16[528,128]{1,0:T(8,128)(2,1)S(1)} %get-tuple-element.25), channel_id=1, source_target_pairs={{0,96},{32,0},{64,32},{96,64},{1,97},{33,1},{65,33},{97,65},{2,98}... | collective-permute-start | bytes 405512 | tf_op jit(solution)/shard_map/ppermute | solution.py:29
  90.6 10.3 %collective-permute-start.5 = (bf16[528,128]{1,0:T(8,128)(2,1)S(1)}, bf16[528,128]{1,0:T(8,128)(2,1)S(1)}, u32[]{:S(2)}, u32[]{:S(2)}) collective-permute-start(bf16[528,128]{1,0:T(8,128)(2,1)S(1)} %get-tuple-element.27), channel_id=1, source_target_pairs={{0,32},{32,64},{64,96},{96,0},{1,33},{33,65},{65,97},{97,1},{2,34}... | collective-permute-start | bytes 405512 | tf_op jit(solution)/shard_map/ppermute | solution.py:29
  101.2 10.9 %collective-permute-start.6 = (bf16[2,528,128]{2,1,0:T(8,128)(2,1)S(1)}, bf16[2,528,128]{2,1,0:T(8,128)(2,1)S(1)}, u32[]{:S(2)}, u32[]{:S(2)}) collective-permute-start(bf16[2,528,128]{2,1,0:T(8,128)(2,1)S(1)} %pad_maximum_fusion.1), channel_id=1, source_target_pairs={{0,96},{32,0},{64,32},{96,64},{1,97},{33,1},{65,33},{97,65},{2,98}... | collective-permute-start | bytes 811016 | tf_op jit(solution)/shard_map/ppermute | solution.py:29
  105.1 17.6 %collective-permute-start.7 = (bf16[2,528,128]{2,1,0:T(8,128)(2,1)S(1)}, bf16[2,528,128]{2,1,0:T(8,128)(2,1)S(1)}, u32[]{:S(2)}, u32[]{:S(2)}) collective-permute-start(bf16[2,528,128]{2,1,0:T(8,128)(2,1)S(1)} %pad_maximum_fusion.2), channel_id=1, source_target_pairs={{0,32},{32,64},{64,96},{96,0},{1,33},{33,65},{65,97},{97,1},{2,34}... | collective-permute-start | bytes 811016 | tf_op jit(solution)/shard_map/ppermute | solution.py:29
Sparse Core Ops, SparseCore 0:
  44.4 34.5 all-gather.2

commit v3 on v2

--- a/solution.py
+++ b/solution.py
@@ -21,7 +21,7 @@
 AXES = ("x", "zh", "core", "y", "zl")
 VMEM = pl.BlockSpec(memory_space=pltpu.VMEM)
 SMEM = pl.BlockSpec(memory_space=pltpu.SMEM)
-ANY = pl.BlockSpec(memory_space=pl.ANY)
+HBM = pl.BlockSpec(memory_space=pltpu.HBM)
 
 
 def shift(field, axis, by):
@@ -185,7 +185,7 @@
     packed, picks = call(
         pack_kernel,
         (jax.ShapeDtypeStruct((NU, 3 * TOK, HD), BF), jax.ShapeDtypeStruct((2, EXTRA, HD), BF)),
-        [SMEM, ANY, ANY, ANY, ANY],
+        [SMEM, HBM, HBM, HBM, HBM],
         head, queries, keys, values, block_mask,
         scratch=[pltpu.VMEM(queries.shape, BF)] * 3
         + [pltpu.VMEM(block_mask.shape[1:], jnp.int32), pltpu.SemaphoreType.DMA((4,))],
@@ -194,8 +194,11 @@
     kv_own = got[:, TOK:]
     q0 = jnp.concatenate([got[:, :TOK].reshape(2, ROWS, HD), picks], axis=1)
 
-    kvs = [lax.all_gather(kv_own, ("x", "core"), axis=0, tiled=False)]
-    columns = [(i // NC * NZ + z) * NC + i % NC for i in range(GROUPS)]
+    kvs, columns = [], []
+    for dx in (1, 3, 0, 2):
+        near = kv_own if dx == 0 else shift(kv_own, "x", dx)
+        kvs += [near, shift(near, "core", 1)]
+        columns += [((x - dx) % NX * NZ + z) * NC + cc for cc in (c, 1 - c)]
     columns = jnp.stack(columns).astype(jnp.int32)
     q1, q3 = shift(q0, "zh", 1), shift(q0, "zh", -1)
     q2a, q2b = shift(q1[0], "zh", 1), shift(q3[1], "zh", -1)

time: 151 us -> 152 us (level)
  between operations: 13.6 us -> 0.28 us
  starting transfers between devices: 38.1 us -> 51.4 us
  local copies, waits for them, and re-layouts: 6.96 us -> 13 us
  waiting for transfers between devices: 28.4 us -> 23.6 us
  blocking collectives: 50.8 us -> 48 us
    ppermute x8 -> x15, starting transfers between devices: 38.1 us -> 51.4 us  [shift(): return lax.ppermute(field, axis, [(i, (i + by) % n) for i in range(n)])]
    ppermute x8 -> x15, waiting for transfers between devices: 28.3 us -> 23.6 us  [shift(): return lax.ppermute(field, axis, [(i, (i + by) % n) for i in range(n)])]
    slice x5, local copies, waits for them, and re-layouts: 0.02 us -> 3.76 us  [picks_of(): h[ROWS:ROWS + HALF]]
    concatenate x1, local copies, waits for them, and re-layouts: 0.09 us -> 3.79 us  [picks_of(): jnp.concatenate([h[ROWS:ROWS + HALF] for h in halves], axis=0)]
    all_to_all x1, blocking collectives: 18.6 us -> 15.8 us  [shards(): lax.all_to_all(whole, ('y', 'zl'), split_axis=0, concat_axis=0, tiled=True)]
    unnamed x12, local copies, waits for them, and re-layouts: 5.86 us -> 3.68 us
    squeeze x1, local copies, waits for them, and re-layouts: 0.01 us -> 1.57 us  [shards(): q1[0]]
  transfers between devices with their start and end apart: 9 -> 15, of which waited for: 6 -> 6; matrix products, arithmetic and copies ran while one was open for 0% -> 7% of each run, Pallas kernels for 4% -> 5%
where the time goes in v3:
time: 152 us; the launch traced here: 150 us
  starting transfers between devices  51.4 us (34%)
  blocking collectives  48 us (32%)
  waiting for transfers between devices  23.6 us (16%)
  local copies, waits for them, and re-layouts  13 us (9%)
  Pallas kernels  12.8 us (8%)
    ppermute x15, starting transfers between devices, shift(): return lax.ppermute(field, axis, [(i, (i + by) % n) for i in range(n)])  51.4 us
    all_to_all x1, blocking collectives, shards(): lax.all_to_all(packed, ('y', 'zl'), split_axis=0, concat_axis=0, tiled=True)  32.2 us
    ppermute x15, waiting for transfers between devices, shift(): return lax.ppermute(field, axis, [(i, (i + by) % n) for i in range(n)])  23.6 us
    all_to_all x1, blocking collectives, shards(): lax.all_to_all(whole, ('y', 'zl'), split_axis=0, concat_axis=0, tiled=True)  15.8 us
    pallas_call x6, Pallas kernels, call(): pl.pallas_call(kernel, out_shape=outs, in_specs=specs, out_specs=jax.tree...  12.8 us
    concatenate x1, local copies, waits for them, and re-layouts, picks_of(): jnp.concatenate([h[ROWS:ROWS + HALF] for h in halves], axis=0)  3.79 us
    slice x5, local copies, waits for them, and re-layouts, picks_of(): h[ROWS:ROWS + HALF]  3.76 us
    unnamed x12, local copies, waits for them, and re-layouts  3.68 us
  transfers between devices with their start and end apart: 15, of which 6 were waited for; matrix products, arithmetic and copies ran while one was open for 7% of the time, Pallas kernels for 5%

profile of v3, /device:TPU:6, one launch (start us, length us, event | category | flops | bytes accessed | tf_op | source)
XLA Modules:
  0.0 149.9 jit_solution(5993372772595468005)
XLA Ops:
  0.0 0.9 copy-done
  0.9 0.9 copy-done.1
  1.9 0.9 copy-done.2
  2.8 0.9 copy-done.3
  3.7 1.1 shard_map.46
  4.7 32.2 %all_to_all.10 = bf16[16,192,128]{2,1,0:T(8,128)(2,1)S(1)} all-to-all(bf16[16,192,128]{2,1,0:T(8,128)(2,1)S(1)} %get-tuple-element.20), channel_id=1, replica_groups=mesh['x'=4,'zh'=4,'core'=2,'y'=8,'zl'=2] {'y','zl'}, dimensions={0} | all-to-all | bytes 1572864 | tf_op jit(solution)/shard_map/all_to_all | solution.py:193
  37.0 10.0 %collective-permute-start.1 = (bf16[2,528,128]{2,1,0:T(8,128)(2,1)S(1)}, bf16[2,528,128]{2,1,0:T(8,128)(2,1)S(1)}, u32[]{:S(2)}, u32[]{:S(2)}) collective-permute-start(bf16[2,528,128]{2,1,0:T(8,128)(2,1)S(1)} %pad_maximum_fusion.refs_0_), channel_id=1, source_target_pairs={{0,96},{32,0},{64,32},{96,64},{1,97},{33,1},{65,33},{97,65},{2,98}... | collective-permute-start | bytes 811016 | tf_op jit(solution)/shard_map/ppermute | solution.py:29
  47.0 1.9 %collective-permute-start = (bf16[2,528,128]{2,1,0:T(8,128)(2,1)S(1)}, bf16[2,528,128]{2,1,0:T(8,128)(2,1)}, u32[]{:S(2)}, u32[]{:S(2)}) collective-permute-start(bf16[2,528,128]{2,1,0:T(8,128)(2,1)S(1)} %pad_maximum_fusion.refs_0_), channel_id=1, source_target_pairs={{0,32},{32,64},{64,96},{96,0},{1,33},{33,65},{65,97},{97,1},{2,34}... | collective-permute-start | bytes 811016 | tf_op jit(solution)/shard_map/ppermute | solution.py:29
  49.0 2.4 %collective-permute-start.2 = (bf16[16,128,128]{2,1,0:T(8,128)(2,1)S(1)}, bf16[16,128,128]{2,1,0:T(8,128)(2,1)S(1)}, u32[]{:S(2)}, u32[]{:S(2)}) collective-permute-start(bf16[16,128,128]{2,1,0:T(8,128)(2,1)S(1)} %slice.107.refs_7_.refs_6_), channel_id=1, source_target_pairs={{0,128},{128,256},{256,384},{384,0},{1,129},{129,257},{257,385},{3... | collective-permute-start | bytes 1572872 | tf_op jit(solution)/shard_map/ppermute | solution.py:29
  51.4 3.5 %collective-permute-start.4 = (bf16[16,128,128]{2,1,0:T(8,128)(2,1)S(1)}, bf16[16,128,128]{2,1,0:T(8,128)(2,1)S(1)}, u32[]{:S(2)}, u32[]{:S(2)}) collective-permute-start(bf16[16,128,128]{2,1,0:T(8,128)(2,1)S(1)} %slice.107.refs_7_.refs_6_), channel_id=1, source_target_pairs={{0,384},{128,0},{256,128},{384,256},{1,385},{129,1},{257,129},{385... | collective-permute-start | bytes 1572872 | tf_op jit(solution)/shard_map/ppermute | solution.py:29
  54.8 3.3 %collective-permute-start.7 = (bf16[16,128,128]{2,1,0:T(8,128)(2,1)S(1)}, bf16[16,128,128]{2,1,0:T(8,128)(2,1)S(1)}, u32[]{:S(2)}, u32[]{:S(2)}) collective-permute-start(bf16[16,128,128]{2,1,0:T(8,128)(2,1)S(1)} %slice.107.refs_7_.refs_6_), channel_id=1, source_target_pairs={{0,256},{128,384},{256,0},{384,128},{1,257},{129,385},{257,1},{385... | collective-permute-start | bytes 1572872 | tf_op jit(solution)/shard_map/ppermute | solution.py:29
  58.9 1.9 %collective-permute-start.6 = (bf16[16,128,128]{2,1,0:T(8,128)(2,1)S(1)}, bf16[16,128,128]{2,1,0:T(8,128)(2,1)S(1)}, u32[]{:S(2)}, u32[]{:S(2)}) collective-permute-start(bf16[16,128,128]{2,1,0:T(8,128)(2,1)S(1)} %slice.107.refs_7_.refs_6_), channel_id=1, source_target_pairs={{0,16},{16,0},{1,17},{17,1},{2,18},{18,2},{3,19},{19,3},{4,20},{20... | collective-permute-start | bytes 1572872 | tf_op jit(solution)/shard_map/ppermute | solution.py:29
  60.9 6.0 %collective-permute-start.10 = (bf16[528,128]{1,0:T(8,128)(2,1)S(1)}, bf16[528,128]{1,0:T(8,128)(2,1)S(1)}, u32[]{:S(2)}, u32[]{:S(2)}) collective-permute-start(bf16[528,128]{1,0:T(8,128)(2,1)S(1)} %slice_bitcast_fusion.4), channel_id=1, source_target_pairs={{0,96},{32,0},{64,32},{96,64},{1,97},{33,1},{65,33},{97,65},{2,98}... | collective-permute-start | bytes 405512 | tf_op jit(solution)/shard_map/ppermute | solution.py:29
  66.8 1.6 %slice_bitcast_fusion.5 = bf16[528,128]{1,0:T(8,128)(2,1)} fusion(bf16[2,528,128]{2,1,0:T(8,128)(2,1)} %collective-permute-done.refs_1_), kind=kLoop, calls=%fused_computation.9 | loop fusion | bytes 270336 | tf_op jit(solution)/shard_map/squeeze | solution.py:209
  68.4 2.1 %collective-permute-start.3 = (bf16[16,128,128]{2,1,0:T(8,128)(2,1)S(1)}, bf16[16,128,128]{2,1,0:T(8,128)(2,1)S(1)}, u32[]{:S(2)}, u32[]{:S(2)}) collective-permute-start(bf16[16,128,128]{2,1,0:T(8,128)(2,1)S(1)} %collective-permute-done.2.refs_3_.refs_2_), channel_id=1, source_target_pairs={{0,16},{16,0},{1,17},{17,1},{2,18},{18,2},{3,19},{19,3},{4,20},{20... | collective-permute-start | bytes 1572872 | tf_op jit(solution)/shard_map/ppermute | solution.py:29
  70.6 6.6 %collective-permute-done.4.refs_5_.refs_4_ = bf16[16,128,128]{2,1,0:T(8,128)(2,1)S(1)} collective-permute-done((bf16[16,128,128]{2,1,0:T(8,128)(2,1)S(1)}, bf16[16,128,128]{2,1,0:T(8,128)(2,1)S(1)}, u32[]{:S(2)}, u32[]{:S(2)}) %collective-permute-start.4) | collective-permute-done | bytes 524320 | tf_op jit(solution)/shard_map/ppermute | solution.py:29
  77.1 1.9 %collective-permute-start.5 = (bf16[16,128,128]{2,1,0:T(8,128)(2,1)S(1)}, bf16[16,128,128]{2,1,0:T(8,128)(2,1)}, u32[]{:S(2)}, u32[]{:S(2)}) collective-permute-start(bf16[16,128,128]{2,1,0:T(8,128)(2,1)S(1)} %collective-permute-done.4.refs_5_.refs_4_), channel_id=1, source_target_pairs={{0,16},{16,0},{1,17},{17,1},{2,18},{18,2},{3,19},{19,3},{4,20},{20... | collective-permute-start | bytes 1572872 | tf_op jit(solution)/shard_map/ppermute | solution.py:29
  79.1 2.4 %collective-permute-start.8 = (bf16[16,128,128]{2,1,0:T(8,128)(2,1)S(1)}, bf16[16,128,128]{2,1,0:T(8,128)(2,1)}, u32[]{:S(2)}, u32[]{:S(2)}) collective-permute-start(bf16[16,128,128]{2,1,0:T(8,128)(2,1)S(1)} %collective-permute-done.7.refs_9_.refs_8_), channel_id=1, source_target_pairs={{0,16},{16,0},{1,17},{17,1},{2,18},{18,2},{3,19},{19,3},{4,20},{20... | collective-permute-start | bytes 1572872 | tf_op jit(solution)/shard_map/ppermute | solution.py:29
  81.5 1.3 slice_bitcast_fusion.8
  82.8 2.4 %collective-permute-start.9 = (bf16[528,128]{1,0:T(8,128)(2,1)}, bf16[528,128]{1,0:T(8,128)(2,1)}, u32[]{:S(2)}, u32[]{:S(2)}) collective-permute-start(bf16[528,128]{1,0:T(8,128)(2,1)} %slice_bitcast_fusion.5), channel_id=1, source_target_pairs={{0,32},{32,64},{64,96},{96,0},{1,33},{33,65},{65,97},{97,1},{2,34}... | collective-permute-start | bytes 405512 | tf_op jit(solution)/shard_map/ppermute | solution.py:29
  85.2 1.2 slice_bitcast_fusion.6
  86.4 3.8 %concatenate.13 = bf16[24,128]{1,0:T(8,128)(2,1)} concatenate(bf16[4,128]{1,0:T(4,128)(2,1)} %get-tuple-element.42, bf16[4,128]{1,0:T(4,128)(2,1)} %get-tuple-element.41, bf16[4,128]{1,0:T(4,128)(2,1)} %get-tuple-element.40, bf16[4,128]{1,0:T(4,128)(2,1)} %get-tuple-element.39, bf16[4,128]{1,0:T(4,128)(2,1)} %get-tuple-element.38, bf16[4,128]{1,0:T(4,128)(2,1)} %get-tuple-element.37), dimensions={0} | concatenate | bytes 12288 | tf_op jit(solution)/shard_map/concatenate | solution.py:178
  90.9 4.4 %collective-permute-done.9.refs_0_ = bf16[528,128]{1,0:T(8,128)(2,1)} collective-permute-done((bf16[528,128]{1,0:T(8,128)(2,1)}, bf16[528,128]{1,0:T(8,128)(2,1)}, u32[]{:S(2)}, u32[]{:S(2)}) %collective-permute-start.9) | collective-permute-done | bytes 135200 | tf_op jit(solution)/shard_map/ppermute | solution.py:29
  96.1 3.4 %shard_map.48 = (bf16[528,128]{1,0:T(8,128)(2,1)S(1)}, bf16[528,128]{1,0:T(8,128)(2,1)S(1)}) custom-call(s32[8]{0:T(128)S(1)} %stack.53.columns_ref, s32[8,128]{1,0:T(8,128)S(1)} %maximum_convert_fusion.picks_ref, bf16[528,128]{1,0:T(8,128)(2,1)} %collective-permute-done.9.refs_0_, bf16[528,128]{1,0:T(8,128)(2,1)S(1)} %collective-permute-done.10.refs_1_, ...), custom_call_target="tpu_custom_call" | custom-call | flops 536870912 | bytes 4194304 | tf_op jit(solution)/shard_map/pallas_call | solution.py:147
  99.5 3.4 %collective-permute-start.11 = (bf16[528,128]{1,0:T(8,128)(2,1)S(1)}, bf16[528,128]{1,0:T(8,128)(2,1)S(1)}, u32[]{:S(2)}, u32[]{:S(2)}) collective-permute-start(bf16[528,128]{1,0:T(8,128)(2,1)S(1)} %get-tuple-element.25), channel_id=1, source_target_pairs={{0,96},{32,0},{64,32},{96,64},{1,97},{33,1},{65,33},{97,65},{2,98}... | collective-permute-start | bytes 405512 | tf_op jit(solution)/shard_map/ppermute | solution.py:29
  103.0 3.3 %collective-permute-start.12 = (bf16[528,128]{1,0:T(8,128)(2,1)S(1)}, bf16[528,128]{1,0:T(8,128)(2,1)S(1)}, u32[]{:S(2)}, u32[]{:S(2)}) collective-permute-start(bf16[528,128]{1,0:T(8,128)(2,1)S(1)} %get-tuple-element.27), channel_id=1, source_target_pairs={{0,32},{32,64},{64,96},{96,0},{1,33},{33,65},{65,97},{97,1},{2,34}... | collective-permute-start | bytes 405512 | tf_op jit(solution)/shard_map/ppermute | solution.py:29
  106.3 6.8 %shard_map.47 = (bf16[528,128]{1,0:T(8,128)(2,1)S(1)}, bf16[528,128]{1,0:T(8,128)(2,1)S(1)}, bf16[528,128]{1,0:T(8,128)(2,1)S(1)}, bf16[528,128]{1,0:T(8,128)(2,...) custom-call(s32[8]{0:T(128)S(1)} %stack.53.columns_ref, s32[24,128]{1,0:T(8,128)S(1)} %convert_element_type.6.picks_ref, ...), custom_call_target="tpu_custom_call" | custom-call | flops 1610612736 | bytes 4194304 | tf_op jit(solution)/shard_map/pallas_call | solution.py:147
  113.9 4.3 %collective-permute-start.13 = (bf16[2,528,128]{2,1,0:T(8,128)(2,1)S(1)}, bf16[2,528,128]{2,1,0:T(8,128)(2,1)S(1)}, u32[]{:S(2)}, u32[]{:S(2)}) collective-permute-start(bf16[2,528,128]{2,1,0:T(8,128)(2,1)S(1)} %pad_maximum_fusion.1), channel_id=1, source_target_pairs={{0,96},{32,0},{64,32},{96,64},{1,97},{33,1},{65,33},{97,65},{2,98}... | collective-permute-start | bytes 811016 | tf_op jit(solution)/shard_map/ppermute | solution.py:29
  118.2 2.4 %collective-permute-start.14 = (bf16[2,528,128]{2,1,0:T(8,128)(2,1)S(1)}, bf16[2,528,128]{2,1,0:T(8,128)(2,1)S(1)}, u32[]{:S(2)}, u32[]{:S(2)}) collective-permute-start(bf16[2,528,128]{2,1,0:T(8,128)(2,1)S(1)} %pad_maximum_fusion.2), channel_id=1, source_target_pairs={{0,32},{32,64},{64,96},{96,0},{1,33},{33,65},{65,97},{97,1},{2,34}... | collective-permute-start | bytes 811016 | tf_op jit(solution)/shard_map/ppermute | solution.py:29
  120.6 7.6 %collective-permute-done.13 = bf16[2,528,128]{2,1,0:T(8,128)(2,1)S(1)} collective-permute-done((bf16[2,528,128]{2,1,0:T(8,128)(2,1)S(1)}, bf16[2,528,128]{2,1,0:T(8,128)(2,1)S(1)}, u32[]{:S(2)}, u32[]{:S(2)}) %collective-permute-start.13) | collective-permute-done | bytes 270368 | tf_op jit(solution)/shard_map/ppermute | solution.py:29
  128.3 4.5 %collective-permute-done.14 = bf16[2,528,128]{2,1,0:T(8,128)(2,1)S(1)} collective-permute-done((bf16[2,528,128]{2,1,0:T(8,128)(2,1)S(1)}, bf16[2,528,128]{2,1,0:T(8,128)(2,1)S(1)}, u32[]{:S(2)}, u32[]{:S(2)}) %collective-permute-start.14) | collective-permute-done | bytes 270368 | tf_op jit(solution)/shard_map/ppermute | solution.py:29
  133.4 15.8 %all_to_all.11.in_ref = bf16[16,64,128]{2,1,0:T(8,128)(2,1)S(1)} all-to-all(bf16[16,64,128]{2,1,0:T(8,128)(2,1)S(1)} %bitcast.43), channel_id=1, replica_groups=mesh['x'=4,'zh'=4,'core'=2,'y'=8,'zl'=2] {'y','zl'}, dimensions={0} | all-to-all | bytes 524288 | tf_op jit(solution)/shard_map/all_to_all | solution.py:217
  (37 shorter events, 4.3 us)
Async XLA Ops:
  0.0 0.9 copy-start
  0.9 0.9 copy-start.1
  1.9 0.9 copy-start.2
  2.8 0.9 copy-start.3
  37.0 21.9 %collective-permute-start.1 = (bf16[2,528,128]{2,1,0:T(8,128)(2,1)S(1)}, bf16[2,528,128]{2,1,0:T(8,128)(2,1)S(1)}, u32[]{:S(2)}, u32[]{:S(2)}) collective-permute-start(bf16[2,528,128]{2,1,0:T(8,128)(2,1)S(1)} %pad_maximum_fusion.refs_0_), channel_id=1, source_target_pairs={{0,96},{32,0},{64,32},{96,64},{1,97},{33,1},{65,33},{97,65},{2,98}... | collective-permute-start | bytes 811016 | tf_op jit(solution)/shard_map/ppermute | solution.py:29
  47.0 13.9 %collective-permute-start = (bf16[2,528,128]{2,1,0:T(8,128)(2,1)S(1)}, bf16[2,528,128]{2,1,0:T(8,128)(2,1)}, u32[]{:S(2)}, u32[]{:S(2)}) collective-permute-start(bf16[2,528,128]{2,1,0:T(8,128)(2,1)S(1)} %pad_maximum_fusion.refs_0_), channel_id=1, source_target_pairs={{0,32},{32,64},{64,96},{96,0},{1,33},{33,65},{65,97},{97,1},{2,34}... | collective-permute-start | bytes 811016 | tf_op jit(solution)/shard_map/ppermute | solution.py:29
  49.0 19.4 %collective-permute-start.2 = (bf16[16,128,128]{2,1,0:T(8,128)(2,1)S(1)}, bf16[16,128,128]{2,1,0:T(8,128)(2,1)S(1)}, u32[]{:S(2)}, u32[]{:S(2)}) collective-permute-start(bf16[16,128,128]{2,1,0:T(8,128)(2,1)S(1)} %slice.107.refs_7_.refs_6_), channel_id=1, source_target_pairs={{0,128},{128,256},{256,384},{384,0},{1,129},{129,257},{257,385},{3... | collective-permute-start | bytes 1572872 | tf_op jit(solution)/shard_map/ppermute | solution.py:29
  51.4 25.8 %collective-permute-start.4 = (bf16[16,128,128]{2,1,0:T(8,128)(2,1)S(1)}, bf16[16,128,128]{2,1,0:T(8,128)(2,1)S(1)}, u32[]{:S(2)}, u32[]{:S(2)}) collective-permute-start(bf16[16,128,128]{2,1,0:T(8,128)(2,1)S(1)} %slice.107.refs_7_.refs_6_), channel_id=1, source_target_pairs={{0,384},{128,0},{256,128},{384,256},{1,385},{129,1},{257,129},{385... | collective-permute-start | bytes 1572872 | tf_op jit(solution)/shard_map/ppermute | solution.py:29
  54.8 24.2 %collective-permute-start.7 = (bf16[16,128,128]{2,1,0:T(8,128)(2,1)S(1)}, bf16[16,128,128]{2,1,0:T(8,128)(2,1)S(1)}, u32[]{:S(2)}, u32[]{:S(2)}) collective-permute-start(bf16[16,128,128]{2,1,0:T(8,128)(2,1)S(1)} %slice.107.refs_7_.refs_6_), channel_id=1, source_target_pairs={{0,256},{128,384},{256,0},{384,128},{1,257},{129,385},{257,1},{385... | collective-permute-start | bytes 1572872 | tf_op jit(solution)/shard_map/ppermute | solution.py:29
  58.8 9.6 %copy-start.4 = (bf16[2,528,128]{2,1,0:T(8,128)(2,1)}, bf16[2,528,128]{2,1,0:T(8,128)(2,1)S(1)}, u32[]{:S(2)}) copy-start(bf16[2,528,128]{2,1,0:T(8,128)(2,1)S(1)} %collective-permute-done.1.refs_2_) | copy-start | bytes 811012
  58.9 37.2 %collective-permute-start.6 = (bf16[16,128,128]{2,1,0:T(8,128)(2,1)S(1)}, bf16[16,128,128]{2,1,0:T(8,128)(2,1)S(1)}, u32[]{:S(2)}, u32[]{:S(2)}) collective-permute-start(bf16[16,128,128]{2,1,0:T(8,128)(2,1)S(1)} %slice.107.refs_7_.refs_6_), channel_id=1, source_target_pairs={{0,16},{16,0},{1,17},{17,1},{2,18},{18,2},{3,19},{19,3},{4,20},{20... | collective-permute-start | bytes 1572872 | tf_op jit(solution)/shard_map/ppermute | solution.py:29
  60.9 21.9 %collective-permute-start.10 = (bf16[528,128]{1,0:T(8,128)(2,1)S(1)}, bf16[528,128]{1,0:T(8,128)(2,1)S(1)}, u32[]{:S(2)}, u32[]{:S(2)}) collective-permute-start(bf16[528,128]{1,0:T(8,128)(2,1)S(1)} %slice_bitcast_fusion.4), channel_id=1, source_target_pairs={{0,96},{32,0},{64,32},{96,64},{1,97},{33,1},{65,33},{97,65},{2,98}... | collective-permute-start | bytes 405512 | tf_op jit(solution)/shard_map/ppermute | solution.py:29
  68.4 27.6 %collective-permute-start.3 = (bf16[16,128,128]{2,1,0:T(8,128)(2,1)S(1)}, bf16[16,128,128]{2,1,0:T(8,128)(2,1)S(1)}, u32[]{:S(2)}, u32[]{:S(2)}) collective-permute-start(bf16[16,128,128]{2,1,0:T(8,128)(2,1)S(1)} %collective-permute-done.2.refs_3_.refs_2_), channel_id=1, source_target_pairs={{0,16},{16,0},{1,17},{17,1},{2,18},{18,2},{3,19},{19,3},{4,20},{20... | collective-permute-start | bytes 1572872 | tf_op jit(solution)/shard_map/ppermute | solution.py:29
  77.1 18.9 %collective-permute-start.5 = (bf16[16,128,128]{2,1,0:T(8,128)(2,1)S(1)}, bf16[16,128,128]{2,1,0:T(8,128)(2,1)}, u32[]{:S(2)}, u32[]{:S(2)}) collective-permute-start(bf16[16,128,128]{2,1,0:T(8,128)(2,1)S(1)} %collective-permute-done.4.refs_5_.refs_4_), channel_id=1, source_target_pairs={{0,16},{16,0},{1,17},{17,1},{2,18},{18,2},{3,19},{19,3},{4,20},{20... | collective-permute-start | bytes 1572872 | tf_op jit(solution)/shard_map/ppermute | solution.py:29
  79.1 17.0 %collective-permute-start.8 = (bf16[16,128,128]{2,1,0:T(8,128)(2,1)S(1)}, bf16[16,128,128]{2,1,0:T(8,128)(2,1)}, u32[]{:S(2)}, u32[]{:S(2)}) collective-permute-start(bf16[16,128,128]{2,1,0:T(8,128)(2,1)S(1)} %collective-permute-done.7.refs_9_.refs_8_), channel_id=1, source_target_pairs={{0,16},{16,0},{1,17},{17,1},{2,18},{18,2},{3,19},{19,3},{4,20},{20... | collective-permute-start | bytes 1572872 | tf_op jit(solution)/shard_map/ppermute | solution.py:29
  82.8 12.6 %collective-permute-start.9 = (bf16[528,128]{1,0:T(8,128)(2,1)}, bf16[528,128]{1,0:T(8,128)(2,1)}, u32[]{:S(2)}, u32[]{:S(2)}) collective-permute-start(bf16[528,128]{1,0:T(8,128)(2,1)} %slice_bitcast_fusion.5), channel_id=1, source_target_pairs={{0,32},{32,64},{64,96},{96,0},{1,33},{33,65},{65,97},{97,1},{2,34}... | collective-permute-start | bytes 405512 | tf_op jit(solution)/shard_map/ppermute | solution.py:29
  96.1 10.2 %copy-start.5 = (bf16[2,528,128]{2,1,0:T(8,128)(2,1)S(1)}, bf16[2,528,128]{2,1,0:T(8,128)(2,1)}, u32[]{:S(2)}) copy-start(bf16[2,528,128]{2,1,0:T(8,128)(2,1)} %copy-done.4) | copy-start | bytes 811012
  99.5 13.6 %collective-permute-start.11 = (bf16[528,128]{1,0:T(8,128)(2,1)S(1)}, bf16[528,128]{1,0:T(8,128)(2,1)S(1)}, u32[]{:S(2)}, u32[]{:S(2)}) collective-permute-start(bf16[528,128]{1,0:T(8,128)(2,1)S(1)} %get-tuple-element.25), channel_id=1, source_target_pairs={{0,96},{32,0},{64,32},{96,64},{1,97},{33,1},{65,33},{97,65},{2,98}... | collective-permute-start | bytes 405512 | tf_op jit(solution)/shard_map/ppermute | solution.py:29
  103.0 10.5 %collective-permute-start.12 = (bf16[528,128]{1,0:T(8,128)(2,1)S(1)}, bf16[528,128]{1,0:T(8,128)(2,1)S(1)}, u32[]{:S(2)}, u32[]{:S(2)}) collective-permute-start(bf16[528,128]{1,0:T(8,128)(2,1)S(1)} %get-tuple-element.27), channel_id=1, source_target_pairs={{0,32},{32,64},{64,96},{96,0},{1,33},{33,65},{65,97},{97,1},{2,34}... | collective-permute-start | bytes 405512 | tf_op jit(solution)/shard_map/ppermute | solution.py:29
  113.9 14.4 %collective-permute-start.13 = (bf16[2,528,128]{2,1,0:T(8,128)(2,1)S(1)}, bf16[2,528,128]{2,1,0:T(8,128)(2,1)S(1)}, u32[]{:S(2)}, u32[]{:S(2)}) collective-permute-start(bf16[2,528,128]{2,1,0:T(8,128)(2,1)S(1)} %pad_maximum_fusion.1), channel_id=1, source_target_pairs={{0,96},{32,0},{64,32},{96,64},{1,97},{33,1},{65,33},{97,65},{2,98}... | collective-permute-start | bytes 811016 | tf_op jit(solution)/shard_map/ppermute | solution.py:29
  118.2 14.6 %collective-permute-start.14 = (bf16[2,528,128]{2,1,0:T(8,128)(2,1)S(1)}, bf16[2,528,128]{2,1,0:T(8,128)(2,1)S(1)}, u32[]{:S(2)}, u32[]{:S(2)}) collective-permute-start(bf16[2,528,128]{2,1,0:T(8,128)(2,1)S(1)} %pad_maximum_fusion.2), channel_id=1, source_target_pairs={{0,32},{32,64},{64,96},{96,0},{1,33},{33,65},{65,97},{97,1},{2,34}... | collective-permute-start | bytes 811016 | tf_op jit(solution)/shard_map/ppermute | solution.py:29

commit v4 on v2

v4 whole, which is shorter than its diff:
```python
import functools
import math

import jax
import jax.numpy as jnp
from jax import lax
from jax.experimental import pallas as pl
from jax.experimental.pallas import tpu as pltpu
from jax.sharding import Mesh, PartitionSpec as P

BF = jnp.bfloat16
F32 = jnp.float32
NX, NZ, NC, NU = 4, 4, 2, 16
HEADS, HD, BS, TOK = 12, 128, 128, 64
SEGB = 8
GROUPS = NX * NC
HALF = 4
ROWS = HALF * BS
EXTRA = 16
EXP2 = math.log2(math.e) / math.sqrt(HD)
SHIFTS = (0, 1, 3, 2)
AXES = ("x", "zh", "core", "y", "zl")
VMEM = pl.BlockSpec(memory_space=pltpu.VMEM)
HBM = pl.BlockSpec(memory_space=pltpu.HBM)


def shift(field, axis, by):
    n = lax.axis_size(axis)
    return lax.ppermute(field, axis, [(i, (i + by) % n) for i in range(n)])


def pack_kernel(q_hbm, k_hbm, v_hbm, mask_hbm, out_ref, picks_ref, q_ref, k_ref, v_ref, mask_ref, sems):
    head = jnp.minimum(lax.axis_index("y") * 2 + lax.axis_index("zl"), HEADS - 1)
    pairs = ((q_hbm, q_ref), (k_hbm, k_ref), (v_hbm, v_ref), (mask_hbm.at[head], mask_ref))
    copies = [pltpu.make_async_copy(src, dst, sems.at[i]) for i, (src, dst) in enumerate(pairs)]
    for copy in copies:
        copy.start()
    for s in range(HEADS, NU):
        out_ref[s] = jnp.zeros((3 * TOK, HD), BF)
    for n, ref in enumerate((q_ref, k_ref, v_ref)):
        copies[n].wait()
        for h in range(HEADS):
            out_ref[h, n * TOK : (n + 1) * TOK, :] = ref[:, h * HD : (h + 1) * HD]
    copies[3].wait()
    live = mask_ref[...].astype(F32).astype(BF)
    cols = live.shape[1]
    i = lax.broadcasted_iota(jnp.int32, (cols, HD), 0)
    g = lax.broadcasted_iota(jnp.int32, (cols, HD), 1)
    weight = jnp.where(i // SEGB == g, i % SEGB, 0).astype(F32).astype(BF)
    picks = jnp.dot(live, weight, preferred_element_type=F32)
    pad = jnp.zeros((EXTRA - HALF, HD), F32)
    for half in range(2):
        picks_ref[half] = jnp.concatenate([picks[half * HALF : (half + 1) * HALF], pad], axis=0).astype(BF)


def split3(lse):
    hi = lse.astype(BF).astype(F32)
    mid = (lse - hi).astype(BF).astype(F32)
    return jnp.concatenate([hi, mid, lse - hi - mid, jnp.zeros_like(hi)], axis=0).astype(BF)


def join3(rows):
    rows = rows.astype(F32)
    return rows[0:HALF] + rows[HALF : 2 * HALF] + rows[2 * HALF : 3 * HALF]


def attend_kernel(halves, n_q, kv_slots, out_slots, *refs):
    def view(group, slot):
        return group[slot[0]] if slot[1] is None else group[slot[0]].at[slot[1]]

    n_kv, n_out = max(r for r, _ in kv_slots) + 1, max(r for r, _ in out_slots) + 1
    q_refs, kv_refs, out_refs = refs[:n_q], refs[n_q : n_q + n_kv], refs[n_q + n_kv : n_q + n_kv + n_out]
    flat_ref, picks_ref, sem = refs[n_q + n_kv + n_out :]
    for h, slot in enumerate(halves):
        flat_ref[h * SEGB : (h + 1) * SEGB, :] = view(q_refs, slot)[ROWS:, :].astype(F32)[:SEGB].astype(jnp.int32)
    fetch = pltpu.make_async_copy(flat_ref, picks_ref, sem)
    fetch.start()
    x, z, c = lax.axis_index("x"), lax.axis_index("zh"), lax.axis_index("core")
    columns = [((x + NX - dx) % NX * NZ + z) * NC + cc for dx in SHIFTS for cc in (c, 1 - c)]
    groups = [view(kv_refs, slot) for slot in kv_slots]
    outs = [view(out_refs, slot) for slot in out_slots]
    fetch.wait()
    blocks = [(h, b) for h in range(len(halves)) for b in range(HALF)]
    n = len(blocks)
    fetched, scores, weights, peaks, totals = {}, {}, {}, {}, {}
    lses = [[] for _ in halves]
    for t in range(n + 2):
        ahead, here, last = t, t - 1, t - 2
        if ahead < n:
            h, b = blocks[ahead]
            q = view(q_refs, halves[h])[b * BS : (b + 1) * BS, :]
            keys, values = [], []
            for g in range(GROUPS):
                j = picks_ref[h * SEGB + b, columns[g]]
                both = groups[g][pl.ds(2 * j, 2)]
                keys.append(both[:, :TOK, :].reshape(BS, HD))
                values.append(both[:, TOK:, :].reshape(BS, HD))
            fetched[ahead], scores[ahead] = (q, keys, values), []
        if 0 <= here < n:
            weights[here], peaks[here], totals[here] = [], [], []
        acc = None
        for step in range(4):
            if ahead < n:
                q, keys, _ = fetched[ahead]
                pair = jnp.concatenate(keys[2 * step : 2 * step + 2], axis=0)
                scores[ahead].append(
                    lax.dot_general(q, pair, (((1,), (1,)), ((), ())), preferred_element_type=F32)
                )
            if 0 <= here < n:
                rows = slice(step * BS // 4, (step + 1) * BS // 4)
                part = [s[rows] for s in scores[here]]
                peak = jnp.max(functools.reduce(jnp.maximum, part), axis=1, keepdims=True)
                w = [jnp.exp2((s - peak) * EXP2) for s in part]
                totals[here].append(jnp.sum(functools.reduce(jnp.add, w), axis=1, keepdims=True))
                peaks[here].append(peak)
                weights[here].append([p.astype(BF) for p in w])
            if 0 <= last < n:
                w = jnp.concatenate([p[step] for p in weights[last]], axis=0)
                pair = jnp.concatenate(fetched[last][2][2 * step : 2 * step + 2], axis=0)
                product = jnp.dot(w, pair, preferred_element_type=F32)
                acc = product if acc is None else acc + product
        if 0 <= last < n:
            h, b = blocks[last]
            peak, total = jnp.concatenate(peaks[last], axis=0), jnp.concatenate(totals[last], axis=0)
            outs[h][b * BS : (b + 1) * BS, :] = (acc * (1.0 / total)).astype(BF)
            lse = peak * EXP2 + jnp.log2(total)
            lses[h].append(jnp.transpose(jnp.broadcast_to(lse, (BS, HD)))[0:1, :])
            if b == HALF - 1:
                outs[h][ROWS:, :] = split3(jnp.concatenate(lses[h], axis=0))
            fetched[last] = scores[last] = weights[last] = None


def merge_halves(ins, out_ref, first, keep):
    lses = [join3(r[ROWS:, :]) for r in ins]
    top = functools.reduce(jnp.maximum, lses)
    parts = [jnp.exp2(s - top) for s in lses]
    total = functools.reduce(jnp.add, parts)
    parts = [p / total for p in parts]
    for b in range(HALF):
        rows = slice(b * BS, (b + 1) * BS)
        acc = jnp.zeros((BS, HD), F32)
        for r, p in zip(ins, parts):
            acc = acc + jnp.transpose(jnp.broadcast_to(p[b : b + 1, :], (BS, HD))) * r[rows, :].astype(F32)
        out_ref[first + b * BS : first + (b + 1) * BS, :] = acc.astype(BF)
    if keep:
        out_ref[ROWS:, :] = split3(top + jnp.log2(total))


def pass_kernel(o1_ref, o3_ref, via_a_ref, via_b_ref, out1_ref, out3_ref):
    out1_ref[0] = o1_ref[0]
    merge_halves([o1_ref.at[1], via_b_ref], out1_ref.at[1], 0, True)
    merge_halves([o3_ref.at[0], via_a_ref], out3_ref.at[0], 0, True)
    out3_ref[1] = o3_ref[1]


def final_kernel(a_ref, b_ref, c_ref, out_ref):
    for half in range(2):
        merge_halves([r.at[half] for r in (a_ref, b_ref, c_ref)], out_ref, half * ROWS, False)


def unpack_kernel(in_ref, out_ref):
    for h in range(HEADS):
        out_ref[:, h * HD : (h + 1) * HD] = in_ref[h]


def call(kernel, outs, specs, *args, scratch=(), flops=0, moved=1 << 18, vmem=24):
    return pl.pallas_call(
        kernel,
        out_shape=outs,
        in_specs=specs,
        out_specs=jax.tree.map(lambda _: VMEM, outs),
        scratch_shapes=list(scratch),
        compiler_params=pltpu.CompilerParams(vmem_limit_bytes=vmem << 20),
        cost_estimate=pl.CostEstimate(flops=flops, bytes_accessed=moved, transcendentals=0),
    )(*args)


def half_shape():
    return jax.ShapeDtypeStruct((ROWS + EXTRA, HD), BF)


def chunk_shape():
    return jax.ShapeDtypeStruct((2, ROWS + EXTRA, HD), BF)


def attend(queries, halves, outs, out_slots, kvs, kv_slots):
    n = len(halves)
    return call(
        functools.partial(attend_kernel, halves, len(queries), kv_slots, out_slots),
        outs, [VMEM] * (len(queries) + len(kvs)), *queries, *kvs,
        scratch=[pltpu.VMEM((n * SEGB, HD), jnp.int32), pltpu.SMEM((n * SEGB, HD), jnp.int32), pltpu.SemaphoreType.DMA],
        flops=n * (1 << 28), moved=4 << 20,
    )


def shards(queries, keys, values, block_mask):
    packed, picks = call(
        pack_kernel,
        (jax.ShapeDtypeStruct((NU, 3 * TOK, HD), BF), jax.ShapeDtypeStruct((2, EXTRA, HD), BF)),
        [HBM] * 4, queries, keys, values, block_mask,
        scratch=[pltpu.VMEM(queries.shape, BF)] * 3
        + [pltpu.VMEM(block_mask.shape[1:], jnp.int32), pltpu.SemaphoreType.DMA((4,))],
        vmem=60,
    )
    got = lax.all_to_all(packed, ("y", "zl"), split_axis=0, concat_axis=0, tiled=True)
    k0 = got[:, TOK:]
    q0 = jnp.concatenate([got[:, :TOK].reshape(2, ROWS, HD), picks], axis=1)

    k1, k3, k2 = (shift(k0, "x", dx) for dx in SHIFTS[1:])
    q1, q3 = shift(q0, "zh", 1), shift(q0, "zh", -1)
    c0 = shift(k0, "core", 1)
    q2a, q2b = shift(q1[0], "zh", 1), shift(q3[1], "zh", -1)
    c13 = shift(jnp.stack([k1, k3]), "core", 1)
    c2 = shift(k2, "core", 1)
    kvs = [k0, c0, k1, k3, c13, k2, c2]
    slots = ((0, None), (1, None), (2, None), (4, 0), (3, None), (4, 1), (5, None), (6, None))

    o2a, o2b = attend([q2a, q2b], ((0, None), (1, None)), [half_shape()] * 2, ((0, None), (1, None)), kvs, slots)
    via_a, via_b = shift(o2a, "zh", 1), shift(o2b, "zh", -1)
    four = ((0, 0), (0, 1), (1, 0), (1, 1))
    o1, o3 = attend([q1, q3], four, [chunk_shape()] * 2, four, kvs, slots)
    m1, m3 = call(pass_kernel, [chunk_shape()] * 2, [VMEM] * 4, o1, o3, via_a, via_b)
    m1, m3, q0 = lax.optimization_barrier((m1, m3, q0))
    back1, back3 = shift(m1, "zh", -1), shift(m3, "zh", 1)
    (o0,) = attend([q0], four[:2], [chunk_shape()], four[:2], kvs, slots)
    whole = call(final_kernel, jax.ShapeDtypeStruct((NU * TOK, HD), BF), [VMEM] * 3, o0, back1, back3)
    home = lax.all_to_all(whole.reshape(NU, TOK, HD), ("y", "zl"), split_axis=0, concat_axis=0, tiled=True)
    return call(unpack_kernel, jax.ShapeDtypeStruct((TOK, HEADS * HD), BF), [VMEM], home)


def solution(mesh):
    fine = Mesh(mesh.devices.reshape(NX, NZ, NC, NU // 2, 2), AXES)
    tokens = P(AXES, None)
    placed = (tokens, tokens, tokens, P(None, AXES[:3], None))
    return jax.shard_map(shards, mesh=fine, in_specs=placed, out_specs=tokens, check_vma=False)
```

time: 151 us -> 155 us (1.026)
  starting transfers between devices: 38.1 us -> 53.9 us
  between operations: 13.6 us -> 0.22 us
  waiting for transfers between devices: 28.4 us -> 35.6 us
  local copies, waits for them, and re-layouts: 6.96 us -> 0.74 us
  Pallas kernels: 11.4 us -> 13.8 us
    ppermute x8 -> x14, starting transfers between devices: 38.1 us -> 53.9 us  [shift(): return lax.ppermute(field, axis, [(i, (i + by) % n) for i in range(n)])]
    ppermute x8 -> x14, waiting for transfers between devices: 28.3 us -> 35.6 us  [shift(): return lax.ppermute(field, axis, [(i, (i + by) % n) for i in range(n)])]
    unnamed x12 -> x2, local copies, waits for them, and re-layouts: 5.86 us -> 0.67 us
    pallas_call x6 -> x7, Pallas kernels: 11.4 us -> 13.8 us  [call(): pl.pallas_call(kernel, out_shape=outs, in_specs=specs, out_specs=jax.tree...]
  transfers between devices with their start and end apart: 9 -> 14, of which waited for: 6 -> 8; matrix products, arithmetic and copies ran while one was open for 0% -> 0% of each run, Pallas kernels for 4% -> 5%
where the time goes in v4:
time: 155 us
  starting transfers between devices  53.9 us (35%)
  blocking collectives  50.2 us (32%)
  waiting for transfers between devices  35.6 us (23%)
  Pallas kernels  13.8 us (9%)
    ppermute x14, starting transfers between devices, shift(): return lax.ppermute(field, axis, [(i, (i + by) % n) for i in range(n)])  53.9 us
    ppermute x14, waiting for transfers between devices, shift(): return lax.ppermute(field, axis, [(i, (i + by) % n) for i in range(n)])  35.6 us
    all_to_all x1, blocking collectives, shards(): lax.all_to_all(packed, ('y', 'zl'), split_axis=0, concat_axis=0, tiled=True)  32.4 us
    all_to_all x1, blocking collectives, shards(): lax.all_to_all(whole.reshape(NU, TOK, HD), ('y', 'zl'), split_axis=0, con...  17.8 us
    pallas_call x7, Pallas kernels, call(): pl.pallas_call(kernel, out_shape=outs, in_specs=specs, out_specs=jax.tree...  13.8 us
  transfers between devices with their start and end apart: 14, of which 8 were waited for; matrix products, arithmetic and copies ran while one was open for 0% of the time, Pallas kernels for 5%

profile of v4, /device:TPU:6, one launch (start us, length us, event | category | flops | bytes accessed | tf_op | source)
XLA Modules:
  0.0 154.6 jit_solution(12304703459954710032)
XLA Ops:
  0.0 2.1 %shard_map.46 = (bf16[16,192,128]{2,1,0:T(8,128)(2,1)}, bf16[2,16,128]{2,1,0:T(8,128)(2,1)}) custom-call(bf16[64,1536]{1,0:T(8,128)(2,1)} %q_hbm.1, bf16[64,1536]{1,0:T(8,128)(2,1)} %k_hbm.1, bf16[64,1536]{1,0:T(8,128)(2,1)} %v_hbm.1, s32[12,8,256]{2,1,0:T(8,128)} %mask_hbm.1), custom_call_target="tpu_custom_call" | custom-call | bytes 262144 | tf_op jit(solution)/shard_map/pallas_call | solution.py:167
  2.1 32.4 %all_to_all.10 = bf16[16,192,128]{2,1,0:T(8,128)(2,1)S(1)} all-to-all(bf16[16,192,128]{2,1,0:T(8,128)(2,1)} %get-tuple-element.16), channel_id=1, replica_groups=mesh['x'=4,'zh'=4,'core'=2,'y'=8,'zl'=2] {'y','zl'}, dimensions={0} | all-to-all | bytes 1572864 | tf_op jit(solution)/shard_map/all_to_all | solution.py:205
  34.5 2.4 %collective-permute-start.3 = (bf16[16,128,128]{2,1,0:T(8,128)(2,1)S(1)}, bf16[16,128,128]{2,1,0:T(8,128)(2,1)S(1)}, u32[]{:S(2)}, u32[]{:S(2)}) collective-permute-start(bf16[16,128,128]{2,1,0:T(8,128)(2,1)S(1)} %slice.17.refs_2_.refs_1_), channel_id=1, source_target_pairs={{0,128},{128,256},{256,384},{384,0},{1,129},{129,257},{257,385},{3... | collective-permute-start | bytes 1572872 | tf_op jit(solution)/shard_map/ppermute | solution.py:29
  36.9 3.5 %collective-permute-start.4 = (bf16[16,128,128]{2,1,0:T(8,128)(2,1)S(1)}, bf16[16,128,128]{2,1,0:T(8,128)(2,1)S(1)}, u32[]{:S(2)}, u32[]{:S(2)}) collective-permute-start(bf16[16,128,128]{2,1,0:T(8,128)(2,1)S(1)} %slice.17.refs_2_.refs_1_), channel_id=1, source_target_pairs={{0,384},{128,0},{256,128},{384,256},{1,385},{129,1},{257,129},{385... | collective-permute-start | bytes 1572872 | tf_op jit(solution)/shard_map/ppermute | solution.py:29
  40.4 3.3 %collective-permute-start.6 = (bf16[16,128,128]{2,1,0:T(8,128)(2,1)S(1)}, bf16[16,128,128]{2,1,0:T(8,128)(2,1)S(1)}, u32[]{:S(2)}, u32[]{:S(2)}) collective-permute-start(bf16[16,128,128]{2,1,0:T(8,128)(2,1)S(1)} %slice.17.refs_2_.refs_1_), channel_id=1, source_target_pairs={{0,256},{128,384},{256,0},{384,128},{1,257},{129,385},{257,1},{385... | collective-permute-start | bytes 1572872 | tf_op jit(solution)/shard_map/ppermute | solution.py:29
  43.7 7.6 %collective-permute-done.3.refs_4_.refs_3_ = bf16[16,128,128]{2,1,0:T(8,128)(2,1)S(1)} collective-permute-done((bf16[16,128,128]{2,1,0:T(8,128)(2,1)S(1)}, bf16[16,128,128]{2,1,0:T(8,128)(2,1)S(1)}, u32[]{:S(2)}, u32[]{:S(2)}) %collective-permute-start.3) | collective-permute-done | bytes 524320 | tf_op jit(solution)/shard_map/ppermute | solution.py:29
  51.3 11.7 %collective-permute-done.4.refs_5_.refs_4_ = bf16[16,128,128]{2,1,0:T(8,128)(2,1)S(1)} collective-permute-done((bf16[16,128,128]{2,1,0:T(8,128)(2,1)S(1)}, bf16[16,128,128]{2,1,0:T(8,128)(2,1)S(1)}, u32[]{:S(2)}, u32[]{:S(2)}) %collective-permute-start.4) | collective-permute-done | bytes 524320 | tf_op jit(solution)/shard_map/ppermute | solution.py:29
  63.1 1.9 %collective-permute-start.5 = (bf16[2,16,128,128]{3,2,1,0:T(8,128)(2,1)S(1)}, bf16[2,16,128,128]{3,2,1,0:T(8,128)(2,1)S(1)}, u32[]{:S(2)}, u32[]{:S(2)}) collective-permute-start(bf16[2,16,128,128]{3,2,1,0:T(8,128)(2,1)S(1)} %pad_maximum_fusion), channel_id=1, source_target_pairs={{0,16},{16,0},{1,17},{17,1},{2,18},{18,2},{3,19},{19,3},{4,20},{20... | collective-permute-start | bytes 3145736 | tf_op jit(solution)/shard_map/ppermute | solution.py:29
  65.0 0.7 copy-done
  65.7 6.1 %collective-permute-start = (bf16[2,528,128]{2,1,0:T(8,128)(2,1)S(1)}, bf16[2,528,128]{2,1,0:T(8,128)(2,1)S(1)}, u32[]{:S(2)}, u32[]{:S(2)}) collective-permute-start(bf16[2,528,128]{2,1,0:T(8,128)(2,1)S(1)} %pad_maximum_fusion.1.refs_0_), channel_id=1, source_target_pairs={{0,32},{32,64},{64,96},{96,0},{1,33},{33,65},{65,97},{97,1},{2,34}... | collective-permute-start | bytes 811016 | tf_op jit(solution)/shard_map/ppermute | solution.py:29
  71.8 5.9 %collective-permute-start.1 = (bf16[2,528,128]{2,1,0:T(8,128)(2,1)S(1)}, bf16[2,528,128]{2,1,0:T(8,128)(2,1)S(1)}, u32[]{:S(2)}, u32[]{:S(2)}) collective-permute-start(bf16[2,528,128]{2,1,0:T(8,128)(2,1)S(1)} %pad_maximum_fusion.1.refs_0_), channel_id=1, source_target_pairs={{0,96},{32,0},{64,32},{96,64},{1,97},{33,1},{65,33},{97,65},{2,98}... | collective-permute-start | bytes 811016 | tf_op jit(solution)/shard_map/ppermute | solution.py:29
  77.7 2.1 %collective-permute-start.2 = (bf16[16,128,128]{2,1,0:T(8,128)(2,1)S(1)}, bf16[16,128,128]{2,1,0:T(8,128)(2,1)S(1)}, u32[]{:S(2)}, u32[]{:S(2)}) collective-permute-start(bf16[16,128,128]{2,1,0:T(8,128)(2,1)S(1)} %slice.17.refs_2_.refs_1_), channel_id=1, source_target_pairs={{0,16},{16,0},{1,17},{17,1},{2,18},{18,2},{3,19},{19,3},{4,20},{20... | collective-permute-start | bytes 1572872 | tf_op jit(solution)/shard_map/ppermute | solution.py:29
  79.8 2.2 %collective-permute-start.7 = (bf16[16,128,128]{2,1,0:T(8,128)(2,1)S(1)}, bf16[16,128,128]{2,1,0:T(8,128)(2,1)S(1)}, u32[]{:S(2)}, u32[]{:S(2)}) collective-permute-start(bf16[16,128,128]{2,1,0:T(8,128)(2,1)S(1)} %collective-permute-done.6.refs_7_.refs_6_), channel_id=1, source_target_pairs={{0,16},{16,0},{1,17},{17,1},{2,18},{18,2},{3,19},{19,3},{4,20},{20... | collective-permute-start | bytes 1572872 | tf_op jit(solution)/shard_map/ppermute | solution.py:29
  82.0 6.6 %collective-permute-done.refs_0_ = bf16[2,528,128]{2,1,0:T(8,128)(2,1)S(1)} collective-permute-done((bf16[2,528,128]{2,1,0:T(8,128)(2,1)S(1)}, bf16[2,528,128]{2,1,0:T(8,128)(2,1)S(1)}, u32[]{:S(2)}, u32[]{:S(2)}) %collective-permute-start) | collective-permute-done | bytes 270368 | tf_op jit(solution)/shard_map/ppermute | solution.py:29
  88.7 1.9 %collective-permute-start.8 = (bf16[528,128]{1,0:T(8,128)(2,1)S(1)}, bf16[528,128]{1,0:T(8,128)(2,1)S(1)}, u32[]{:S(2)}, u32[]{:S(2)}) collective-permute-start(bf16[528,128]{1,0:T(8,128)(2,1)S(1)} %slice_bitcast_fusion.1), channel_id=1, source_target_pairs={{0,32},{32,64},{64,96},{96,0},{1,33},{33,65},{65,97},{97,1},{2,34}... | collective-permute-start | bytes 405512 | tf_op jit(solution)/shard_map/ppermute | solution.py:29
  90.6 6.0 %collective-permute-start.9 = (bf16[528,128]{1,0:T(8,128)(2,1)S(1)}, bf16[528,128]{1,0:T(8,128)(2,1)S(1)}, u32[]{:S(2)}, u32[]{:S(2)}) collective-permute-start(bf16[528,128]{1,0:T(8,128)(2,1)S(1)} %slice_bitcast_fusion), channel_id=1, source_target_pairs={{0,96},{32,0},{64,32},{96,64},{1,97},{33,1},{65,33},{97,65},{2,98}... | collective-permute-start | bytes 405512 | tf_op jit(solution)/shard_map/ppermute | solution.py:29
  96.7 2.4 %collective-permute-done.8.refs_0_ = bf16[528,128]{1,0:T(8,128)(2,1)S(1)} collective-permute-done((bf16[528,128]{1,0:T(8,128)(2,1)S(1)}, bf16[528,128]{1,0:T(8,128)(2,1)S(1)}, u32[]{:S(2)}, u32[]{:S(2)}) %collective-permute-start.8) | collective-permute-done | bytes 135200 | tf_op jit(solution)/shard_map/ppermute | solution.py:29
  99.0 2.5 %collective-permute-done.9.refs_1_ = bf16[528,128]{1,0:T(8,128)(2,1)S(1)} collective-permute-done((bf16[528,128]{1,0:T(8,128)(2,1)S(1)}, bf16[528,128]{1,0:T(8,128)(2,1)S(1)}, u32[]{:S(2)}, u32[]{:S(2)}) %collective-permute-start.9) | collective-permute-done | bytes 135200 | tf_op jit(solution)/shard_map/ppermute | solution.py:29
  101.5 2.8 %shard_map.48 = (bf16[528,128]{1,0:T(8,128)(2,1)S(1)}, bf16[528,128]{1,0:T(8,128)(2,1)S(1)}) custom-call(bf16[528,128]{1,0:T(8,128)(2,1)S(1)} %collective-permute-done.8.refs_0_, bf16[528,128]{1,0:T(8,128)(2,1)S(1)} %collective-permute-done.9.refs_1_, bf16[16,128,128]{2,1,0:T(8,128)(2,1)S(1)} %slice.17.refs_2_.refs_1_, ...), custom_call_target="tpu_custom_call" | custom-call | flops 536870912 | bytes 4194304 | tf_op jit(solution)/shard_map/pallas_call | solution.py:167
  104.4 4.4 %collective-permute-start.10 = (bf16[528,128]{1,0:T(8,128)(2,1)S(1)}, bf16[528,128]{1,0:T(8,128)(2,1)S(1)}, u32[]{:S(2)}, u32[]{:S(2)}) collective-permute-start(bf16[528,128]{1,0:T(8,128)(2,1)S(1)} %get-tuple-element.20), channel_id=1, source_target_pairs={{0,32},{32,64},{64,96},{96,0},{1,33},{33,65},{65,97},{97,1},{2,34}... | collective-permute-start | bytes 405512 | tf_op jit(solution)/shard_map/ppermute | solution.py:29
  108.8 3.6 %collective-permute-start.11 = (bf16[528,128]{1,0:T(8,128)(2,1)S(1)}, bf16[528,128]{1,0:T(8,128)(2,1)S(1)}, u32[]{:S(2)}, u32[]{:S(2)}) collective-permute-start(bf16[528,128]{1,0:T(8,128)(2,1)S(1)} %get-tuple-element.21), channel_id=1, source_target_pairs={{0,96},{32,0},{64,32},{96,64},{1,97},{33,1},{65,33},{97,65},{2,98}... | collective-permute-start | bytes 405512 | tf_op jit(solution)/shard_map/ppermute | solution.py:29
  112.3 4.6 %shard_map.47 = (bf16[2,528,128]{2,1,0:T(8,128)(2,1)S(1)}, bf16[2,528,128]{2,1,0:T(8,128)(2,1)S(1)}) custom-call(bf16[2,528,128]{2,1,0:T(8,128)(2,1)S(1)} %collective-permute-done.refs_0_, bf16[2,528,128]{2,1,0:T(8,128)(2,1)S(1)} %collective-permute-done.1.refs_1_, bf16[16,128,128]{2,1,0:T(8,128)(2,1)S(1)} %slice.17.refs_2_.refs_1_, ...), custom_call_target="tpu_custom_call" | custom-call | flops 1073741824 | bytes 4194304 | tf_op jit(solution)/shard_map/pallas_call | solution.py:167
  116.9 0.1 collective-permute-done.11.via_b_ref
  117.0 0.4 shard_map.49
  117.4 4.8 %collective-permute-start.12 = (bf16[2,528,128]{2,1,0:T(8,128)(2,1)S(1)}, bf16[2,528,128]{2,1,0:T(8,128)(2,1)S(1)}, u32[]{:S(2)}, u32[]{:S(2)}) collective-permute-start(bf16[2,528,128]{2,1,0:T(8,128)(2,1)S(1)} %get-tuple-element.25), channel_id=1, source_target_pairs={{0,96},{32,0},{64,32},{96,64},{1,97},{33,1},{65,33},{97,65},{2,98}... | collective-permute-start | bytes 811016 | tf_op jit(solution)/shard_map/ppermute | solution.py:29
  122.2 5.8 %collective-permute-start.13 = (bf16[2,528,128]{2,1,0:T(8,128)(2,1)S(1)}, bf16[2,528,128]{2,1,0:T(8,128)(2,1)S(1)}, u32[]{:S(2)}, u32[]{:S(2)}) collective-permute-start(bf16[2,528,128]{2,1,0:T(8,128)(2,1)S(1)} %get-tuple-element.26), channel_id=1, source_target_pairs={{0,32},{32,64},{64,96},{96,0},{1,33},{33,65},{65,97},{97,1},{2,34}... | collective-permute-start | bytes 811016 | tf_op jit(solution)/shard_map/ppermute | solution.py:29
  128.1 2.8 %shard_map.50.a_ref = bf16[2,528,128]{2,1,0:T(8,128)(2,1)S(1)} custom-call(bf16[2,528,128]{2,1,0:T(8,128)(2,1)S(1)} %pad_maximum_fusion.1.refs_0_, bf16[16,128,128]{2,1,0:T(8,128)(2,1)S(1)} %slice.17.refs_2_.refs_1_, bf16[16,128,128]{2,1,0:T(8,128)(2,1)S(1)} %collective-permute-done.2.refs_3_.refs_2_, ...), custom_call_target="tpu_custom_call" | custom-call | flops 536870912 | bytes 4194304 | tf_op jit(solution)/shard_map/pallas_call | solution.py:167
  130.9 2.6 %collective-permute-done.12.b_ref = bf16[2,528,128]{2,1,0:T(8,128)(2,1)S(1)} collective-permute-done((bf16[2,528,128]{2,1,0:T(8,128)(2,1)S(1)}, bf16[2,528,128]{2,1,0:T(8,128)(2,1)S(1)}, u32[]{:S(2)}, u32[]{:S(2)}) %collective-permute-start.12) | collective-permute-done | bytes 270368 | tf_op jit(solution)/shard_map/ppermute | solution.py:29
  133.5 2.1 %collective-permute-done.13.c_ref = bf16[2,528,128]{2,1,0:T(8,128)(2,1)S(1)} collective-permute-done((bf16[2,528,128]{2,1,0:T(8,128)(2,1)S(1)}, bf16[2,528,128]{2,1,0:T(8,128)(2,1)S(1)}, u32[]{:S(2)}, u32[]{:S(2)}) %collective-permute-start.13) | collective-permute-done | bytes 270368 | tf_op jit(solution)/shard_map/ppermute | solution.py:29
  135.6 0.5 shard_map.51
  136.1 17.8 %all_to_all.11.in_ref = bf16[16,64,128]{2,1,0:T(8,128)(2,1)S(1)} all-to-all(bf16[16,64,128]{2,1,0:T(8,128)(2,1)S(1)} %bitcast.10), channel_id=1, replica_groups=mesh['x'=4,'zh'=4,'core'=2,'y'=8,'zl'=2] {'y','zl'}, dimensions={0} | all-to-all | bytes 524288 | tf_op jit(solution)/shard_map/all_to_all | solution.py:227
  153.9 0.7 shard_map.52
  (13 shorter events, 0.2 us)
Async XLA Ops:
  34.5 16.8 %collective-permute-start.3 = (bf16[16,128,128]{2,1,0:T(8,128)(2,1)S(1)}, bf16[16,128,128]{2,1,0:T(8,128)(2,1)S(1)}, u32[]{:S(2)}, u32[]{:S(2)}) collective-permute-start(bf16[16,128,128]{2,1,0:T(8,128)(2,1)S(1)} %slice.17.refs_2_.refs_1_), channel_id=1, source_target_pairs={{0,128},{128,256},{256,384},{384,0},{1,129},{129,257},{257,385},{3... | collective-permute-start | bytes 1572872 | tf_op jit(solution)/shard_map/ppermute | solution.py:29
  36.9 26.0 %collective-permute-start.4 = (bf16[16,128,128]{2,1,0:T(8,128)(2,1)S(1)}, bf16[16,128,128]{2,1,0:T(8,128)(2,1)S(1)}, u32[]{:S(2)}, u32[]{:S(2)}) collective-permute-start(bf16[16,128,128]{2,1,0:T(8,128)(2,1)S(1)} %slice.17.refs_2_.refs_1_), channel_id=1, source_target_pairs={{0,384},{128,0},{256,128},{384,256},{1,385},{129,1},{257,129},{385... | collective-permute-start | bytes 1572872 | tf_op jit(solution)/shard_map/ppermute | solution.py:29
  40.4 39.4 %collective-permute-start.6 = (bf16[16,128,128]{2,1,0:T(8,128)(2,1)S(1)}, bf16[16,128,128]{2,1,0:T(8,128)(2,1)S(1)}, u32[]{:S(2)}, u32[]{:S(2)}) collective-permute-start(bf16[16,128,128]{2,1,0:T(8,128)(2,1)S(1)} %slice.17.refs_2_.refs_1_), channel_id=1, source_target_pairs={{0,256},{128,384},{256,0},{384,128},{1,257},{129,385},{257,1},{385... | collective-permute-start | bytes 1572872 | tf_op jit(solution)/shard_map/ppermute | solution.py:29
  63.1 38.5 %collective-permute-start.5 = (bf16[2,16,128,128]{3,2,1,0:T(8,128)(2,1)S(1)}, bf16[2,16,128,128]{3,2,1,0:T(8,128)(2,1)S(1)}, u32[]{:S(2)}, u32[]{:S(2)}) collective-permute-start(bf16[2,16,128,128]{3,2,1,0:T(8,128)(2,1)S(1)} %pad_maximum_fusion), channel_id=1, source_target_pairs={{0,16},{16,0},{1,17},{17,1},{2,18},{18,2},{3,19},{19,3},{4,20},{20... | collective-permute-start | bytes 3145736 | tf_op jit(solution)/shard_map/ppermute | solution.py:29
  65.0 0.7 copy-start
  65.7 23.0 %collective-permute-start = (bf16[2,528,128]{2,1,0:T(8,128)(2,1)S(1)}, bf16[2,528,128]{2,1,0:T(8,128)(2,1)S(1)}, u32[]{:S(2)}, u32[]{:S(2)}) collective-permute-start(bf16[2,528,128]{2,1,0:T(8,128)(2,1)S(1)} %pad_maximum_fusion.1.refs_0_), channel_id=1, source_target_pairs={{0,32},{32,64},{64,96},{96,0},{1,33},{33,65},{65,97},{97,1},{2,34}... | collective-permute-start | bytes 811016 | tf_op jit(solution)/shard_map/ppermute | solution.py:29
  71.8 18.8 %collective-permute-start.1 = (bf16[2,528,128]{2,1,0:T(8,128)(2,1)S(1)}, bf16[2,528,128]{2,1,0:T(8,128)(2,1)S(1)}, u32[]{:S(2)}, u32[]{:S(2)}) collective-permute-start(bf16[2,528,128]{2,1,0:T(8,128)(2,1)S(1)} %pad_maximum_fusion.1.refs_0_), channel_id=1, source_target_pairs={{0,96},{32,0},{64,32},{96,64},{1,97},{33,1},{65,33},{97,65},{2,98}... | collective-permute-start | bytes 811016 | tf_op jit(solution)/shard_map/ppermute | solution.py:29
  77.7 23.8 %collective-permute-start.2 = (bf16[16,128,128]{2,1,0:T(8,128)(2,1)S(1)}, bf16[16,128,128]{2,1,0:T(8,128)(2,1)S(1)}, u32[]{:S(2)}, u32[]{:S(2)}) collective-permute-start(bf16[16,128,128]{2,1,0:T(8,128)(2,1)S(1)} %slice.17.refs_2_.refs_1_), channel_id=1, source_target_pairs={{0,16},{16,0},{1,17},{17,1},{2,18},{18,2},{3,19},{19,3},{4,20},{20... | collective-permute-start | bytes 1572872 | tf_op jit(solution)/shard_map/ppermute | solution.py:29
  79.8 21.7 %collective-permute-start.7 = (bf16[16,128,128]{2,1,0:T(8,128)(2,1)S(1)}, bf16[16,128,128]{2,1,0:T(8,128)(2,1)S(1)}, u32[]{:S(2)}, u32[]{:S(2)}) collective-permute-start(bf16[16,128,128]{2,1,0:T(8,128)(2,1)S(1)} %collective-permute-done.6.refs_7_.refs_6_), channel_id=1, source_target_pairs={{0,16},{16,0},{1,17},{17,1},{2,18},{18,2},{3,19},{19,3},{4,20},{20... | collective-permute-start | bytes 1572872 | tf_op jit(solution)/shard_map/ppermute | solution.py:29
  88.7 10.4 %collective-permute-start.8 = (bf16[528,128]{1,0:T(8,128)(2,1)S(1)}, bf16[528,128]{1,0:T(8,128)(2,1)S(1)}, u32[]{:S(2)}, u32[]{:S(2)}) collective-permute-start(bf16[528,128]{1,0:T(8,128)(2,1)S(1)} %slice_bitcast_fusion.1), channel_id=1, source_target_pairs={{0,32},{32,64},{64,96},{96,0},{1,33},{33,65},{65,97},{97,1},{2,34}... | collective-permute-start | bytes 405512 | tf_op jit(solution)/shard_map/ppermute | solution.py:29
  90.6 10.9 %collective-permute-start.9 = (bf16[528,128]{1,0:T(8,128)(2,1)S(1)}, bf16[528,128]{1,0:T(8,128)(2,1)S(1)}, u32[]{:S(2)}, u32[]{:S(2)}) collective-permute-start(bf16[528,128]{1,0:T(8,128)(2,1)S(1)} %slice_bitcast_fusion), channel_id=1, source_target_pairs={{0,96},{32,0},{64,32},{96,64},{1,97},{33,1},{65,33},{97,65},{2,98}... | collective-permute-start | bytes 405512 | tf_op jit(solution)/shard_map/ppermute | solution.py:29
  104.4 12.5 %collective-permute-start.10 = (bf16[528,128]{1,0:T(8,128)(2,1)S(1)}, bf16[528,128]{1,0:T(8,128)(2,1)S(1)}, u32[]{:S(2)}, u32[]{:S(2)}) collective-permute-start(bf16[528,128]{1,0:T(8,128)(2,1)S(1)} %get-tuple-element.20), channel_id=1, source_target_pairs={{0,32},{32,64},{64,96},{96,0},{1,33},{33,65},{65,97},{97,1},{2,34}... | collective-permute-start | bytes 405512 | tf_op jit(solution)/shard_map/ppermute | solution.py:29
  108.8 8.3 %collective-permute-start.11 = (bf16[528,128]{1,0:T(8,128)(2,1)S(1)}, bf16[528,128]{1,0:T(8,128)(2,1)S(1)}, u32[]{:S(2)}, u32[]{:S(2)}) collective-permute-start(bf16[528,128]{1,0:T(8,128)(2,1)S(1)} %get-tuple-element.21), channel_id=1, source_target_pairs={{0,96},{32,0},{64,32},{96,64},{1,97},{33,1},{65,33},{97,65},{2,98}... | collective-permute-start | bytes 405512 | tf_op jit(solution)/shard_map/ppermute | solution.py:29
  117.4 16.1 %collective-permute-start.12 = (bf16[2,528,128]{2,1,0:T(8,128)(2,1)S(1)}, bf16[2,528,128]{2,1,0:T(8,128)(2,1)S(1)}, u32[]{:S(2)}, u32[]{:S(2)}) collective-permute-start(bf16[2,528,128]{2,1,0:T(8,128)(2,1)S(1)} %get-tuple-element.25), channel_id=1, source_target_pairs={{0,96},{32,0},{64,32},{96,64},{1,97},{33,1},{65,33},{97,65},{2,98}... | collective-permute-start | bytes 811016 | tf_op jit(solution)/shard_map/ppermute | solution.py:29
  122.2 13.4 %collective-permute-start.13 = (bf16[2,528,128]{2,1,0:T(8,128)(2,1)S(1)}, bf16[2,528,128]{2,1,0:T(8,128)(2,1)S(1)}, u32[]{:S(2)}, u32[]{:S(2)}) collective-permute-start(bf16[2,528,128]{2,1,0:T(8,128)(2,1)S(1)} %get-tuple-element.26), channel_id=1, source_target_pairs={{0,32},{32,64},{64,96},{96,0},{1,33},{33,65},{65,97},{97,1},{2,34}... | collective-permute-start | bytes 811016 | tf_op jit(solution)/shard_map/ppermute | solution.py:29

commit v5 on v4

--- a/solution.py
+++ b/solution.py
@@ -208,12 +208,13 @@
 
     k1, k3, k2 = (shift(k0, "x", dx) for dx in SHIFTS[1:])
     q1, q3 = shift(q0, "zh", 1), shift(q0, "zh", -1)
+    q1, q3, k0, k1, k3, k2 = lax.optimization_barrier((q1, q3, k0, k1, k3, k2))
     c0 = shift(k0, "core", 1)
     q2a, q2b = shift(q1[0], "zh", 1), shift(q3[1], "zh", -1)
-    c13 = shift(jnp.stack([k1, k3]), "core", 1)
-    c2 = shift(k2, "core", 1)
-    kvs = [k0, c0, k1, k3, c13, k2, c2]
-    slots = ((0, None), (1, None), (2, None), (4, 0), (3, None), (4, 1), (5, None), (6, None))
+    near = jnp.stack([k1, k3, k2])
+    far = shift(near, "core", 1)
+    kvs = [k0, c0, near, far]
+    slots = ((0, None), (1, None), (2, 0), (3, 0), (2, 1), (3, 1), (2, 2), (3, 2))
 
     o2a, o2b = attend([q2a, q2b], ((0, None), (1, None)), [half_shape()] * 2, ((0, None), (1, None)), kvs, slots)
     via_a, via_b = shift(o2a, "zh", 1), shift(o2b, "zh", -1)

time: 155 us -> 141 us (0.910)
  waiting for transfers between devices: 35.6 us -> 26.8 us
  starting transfers between devices: 53.9 us -> 49.8 us
    ppermute x14 -> x13, waiting for transfers between devices: 35.6 us -> 26.8 us  [shift(): return lax.ppermute(field, axis, [(i, (i + by) % n) for i in range(n)])]
    ppermute x14 -> x13, starting transfers between devices: 53.9 us -> 49.8 us  [shift(): return lax.ppermute(field, axis, [(i, (i + by) % n) for i in range(n)])]
  transfers between devices with their start and end apart: 14 -> 13, of which waited for: 8 -> 7; matrix products, arithmetic and copies ran while one was open for 0% -> 0% of each run, Pallas kernels for 5% -> 5%
where the time goes in v5:
time: 141 us; the launch traced here: 140 us
  starting transfers between devices  49.8 us (35%)
  blocking collectives  49.6 us (35%)
  waiting for transfers between devices  26.8 us (19%)
  Pallas kernels  13.8 us (10%)
    ppermute x13, starting transfers between devices, shift(): return lax.ppermute(field, axis, [(i, (i + by) % n) for i in range(n)])  49.8 us
    all_to_all x1, blocking collectives, shards(): lax.all_to_all(packed, ('y', 'zl'), split_axis=0, concat_axis=0, tiled=True)  32.4 us
    ppermute x13, waiting for transfers between devices, shift(): return lax.ppermute(field, axis, [(i, (i + by) % n) for i in range(n)])  26.8 us
    all_to_all x1, blocking collectives, shards(): lax.all_to_all(whole.reshape(NU, TOK, HD), ('y', 'zl'), split_axis=0, con...  17.2 us
    pallas_call x7, Pallas kernels, call(): pl.pallas_call(kernel, out_shape=outs, in_specs=specs, out_specs=jax.tree...  13.8 us
  transfers between devices with their start and end apart: 13, of which 7 were waited for; matrix products, arithmetic and copies ran while one was open for 0% of the time, Pallas kernels for 5%

profile of v5, /device:TPU:6, one launch (start us, length us, event | category | flops | bytes accessed | tf_op | source)
XLA Modules:
  0.0 140.4 jit_solution(4567747492740639664)
XLA Ops:
  0.0 2.1 %shard_map.46 = (bf16[16,192,128]{2,1,0:T(8,128)(2,1)}, bf16[2,16,128]{2,1,0:T(8,128)(2,1)}) custom-call(bf16[64,1536]{1,0:T(8,128)(2,1)} %q_hbm.1, bf16[64,1536]{1,0:T(8,128)(2,1)} %k_hbm.1, bf16[64,1536]{1,0:T(8,128)(2,1)} %v_hbm.1, s32[12,8,256]{2,1,0:T(8,128)} %mask_hbm.1), custom_call_target="tpu_custom_call" | custom-call | bytes 262144 | tf_op jit(solution)/shard_map/pallas_call | solution.py:167
  2.1 0.0 copy-start
  2.1 32.4 %all_to_all.10 = bf16[16,192,128]{2,1,0:T(8,128)(2,1)S(1)} all-to-all(bf16[16,192,128]{2,1,0:T(8,128)(2,1)} %get-tuple-element.22), channel_id=1, replica_groups=mesh['x'=4,'zh'=4,'core'=2,'y'=8,'zl'=2] {'y','zl'}, dimensions={0} | all-to-all | bytes 1572864 | tf_op jit(solution)/shard_map/all_to_all | solution.py:205
  34.5 3.3 %collective-permute-start.4 = (bf16[16,128,128]{2,1,0:T(8,128)(2,1)S(1)}, bf16[16,128,128]{2,1,0:T(8,128)(2,1)S(1)}, u32[]{:S(2)}, u32[]{:S(2)}) collective-permute-start(bf16[16,128,128]{2,1,0:T(8,128)(2,1)S(1)} %slice.17.refs_2_.refs_1_), channel_id=1, source_target_pairs={{0,256},{128,384},{256,0},{384,128},{1,257},{129,385},{257,1},{385... | collective-permute-start | bytes 1572872 | tf_op jit(solution)/shard_map/ppermute | solution.py:29
  37.9 1.9 %collective-permute-start.3 = (bf16[16,128,128]{2,1,0:T(8,128)(2,1)S(1)}, bf16[16,128,128]{2,1,0:T(8,128)(2,1)S(1)}, u32[]{:S(2)}, u32[]{:S(2)}) collective-permute-start(bf16[16,128,128]{2,1,0:T(8,128)(2,1)S(1)} %slice.17.refs_2_.refs_1_), channel_id=1, source_target_pairs={{0,384},{128,0},{256,128},{384,256},{1,385},{129,1},{257,129},{385... | collective-permute-start | bytes 1572872 | tf_op jit(solution)/shard_map/ppermute | solution.py:29
  39.8 5.1 %collective-permute-start.2 = (bf16[16,128,128]{2,1,0:T(8,128)(2,1)S(1)}, bf16[16,128,128]{2,1,0:T(8,128)(2,1)S(1)}, u32[]{:S(2)}, u32[]{:S(2)}) collective-permute-start(bf16[16,128,128]{2,1,0:T(8,128)(2,1)S(1)} %slice.17.refs_2_.refs_1_), channel_id=1, source_target_pairs={{0,128},{128,256},{256,384},{384,0},{1,129},{129,257},{257,385},{3... | collective-permute-start | bytes 1572872 | tf_op jit(solution)/shard_map/ppermute | solution.py:29
  45.0 10.0 %collective-permute-start.1 = (bf16[2,528,128]{2,1,0:T(8,128)(2,1)S(1)}, bf16[2,528,128]{2,1,0:T(8,128)(2,1)S(1)}, u32[]{:S(2)}, u32[]{:S(2)}) collective-permute-start(bf16[2,528,128]{2,1,0:T(8,128)(2,1)S(1)} %pad_maximum_fusion.1.refs_0_), channel_id=1, source_target_pairs={{0,96},{32,0},{64,32},{96,64},{1,97},{33,1},{65,33},{97,65},{2,98}... | collective-permute-start | bytes 811016 | tf_op jit(solution)/shard_map/ppermute | solution.py:29
  55.0 1.9 %collective-permute-start = (bf16[2,528,128]{2,1,0:T(8,128)(2,1)S(1)}, bf16[2,528,128]{2,1,0:T(8,128)(2,1)S(1)}, u32[]{:S(2)}, u32[]{:S(2)}) collective-permute-start(bf16[2,528,128]{2,1,0:T(8,128)(2,1)S(1)} %pad_maximum_fusion.1.refs_0_), channel_id=1, source_target_pairs={{0,32},{32,64},{64,96},{96,0},{1,33},{33,65},{65,97},{97,1},{2,34}... | collective-permute-start | bytes 811016 | tf_op jit(solution)/shard_map/ppermute | solution.py:29
  57.0 6.8 %collective-permute-done.1.refs_1_ = bf16[2,528,128]{2,1,0:T(8,128)(2,1)S(1)} collective-permute-done((bf16[2,528,128]{2,1,0:T(8,128)(2,1)S(1)}, bf16[2,528,128]{2,1,0:T(8,128)(2,1)S(1)}, u32[]{:S(2)}, u32[]{:S(2)}) %collective-permute-start.1) | collective-permute-done | bytes 270368 | tf_op jit(solution)/shard_map/ppermute | solution.py:29
  63.8 3.5 %collective-permute-done.refs_0_ = bf16[2,528,128]{2,1,0:T(8,128)(2,1)S(1)} collective-permute-done((bf16[2,528,128]{2,1,0:T(8,128)(2,1)S(1)}, bf16[2,528,128]{2,1,0:T(8,128)(2,1)S(1)}, u32[]{:S(2)}, u32[]{:S(2)}) %collective-permute-start) | collective-permute-done | bytes 270368 | tf_op jit(solution)/shard_map/ppermute | solution.py:29
  67.3 0.0 collective-permute-done.4
  67.3 0.2 pad_maximum_fusion.refs_4_.refs_3_
  67.5 1.9 %collective-permute-start.6 = (bf16[3,16,128,128]{3,2,1,0:T(8,128)(2,1)S(1)}, bf16[3,16,128,128]{3,2,1,0:T(8,128)(2,1)S(1)}, u32[]{:S(2)}, u32[]{:S(2)}) collective-permute-start(bf16[3,16,128,128]{3,2,1,0:T(8,128)(2,1)S(1)} %pad_maximum_fusion.refs_4_.refs_3_), channel_id=1, source_target_pairs={{0,16},{16,0},{1,17},{17,1},{2,18},{18,2},{3,19},{19,3},{4,20},{20... | collective-permute-start | bytes 4718600 | tf_op jit(solution)/shard_map/ppermute | solution.py:29
  69.4 2.4 %collective-permute-start.5 = (bf16[16,128,128]{2,1,0:T(8,128)(2,1)S(1)}, bf16[16,128,128]{2,1,0:T(8,128)(2,1)S(1)}, u32[]{:S(2)}, u32[]{:S(2)}) collective-permute-start(bf16[16,128,128]{2,1,0:T(8,128)(2,1)S(1)} %slice.17.refs_2_.refs_1_), channel_id=1, source_target_pairs={{0,16},{16,0},{1,17},{17,1},{2,18},{18,2},{3,19},{19,3},{4,20},{20... | collective-permute-start | bytes 1572872 | tf_op jit(solution)/shard_map/ppermute | solution.py:29
  71.9 3.9 %collective-permute-start.8 = (bf16[528,128]{1,0:T(8,128)(2,1)S(1)}, bf16[528,128]{1,0:T(8,128)(2,1)S(1)}, u32[]{:S(2)}, u32[]{:S(2)}) collective-permute-start(bf16[528,128]{1,0:T(8,128)(2,1)S(1)} %slice_bitcast_fusion), channel_id=1, source_target_pairs={{0,96},{32,0},{64,32},{96,64},{1,97},{33,1},{65,33},{97,65},{2,98}... | collective-permute-start | bytes 405512 | tf_op jit(solution)/shard_map/ppermute | solution.py:29
  75.8 2.8 %collective-permute-start.7 = (bf16[528,128]{1,0:T(8,128)(2,1)S(1)}, bf16[528,128]{1,0:T(8,128)(2,1)S(1)}, u32[]{:S(2)}, u32[]{:S(2)}) collective-permute-start(bf16[528,128]{1,0:T(8,128)(2,1)S(1)} %slice_bitcast_fusion.1), channel_id=1, source_target_pairs={{0,32},{32,64},{64,96},{96,0},{1,33},{33,65},{65,97},{97,1},{2,34}... | collective-permute-start | bytes 405512 | tf_op jit(solution)/shard_map/ppermute | solution.py:29
  78.6 3.9 %collective-permute-done.8.refs_1_ = bf16[528,128]{1,0:T(8,128)(2,1)S(1)} collective-permute-done((bf16[528,128]{1,0:T(8,128)(2,1)S(1)}, bf16[528,128]{1,0:T(8,128)(2,1)S(1)}, u32[]{:S(2)}, u32[]{:S(2)}) %collective-permute-start.8) | collective-permute-done | bytes 135200 | tf_op jit(solution)/shard_map/ppermute | solution.py:29
  82.6 5.0 %collective-permute-done.7.refs_0_ = bf16[528,128]{1,0:T(8,128)(2,1)S(1)} collective-permute-done((bf16[528,128]{1,0:T(8,128)(2,1)S(1)}, bf16[528,128]{1,0:T(8,128)(2,1)S(1)}, u32[]{:S(2)}, u32[]{:S(2)}) %collective-permute-start.7) | collective-permute-done | bytes 135200 | tf_op jit(solution)/shard_map/ppermute | solution.py:29
  87.5 2.8 %shard_map.48 = (bf16[528,128]{1,0:T(8,128)(2,1)S(1)}, bf16[528,128]{1,0:T(8,128)(2,1)S(1)}) custom-call(bf16[528,128]{1,0:T(8,128)(2,1)S(1)} %collective-permute-done.7.refs_0_, bf16[528,128]{1,0:T(8,128)(2,1)S(1)} %collective-permute-done.8.refs_1_, bf16[16,128,128]{2,1,0:T(8,128)(2,1)S(1)} %slice.17.refs_2_.refs_1_, ...), custom_call_target="tpu_custom_call" | custom-call | flops 536870912 | bytes 4194304 | tf_op jit(solution)/shard_map/pallas_call | solution.py:167
  90.3 1.9 %collective-permute-start.9 = (bf16[528,128]{1,0:T(8,128)(2,1)S(1)}, bf16[528,128]{1,0:T(8,128)(2,1)S(1)}, u32[]{:S(2)}, u32[]{:S(2)}) collective-permute-start(bf16[528,128]{1,0:T(8,128)(2,1)S(1)} %get-tuple-element.32), channel_id=1, source_target_pairs={{0,32},{32,64},{64,96},{96,0},{1,33},{33,65},{65,97},{97,1},{2,34}... | collective-permute-start | bytes 405512 | tf_op jit(solution)/shard_map/ppermute | solution.py:29
  92.3 6.0 %collective-permute-start.10 = (bf16[528,128]{1,0:T(8,128)(2,1)S(1)}, bf16[528,128]{1,0:T(8,128)(2,1)S(1)}, u32[]{:S(2)}, u32[]{:S(2)}) collective-permute-start(bf16[528,128]{1,0:T(8,128)(2,1)S(1)} %get-tuple-element.33), channel_id=1, source_target_pairs={{0,96},{32,0},{64,32},{96,64},{1,97},{33,1},{65,33},{97,65},{2,98}... | collective-permute-start | bytes 405512 | tf_op jit(solution)/shard_map/ppermute | solution.py:29
  98.3 4.5 %shard_map.47 = (bf16[2,528,128]{2,1,0:T(8,128)(2,1)S(1)}, bf16[2,528,128]{2,1,0:T(8,128)(2,1)S(1)}) custom-call(bf16[2,528,128]{2,1,0:T(8,128)(2,1)S(1)} %collective-permute-done.refs_0_, bf16[2,528,128]{2,1,0:T(8,128)(2,1)S(1)} %collective-permute-done.1.refs_1_, bf16[16,128,128]{2,1,0:T(8,128)(2,1)S(1)} %slice.17.refs_2_.refs_1_, ...), custom_call_target="tpu_custom_call" | custom-call | flops 1073741824 | bytes 4194304 | tf_op jit(solution)/shard_map/pallas_call | solution.py:167
  102.9 1.7 %collective-permute-done.10.via_b_ref = bf16[528,128]{1,0:T(8,128)(2,1)S(1)} collective-permute-done((bf16[528,128]{1,0:T(8,128)(2,1)S(1)}, bf16[528,128]{1,0:T(8,128)(2,1)S(1)}, u32[]{:S(2)}, u32[]{:S(2)}) %collective-permute-start.10) | collective-permute-done | bytes 135200 | tf_op jit(solution)/shard_map/ppermute | solution.py:29
  104.5 0.4 shard_map.49
  104.9 6.5 %collective-permute-start.11 = (bf16[2,528,128]{2,1,0:T(8,128)(2,1)S(1)}, bf16[2,528,128]{2,1,0:T(8,128)(2,1)S(1)}, u32[]{:S(2)}, u32[]{:S(2)}) collective-permute-start(bf16[2,528,128]{2,1,0:T(8,128)(2,1)S(1)} %get-tuple-element.37), channel_id=1, source_target_pairs={{0,96},{32,0},{64,32},{96,64},{1,97},{33,1},{65,33},{97,65},{2,98}... | collective-permute-start | bytes 811016 | tf_op jit(solution)/shard_map/ppermute | solution.py:29
  111.4 1.9 %collective-permute-start.12 = (bf16[2,528,128]{2,1,0:T(8,128)(2,1)S(1)}, bf16[2,528,128]{2,1,0:T(8,128)(2,1)S(1)}, u32[]{:S(2)}, u32[]{:S(2)}) collective-permute-start(bf16[2,528,128]{2,1,0:T(8,128)(2,1)S(1)} %get-tuple-element.38), channel_id=1, source_target_pairs={{0,32},{32,64},{64,96},{96,0},{1,33},{33,65},{65,97},{97,1},{2,34}... | collective-permute-start | bytes 811016 | tf_op jit(solution)/shard_map/ppermute | solution.py:29
  113.3 2.8 %shard_map.50.a_ref = bf16[2,528,128]{2,1,0:T(8,128)(2,1)S(1)} custom-call(bf16[2,528,128]{2,1,0:T(8,128)(2,1)S(1)} %pad_maximum_fusion.1.refs_0_, bf16[16,128,128]{2,1,0:T(8,128)(2,1)S(1)} %slice.17.refs_2_.refs_1_, bf16[16,128,128]{2,1,0:T(8,128)(2,1)S(1)} %collective-permute-done.5.refs_3_.refs_2_, ...), custom_call_target="tpu_custom_call" | custom-call | flops 536870912 | bytes 4194304 | tf_op jit(solution)/shard_map/pallas_call | solution.py:167
  116.1 2.2 %collective-permute-done.11.b_ref = bf16[2,528,128]{2,1,0:T(8,128)(2,1)S(1)} collective-permute-done((bf16[2,528,128]{2,1,0:T(8,128)(2,1)S(1)}, bf16[2,528,128]{2,1,0:T(8,128)(2,1)S(1)}, u32[]{:S(2)}, u32[]{:S(2)}) %collective-permute-start.11) | collective-permute-done | bytes 270368 | tf_op jit(solution)/shard_map/ppermute | solution.py:29
  118.4 3.6 %collective-permute-done.12.c_ref = bf16[2,528,128]{2,1,0:T(8,128)(2,1)S(1)} collective-permute-done((bf16[2,528,128]{2,1,0:T(8,128)(2,1)S(1)}, bf16[2,528,128]{2,1,0:T(8,128)(2,1)S(1)}, u32[]{:S(2)}, u32[]{:S(2)}) %collective-permute-start.12) | collective-permute-done | bytes 270368 | tf_op jit(solution)/shard_map/ppermute | solution.py:29
  122.0 0.5 shard_map.51
  122.5 17.2 %all_to_all.11.in_ref = bf16[16,64,128]{2,1,0:T(8,128)(2,1)S(1)} all-to-all(bf16[16,64,128]{2,1,0:T(8,128)(2,1)S(1)} %bitcast.9), channel_id=1, replica_groups=mesh['x'=4,'zh'=4,'core'=2,'y'=8,'zl'=2] {'y','zl'}, dimensions={0} | all-to-all | bytes 524288 | tf_op jit(solution)/shard_map/all_to_all | solution.py:228
  139.7 0.7 shard_map.52
  (11 shorter events, 0.1 us)
Async XLA Ops:
  2.1 42.9 %copy-start = (bf16[2,16,128]{2,1,0:T(8,128)(2,1)S(1)}, bf16[2,16,128]{2,1,0:T(8,128)(2,1)}, u32[]{:S(2)}) copy-start(bf16[2,16,128]{2,1,0:T(8,128)(2,1)} %get-tuple-element.23) | copy-start | bytes 24580
  34.5 32.8 %collective-permute-start.4 = (bf16[16,128,128]{2,1,0:T(8,128)(2,1)S(1)}, bf16[16,128,128]{2,1,0:T(8,128)(2,1)S(1)}, u32[]{:S(2)}, u32[]{:S(2)}) collective-permute-start(bf16[16,128,128]{2,1,0:T(8,128)(2,1)S(1)} %slice.17.refs_2_.refs_1_), channel_id=1, source_target_pairs={{0,256},{128,384},{256,0},{384,128},{1,257},{129,385},{257,1},{385... | collective-permute-start | bytes 1572872 | tf_op jit(solution)/shard_map/ppermute | solution.py:29
  37.9 29.5 %collective-permute-start.3 = (bf16[16,128,128]{2,1,0:T(8,128)(2,1)S(1)}, bf16[16,128,128]{2,1,0:T(8,128)(2,1)S(1)}, u32[]{:S(2)}, u32[]{:S(2)}) collective-permute-start(bf16[16,128,128]{2,1,0:T(8,128)(2,1)S(1)} %slice.17.refs_2_.refs_1_), channel_id=1, source_target_pairs={{0,384},{128,0},{256,128},{384,256},{1,385},{129,1},{257,129},{385... | collective-permute-start | bytes 1572872 | tf_op jit(solution)/shard_map/ppermute | solution.py:29
  39.8 27.5 %collective-permute-start.2 = (bf16[16,128,128]{2,1,0:T(8,128)(2,1)S(1)}, bf16[16,128,128]{2,1,0:T(8,128)(2,1)S(1)}, u32[]{:S(2)}, u32[]{:S(2)}) collective-permute-start(bf16[16,128,128]{2,1,0:T(8,128)(2,1)S(1)} %slice.17.refs_2_.refs_1_), channel_id=1, source_target_pairs={{0,128},{128,256},{256,384},{384,0},{1,129},{129,257},{257,385},{3... | collective-permute-start | bytes 1572872 | tf_op jit(solution)/shard_map/ppermute | solution.py:29
  45.0 18.8 %collective-permute-start.1 = (bf16[2,528,128]{2,1,0:T(8,128)(2,1)S(1)}, bf16[2,528,128]{2,1,0:T(8,128)(2,1)S(1)}, u32[]{:S(2)}, u32[]{:S(2)}) collective-permute-start(bf16[2,528,128]{2,1,0:T(8,128)(2,1)S(1)} %pad_maximum_fusion.1.refs_0_), channel_id=1, source_target_pairs={{0,96},{32,0},{64,32},{96,64},{1,97},{33,1},{65,33},{97,65},{2,98}... | collective-permute-start | bytes 811016 | tf_op jit(solution)/shard_map/ppermute | solution.py:29
  55.0 12.3 %collective-permute-start = (bf16[2,528,128]{2,1,0:T(8,128)(2,1)S(1)}, bf16[2,528,128]{2,1,0:T(8,128)(2,1)S(1)}, u32[]{:S(2)}, u32[]{:S(2)}) collective-permute-start(bf16[2,528,128]{2,1,0:T(8,128)(2,1)S(1)} %pad_maximum_fusion.1.refs_0_), channel_id=1, source_target_pairs={{0,32},{32,64},{64,96},{96,0},{1,33},{33,65},{65,97},{97,1},{2,34}... | collective-permute-start | bytes 811016 | tf_op jit(solution)/shard_map/ppermute | solution.py:29
  67.5 20.0 %collective-permute-start.6 = (bf16[3,16,128,128]{3,2,1,0:T(8,128)(2,1)S(1)}, bf16[3,16,128,128]{3,2,1,0:T(8,128)(2,1)S(1)}, u32[]{:S(2)}, u32[]{:S(2)}) collective-permute-start(bf16[3,16,128,128]{3,2,1,0:T(8,128)(2,1)S(1)} %pad_maximum_fusion.refs_4_.refs_3_), channel_id=1, source_target_pairs={{0,16},{16,0},{1,17},{17,1},{2,18},{18,2},{3,19},{19,3},{4,20},{20... | collective-permute-start | bytes 4718600 | tf_op jit(solution)/shard_map/ppermute | solution.py:29
  69.4 18.1 %collective-permute-start.5 = (bf16[16,128,128]{2,1,0:T(8,128)(2,1)S(1)}, bf16[16,128,128]{2,1,0:T(8,128)(2,1)S(1)}, u32[]{:S(2)}, u32[]{:S(2)}) collective-permute-start(bf16[16,128,128]{2,1,0:T(8,128)(2,1)S(1)} %slice.17.refs_2_.refs_1_), channel_id=1, source_target_pairs={{0,16},{16,0},{1,17},{17,1},{2,18},{18,2},{3,19},{19,3},{4,20},{20... | collective-permute-start | bytes 1572872 | tf_op jit(solution)/shard_map/ppermute | solution.py:29
  71.9 10.7 %collective-permute-start.8 = (bf16[528,128]{1,0:T(8,128)(2,1)S(1)}, bf16[528,128]{1,0:T(8,128)(2,1)S(1)}, u32[]{:S(2)}, u32[]{:S(2)}) collective-permute-start(bf16[528,128]{1,0:T(8,128)(2,1)S(1)} %slice_bitcast_fusion), channel_id=1, source_target_pairs={{0,96},{32,0},{64,32},{96,64},{1,97},{33,1},{65,33},{97,65},{2,98}... | collective-permute-start | bytes 405512 | tf_op jit(solution)/shard_map/ppermute | solution.py:29
  75.8 11.7 %collective-permute-start.7 = (bf16[528,128]{1,0:T(8,128)(2,1)S(1)}, bf16[528,128]{1,0:T(8,128)(2,1)S(1)}, u32[]{:S(2)}, u32[]{:S(2)}) collective-permute-start(bf16[528,128]{1,0:T(8,128)(2,1)S(1)} %slice_bitcast_fusion.1), channel_id=1, source_target_pairs={{0,32},{32,64},{64,96},{96,0},{1,33},{33,65},{65,97},{97,1},{2,34}... | collective-permute-start | bytes 405512 | tf_op jit(solution)/shard_map/ppermute | solution.py:29
  90.3 12.5 %collective-permute-start.9 = (bf16[528,128]{1,0:T(8,128)(2,1)S(1)}, bf16[528,128]{1,0:T(8,128)(2,1)S(1)}, u32[]{:S(2)}, u32[]{:S(2)}) collective-permute-start(bf16[528,128]{1,0:T(8,128)(2,1)S(1)} %get-tuple-element.32), channel_id=1, source_target_pairs={{0,32},{32,64},{64,96},{96,0},{1,33},{33,65},{65,97},{97,1},{2,34}... | collective-permute-start | bytes 405512 | tf_op jit(solution)/shard_map/ppermute | solution.py:29
  92.3 12.3 %collective-permute-start.10 = (bf16[528,128]{1,0:T(8,128)(2,1)S(1)}, bf16[528,128]{1,0:T(8,128)(2,1)S(1)}, u32[]{:S(2)}, u32[]{:S(2)}) collective-permute-start(bf16[528,128]{1,0:T(8,128)(2,1)S(1)} %get-tuple-element.33), channel_id=1, source_target_pairs={{0,96},{32,0},{64,32},{96,64},{1,97},{33,1},{65,33},{97,65},{2,98}... | collective-permute-start | bytes 405512 | tf_op jit(solution)/shard_map/ppermute | solution.py:29
  104.9 13.5 %collective-permute-start.11 = (bf16[2,528,128]{2,1,0:T(8,128)(2,1)S(1)}, bf16[2,528,128]{2,1,0:T(8,128)(2,1)S(1)}, u32[]{:S(2)}, u32[]{:S(2)}) collective-permute-start(bf16[2,528,128]{2,1,0:T(8,128)(2,1)S(1)} %get-tuple-element.37), channel_id=1, source_target_pairs={{0,96},{32,0},{64,32},{96,64},{1,97},{33,1},{65,33},{97,65},{2,98}... | collective-permute-start | bytes 811016 | tf_op jit(solution)/shard_map/ppermute | solution.py:29
  111.4 10.6 %collective-permute-start.12 = (bf16[2,528,128]{2,1,0:T(8,128)(2,1)S(1)}, bf16[2,528,128]{2,1,0:T(8,128)(2,1)S(1)}, u32[]{:S(2)}, u32[]{:S(2)}) collective-permute-start(bf16[2,528,128]{2,1,0:T(8,128)(2,1)S(1)} %get-tuple-element.38), channel_id=1, source_target_pairs={{0,32},{32,64},{64,96},{96,0},{1,33},{33,65},{65,97},{97,1},{2,34}... | collective-permute-start | bytes 811016 | tf_op jit(solution)/shard_map/ppermute | solution.py:29

commit v6 on v5

--- a/solution.py
+++ b/solution.py
@@ -208,13 +208,12 @@
 
     k1, k3, k2 = (shift(k0, "x", dx) for dx in SHIFTS[1:])
     q1, q3 = shift(q0, "zh", 1), shift(q0, "zh", -1)
-    q1, q3, k0, k1, k3, k2 = lax.optimization_barrier((q1, q3, k0, k1, k3, k2))
-    c0 = shift(k0, "core", 1)
     q2a, q2b = shift(q1[0], "zh", 1), shift(q3[1], "zh", -1)
-    near = jnp.stack([k1, k3, k2])
+    k1, k3, k2, q2a, q2b = lax.optimization_barrier((k1, k3, k2, q2a, q2b))
+    near = jnp.stack([k0, k1, k3, k2])
     far = shift(near, "core", 1)
-    kvs = [k0, c0, near, far]
-    slots = ((0, None), (1, None), (2, 0), (3, 0), (2, 1), (3, 1), (2, 2), (3, 2))
+    kvs = [near, far]
+    slots = tuple((ref, n) for n in range(NX) for ref in range(NC))
 
     o2a, o2b = attend([q2a, q2b], ((0, None), (1, None)), [half_shape()] * 2, ((0, None), (1, None)), kvs, slots)
     via_a, via_b = shift(o2a, "zh", 1), shift(o2b, "zh", -1)

time: 141 us -> 139 us (0.986); the launches traced: 140 us -> 136 us
  waiting for transfers between devices: 26.8 us -> 23.9 us
  starting transfers between devices: 49.8 us -> 47.5 us
    ppermute x13 -> x12, waiting for transfers between devices: 26.8 us -> 23.9 us  [shift(): return lax.ppermute(field, axis, [(i, (i + by) % n) for i in range(n)])]
    ppermute x13 -> x12, starting transfers between devices: 49.8 us -> 47.5 us  [shift(): return lax.ppermute(field, axis, [(i, (i + by) % n) for i in range(n)])]
  transfers between devices with their start and end apart: 13 -> 12, of which waited for: 7 -> 8; matrix products, arithmetic and copies ran while one was open for 0% -> 0% of each run, Pallas kernels for 5% -> 5%
where the time goes in v6:
time: 139 us; the launch traced here: 136 us
  blocking collectives  50.4 us (36%)
  starting transfers between devices  47.5 us (34%)
  waiting for transfers between devices  23.9 us (17%)
  Pallas kernels  13.7 us (10%)
    ppermute x12, starting transfers between devices, shift(): return lax.ppermute(field, axis, [(i, (i + by) % n) for i in range(n)])  47.5 us
    all_to_all x1, blocking collectives, shards(): lax.all_to_all(packed, ('y', 'zl'), split_axis=0, concat_axis=0, tiled=True)  32.4 us
    ppermute x12, waiting for transfers between devices, shift(): return lax.ppermute(field, axis, [(i, (i + by) % n) for i in range(n)])  23.9 us
    all_to_all x1, blocking collectives, shards(): lax.all_to_all(whole.reshape(NU, TOK, HD), ('y', 'zl'), split_axis=0, con...  18 us
    pallas_call x7, Pallas kernels, call(): pl.pallas_call(kernel, out_shape=outs, in_specs=specs, out_specs=jax.tree...  13.7 us
  transfers between devices with their start and end apart: 12, of which 8 were waited for; matrix products, arithmetic and copies ran while one was open for 0% of the time, Pallas kernels for 5%

profile of v6, /device:TPU:6, one launch (start us, length us, event | category | flops | bytes accessed | tf_op | source)
XLA Modules:
  0.0 136.4 jit_solution(15142364944469638129)
XLA Ops:
  0.0 2.1 %shard_map.46 = (bf16[16,192,128]{2,1,0:T(8,128)(2,1)}, bf16[2,16,128]{2,1,0:T(8,128)(2,1)}) custom-call(bf16[64,1536]{1,0:T(8,128)(2,1)} %q_hbm.1, bf16[64,1536]{1,0:T(8,128)(2,1)} %k_hbm.1, bf16[64,1536]{1,0:T(8,128)(2,1)} %v_hbm.1, s32[12,8,256]{2,1,0:T(8,128)} %mask_hbm.1), custom_call_target="tpu_custom_call" | custom-call | bytes 262144 | tf_op jit(solution)/shard_map/pallas_call | solution.py:167
  2.1 0.0 copy-start
  2.1 32.4 %all_to_all.10 = bf16[16,192,128]{2,1,0:T(8,128)(2,1)S(1)} all-to-all(bf16[16,192,128]{2,1,0:T(8,128)(2,1)} %get-tuple-element.21), channel_id=1, replica_groups=mesh['x'=4,'zh'=4,'core'=2,'y'=8,'zl'=2] {'y','zl'}, dimensions={0} | all-to-all | bytes 1572864 | tf_op jit(solution)/shard_map/all_to_all | solution.py:205
  34.6 10.0 %collective-permute-start.1 = (bf16[2,528,128]{2,1,0:T(8,128)(2,1)S(1)}, bf16[2,528,128]{2,1,0:T(8,128)(2,1)S(1)}, u32[]{:S(2)}, u32[]{:S(2)}) collective-permute-start(bf16[2,528,128]{2,1,0:T(8,128)(2,1)S(1)} %pad_maximum_fusion.1.refs_0_), channel_id=1, source_target_pairs={{0,96},{32,0},{64,32},{96,64},{1,97},{33,1},{65,33},{97,65},{2,98}... | collective-permute-start | bytes 811016 | tf_op jit(solution)/shard_map/ppermute | solution.py:29
  44.6 1.9 %collective-permute-start = (bf16[2,528,128]{2,1,0:T(8,128)(2,1)S(1)}, bf16[2,528,128]{2,1,0:T(8,128)(2,1)S(1)}, u32[]{:S(2)}, u32[]{:S(2)}) collective-permute-start(bf16[2,528,128]{2,1,0:T(8,128)(2,1)S(1)} %pad_maximum_fusion.1.refs_0_), channel_id=1, source_target_pairs={{0,32},{32,64},{64,96},{96,0},{1,33},{33,65},{65,97},{97,1},{2,34}... | collective-permute-start | bytes 811016 | tf_op jit(solution)/shard_map/ppermute | solution.py:29
  46.5 0.3 slice_bitcast_fusion.2
  46.8 2.7 %collective-permute-start.3 = (bf16[16,128,128]{2,1,0:T(8,128)(2,1)S(1)}, bf16[16,128,128]{2,1,0:T(8,128)(2,1)S(1)}, u32[]{:S(2)}, u32[]{:S(2)}) collective-permute-start(bf16[16,128,128]{2,1,0:T(8,128)(2,1)S(1)} %get-tuple-element.38), channel_id=1, source_target_pairs={{0,384},{128,0},{256,128},{384,256},{1,385},{129,1},{257,129},{385... | collective-permute-start | bytes 1572872 | tf_op jit(solution)/shard_map/ppermute | solution.py:29
  49.5 4.3 %collective-permute-start.2 = (bf16[16,128,128]{2,1,0:T(8,128)(2,1)S(1)}, bf16[16,128,128]{2,1,0:T(8,128)(2,1)S(1)}, u32[]{:S(2)}, u32[]{:S(2)}) collective-permute-start(bf16[16,128,128]{2,1,0:T(8,128)(2,1)S(1)} %get-tuple-element.38), channel_id=1, source_target_pairs={{0,128},{128,256},{256,384},{384,0},{1,129},{129,257},{257,385},{3... | collective-permute-start | bytes 1572872 | tf_op jit(solution)/shard_map/ppermute | solution.py:29
  53.9 2.1 %collective-permute-start.4 = (bf16[16,128,128]{2,1,0:T(8,128)(2,1)S(1)}, bf16[16,128,128]{2,1,0:T(8,128)(2,1)S(1)}, u32[]{:S(2)}, u32[]{:S(2)}) collective-permute-start(bf16[16,128,128]{2,1,0:T(8,128)(2,1)S(1)} %get-tuple-element.38), channel_id=1, source_target_pairs={{0,256},{128,384},{256,0},{384,128},{1,257},{129,385},{257,1},{385... | collective-permute-start | bytes 1572872 | tf_op jit(solution)/shard_map/ppermute | solution.py:29
  56.0 6.0 %collective-permute-start.6 = (bf16[528,128]{1,0:T(8,128)(2,1)S(1)}, bf16[528,128]{1,0:T(8,128)(2,1)S(1)}, u32[]{:S(2)}, u32[]{:S(2)}) collective-permute-start(bf16[528,128]{1,0:T(8,128)(2,1)S(1)} %slice_bitcast_fusion), channel_id=1, source_target_pairs={{0,96},{32,0},{64,32},{96,64},{1,97},{33,1},{65,33},{97,65},{2,98}... | collective-permute-start | bytes 405512 | tf_op jit(solution)/shard_map/ppermute | solution.py:29
  62.1 1.9 %collective-permute-start.5 = (bf16[528,128]{1,0:T(8,128)(2,1)S(1)}, bf16[528,128]{1,0:T(8,128)(2,1)S(1)}, u32[]{:S(2)}, u32[]{:S(2)}) collective-permute-start(bf16[528,128]{1,0:T(8,128)(2,1)S(1)} %slice_bitcast_fusion.1), channel_id=1, source_target_pairs={{0,32},{32,64},{64,96},{96,0},{1,33},{33,65},{65,97},{97,1},{2,34}... | collective-permute-start | bytes 405512 | tf_op jit(solution)/shard_map/ppermute | solution.py:29
  64.0 2.0 %collective-permute-done.6.refs_1_ = bf16[528,128]{1,0:T(8,128)(2,1)S(1)} collective-permute-done((bf16[528,128]{1,0:T(8,128)(2,1)S(1)}, bf16[528,128]{1,0:T(8,128)(2,1)S(1)}, u32[]{:S(2)}, u32[]{:S(2)}) %collective-permute-start.6) | collective-permute-done | bytes 135200 | tf_op jit(solution)/shard_map/ppermute | solution.py:29
  66.0 5.2 %collective-permute-done.5.refs_0_ = bf16[528,128]{1,0:T(8,128)(2,1)S(1)} collective-permute-done((bf16[528,128]{1,0:T(8,128)(2,1)S(1)}, bf16[528,128]{1,0:T(8,128)(2,1)S(1)}, u32[]{:S(2)}, u32[]{:S(2)}) %collective-permute-start.5) | collective-permute-done | bytes 135200 | tf_op jit(solution)/shard_map/ppermute | solution.py:29
  71.2 1.6 %collective-permute-done.3 = bf16[16,128,128]{2,1,0:T(8,128)(2,1)S(1)} collective-permute-done((bf16[16,128,128]{2,1,0:T(8,128)(2,1)S(1)}, bf16[16,128,128]{2,1,0:T(8,128)(2,1)S(1)}, u32[]{:S(2)}, u32[]{:S(2)}) %collective-permute-start.3) | collective-permute-done | bytes 524320 | tf_op jit(solution)/shard_map/ppermute | solution.py:29
  72.8 1.2 collective-permute-done.2
  74.1 0.3 pad_maximum_fusion.refs_2_.refs_1_
  74.3 1.9 %collective-permute-start.7 = (bf16[4,16,128,128]{3,2,1,0:T(8,128)(2,1)S(1)}, bf16[4,16,128,128]{3,2,1,0:T(8,128)(2,1)S(1)}, u32[]{:S(2)}, u32[]{:S(2)}) collective-permute-start(bf16[4,16,128,128]{3,2,1,0:T(8,128)(2,1)S(1)} %pad_maximum_fusion.refs_2_.refs_1_), channel_id=1, source_target_pairs={{0,16},{16,0},{1,17},{17,1},{2,18},{18,2},{3,19},{19,3},{4,20},{20... | collective-permute-start | bytes 6291464 | tf_op jit(solution)/shard_map/ppermute | solution.py:29
  76.2 4.1 %collective-permute-done.7.refs_3_.refs_2_ = bf16[4,16,128,128]{3,2,1,0:T(8,128)(2,1)S(1)} collective-permute-done((bf16[4,16,128,128]{3,2,1,0:T(8,128)(2,1)S(1)}, bf16[4,16,128,128]{3,2,1,0:T(8,128)(2,1)S(1)}, u32[]{:S(2)}, u32[]{:S(2)}) %collective-permute-start.7) | collective-permute-done | bytes 2097184 | tf_op jit(solution)/shard_map/ppermute | solution.py:29
  80.4 2.8 %shard_map.48 = (bf16[528,128]{1,0:T(8,128)(2,1)S(1)}, bf16[528,128]{1,0:T(8,128)(2,1)S(1)}) custom-call(bf16[528,128]{1,0:T(8,128)(2,1)S(1)} %collective-permute-done.5.refs_0_, bf16[528,128]{1,0:T(8,128)(2,1)S(1)} %collective-permute-done.6.refs_1_, bf16[4,16,128,128]{3,2,1,0:T(8,128)(2,1)S(1)} %pad_maximum_fusion.refs_2_.refs_1_, ...), custom_call_target="tpu_custom_call" | custom-call | flops 536870912 | bytes 4194304 | tf_op jit(solution)/shard_map/pallas_call | solution.py:167
  83.1 2.5 %collective-permute-start.8 = (bf16[528,128]{1,0:T(8,128)(2,1)S(1)}, bf16[528,128]{1,0:T(8,128)(2,1)S(1)}, u32[]{:S(2)}, u32[]{:S(2)}) collective-permute-start(bf16[528,128]{1,0:T(8,128)(2,1)S(1)} %get-tuple-element.30), channel_id=1, source_target_pairs={{0,32},{32,64},{64,96},{96,0},{1,33},{33,65},{65,97},{97,1},{2,34}... | collective-permute-start | bytes 405512 | tf_op jit(solution)/shard_map/ppermute | solution.py:29
  85.6 5.5 %collective-permute-start.9 = (bf16[528,128]{1,0:T(8,128)(2,1)S(1)}, bf16[528,128]{1,0:T(8,128)(2,1)S(1)}, u32[]{:S(2)}, u32[]{:S(2)}) collective-permute-start(bf16[528,128]{1,0:T(8,128)(2,1)S(1)} %get-tuple-element.31), channel_id=1, source_target_pairs={{0,96},{32,0},{64,32},{96,64},{1,97},{33,1},{65,33},{97,65},{2,98}... | collective-permute-start | bytes 405512 | tf_op jit(solution)/shard_map/ppermute | solution.py:29
  91.1 4.5 %shard_map.47 = (bf16[2,528,128]{2,1,0:T(8,128)(2,1)S(1)}, bf16[2,528,128]{2,1,0:T(8,128)(2,1)S(1)}) custom-call(bf16[2,528,128]{2,1,0:T(8,128)(2,1)S(1)} %collective-permute-done.refs_0_, bf16[2,528,128]{2,1,0:T(8,128)(2,1)S(1)} %collective-permute-done.1.refs_1_, bf16[4,16,128,128]{3,2,1,0:T(8,128)(2,1)S(1)} %pad_maximum_fusion.refs_2_.refs_1_, ...), custom_call_target="tpu_custom_call" | custom-call | flops 1073741824 | bytes 4194304 | tf_op jit(solution)/shard_map/pallas_call | solution.py:167
  95.7 0.7 collective-permute-done.9.via_b_ref
  96.4 0.4 shard_map.49
  96.8 6.7 %collective-permute-start.10 = (bf16[2,528,128]{2,1,0:T(8,128)(2,1)S(1)}, bf16[2,528,128]{2,1,0:T(8,128)(2,1)S(1)}, u32[]{:S(2)}, u32[]{:S(2)}) collective-permute-start(bf16[2,528,128]{2,1,0:T(8,128)(2,1)S(1)} %get-tuple-element.35), channel_id=1, source_target_pairs={{0,96},{32,0},{64,32},{96,64},{1,97},{33,1},{65,33},{97,65},{2,98}... | collective-permute-start | bytes 811016 | tf_op jit(solution)/shard_map/ppermute | solution.py:29
  103.4 1.9 %collective-permute-start.11 = (bf16[2,528,128]{2,1,0:T(8,128)(2,1)S(1)}, bf16[2,528,128]{2,1,0:T(8,128)(2,1)S(1)}, u32[]{:S(2)}, u32[]{:S(2)}) collective-permute-start(bf16[2,528,128]{2,1,0:T(8,128)(2,1)S(1)} %get-tuple-element.36), channel_id=1, source_target_pairs={{0,32},{32,64},{64,96},{96,0},{1,33},{33,65},{65,97},{97,1},{2,34}... | collective-permute-start | bytes 811016 | tf_op jit(solution)/shard_map/ppermute | solution.py:29
  105.4 2.8 %shard_map.50.a_ref = bf16[2,528,128]{2,1,0:T(8,128)(2,1)S(1)} custom-call(bf16[2,528,128]{2,1,0:T(8,128)(2,1)S(1)} %pad_maximum_fusion.1.refs_0_, bf16[4,16,128,128]{3,2,1,0:T(8,128)(2,1)S(1)} %pad_maximum_fusion.refs_2_.refs_1_, bf16[4,16,128,128]{3,2,1,0:T(8,128)(2,1)S(1)} %collective-permute-done.7.refs_3_.refs_2_), custom_call_target="tpu_custom_call" | custom-call | flops 536870912 | bytes 4194304 | tf_op jit(solution)/shard_map/pallas_call | solution.py:167
  108.1 4.2 %collective-permute-done.10.b_ref = bf16[2,528,128]{2,1,0:T(8,128)(2,1)S(1)} collective-permute-done((bf16[2,528,128]{2,1,0:T(8,128)(2,1)S(1)}, bf16[2,528,128]{2,1,0:T(8,128)(2,1)S(1)}, u32[]{:S(2)}, u32[]{:S(2)}) %collective-permute-start.10) | collective-permute-done | bytes 270368 | tf_op jit(solution)/shard_map/ppermute | solution.py:29
  112.4 4.7 %collective-permute-done.11.c_ref = bf16[2,528,128]{2,1,0:T(8,128)(2,1)S(1)} collective-permute-done((bf16[2,528,128]{2,1,0:T(8,128)(2,1)S(1)}, bf16[2,528,128]{2,1,0:T(8,128)(2,1)S(1)}, u32[]{:S(2)}, u32[]{:S(2)}) %collective-permute-start.11) | collective-permute-done | bytes 270368 | tf_op jit(solution)/shard_map/ppermute | solution.py:29
  117.1 0.5 shard_map.51
  117.6 18.0 %all_to_all.11.in_ref = bf16[16,64,128]{2,1,0:T(8,128)(2,1)S(1)} all-to-all(bf16[16,64,128]{2,1,0:T(8,128)(2,1)S(1)} %bitcast.11), channel_id=1, replica_groups=mesh['x'=4,'zh'=4,'core'=2,'y'=8,'zl'=2] {'y','zl'}, dimensions={0} | all-to-all | bytes 524288 | tf_op jit(solution)/shard_map/all_to_all | solution.py:227
  135.6 0.7 shard_map.52
  (9 shorter events, 0.1 us)
Async XLA Ops:
  2.1 32.4 %copy-start = (bf16[2,16,128]{2,1,0:T(8,128)(2,1)S(1)}, bf16[2,16,128]{2,1,0:T(8,128)(2,1)}, u32[]{:S(2)}) copy-start(bf16[2,16,128]{2,1,0:T(8,128)(2,1)} %get-tuple-element.22) | copy-start | bytes 24580
  34.6 21.4 %collective-permute-start.1 = (bf16[2,528,128]{2,1,0:T(8,128)(2,1)S(1)}, bf16[2,528,128]{2,1,0:T(8,128)(2,1)S(1)}, u32[]{:S(2)}, u32[]{:S(2)}) collective-permute-start(bf16[2,528,128]{2,1,0:T(8,128)(2,1)S(1)} %pad_maximum_fusion.1.refs_0_), channel_id=1, source_target_pairs={{0,96},{32,0},{64,32},{96,64},{1,97},{33,1},{65,33},{97,65},{2,98}... | collective-permute-start | bytes 811016 | tf_op jit(solution)/shard_map/ppermute | solution.py:29
  44.6 17.4 %collective-permute-start = (bf16[2,528,128]{2,1,0:T(8,128)(2,1)S(1)}, bf16[2,528,128]{2,1,0:T(8,128)(2,1)S(1)}, u32[]{:S(2)}, u32[]{:S(2)}) collective-permute-start(bf16[2,528,128]{2,1,0:T(8,128)(2,1)S(1)} %pad_maximum_fusion.1.refs_0_), channel_id=1, source_target_pairs={{0,32},{32,64},{64,96},{96,0},{1,33},{33,65},{65,97},{97,1},{2,34}... | collective-permute-start | bytes 811016 | tf_op jit(solution)/shard_map/ppermute | solution.py:29
  46.8 26.0 %collective-permute-start.3 = (bf16[16,128,128]{2,1,0:T(8,128)(2,1)S(1)}, bf16[16,128,128]{2,1,0:T(8,128)(2,1)S(1)}, u32[]{:S(2)}, u32[]{:S(2)}) collective-permute-start(bf16[16,128,128]{2,1,0:T(8,128)(2,1)S(1)} %get-tuple-element.38), channel_id=1, source_target_pairs={{0,384},{128,0},{256,128},{384,256},{1,385},{129,1},{257,129},{385... | collective-permute-start | bytes 1572872 | tf_op jit(solution)/shard_map/ppermute | solution.py:29
  49.5 24.5 %collective-permute-start.2 = (bf16[16,128,128]{2,1,0:T(8,128)(2,1)S(1)}, bf16[16,128,128]{2,1,0:T(8,128)(2,1)S(1)}, u32[]{:S(2)}, u32[]{:S(2)}) collective-permute-start(bf16[16,128,128]{2,1,0:T(8,128)(2,1)S(1)} %get-tuple-element.38), channel_id=1, source_target_pairs={{0,128},{128,256},{256,384},{384,0},{1,129},{129,257},{257,385},{3... | collective-permute-start | bytes 1572872 | tf_op jit(solution)/shard_map/ppermute | solution.py:29
  53.9 20.2 %collective-permute-start.4 = (bf16[16,128,128]{2,1,0:T(8,128)(2,1)S(1)}, bf16[16,128,128]{2,1,0:T(8,128)(2,1)S(1)}, u32[]{:S(2)}, u32[]{:S(2)}) collective-permute-start(bf16[16,128,128]{2,1,0:T(8,128)(2,1)S(1)} %get-tuple-element.38), channel_id=1, source_target_pairs={{0,256},{128,384},{256,0},{384,128},{1,257},{129,385},{257,1},{385... | collective-permute-start | bytes 1572872 | tf_op jit(solution)/shard_map/ppermute | solution.py:29
  56.0 10.0 %collective-permute-start.6 = (bf16[528,128]{1,0:T(8,128)(2,1)S(1)}, bf16[528,128]{1,0:T(8,128)(2,1)S(1)}, u32[]{:S(2)}, u32[]{:S(2)}) collective-permute-start(bf16[528,128]{1,0:T(8,128)(2,1)S(1)} %slice_bitcast_fusion), channel_id=1, source_target_pairs={{0,96},{32,0},{64,32},{96,64},{1,97},{33,1},{65,33},{97,65},{2,98}... | collective-permute-start | bytes 405512 | tf_op jit(solution)/shard_map/ppermute | solution.py:29
  62.1 9.1 %collective-permute-start.5 = (bf16[528,128]{1,0:T(8,128)(2,1)S(1)}, bf16[528,128]{1,0:T(8,128)(2,1)S(1)}, u32[]{:S(2)}, u32[]{:S(2)}) collective-permute-start(bf16[528,128]{1,0:T(8,128)(2,1)S(1)} %slice_bitcast_fusion.1), channel_id=1, source_target_pairs={{0,32},{32,64},{64,96},{96,0},{1,33},{33,65},{65,97},{97,1},{2,34}... | collective-permute-start | bytes 405512 | tf_op jit(solution)/shard_map/ppermute | solution.py:29
  74.3 6.1 %collective-permute-start.7 = (bf16[4,16,128,128]{3,2,1,0:T(8,128)(2,1)S(1)}, bf16[4,16,128,128]{3,2,1,0:T(8,128)(2,1)S(1)}, u32[]{:S(2)}, u32[]{:S(2)}) collective-permute-start(bf16[4,16,128,128]{3,2,1,0:T(8,128)(2,1)S(1)} %pad_maximum_fusion.refs_2_.refs_1_), channel_id=1, source_target_pairs={{0,16},{16,0},{1,17},{17,1},{2,18},{18,2},{3,19},{19,3},{4,20},{20... | collective-permute-start | bytes 6291464 | tf_op jit(solution)/shard_map/ppermute | solution.py:29
  83.1 12.5 %collective-permute-start.8 = (bf16[528,128]{1,0:T(8,128)(2,1)S(1)}, bf16[528,128]{1,0:T(8,128)(2,1)S(1)}, u32[]{:S(2)}, u32[]{:S(2)}) collective-permute-start(bf16[528,128]{1,0:T(8,128)(2,1)S(1)} %get-tuple-element.30), channel_id=1, source_target_pairs={{0,32},{32,64},{64,96},{96,0},{1,33},{33,65},{65,97},{97,1},{2,34}... | collective-permute-start | bytes 405512 | tf_op jit(solution)/shard_map/ppermute | solution.py:29
  85.6 10.8 %collective-permute-start.9 = (bf16[528,128]{1,0:T(8,128)(2,1)S(1)}, bf16[528,128]{1,0:T(8,128)(2,1)S(1)}, u32[]{:S(2)}, u32[]{:S(2)}) collective-permute-start(bf16[528,128]{1,0:T(8,128)(2,1)S(1)} %get-tuple-element.31), channel_id=1, source_target_pairs={{0,96},{32,0},{64,32},{96,64},{1,97},{33,1},{65,33},{97,65},{2,98}... | collective-permute-start | bytes 405512 | tf_op jit(solution)/shard_map/ppermute | solution.py:29
  96.8 15.6 %collective-permute-start.10 = (bf16[2,528,128]{2,1,0:T(8,128)(2,1)S(1)}, bf16[2,528,128]{2,1,0:T(8,128)(2,1)S(1)}, u32[]{:S(2)}, u32[]{:S(2)}) collective-permute-start(bf16[2,528,128]{2,1,0:T(8,128)(2,1)S(1)} %get-tuple-element.35), channel_id=1, source_target_pairs={{0,96},{32,0},{64,32},{96,64},{1,97},{33,1},{65,33},{97,65},{2,98}... | collective-permute-start | bytes 811016 | tf_op jit(solution)/shard_map/ppermute | solution.py:29
  103.4 13.7 %collective-permute-start.11 = (bf16[2,528,128]{2,1,0:T(8,128)(2,1)S(1)}, bf16[2,528,128]{2,1,0:T(8,128)(2,1)S(1)}, u32[]{:S(2)}, u32[]{:S(2)}) collective-permute-start(bf16[2,528,128]{2,1,0:T(8,128)(2,1)S(1)} %get-tuple-element.36), channel_id=1, source_target_pairs={{0,32},{32,64},{64,96},{96,0},{1,33},{33,65},{65,97},{97,1},{2,34}... | collective-permute-start | bytes 811016 | tf_op jit(solution)/shard_map/ppermute | solution.py:29

commit v7 on v6

v7 whole, which is shorter than its diff:
```python
import functools
import math

import jax
import jax.numpy as jnp
from jax import lax
from jax.experimental import pallas as pl
from jax.experimental.pallas import tpu as pltpu
from jax.sharding import Mesh, PartitionSpec as P

BF = jnp.bfloat16
F32 = jnp.float32
NX, NZ, NC, NU = 4, 4, 2, 16
HEADS, HD, BS, TOK = 12, 128, 128, 64
SEGB = 8
ROWS = SEGB * BS
PICKS = 16
LSE = 32
STEPS = 4
EXP2 = math.log2(math.e) / math.sqrt(HD)
AXES = ("x", "zh", "core", "y", "zl")
VMEM = pl.BlockSpec(memory_space=pltpu.VMEM)
HBM = pl.BlockSpec(memory_space=pltpu.HBM)


def shift(field, axis, by):
    n = lax.axis_size(axis)
    return lax.ppermute(field, axis, [(i, (i + by) % n) for i in range(n)])


def pack_kernel(q_hbm, k_hbm, v_hbm, mask_hbm, out_ref, picks_ref, q_ref, k_ref, v_ref, mask_ref, sems):
    head = jnp.minimum(lax.axis_index("y") * 2 + lax.axis_index("zl"), HEADS - 1)
    pairs = ((q_hbm, q_ref), (k_hbm, k_ref), (v_hbm, v_ref), (mask_hbm.at[head], mask_ref))
    copies = [pltpu.make_async_copy(src, dst, sems.at[i]) for i, (src, dst) in enumerate(pairs)]
    for copy in copies:
        copy.start()
    for s in range(HEADS, NU):
        out_ref[s] = jnp.zeros((3 * TOK, HD), BF)
    for n, ref in enumerate((q_ref, k_ref, v_ref)):
        copies[n].wait()
        for h in range(HEADS):
            out_ref[h, n * TOK : (n + 1) * TOK, :] = ref[:, h * HD : (h + 1) * HD]
    copies[3].wait()
    live = mask_ref[...].astype(F32).astype(BF)
    cols = live.shape[1]
    i = lax.broadcasted_iota(jnp.int32, (cols, HD), 0)
    g = lax.broadcasted_iota(jnp.int32, (cols, HD), 1)
    weight = jnp.where(i // SEGB == g, i % SEGB, 0).astype(F32).astype(BF)
    picks = jnp.dot(live, weight, preferred_element_type=F32)
    picks_ref[...] = jnp.concatenate([picks, jnp.zeros((PICKS - SEGB, HD), F32)], axis=0).astype(BF)


def split3(lse):
    hi = lse.astype(BF).astype(F32)
    mid = (lse - hi).astype(BF).astype(F32)
    return jnp.concatenate([hi, mid, lse - hi - mid, jnp.zeros_like(hi)], axis=0).astype(BF)


def join3(rows):
    rows = rows.astype(F32)
    return rows[0:SEGB] + rows[SEGB : 2 * SEGB] + rows[2 * SEGB : 3 * SEGB]


def attend_kernel(chunks, shifts, opening, *refs):
    q_refs, (near_ref, far_ref), rest = refs[:chunks], refs[chunks : chunks + 2], refs[chunks + 2 :]
    acc_refs, ml_refs, rest = rest[:chunks], rest[chunks : 2 * chunks], rest[2 * chunks :]
    out_refs = rest[:-3]
    flat_ref, picks_ref, sem = rest[-3:]
    for n, q_ref in enumerate(q_refs):
        flat_ref[n * SEGB : (n + 1) * SEGB, :] = q_ref[ROWS:, :].astype(F32)[:SEGB].astype(jnp.int32)
    fetch = pltpu.make_async_copy(flat_ref, picks_ref, sem)
    fetch.start()
    x, z, c = lax.axis_index("x"), lax.axis_index("zh"), lax.axis_index("core")
    columns = [(x * NZ + (z + NZ - dz) % NZ) * NC + cc for dz in shifts for cc in (c, 1 - c)]
    groups = [ref.at[n] for n in range(len(shifts)) for ref in (near_ref, far_ref)]
    lane = lax.broadcasted_iota(jnp.int32, (BS // STEPS, HD), 1)
    fetch.wait()
    blocks = [(n, b) for n in range(chunks) for b in range(SEGB)]
    fetched, scores, weights, peaks, totals, fades = {}, {}, {}, {}, {}, {}
    lses = [[] for _ in q_refs]
    for t in range(len(blocks) + 2):
        ahead, here, last = t, t - 1, t - 2
        runs = [0 <= i < len(blocks) for i in (ahead, here, last)]
        if runs[0]:
            n, b = blocks[ahead]
            keys, values = [], []
            for group, column in zip(groups, columns):
                both = group[pl.ds(2 * picks_ref[n * SEGB + b, column], 2)]
                keys.append(both[:, :TOK, :].reshape(BS, HD))
                values.append(both[:, TOK:, :].reshape(BS, HD))
            fetched[ahead] = q_refs[n][b * BS : (b + 1) * BS, :], keys, values
            scores[ahead] = []
        if runs[1]:
            weights[here], peaks[here], totals[here], fades[here] = [], [], [], []
        products = []
        for step in range(STEPS):
            pair = slice(2 * step, 2 * step + 2)
            if runs[0] and step < len(shifts):
                q, keys, _ = fetched[ahead]
                both = jnp.concatenate(keys[pair], axis=0)
                scores[ahead].append(
                    lax.dot_general(q, both, (((1,), (1,)), ((), ())), preferred_element_type=F32)
                )
            if runs[1]:
                n, b = blocks[here]
                rows = slice(step * BS // STEPS, (step + 1) * BS // STEPS)
                part = [s[rows] for s in scores[here]]
                peak = jnp.max(functools.reduce(jnp.maximum, part), axis=1, keepdims=True)
                if not opening:
                    old = ml_refs[n][b * BS + rows.start : b * BS + rows.stop, :]
                    old_peak = old[:, 0:1]
                    old_total = jnp.sum(jnp.where(lane == 1, old, 0.0), axis=1, keepdims=True)
                    peak = jnp.maximum(peak, old_peak)
                    fade = jnp.exp2((old_peak - peak) * EXP2)
                    fades[here].append(fade)
                w = [jnp.exp2((s - peak) * EXP2) for s in part]
                total = jnp.sum(functools.reduce(jnp.add, w), axis=1, keepdims=True)
                totals[here].append(total if opening else total + old_total * fade)
                peaks[here].append(peak)
                weights[here].append([p.astype(BF) for p in w])
            if runs[2] and step < len(shifts):
                w = jnp.concatenate([p[step] for p in weights[last]], axis=0)
                both = jnp.concatenate(fetched[last][2][pair], axis=0)
                products.append(jnp.dot(w, both, preferred_element_type=F32))
        if runs[2]:
            n, b = blocks[last]
            rows = slice(b * BS, (b + 1) * BS)
            peak, total = jnp.concatenate(peaks[last], axis=0), jnp.concatenate(totals[last], axis=0)
            if opening:
                acc_refs[n][rows, :] = functools.reduce(jnp.add, products)
                lanes = lax.broadcasted_iota(jnp.int32, (BS, HD), 1)
                ml_refs[n][rows, :] = jnp.where(lanes == 0, peak, total)
            else:
                products.append(acc_refs[n][rows, :] * jnp.concatenate(fades[last], axis=0))
                out_refs[n][rows, :] = (functools.reduce(jnp.add, products) * (1.0 / total)).astype(BF)
                lse = peak * EXP2 + jnp.log2(total)
                lses[n].append(jnp.transpose(jnp.broadcast_to(lse, (BS, HD)))[0:1, :])
                if b == SEGB - 1:
                    out_refs[n][ROWS:, :] = split3(jnp.concatenate(lses[n], axis=0))
            fetched[last] = scores[last] = weights[last] = None


def merge_kernel(*refs):
    ins, out_ref = refs[:-1], refs[-1]
    lses = [join3(r[ROWS:, :]) for r in ins]
    top = functools.reduce(jnp.maximum, lses)
    parts = [jnp.exp2(s - top) for s in lses]
    total = functools.reduce(jnp.add, parts)
    parts = [p / total for p in parts]
    for b in range(SEGB):
        rows = slice(b * BS, (b + 1) * BS)
        acc = jnp.zeros((BS, HD), F32)
        for r, p in zip(ins, parts):
            acc = acc + jnp.transpose(jnp.broadcast_to(p[b : b + 1, :], (BS, HD))) * r[rows, :].astype(F32)
        out_ref[rows, :] = acc.astype(BF)


def unpack_kernel(in_ref, out_ref):
    for h in range(HEADS):
        out_ref[:, h * HD : (h + 1) * HD] = in_ref[h]


def call(kernel, outs, specs, *args, scratch=(), flops=0, moved=1 << 18, vmem=24):
    return pl.pallas_call(
        kernel,
        out_shape=outs,
        in_specs=specs,
        out_specs=jax.tree.map(lambda _: VMEM, outs),
        scratch_shapes=list(scratch),
        compiler_params=pltpu.CompilerParams(vmem_limit_bytes=vmem << 20),
        cost_estimate=pl.CostEstimate(flops=flops, bytes_accessed=moved, transcendentals=0),
    )(*args)


def attend(queries, shifts, near, far, state=None):
    n = len(queries)
    if state is None:
        outs = [jax.ShapeDtypeStruct((ROWS, HD), F32)] * (2 * n)
    else:
        outs = [jax.ShapeDtypeStruct((ROWS + LSE, HD), BF)] * n
    ins = [*queries, near, far, *(state or [])]
    return call(
        functools.partial(attend_kernel, n, shifts, state is None),
        outs, [VMEM] * len(ins), *ins,
        scratch=[pltpu.VMEM((n * SEGB, HD), jnp.int32), pltpu.SMEM((n * SEGB, HD), jnp.int32), pltpu.SemaphoreType.DMA],
        flops=n * len(shifts) * (1 << 27), moved=2 << 20,
    )


def shards(queries, keys, values, block_mask):
    packed, picks = call(
        pack_kernel,
        (jax.ShapeDtypeStruct((NU, 3 * TOK, HD), BF), jax.ShapeDtypeStruct((PICKS, HD), BF)),
        [HBM] * 4, queries, keys, values, block_mask,
        scratch=[pltpu.VMEM(queries.shape, BF)] * 3
        + [pltpu.VMEM(block_mask.shape[1:], jnp.int32), pltpu.SemaphoreType.DMA((4,))],
        vmem=60,
    )
    got = lax.all_to_all(packed, ("y", "zl"), split_axis=0, concat_axis=0, tiled=True)
    k0 = got[:, TOK:]
    q0 = jnp.concatenate([got[:, :TOK].reshape(ROWS, HD), picks], axis=0)

    k1, k3 = shift(k0, "zh", 1), shift(k0, "zh", -1)
    q1, q2, q3 = (shift(q0, "x", dx) for dx in (1, 2, 3))
    k1, k3, q1, q2, q3 = lax.optimization_barrier((k1, k3, q1, q2, q3))
    k2a, k2b = shift(k1[: NU // 2], "zh", 1), shift(k3[NU // 2 :], "zh", -1)
    near = jnp.stack([k0, k1, k3])
    far = shift(near, "core", 1)
    state = attend([q0, q1, q2, q3], (0, 1, 3), near, far)
    k2a, k2b, *state = lax.optimization_barrier((k2a, k2b, *state))
    acc, ml = state[:NX], state[NX:]

    near = jnp.concatenate([k2a, k2b], axis=0)[None]
    far = shift(near, "core", 1)
    (o2,) = attend([q2], (2,), near, far, [acc[2], ml[2]])
    o2, far = lax.optimization_barrier((o2, far))
    back2 = shift(o2, "x", -2)
    o1, o3 = attend([q1, q3], (2,), near, far, [acc[1], acc[3], ml[1], ml[3]])
    o1, o3, far = lax.optimization_barrier((o1, o3, far))
    back1, back3 = shift(o1, "x", -1), shift(o3, "x", -3)
    (o0,) = attend([q0], (2,), near, far, [acc[0], ml[0]])
    whole = call(merge_kernel, jax.ShapeDtypeStruct((ROWS, HD), BF), [VMEM] * NX, o0, back1, back2, back3)
    home = lax.all_to_all(whole.reshape(NU, TOK, HD), ("y", "zl"), split_axis=0, concat_axis=0, tiled=True)
    return call(unpack_kernel, jax.ShapeDtypeStruct((TOK, HEADS * HD), BF), [VMEM], home)


def solution(mesh):
    fine = Mesh(mesh.devices.reshape(NX, NZ, NC, NU // 2, 2), AXES)
    tokens = P(AXES, None)
    placed = (tokens, tokens, tokens, P(None, AXES[:3], None))
    return jax.shard_map(shards, mesh=fine, in_specs=placed, out_specs=tokens, check_vma=False)
```

time: 139 us -> 151 us (1.086)
  Pallas kernels: 13.7 us -> 34.9 us
  starting transfers between devices: 47.5 us -> 41.6 us
  blocking collectives: 50.4 us -> 48.3 us
    pallas_call x7, Pallas kernels: 13.7 us -> 34.9 us  [call(): pl.pallas_call(kernel, out_shape=outs, in_specs=specs, out_specs=jax.tree...]
    ppermute x12, starting transfers between devices: 47.5 us -> 41.6 us  [shift(): return lax.ppermute(field, axis, [(i, (i + by) % n) for i in range(n)])]
    all_to_all x1, blocking collectives: 18 us -> 15.9 us  [shards(): lax.all_to_all(whole.reshape(NU, TOK, HD), ('y', 'zl'), split_axis=0, con...]
  transfers between devices with their start and end apart: 12 -> 12, of which waited for: 8 -> 6; matrix products, arithmetic and copies ran while one was open for 0% -> 0% of each run, Pallas kernels for 5% -> 10%
where the time goes in v7:
time: 151 us; the launch traced here: 149 us
  blocking collectives  48.3 us (32%)
  starting transfers between devices  41.6 us (28%)
  Pallas kernels  34.9 us (23%)
  waiting for transfers between devices  23.1 us (15%)
    ppermute x12, starting transfers between devices, shift(): return lax.ppermute(field, axis, [(i, (i + by) % n) for i in range(n)])  41.6 us
    pallas_call x7, Pallas kernels, call(): pl.pallas_call(kernel, out_shape=outs, in_specs=specs, out_specs=jax.tree...  34.9 us
    all_to_all x1, blocking collectives, shards(): lax.all_to_all(packed, ('y', 'zl'), split_axis=0, concat_axis=0, tiled=True)  32.4 us
    ppermute x12, waiting for transfers between devices, shift(): return lax.ppermute(field, axis, [(i, (i + by) % n) for i in range(n)])  23.1 us
    all_to_all x1, blocking collectives, shards(): lax.all_to_all(whole.reshape(NU, TOK, HD), ('y', 'zl'), split_axis=0, con...  15.9 us
  transfers between devices with their start and end apart: 12, of which 6 were waited for; matrix products, arithmetic and copies ran while one was open for 0% of the time, Pallas kernels for 10%

profile of v7, /device:TPU:6, one launch (start us, length us, event | category | flops | bytes accessed | tf_op | source)
XLA Modules:
  0.0 148.6 jit_solution(13533303240162512162)
XLA Ops:
  0.0 2.1 %shard_map.46 = (bf16[16,192,128]{2,1,0:T(8,128)(2,1)}, bf16[16,128]{1,0:T(8,128)(2,1)}) custom-call(bf16[64,1536]{1,0:T(8,128)(2,1)} %q_hbm.1, bf16[64,1536]{1,0:T(8,128)(2,1)} %k_hbm.1, bf16[64,1536]{1,0:T(8,128)(2,1)} %v_hbm.1, s32[12,8,256]{2,1,0:T(8,128)} %mask_hbm.1), custom_call_target="tpu_custom_call" | custom-call | bytes 262144 | tf_op jit(solution)/shard_map/pallas_call | solution.py:164
  2.1 0.0 copy-start
  2.1 32.4 %all_to_all.10 = bf16[16,192,128]{2,1,0:T(8,128)(2,1)S(1)} all-to-all(bf16[16,192,128]{2,1,0:T(8,128)(2,1)} %get-tuple-element.37), channel_id=1, replica_groups=mesh['x'=4,'zh'=4,'core'=2,'y'=8,'zl'=2] {'y','zl'}, dimensions={0} | all-to-all | bytes 1572864 | tf_op jit(solution)/shard_map/all_to_all | solution.py:199
  34.5 0.1 slice_bitcast_fusion
  34.6 10.0 %collective-permute-start.1 = (bf16[16,128,128]{2,1,0:T(8,128)(2,1)S(1)}, bf16[16,128,128]{2,1,0:T(8,128)(2,1)S(1)}, u32[]{:S(2)}, u32[]{:S(2)}) collective-permute-start(bf16[16,128,128]{2,1,0:T(8,128)(2,1)S(1)} %get-tuple-element.70), channel_id=1, source_target_pairs={{0,96},{32,0},{64,32},{96,64},{1,97},{33,1},{65,33},{97,65},{2,98}... | collective-permute-start | bytes 1572872 | tf_op jit(solution)/shard_map/ppermute | solution.py:28
  44.7 1.9 %collective-permute-start = (bf16[16,128,128]{2,1,0:T(8,128)(2,1)S(1)}, bf16[16,128,128]{2,1,0:T(8,128)(2,1)S(1)}, u32[]{:S(2)}, u32[]{:S(2)}) collective-permute-start(bf16[16,128,128]{2,1,0:T(8,128)(2,1)S(1)} %get-tuple-element.70), channel_id=1, source_target_pairs={{0,32},{32,64},{64,96},{96,0},{1,33},{33,65},{65,97},{97,1},{2,34}... | collective-permute-start | bytes 1572872 | tf_op jit(solution)/shard_map/ppermute | solution.py:28
  46.7 2.7 %collective-permute-start.4 = (bf16[1040,128]{1,0:T(8,128)(2,1)S(1)}, bf16[1040,128]{1,0:T(8,128)(2,1)S(1)}, u32[]{:S(2)}, u32[]{:S(2)}) collective-permute-start(bf16[1040,128]{1,0:T(8,128)(2,1)S(1)} %pad_maximum_fusion.1.refs_0_), channel_id=1, source_target_pairs={{0,384},{128,0},{256,128},{384,256},{1,385},{129,1},{257,129},{385... | collective-permute-start | bytes 798728 | tf_op jit(solution)/shard_map/ppermute | solution.py:28
  49.4 3.0 %collective-permute-start.3 = (bf16[1040,128]{1,0:T(8,128)(2,1)S(1)}, bf16[1040,128]{1,0:T(8,128)(2,1)S(1)}, u32[]{:S(2)}, u32[]{:S(2)}) collective-permute-start(bf16[1040,128]{1,0:T(8,128)(2,1)S(1)} %pad_maximum_fusion.1.refs_0_), channel_id=1, source_target_pairs={{0,256},{128,384},{256,0},{384,128},{1,257},{129,385},{257,1},{385... | collective-permute-start | bytes 798728 | tf_op jit(solution)/shard_map/ppermute | solution.py:28
  52.4 4.0 %collective-permute-start.2 = (bf16[1040,128]{1,0:T(8,128)(2,1)S(1)}, bf16[1040,128]{1,0:T(8,128)(2,1)S(1)}, u32[]{:S(2)}, u32[]{:S(2)}) collective-permute-start(bf16[1040,128]{1,0:T(8,128)(2,1)S(1)} %pad_maximum_fusion.1.refs_0_), channel_id=1, source_target_pairs={{0,128},{128,256},{256,384},{384,0},{1,129},{129,257},{257,385},{3... | collective-permute-start | bytes 798728 | tf_op jit(solution)/shard_map/ppermute | solution.py:28
  56.5 5.3 %collective-permute-done.4.refs_3_.refs_1_ = bf16[1040,128]{1,0:T(8,128)(2,1)S(1)} collective-permute-done((bf16[1040,128]{1,0:T(8,128)(2,1)S(1)}, bf16[1040,128]{1,0:T(8,128)(2,1)S(1)}, u32[]{:S(2)}, u32[]{:S(2)}) %collective-permute-start.4) | collective-permute-done | bytes 266272 | tf_op jit(solution)/shard_map/ppermute | solution.py:28
  61.7 2.4 %collective-permute-done.2.refs_1_.refs_0_ = bf16[1040,128]{1,0:T(8,128)(2,1)S(1)} collective-permute-done((bf16[1040,128]{1,0:T(8,128)(2,1)S(1)}, bf16[1040,128]{1,0:T(8,128)(2,1)S(1)}, u32[]{:S(2)}, u32[]{:S(2)}) %collective-permute-start.2) | collective-permute-done | bytes 266272 | tf_op jit(solution)/shard_map/ppermute | solution.py:28
  64.2 0.0 collective-permute-done.1
  64.2 5.2 %collective-permute-done = bf16[16,128,128]{2,1,0:T(8,128)(2,1)S(1)} collective-permute-done((bf16[16,128,128]{2,1,0:T(8,128)(2,1)S(1)}, bf16[16,128,128]{2,1,0:T(8,128)(2,1)S(1)}, u32[]{:S(2)}, u32[]{:S(2)}) %collective-permute-start) | collective-permute-done | bytes 524320 | tf_op jit(solution)/shard_map/ppermute | solution.py:28
  69.4 0.2 pad_maximum_fusion.refs_4_
  69.6 1.9 %collective-permute-start.7 = (bf16[3,16,128,128]{3,2,1,0:T(8,128)(2,1)S(1)}, bf16[3,16,128,128]{3,2,1,0:T(8,128)(2,1)S(1)}, u32[]{:S(2)}, u32[]{:S(2)}) collective-permute-start(bf16[3,16,128,128]{3,2,1,0:T(8,128)(2,1)S(1)} %pad_maximum_fusion.refs_4_), channel_id=1, source_target_pairs={{0,16},{16,0},{1,17},{17,1},{2,18},{18,2},{3,19},{19,3},{4,20},{20... | collective-permute-start | bytes 4718600 | tf_op jit(solution)/shard_map/ppermute | solution.py:28
  71.6 3.4 %collective-permute-start.6 = (bf16[8,128,128]{2,1,0:T(8,128)(2,1)S(1)}, bf16[8,128,128]{2,1,0:T(8,128)(2,1)S(1)}, u32[]{:S(2)}, u32[]{:S(2)}) collective-permute-start(bf16[8,128,128]{2,1,0:T(8,128)(2,1)S(1)} %slice.15), channel_id=1, source_target_pairs={{0,96},{32,0},{64,32},{96,64},{1,97},{33,1},{65,33},{97,65},{2,98}... | collective-permute-start | bytes 786440 | tf_op jit(solution)/shard_map/ppermute | solution.py:28
  74.9 3.4 %collective-permute-start.5 = (bf16[8,128,128]{2,1,0:T(8,128)(2,1)S(1)}, bf16[8,128,128]{2,1,0:T(8,128)(2,1)S(1)}, u32[]{:S(2)}, u32[]{:S(2)}) collective-permute-start(bf16[8,128,128]{2,1,0:T(8,128)(2,1)S(1)} %slice.14), channel_id=1, source_target_pairs={{0,32},{32,64},{64,96},{96,0},{1,33},{33,65},{65,97},{97,1},{2,34}... | collective-permute-start | bytes 786440 | tf_op jit(solution)/shard_map/ppermute | solution.py:28
  78.3 0.0 collective-permute-done.7.refs_5_
  78.3 9.9 %shard_map.47 = (f32[1024,128]{1,0:T(8,128)S(1)}, f32[1024,128]{1,0:T(8,128)S(1)}, f32[1024,128]{1,0:T(8,128)S(1)}, f32[1024,128]{1,0:T(8,128)S(1)}, f32[1024,12...) custom-call(bf16[1040,128]{1,0:T(8,128)(2,1)S(1)} %pad_maximum_fusion.1.refs_0_, ...), custom_call_target="tpu_custom_call" | custom-call | flops 1610612736 | bytes 2097152 | tf_op jit(solution)/shard_map/pallas_call | solution.py:164
  88.3 4.3 %collective-permute-done.5 = bf16[8,128,128]{2,1,0:T(8,128)(2,1)S(1)} collective-permute-done((bf16[8,128,128]{2,1,0:T(8,128)(2,1)S(1)}, bf16[8,128,128]{2,1,0:T(8,128)(2,1)S(1)}, u32[]{:S(2)}, u32[]{:S(2)}) %collective-permute-start.5) | collective-permute-done | bytes 262176 | tf_op jit(solution)/shard_map/ppermute | solution.py:28
  92.7 2.1 %collective-permute-start.8 = (bf16[1,16,128,128]{3,2,1,0:T(8,128)(2,1)S(1)}, bf16[1,16,128,128]{3,2,1,0:T(8,128)(2,1)S(1)}, u32[]{:S(2)}, u32[]{:S(2)}) collective-permute-start(bf16[1,16,128,128]{3,2,1,0:T(8,128)(2,1)S(1)} %maximum_bitcast_fusion.refs_1_.refs_2_), channel_id=1, source_target_pairs={{0,16},{16,0},{1,17},{17,1},{2,18},{18,2},{3,19},{19,3},{4,20},{20... | collective-permute-start | bytes 1572872 | tf_op jit(solution)/shard_map/ppermute | solution.py:28
  94.8 1.7 %collective-permute-done.8.refs_2_.refs_3_ = bf16[1,16,128,128]{3,2,1,0:T(8,128)(2,1)S(1)} collective-permute-done((bf16[1,16,128,128]{3,2,1,0:T(8,128)(2,1)S(1)}, bf16[1,16,128,128]{3,2,1,0:T(8,128)(2,1)S(1)}, u32[]{:S(2)}, u32[]{:S(2)}) %collective-permute-start.8) | collective-permute-done | bytes 524320 | tf_op jit(solution)/shard_map/ppermute | solution.py:28
  96.5 5.4 %shard_map.48 = bf16[1056,128]{1,0:T(8,128)(2,1)S(1)} custom-call(bf16[1040,128]{1,0:T(8,128)(2,1)S(1)} %collective-permute-done.3.refs_2_.refs_0_, bf16[1,16,128,128]{3,2,1,0:T(8,128)(2,1)S(1)} %maximum_bitcast_fusion.refs_1_.refs_2_, bf16[1,16,128,128]{3,2,1,0:T(8,128)(2,1)S(1)} %collective-permute-done.8.refs_2_.refs_3_, ...), custom_call_target="tpu_custom_call" | custom-call | flops 134217728 | bytes 2097152 | tf_op jit(solution)/shard_map/pallas_call | solution.py:164
  101.9 10.8 %shard_map.49 = (bf16[1056,128]{1,0:T(8,128)(2,1)S(1)}, bf16[1056,128]{1,0:T(8,128)(2,1)S(1)}) custom-call(bf16[1040,128]{1,0:T(8,128)(2,1)S(1)} %collective-permute-done.2.refs_1_.refs_0_, bf16[1040,128]{1,0:T(8,128)(2,1)S(1)} %collective-permute-done.4.refs_3_.refs_1_, bf16[1,16,128,128]{3,2,1,0:T(8,128)(2,1)S(1)} %maximum_bitcast_fusion.refs_1_.refs_2_, ...), custom_call_target="tpu_custom_call" | custom-call | flops 268435456 | bytes 2097152 | tf_op jit(solution)/shard_map/pallas_call | solution.py:164
  112.7 2.7 %collective-permute-start.9 = (bf16[1056,128]{1,0:T(8,128)(2,1)S(1)}, bf16[1056,128]{1,0:T(8,128)(2,1)S(1)}, u32[]{:S(2)}, u32[]{:S(2)}) collective-permute-start(bf16[1056,128]{1,0:T(8,128)(2,1)S(1)} %get-tuple-element.66), channel_id=1, source_target_pairs={{0,384},{128,0},{256,128},{384,256},{1,385},{129,1},{257,129},{385... | collective-permute-start | bytes 811016 | tf_op jit(solution)/shard_map/ppermute | solution.py:28
  115.4 4.3 %collective-permute-start.11 = (bf16[1056,128]{1,0:T(8,128)(2,1)S(1)}, bf16[1056,128]{1,0:T(8,128)(2,1)S(1)}, u32[]{:S(2)}, u32[]{:S(2)}) collective-permute-start(bf16[1056,128]{1,0:T(8,128)(2,1)S(1)} %get-tuple-element.68), channel_id=1, source_target_pairs={{0,128},{128,256},{256,384},{384,0},{1,129},{129,257},{257,385},{3... | collective-permute-start | bytes 811016 | tf_op jit(solution)/shard_map/ppermute | solution.py:28
  119.8 2.1 %collective-permute-start.10 = (bf16[1056,128]{1,0:T(8,128)(2,1)S(1)}, bf16[1056,128]{1,0:T(8,128)(2,1)S(1)}, u32[]{:S(2)}, u32[]{:S(2)}) collective-permute-start(bf16[1056,128]{1,0:T(8,128)(2,1)S(1)} %shard_map.48), channel_id=1, source_target_pairs={{0,256},{128,384},{256,0},{384,128},{1,257},{129,385},{257,1},{385... | collective-permute-start | bytes 811016 | tf_op jit(solution)/shard_map/ppermute | solution.py:28
  121.9 5.4 %shard_map.50.refs_0_ = bf16[1056,128]{1,0:T(8,128)(2,1)S(1)} custom-call(bf16[1040,128]{1,0:T(8,128)(2,1)S(1)} %pad_maximum_fusion.1.refs_0_, bf16[1,16,128,128]{3,2,1,0:T(8,128)(2,1)S(1)} %maximum_bitcast_fusion.refs_1_.refs_2_, bf16[1,16,128,128]{3,2,1,0:T(8,128)(2,1)S(1)} %collective-permute-done.8.refs_2_.refs_3_, ...), custom_call_target="tpu_custom_call" | custom-call | flops 134217728 | bytes 2097152 | tf_op jit(solution)/shard_map/pallas_call | solution.py:164
  127.3 4.1 %collective-permute-done.11.refs_3_ = bf16[1056,128]{1,0:T(8,128)(2,1)S(1)} collective-permute-done((bf16[1056,128]{1,0:T(8,128)(2,1)S(1)}, bf16[1056,128]{1,0:T(8,128)(2,1)S(1)}, u32[]{:S(2)}, u32[]{:S(2)}) %collective-permute-start.11) | collective-permute-done | bytes 270368 | tf_op jit(solution)/shard_map/ppermute | solution.py:28
  131.3 0.6 shard_map.51
  132.0 15.9 %all_to_all.11.in_ref = bf16[16,64,128]{2,1,0:T(8,128)(2,1)S(1)} all-to-all(bf16[16,64,128]{2,1,0:T(8,128)(2,1)S(1)} %bitcast.8), channel_id=1, replica_groups=mesh['x'=4,'zh'=4,'core'=2,'y'=8,'zl'=2] {'y','zl'}, dimensions={0} | all-to-all | bytes 524288 | tf_op jit(solution)/shard_map/all_to_all | solution.py:223
  147.9 0.7 shard_map.52
  (10 shorter events, 0.1 us)
Async XLA Ops:
  2.1 44.5 %copy-start = (bf16[16,128]{1,0:T(8,128)(2,1)S(1)}, bf16[16,128]{1,0:T(8,128)(2,1)}, u32[]{:S(2)}) copy-start(bf16[16,128]{1,0:T(8,128)(2,1)} %get-tuple-element.38) | copy-start | bytes 12292
  34.6 29.5 %collective-permute-start.1 = (bf16[16,128,128]{2,1,0:T(8,128)(2,1)S(1)}, bf16[16,128,128]{2,1,0:T(8,128)(2,1)S(1)}, u32[]{:S(2)}, u32[]{:S(2)}) collective-permute-start(bf16[16,128,128]{2,1,0:T(8,128)(2,1)S(1)} %get-tuple-element.70), channel_id=1, source_target_pairs={{0,96},{32,0},{64,32},{96,64},{1,97},{33,1},{65,33},{97,65},{2,98}... | collective-permute-start | bytes 1572872 | tf_op jit(solution)/shard_map/ppermute | solution.py:28
  44.7 24.7 %collective-permute-start = (bf16[16,128,128]{2,1,0:T(8,128)(2,1)S(1)}, bf16[16,128,128]{2,1,0:T(8,128)(2,1)S(1)}, u32[]{:S(2)}, u32[]{:S(2)}) collective-permute-start(bf16[16,128,128]{2,1,0:T(8,128)(2,1)S(1)} %get-tuple-element.70), channel_id=1, source_target_pairs={{0,32},{32,64},{64,96},{96,0},{1,33},{33,65},{65,97},{97,1},{2,34}... | collective-permute-start | bytes 1572872 | tf_op jit(solution)/shard_map/ppermute | solution.py:28
  46.7 15.1 %collective-permute-start.4 = (bf16[1040,128]{1,0:T(8,128)(2,1)S(1)}, bf16[1040,128]{1,0:T(8,128)(2,1)S(1)}, u32[]{:S(2)}, u32[]{:S(2)}) collective-permute-start(bf16[1040,128]{1,0:T(8,128)(2,1)S(1)} %pad_maximum_fusion.1.refs_0_), channel_id=1, source_target_pairs={{0,384},{128,0},{256,128},{384,256},{1,385},{129,1},{257,129},{385... | collective-permute-start | bytes 798728 | tf_op jit(solution)/shard_map/ppermute | solution.py:28
  49.4 12.3 %collective-permute-start.3 = (bf16[1040,128]{1,0:T(8,128)(2,1)S(1)}, bf16[1040,128]{1,0:T(8,128)(2,1)S(1)}, u32[]{:S(2)}, u32[]{:S(2)}) collective-permute-start(bf16[1040,128]{1,0:T(8,128)(2,1)S(1)} %pad_maximum_fusion.1.refs_0_), channel_id=1, source_target_pairs={{0,256},{128,384},{256,0},{384,128},{1,257},{129,385},{257,1},{385... | collective-permute-start | bytes 798728 | tf_op jit(solution)/shard_map/ppermute | solution.py:28
  52.4 11.7 %collective-permute-start.2 = (bf16[1040,128]{1,0:T(8,128)(2,1)S(1)}, bf16[1040,128]{1,0:T(8,128)(2,1)S(1)}, u32[]{:S(2)}, u32[]{:S(2)}) collective-permute-start(bf16[1040,128]{1,0:T(8,128)(2,1)S(1)} %pad_maximum_fusion.1.refs_0_), channel_id=1, source_target_pairs={{0,128},{128,256},{256,384},{384,0},{1,129},{129,257},{257,385},{3... | collective-permute-start | bytes 798728 | tf_op jit(solution)/shard_map/ppermute | solution.py:28
  69.6 8.7 %collective-permute-start.7 = (bf16[3,16,128,128]{3,2,1,0:T(8,128)(2,1)S(1)}, bf16[3,16,128,128]{3,2,1,0:T(8,128)(2,1)S(1)}, u32[]{:S(2)}, u32[]{:S(2)}) collective-permute-start(bf16[3,16,128,128]{3,2,1,0:T(8,128)(2,1)S(1)} %pad_maximum_fusion.refs_4_), channel_id=1, source_target_pairs={{0,16},{16,0},{1,17},{17,1},{2,18},{18,2},{3,19},{19,3},{4,20},{20... | collective-permute-start | bytes 4718600 | tf_op jit(solution)/shard_map/ppermute | solution.py:28
  71.6 16.7 %collective-permute-start.6 = (bf16[8,128,128]{2,1,0:T(8,128)(2,1)S(1)}, bf16[8,128,128]{2,1,0:T(8,128)(2,1)S(1)}, u32[]{:S(2)}, u32[]{:S(2)}) collective-permute-start(bf16[8,128,128]{2,1,0:T(8,128)(2,1)S(1)} %slice.15), channel_id=1, source_target_pairs={{0,96},{32,0},{64,32},{96,64},{1,97},{33,1},{65,33},{97,65},{2,98}... | collective-permute-start | bytes 786440 | tf_op jit(solution)/shard_map/ppermute | solution.py:28
  74.9 17.7 %collective-permute-start.5 = (bf16[8,128,128]{2,1,0:T(8,128)(2,1)S(1)}, bf16[8,128,128]{2,1,0:T(8,128)(2,1)S(1)}, u32[]{:S(2)}, u32[]{:S(2)}) collective-permute-start(bf16[8,128,128]{2,1,0:T(8,128)(2,1)S(1)} %slice.14), channel_id=1, source_target_pairs={{0,32},{32,64},{64,96},{96,0},{1,33},{33,65},{65,97},{97,1},{2,34}... | collective-permute-start | bytes 786440 | tf_op jit(solution)/shard_map/ppermute | solution.py:28
  92.7 3.8 %collective-permute-start.8 = (bf16[1,16,128,128]{3,2,1,0:T(8,128)(2,1)S(1)}, bf16[1,16,128,128]{3,2,1,0:T(8,128)(2,1)S(1)}, u32[]{:S(2)}, u32[]{:S(2)}) collective-permute-start(bf16[1,16,128,128]{3,2,1,0:T(8,128)(2,1)S(1)} %maximum_bitcast_fusion.refs_1_.refs_2_), channel_id=1, source_target_pairs={{0,16},{16,0},{1,17},{17,1},{2,18},{18,2},{3,19},{19,3},{4,20},{20... | collective-permute-start | bytes 1572872 | tf_op jit(solution)/shard_map/ppermute | solution.py:28
  112.7 14.5 %collective-permute-start.9 = (bf16[1056,128]{1,0:T(8,128)(2,1)S(1)}, bf16[1056,128]{1,0:T(8,128)(2,1)S(1)}, u32[]{:S(2)}, u32[]{:S(2)}) collective-permute-start(bf16[1056,128]{1,0:T(8,128)(2,1)S(1)} %get-tuple-element.66), channel_id=1, source_target_pairs={{0,384},{128,0},{256,128},{384,256},{1,385},{129,1},{257,129},{385... | collective-permute-start | bytes 811016 | tf_op jit(solution)/shard_map/ppermute | solution.py:28
  115.4 15.9 %collective-permute-start.11 = (bf16[1056,128]{1,0:T(8,128)(2,1)S(1)}, bf16[1056,128]{1,0:T(8,128)(2,1)S(1)}, u32[]{:S(2)}, u32[]{:S(2)}) collective-permute-start(bf16[1056,128]{1,0:T(8,128)(2,1)S(1)} %get-tuple-element.68), channel_id=1, source_target_pairs={{0,128},{128,256},{256,384},{384,0},{1,129},{129,257},{257,385},{3... | collective-permute-start | bytes 811016 | tf_op jit(solution)/shard_map/ppermute | solution.py:28
  119.8 11.6 %collective-permute-start.10 = (bf16[1056,128]{1,0:T(8,128)(2,1)S(1)}, bf16[1056,128]{1,0:T(8,128)(2,1)S(1)}, u32[]{:S(2)}, u32[]{:S(2)}) collective-permute-start(bf16[1056,128]{1,0:T(8,128)(2,1)S(1)} %shard_map.48), channel_id=1, source_target_pairs={{0,256},{128,384},{256,0},{384,128},{1,257},{129,385},{257,1},{385... | collective-permute-start | bytes 811016 | tf_op jit(solution)/shard_map/ppermute | solution.py:28

commit v8 on v7

v8 whole, which is shorter than its diff:
```python
import functools
import math

import jax
import jax.numpy as jnp
from jax import lax
from jax.experimental import pallas as pl
from jax.experimental.pallas import tpu as pltpu
from jax.sharding import Mesh, PartitionSpec as P

BF = jnp.bfloat16
F32 = jnp.float32
NX, NZ, NC, NU = 4, 4, 2, 16
HEADS, HD, BS, TOK = 12, 128, 128, 64
SEGB = 8
ROWS = SEGB * BS
PICKS = 16
LSE = 32
STEPS = 4
EXP2 = math.log2(math.e) / math.sqrt(HD)
AXES = ("x", "zh", "core", "y", "zl")
VMEM = pl.BlockSpec(memory_space=pltpu.VMEM)
HBM = pl.BlockSpec(memory_space=pltpu.HBM)


def shift(field, axis, by):
    n = lax.axis_size(axis)
    return lax.ppermute(field, axis, [(i, (i + by) % n) for i in range(n)])


def exchange(field, axes):
    return lax.all_to_all(field, axes, split_axis=0, concat_axis=0, tiled=True)


def pack_kernel(q_hbm, k_hbm, v_hbm, mask_hbm, out_ref, picks_ref, q_ref, k_ref, v_ref, mask_ref, sems):
    head = jnp.minimum(lax.axis_index("y") * 2 + lax.axis_index("zl"), HEADS - 1)
    pairs = ((q_hbm, q_ref), (k_hbm, k_ref), (v_hbm, v_ref), (mask_hbm.at[head], mask_ref))
    copies = [pltpu.make_async_copy(src, dst, sems.at[i]) for i, (src, dst) in enumerate(pairs)]
    for copy in copies:
        copy.start()
    for s in range(HEADS, NU):
        out_ref[s] = jnp.zeros((3 * TOK, HD), BF)
    for n, ref in enumerate((q_ref, k_ref, v_ref)):
        copies[n].wait()
        for h in range(HEADS):
            out_ref[h, n * TOK : (n + 1) * TOK, :] = ref[:, h * HD : (h + 1) * HD]
    copies[3].wait()
    live = mask_ref[...].astype(F32).astype(BF)
    cols = live.shape[1]
    i = lax.broadcasted_iota(jnp.int32, (cols, HD), 0)
    g = lax.broadcasted_iota(jnp.int32, (cols, HD), 1)
    weight = jnp.where(i // SEGB == g, i % SEGB, 0).astype(F32).astype(BF)
    picks = jnp.dot(live, weight, preferred_element_type=F32)
    picks_ref[...] = jnp.concatenate([picks, jnp.zeros((PICKS - SEGB, HD), F32)], axis=0).astype(BF)


def split3(lse):
    hi = lse.astype(BF).astype(F32)
    mid = (lse - hi).astype(BF).astype(F32)
    return jnp.concatenate([hi, mid, lse - hi - mid, jnp.zeros_like(hi)], axis=0).astype(BF)


def join3(rows):
    rows = rows.astype(F32)
    return rows[0:SEGB] + rows[SEGB : 2 * SEGB] + rows[2 * SEGB : 3 * SEGB]


def attend_kernel(chunks, shifts, unit, opening, *refs):
    q_refs, (near_ref, far_ref), rest = refs[:chunks], refs[chunks : chunks + 2], refs[chunks + 2 :]
    old_refs = () if opening else rest[:chunks]
    rest = rest[len(old_refs) :]
    out_refs, (flat_ref, picks_ref, sem) = rest[:-3], rest[-3:]
    for n, q_ref in enumerate(q_refs):
        flat_ref[n * SEGB : (n + 1) * SEGB, :] = q_ref[ROWS:, :].astype(F32)[:SEGB].astype(jnp.int32)
    fetch = pltpu.make_async_copy(flat_ref, picks_ref, sem)
    fetch.start()
    x, z, c = lax.axis_index("x"), lax.axis_index("zh"), lax.axis_index("core")
    if not opening:
        out_refs = [out_refs[0].at[(x + NX - n) % NX] for n in range(chunks)]
    columns = [(x * NZ + (z + NZ - dz) % NZ) * NC + cc for dz in shifts for cc in (c, 1 - c)]
    groups = [ref.at[n] for n in range(len(shifts)) for ref in (near_ref, far_ref)]
    fetch.wait()
    blocks = [(n, b) for n in range(chunks) for b in range(SEGB)]
    units = [blocks[i : i + unit] for i in range(0, len(blocks), unit)]
    fetched, scores, weights, peaks, totals, products = {}, {}, {}, {}, {}, {}
    lses = [[] for _ in q_refs]
    for t in range(len(units) + 2):
        ahead, here, last = (units[i] if 0 <= i < len(units) else [] for i in (t, t - 1, t - 2))
        for n, b in ahead:
            keys, values = [], []
            for group, column in zip(groups, columns):
                both = group[pl.ds(2 * picks_ref[n * SEGB + b, column], 2)]
                keys.append(both[:, :TOK, :].reshape(BS, HD))
                values.append(both[:, TOK:, :].reshape(BS, HD))
            fetched[n, b] = q_refs[n][b * BS : (b + 1) * BS, :], keys, values
            scores[n, b] = []
        for block in here:
            weights[block], peaks[block], totals[block] = [], [], []
        for block in last:
            products[block] = []
        for step in range(STEPS):
            pair = slice(2 * step, 2 * step + 2)
            rows = slice(step * BS // STEPS, (step + 1) * BS // STEPS)
            for i in range(unit):
                if i < len(ahead) and step < len(shifts):
                    q, keys, _ = fetched[ahead[i]]
                    both = jnp.concatenate(keys[pair], axis=0)
                    scores[ahead[i]].append(
                        lax.dot_general(q, both, (((1,), (1,)), ((), ())), preferred_element_type=F32)
                    )
                if i < len(here):
                    part = [s[rows] for s in scores[here[i]]]
                    peak = jnp.max(functools.reduce(jnp.maximum, part), axis=1, keepdims=True)
                    w = [jnp.exp2((s - peak) * EXP2) for s in part]
                    totals[here[i]].append(jnp.sum(functools.reduce(jnp.add, w), axis=1, keepdims=True))
                    peaks[here[i]].append(peak)
                    weights[here[i]].append([p.astype(BF) for p in w])
                if i < len(last) and step < len(shifts):
                    w = jnp.concatenate([p[step] for p in weights[last[i]]], axis=0)
                    both = jnp.concatenate(fetched[last[i]][2][pair], axis=0)
                    products[last[i]].append(jnp.dot(w, both, preferred_element_type=F32))
        for block in last:
            n, b = block
            peak, total = jnp.concatenate(peaks[block], axis=0), jnp.concatenate(totals[block], axis=0)
            rows = slice(b * BS, (b + 1) * BS)
            o = functools.reduce(jnp.add, products[block]) * (1.0 / total)
            lse = jnp.broadcast_to(peak * EXP2 + jnp.log2(total), (BS, HD))
            if opening:
                out_refs[n][0, rows, :] = o
                out_refs[n][1, rows, :] = lse
            else:
                old, old_lse = old_refs[n][0, rows, :], old_refs[n][1, rows, :]
                top = jnp.maximum(lse, old_lse)
                share, old_share = jnp.exp2(lse - top), jnp.exp2(old_lse - top)
                total = share + old_share
                out_refs[n][rows, :] = ((o * share + old * old_share) * (1.0 / total)).astype(BF)
                lses[n].append(jnp.transpose(top + jnp.log2(total))[0:1, :])
                if b == SEGB - 1:
                    out_refs[n][ROWS:, :] = split3(jnp.concatenate(lses[n], axis=0))
            fetched[block] = scores[block] = weights[block] = products[block] = None


def merge_kernel(in_ref, out_ref):
    ins = [in_ref.at[n] for n in range(NX)]
    lses = [join3(r[ROWS:, :]) for r in ins]
    top = functools.reduce(jnp.maximum, lses)
    parts = [jnp.exp2(s - top) for s in lses]
    total = functools.reduce(jnp.add, parts)
    parts = [p / total for p in parts]
    for b in range(SEGB):
        rows = slice(b * BS, (b + 1) * BS)
        acc = jnp.zeros((BS, HD), F32)
        for r, p in zip(ins, parts):
            acc = acc + jnp.transpose(jnp.broadcast_to(p[b : b + 1, :], (BS, HD))) * r[rows, :].astype(F32)
        out_ref[rows, :] = acc.astype(BF)


def unpack_kernel(in_ref, out_ref):
    for h in range(HEADS):
        out_ref[:, h * HD : (h + 1) * HD] = in_ref[h]


def call(kernel, outs, specs, *args, scratch=(), flops=0, moved=1 << 18, vmem=24):
    return pl.pallas_call(
        kernel,
        out_shape=outs,
        in_specs=specs,
        out_specs=jax.tree.map(lambda _: VMEM, outs),
        scratch_shapes=list(scratch),
        compiler_params=pltpu.CompilerParams(vmem_limit_bytes=vmem << 20),
        cost_estimate=pl.CostEstimate(flops=flops, bytes_accessed=moved, transcendentals=0),
    )(*args)


def attend(queries, shifts, near, far, old=None):
    n = len(queries)
    if old is None:
        outs = [jax.ShapeDtypeStruct((2, ROWS, HD), F32)] * n
        unit = 4
    else:
        outs = jax.ShapeDtypeStruct((n, ROWS + LSE, HD), BF)
        unit = 8
    ins = [*queries, near, far, *(old or [])]
    return call(
        functools.partial(attend_kernel, n, shifts, unit, old is None),
        outs, [VMEM] * len(ins), *ins,
        scratch=[pltpu.VMEM((n * SEGB, HD), jnp.int32), pltpu.SMEM((n * SEGB, HD), jnp.int32), pltpu.SemaphoreType.DMA],
        flops=n * len(shifts) * (1 << 27), moved=2 << 20,
    )


def shards(queries, keys, values, block_mask):
    packed, picks = call(
        pack_kernel,
        (jax.ShapeDtypeStruct((NU, 3 * TOK, HD), BF), jax.ShapeDtypeStruct((PICKS, HD), BF)),
        [HBM] * 4, queries, keys, values, block_mask,
        scratch=[pltpu.VMEM(queries.shape, BF)] * 3
        + [pltpu.VMEM(block_mask.shape[1:], jnp.int32), pltpu.SemaphoreType.DMA((4,))],
        vmem=60,
    )
    got = exchange(packed, ("y", "zl"))
    k0 = got[:, TOK:]
    q0 = jnp.concatenate([got[:, :TOK].reshape(ROWS, HD), picks], axis=0)

    k1, k3 = shift(k0, "zh", 1), shift(k0, "zh", -1)
    q1, q2, q3 = (shift(q0, "x", dx) for dx in (1, 2, 3))
    k1, k3, q1, q2, q3 = lax.optimization_barrier((k1, k3, q1, q2, q3))
    k2a, k2b = shift(k1[: NU // 2], "zh", 1), shift(k3[NU // 2 :], "zh", -1)
    near = jnp.stack([k0, k1, k3])
    far = shift(near, "core", 1)
    old = attend([q0, q1, q2, q3], (0, 1, 3), near, far)

    k2a, k2b, *old = lax.optimization_barrier((k2a, k2b, *old))
    near = jnp.concatenate([k2a, k2b], axis=0)[None]
    far = shift(near, "core", 1)
    parts = attend([q0, q1, q2, q3], (2,), near, far, old)
    parts = exchange(parts, "x")
    whole = call(merge_kernel, jax.ShapeDtypeStruct((ROWS, HD), BF), [VMEM], parts)
    home = exchange(whole.reshape(NU, TOK, HD), ("y", "zl"))
    return call(unpack_kernel, jax.ShapeDtypeStruct((TOK, HEADS * HD), BF), [VMEM], home)


def solution(mesh):
    fine = Mesh(mesh.devices.reshape(NX, NZ, NC, NU // 2, 2), AXES)
    tokens = P(AXES, None)
    placed = (tokens, tokens, tokens, P(None, AXES[:3], None))
    return jax.shard_map(shards, mesh=fine, in_specs=placed, out_specs=tokens, check_vma=False)
```

time: 151 us -> 143 us (0.947)
  blocking collectives: 48.3 us -> 66.7 us
  Pallas kernels: 34.9 us -> 19.8 us
  starting transfers between devices: 41.6 us -> 32.5 us
    all_to_all x2 -> x3, blocking collectives: 48.3 us -> 66.7 us  [exchange(): return lax.all_to_all(field, axes, split_axis=0, concat_axis=0, tiled=True)]
    pallas_call x7 -> x5, Pallas kernels: 34.9 us -> 19.8 us  [call(): pl.pallas_call(kernel, out_shape=outs, in_specs=specs, out_specs=jax.tree...]
    ppermute x12 -> x9, starting transfers between devices: 41.6 us -> 32.5 us  [shift(): return lax.ppermute(field, axis, [(i, (i + by) % n) for i in range(n)])]
    ppermute x12 -> x9, waiting for transfers between devices: 23.1 us -> 21.7 us  [shift(): return lax.ppermute(field, axis, [(i, (i + by) % n) for i in range(n)])]
  transfers between devices with their start and end apart: 12 -> 9, of which waited for: 6 -> 6; matrix products, arithmetic and copies ran while one was open for 0% -> 0% of each run, Pallas kernels for 10% -> 5%
where the time goes in v8:
time: 143 us; the launch traced here: 141 us
  blocking collectives  66.7 us (47%)
  starting transfers between devices  32.5 us (23%)
  waiting for transfers between devices  21.7 us (15%)
  Pallas kernels  19.8 us (14%)
    all_to_all x3, blocking collectives, exchange(): return lax.all_to_all(field, axes, split_axis=0, concat_axis=0, tiled=True)  66.7 us
    ppermute x9, starting transfers between devices, shift(): return lax.ppermute(field, axis, [(i, (i + by) % n) for i in range(n)])  32.5 us
    ppermute x9, waiting for transfers between devices, shift(): return lax.ppermute(field, axis, [(i, (i + by) % n) for i in range(n)])  21.7 us
    pallas_call x5, Pallas kernels, call(): pl.pallas_call(kernel, out_shape=outs, in_specs=specs, out_specs=jax.tree...  19.8 us
  transfers between devices with their start and end apart: 9, of which 6 were waited for; matrix products, arithmetic and copies ran while one was open for 0% of the time, Pallas kernels for 5%

profile of v8, /device:TPU:6, one launch (start us, length us, event | category | flops | bytes accessed | tf_op | source)
XLA Modules:
  0.0 141.3 jit_solution(2241017649368840676)
XLA Ops:
  0.0 2.1 %shard_map.46 = (bf16[16,192,128]{2,1,0:T(8,128)(2,1)}, bf16[16,128]{1,0:T(8,128)(2,1)}) custom-call(bf16[64,1536]{1,0:T(8,128)(2,1)} %q_hbm.1, bf16[64,1536]{1,0:T(8,128)(2,1)} %k_hbm.1, bf16[64,1536]{1,0:T(8,128)(2,1)} %v_hbm.1, s32[12,8,256]{2,1,0:T(8,128)} %mask_hbm.1), custom_call_target="tpu_custom_call" | custom-call | bytes 262144 | tf_op jit(solution)/shard_map/pallas_call | solution.py:164
  2.1 0.0 copy-start
  2.1 32.4 %all_to_all.15 = bf16[16,192,128]{2,1,0:T(8,128)(2,1)S(1)} all-to-all(bf16[16,192,128]{2,1,0:T(8,128)(2,1)} %get-tuple-element.22), channel_id=1, replica_groups=mesh['x'=4,'zh'=4,'core'=2,'y'=8,'zl'=2] {'y','zl'}, dimensions={0} | all-to-all | bytes 1572864 | tf_op jit(solution)/shard_map/all_to_all | solution.py:32
  34.5 0.1 slice_bitcast_fusion
  34.6 10.0 %collective-permute-start.1 = (bf16[16,128,128]{2,1,0:T(8,128)(2,1)S(1)}, bf16[16,128,128]{2,1,0:T(8,128)(2,1)S(1)}, u32[]{:S(2)}, u32[]{:S(2)}) collective-permute-start(bf16[16,128,128]{2,1,0:T(8,128)(2,1)S(1)} %get-tuple-element.40), channel_id=1, source_target_pairs={{0,96},{32,0},{64,32},{96,64},{1,97},{33,1},{65,33},{97,65},{2,98}... | collective-permute-start | bytes 1572872 | tf_op jit(solution)/shard_map/ppermute | solution.py:28
  44.7 1.9 %collective-permute-start = (bf16[16,128,128]{2,1,0:T(8,128)(2,1)S(1)}, bf16[16,128,128]{2,1,0:T(8,128)(2,1)S(1)}, u32[]{:S(2)}, u32[]{:S(2)}) collective-permute-start(bf16[16,128,128]{2,1,0:T(8,128)(2,1)S(1)} %get-tuple-element.40), channel_id=1, source_target_pairs={{0,32},{32,64},{64,96},{96,0},{1,33},{33,65},{65,97},{97,1},{2,34}... | collective-permute-start | bytes 1572872 | tf_op jit(solution)/shard_map/ppermute | solution.py:28
  46.6 0.0 copy-done
  46.7 2.7 %collective-permute-start.4 = (bf16[1040,128]{1,0:T(8,128)(2,1)S(1)}, bf16[1040,128]{1,0:T(8,128)(2,1)S(1)}, u32[]{:S(2)}, u32[]{:S(2)}) collective-permute-start(bf16[1040,128]{1,0:T(8,128)(2,1)S(1)} %pad_maximum_fusion.1.refs_0_), channel_id=1, source_target_pairs={{0,384},{128,0},{256,128},{384,256},{1,385},{129,1},{257,129},{385... | collective-permute-start | bytes 798728 | tf_op jit(solution)/shard_map/ppermute | solution.py:28
  49.4 3.0 %collective-permute-start.3 = (bf16[1040,128]{1,0:T(8,128)(2,1)S(1)}, bf16[1040,128]{1,0:T(8,128)(2,1)S(1)}, u32[]{:S(2)}, u32[]{:S(2)}) collective-permute-start(bf16[1040,128]{1,0:T(8,128)(2,1)S(1)} %pad_maximum_fusion.1.refs_0_), channel_id=1, source_target_pairs={{0,256},{128,384},{256,0},{384,128},{1,257},{129,385},{257,1},{385... | collective-permute-start | bytes 798728 | tf_op jit(solution)/shard_map/ppermute | solution.py:28
  52.4 4.0 %collective-permute-start.2 = (bf16[1040,128]{1,0:T(8,128)(2,1)S(1)}, bf16[1040,128]{1,0:T(8,128)(2,1)S(1)}, u32[]{:S(2)}, u32[]{:S(2)}) collective-permute-start(bf16[1040,128]{1,0:T(8,128)(2,1)S(1)} %pad_maximum_fusion.1.refs_0_), channel_id=1, source_target_pairs={{0,128},{128,256},{256,384},{384,0},{1,129},{129,257},{257,385},{3... | collective-permute-start | bytes 798728 | tf_op jit(solution)/shard_map/ppermute | solution.py:28
  56.4 5.3 %collective-permute-done.4.refs_3_ = bf16[1040,128]{1,0:T(8,128)(2,1)S(1)} collective-permute-done((bf16[1040,128]{1,0:T(8,128)(2,1)S(1)}, bf16[1040,128]{1,0:T(8,128)(2,1)S(1)}, u32[]{:S(2)}, u32[]{:S(2)}) %collective-permute-start.4) | collective-permute-done | bytes 266272 | tf_op jit(solution)/shard_map/ppermute | solution.py:28
  61.7 0.0 collective-permute-done.3.refs_2_
  61.7 2.4 %collective-permute-done.2.refs_1_ = bf16[1040,128]{1,0:T(8,128)(2,1)S(1)} collective-permute-done((bf16[1040,128]{1,0:T(8,128)(2,1)S(1)}, bf16[1040,128]{1,0:T(8,128)(2,1)S(1)}, u32[]{:S(2)}, u32[]{:S(2)}) %collective-permute-start.2) | collective-permute-done | bytes 266272 | tf_op jit(solution)/shard_map/ppermute | solution.py:28
  64.1 0.0 collective-permute-done.1
  64.1 5.2 %collective-permute-done = bf16[16,128,128]{2,1,0:T(8,128)(2,1)S(1)} collective-permute-done((bf16[16,128,128]{2,1,0:T(8,128)(2,1)S(1)}, bf16[16,128,128]{2,1,0:T(8,128)(2,1)S(1)}, u32[]{:S(2)}, u32[]{:S(2)}) %collective-permute-start) | collective-permute-done | bytes 524320 | tf_op jit(solution)/shard_map/ppermute | solution.py:28
  69.4 0.2 pad_maximum_fusion.refs_4_
  69.6 1.9 %collective-permute-start.7 = (bf16[3,16,128,128]{3,2,1,0:T(8,128)(2,1)S(1)}, bf16[3,16,128,128]{3,2,1,0:T(8,128)(2,1)S(1)}, u32[]{:S(2)}, u32[]{:S(2)}) collective-permute-start(bf16[3,16,128,128]{3,2,1,0:T(8,128)(2,1)S(1)} %pad_maximum_fusion.refs_4_), channel_id=1, source_target_pairs={{0,16},{16,0},{1,17},{17,1},{2,18},{18,2},{3,19},{19,3},{4,20},{20... | collective-permute-start | bytes 4718600 | tf_op jit(solution)/shard_map/ppermute | solution.py:28
  71.5 3.4 %collective-permute-start.6 = (bf16[8,128,128]{2,1,0:T(8,128)(2,1)S(1)}, bf16[8,128,128]{2,1,0:T(8,128)(2,1)S(1)}, u32[]{:S(2)}, u32[]{:S(2)}) collective-permute-start(bf16[8,128,128]{2,1,0:T(8,128)(2,1)S(1)} %slice.15), channel_id=1, source_target_pairs={{0,96},{32,0},{64,32},{96,64},{1,97},{33,1},{65,33},{97,65},{2,98}... | collective-permute-start | bytes 786440 | tf_op jit(solution)/shard_map/ppermute | solution.py:28
  74.9 3.4 %collective-permute-start.5 = (bf16[8,128,128]{2,1,0:T(8,128)(2,1)S(1)}, bf16[8,128,128]{2,1,0:T(8,128)(2,1)S(1)}, u32[]{:S(2)}, u32[]{:S(2)}) collective-permute-start(bf16[8,128,128]{2,1,0:T(8,128)(2,1)S(1)} %slice.14), channel_id=1, source_target_pairs={{0,32},{32,64},{64,96},{96,0},{1,33},{33,65},{65,97},{97,1},{2,34}... | collective-permute-start | bytes 786440 | tf_op jit(solution)/shard_map/ppermute | solution.py:28
  78.3 0.0 collective-permute-done.7.refs_5_
  78.3 7.3 %shard_map.47 = (f32[2,1024,128]{2,1,0:T(8,128)S(1)}, f32[2,1024,128]{2,1,0:T(8,128)S(1)}, f32[2,1024,128]{2,1,0:T(8,128)S(1)}, f32[2,1024,128]{2,1,0:T(8,128)S(1)}) custom-call(bf16[1040,128]{1,0:T(8,128)(2,1)S(1)} %pad_maximum_fusion.1.refs_0_, bf16[1040,128]{1,0:T(8,128)(2,1)S(1)} %collective-permute-done.2.refs_1_, ...), custom_call_target="tpu_custom_call" | custom-call | flops 1610612736 | bytes 2097152 | tf_op jit(solution)/shard_map/pallas_call | solution.py:164
  85.6 2.1 %collective-permute-done.6 = bf16[8,128,128]{2,1,0:T(8,128)(2,1)S(1)} collective-permute-done((bf16[8,128,128]{2,1,0:T(8,128)(2,1)S(1)}, bf16[8,128,128]{2,1,0:T(8,128)(2,1)S(1)}, u32[]{:S(2)}, u32[]{:S(2)}) %collective-permute-start.6) | collective-permute-done | bytes 262176 | tf_op jit(solution)/shard_map/ppermute | solution.py:28
  87.7 5.0 %collective-permute-done.5 = bf16[8,128,128]{2,1,0:T(8,128)(2,1)S(1)} collective-permute-done((bf16[8,128,128]{2,1,0:T(8,128)(2,1)S(1)}, bf16[8,128,128]{2,1,0:T(8,128)(2,1)S(1)}, u32[]{:S(2)}, u32[]{:S(2)}) %collective-permute-start.5) | collective-permute-done | bytes 262176 | tf_op jit(solution)/shard_map/ppermute | solution.py:28
  92.7 2.1 %collective-permute-start.8 = (bf16[1,16,128,128]{3,2,1,0:T(8,128)(2,1)S(1)}, bf16[1,16,128,128]{3,2,1,0:T(8,128)(2,1)S(1)}, u32[]{:S(2)}, u32[]{:S(2)}) collective-permute-start(bf16[1,16,128,128]{3,2,1,0:T(8,128)(2,1)S(1)} %maximum_bitcast_fusion.refs_4_), channel_id=1, source_target_pairs={{0,16},{16,0},{1,17},{17,1},{2,18},{18,2},{3,19},{19,3},{4,20},{20... | collective-permute-start | bytes 1572872 | tf_op jit(solution)/shard_map/ppermute | solution.py:28
  94.8 1.7 %collective-permute-done.8.refs_5_ = bf16[1,16,128,128]{3,2,1,0:T(8,128)(2,1)S(1)} collective-permute-done((bf16[1,16,128,128]{3,2,1,0:T(8,128)(2,1)S(1)}, bf16[1,16,128,128]{3,2,1,0:T(8,128)(2,1)S(1)}, u32[]{:S(2)}, u32[]{:S(2)}) %collective-permute-start.8) | collective-permute-done | bytes 524320 | tf_op jit(solution)/shard_map/ppermute | solution.py:28
  96.5 9.2 %shard_map.48 = bf16[4,1056,128]{2,1,0:T(8,128)(2,1)S(1)} custom-call(bf16[1040,128]{1,0:T(8,128)(2,1)S(1)} %pad_maximum_fusion.1.refs_0_, bf16[1040,128]{1,0:T(8,128)(2,1)S(1)} %collective-permute-done.2.refs_1_, bf16[1040,128]{1,0:T(8,128)(2,1)S(1)} %collective-permute-done.3.refs_2_, bf16[1040,128]{1,0:T(8,128)(2,1)S(1)} %collective-permute-done.4.refs_3_, ...), custom_call_target="tpu_custom_call" | custom-call | flops 536870912 | bytes 2097152 | tf_op jit(solution)/shard_map/pallas_call | solution.py:164
  105.6 18.3 %all_to_all.16.in_ref = bf16[4,1056,128]{2,1,0:T(8,128)(2,1)S(1)} all-to-all(bf16[4,1056,128]{2,1,0:T(8,128)(2,1)S(1)} %shard_map.48), channel_id=1, replica_groups=mesh['x'=4,'zh'=4,'core'=2,'y'=8,'zl'=2] {'x'}, dimensions={0} | all-to-all | bytes 2162688 | tf_op jit(solution)/shard_map/all_to_all | solution.py:32
  123.9 0.6 shard_map.49
  124.5 16.1 %all_to_all.17.in_ref = bf16[16,64,128]{2,1,0:T(8,128)(2,1)S(1)} all-to-all(bf16[16,64,128]{2,1,0:T(8,128)(2,1)S(1)} %bitcast.8), channel_id=1, replica_groups=mesh['x'=4,'zh'=4,'core'=2,'y'=8,'zl'=2] {'y','zl'}, dimensions={0} | all-to-all | bytes 524288 | tf_op jit(solution)/shard_map/all_to_all | solution.py:32
  140.6 0.7 shard_map.50
  (5 shorter events, 0.1 us)
Async XLA Ops:
  2.1 44.5 %copy-start = (bf16[16,128]{1,0:T(8,128)(2,1)S(1)}, bf16[16,128]{1,0:T(8,128)(2,1)}, u32[]{:S(2)}) copy-start(bf16[16,128]{1,0:T(8,128)(2,1)} %get-tuple-element.23) | copy-start | bytes 12292
  34.6 29.5 %collective-permute-start.1 = (bf16[16,128,128]{2,1,0:T(8,128)(2,1)S(1)}, bf16[16,128,128]{2,1,0:T(8,128)(2,1)S(1)}, u32[]{:S(2)}, u32[]{:S(2)}) collective-permute-start(bf16[16,128,128]{2,1,0:T(8,128)(2,1)S(1)} %get-tuple-element.40), channel_id=1, source_target_pairs={{0,96},{32,0},{64,32},{96,64},{1,97},{33,1},{65,33},{97,65},{2,98}... | collective-permute-start | bytes 1572872 | tf_op jit(solution)/shard_map/ppermute | solution.py:28
  44.7 24.7 %collective-permute-start = (bf16[16,128,128]{2,1,0:T(8,128)(2,1)S(1)}, bf16[16,128,128]{2,1,0:T(8,128)(2,1)S(1)}, u32[]{:S(2)}, u32[]{:S(2)}) collective-permute-start(bf16[16,128,128]{2,1,0:T(8,128)(2,1)S(1)} %get-tuple-element.40), channel_id=1, source_target_pairs={{0,32},{32,64},{64,96},{96,0},{1,33},{33,65},{65,97},{97,1},{2,34}... | collective-permute-start | bytes 1572872 | tf_op jit(solution)/shard_map/ppermute | solution.py:28
  46.7 15.1 %collective-permute-start.4 = (bf16[1040,128]{1,0:T(8,128)(2,1)S(1)}, bf16[1040,128]{1,0:T(8,128)(2,1)S(1)}, u32[]{:S(2)}, u32[]{:S(2)}) collective-permute-start(bf16[1040,128]{1,0:T(8,128)(2,1)S(1)} %pad_maximum_fusion.1.refs_0_), channel_id=1, source_target_pairs={{0,384},{128,0},{256,128},{384,256},{1,385},{129,1},{257,129},{385... | collective-permute-start | bytes 798728 | tf_op jit(solution)/shard_map/ppermute | solution.py:28
  49.4 12.3 %collective-permute-start.3 = (bf16[1040,128]{1,0:T(8,128)(2,1)S(1)}, bf16[1040,128]{1,0:T(8,128)(2,1)S(1)}, u32[]{:S(2)}, u32[]{:S(2)}) collective-permute-start(bf16[1040,128]{1,0:T(8,128)(2,1)S(1)} %pad_maximum_fusion.1.refs_0_), channel_id=1, source_target_pairs={{0,256},{128,384},{256,0},{384,128},{1,257},{129,385},{257,1},{385... | collective-permute-start | bytes 798728 | tf_op jit(solution)/shard_map/ppermute | solution.py:28
  52.4 11.7 %collective-permute-start.2 = (bf16[1040,128]{1,0:T(8,128)(2,1)S(1)}, bf16[1040,128]{1,0:T(8,128)(2,1)S(1)}, u32[]{:S(2)}, u32[]{:S(2)}) collective-permute-start(bf16[1040,128]{1,0:T(8,128)(2,1)S(1)} %pad_maximum_fusion.1.refs_0_), channel_id=1, source_target_pairs={{0,128},{128,256},{256,384},{384,0},{1,129},{129,257},{257,385},{3... | collective-permute-start | bytes 798728 | tf_op jit(solution)/shard_map/ppermute | solution.py:28
  69.6 8.7 %collective-permute-start.7 = (bf16[3,16,128,128]{3,2,1,0:T(8,128)(2,1)S(1)}, bf16[3,16,128,128]{3,2,1,0:T(8,128)(2,1)S(1)}, u32[]{:S(2)}, u32[]{:S(2)}) collective-permute-start(bf16[3,16,128,128]{3,2,1,0:T(8,128)(2,1)S(1)} %pad_maximum_fusion.refs_4_), channel_id=1, source_target_pairs={{0,16},{16,0},{1,17},{17,1},{2,18},{18,2},{3,19},{19,3},{4,20},{20... | collective-permute-start | bytes 4718600 | tf_op jit(solution)/shard_map/ppermute | solution.py:28
  71.5 16.1 %collective-permute-start.6 = (bf16[8,128,128]{2,1,0:T(8,128)(2,1)S(1)}, bf16[8,128,128]{2,1,0:T(8,128)(2,1)S(1)}, u32[]{:S(2)}, u32[]{:S(2)}) collective-permute-start(bf16[8,128,128]{2,1,0:T(8,128)(2,1)S(1)} %slice.15), channel_id=1, source_target_pairs={{0,96},{32,0},{64,32},{96,64},{1,97},{33,1},{65,33},{97,65},{2,98}... | collective-permute-start | bytes 786440 | tf_op jit(solution)/shard_map/ppermute | solution.py:28
  74.9 17.7 %collective-permute-start.5 = (bf16[8,128,128]{2,1,0:T(8,128)(2,1)S(1)}, bf16[8,128,128]{2,1,0:T(8,128)(2,1)S(1)}, u32[]{:S(2)}, u32[]{:S(2)}) collective-permute-start(bf16[8,128,128]{2,1,0:T(8,128)(2,1)S(1)} %slice.14), channel_id=1, source_target_pairs={{0,32},{32,64},{64,96},{96,0},{1,33},{33,65},{65,97},{97,1},{2,34}... | collective-permute-start | bytes 786440 | tf_op jit(solution)/shard_map/ppermute | solution.py:28
  92.7 3.8 %collective-permute-start.8 = (bf16[1,16,128,128]{3,2,1,0:T(8,128)(2,1)S(1)}, bf16[1,16,128,128]{3,2,1,0:T(8,128)(2,1)S(1)}, u32[]{:S(2)}, u32[]{:S(2)}) collective-permute-start(bf16[1,16,128,128]{3,2,1,0:T(8,128)(2,1)S(1)} %maximum_bitcast_fusion.refs_4_), channel_id=1, source_target_pairs={{0,16},{16,0},{1,17},{17,1},{2,18},{18,2},{3,19},{19,3},{4,20},{20... | collective-permute-start | bytes 1572872 | tf_op jit(solution)/shard_map/ppermute | solution.py:28

commit v9 on v6

--- a/solution.py
+++ b/solution.py
@@ -18,6 +18,7 @@
 ROWS = HALF * BS
 EXTRA = 16
 EXP2 = math.log2(math.e) / math.sqrt(HD)
+UNIT = 2
 SHIFTS = (0, 1, 3, 2)
 AXES = ("x", "zh", "core", "y", "zl")
 VMEM = pl.BlockSpec(memory_space=pltpu.VMEM)
@@ -81,53 +82,54 @@
     outs = [view(out_refs, slot) for slot in out_slots]
     fetch.wait()
     blocks = [(h, b) for h in range(len(halves)) for b in range(HALF)]
-    n = len(blocks)
-    fetched, scores, weights, peaks, totals = {}, {}, {}, {}, {}
+    units = [blocks[i : i + UNIT] for i in range(0, len(blocks), UNIT)]
+    fetched, scores, weights, peaks, totals, products = {}, {}, {}, {}, {}, {}
     lses = [[] for _ in halves]
-    for t in range(n + 2):
-        ahead, here, last = t, t - 1, t - 2
-        if ahead < n:
-            h, b = blocks[ahead]
-            q = view(q_refs, halves[h])[b * BS : (b + 1) * BS, :]
+    for t in range(len(units) + 2):
+        ahead, here, last = (units[i] if 0 <= i < len(units) else [] for i in (t, t - 1, t - 2))
+        for h, b in ahead:
             keys, values = [], []
-            for g in range(GROUPS):
-                j = picks_ref[h * SEGB + b, columns[g]]
-                both = groups[g][pl.ds(2 * j, 2)]
+            for group, column in zip(groups, columns):
+                both = group[pl.ds(2 * picks_ref[h * SEGB + b, column], 2)]
                 keys.append(both[:, :TOK, :].reshape(BS, HD))
                 values.append(both[:, TOK:, :].reshape(BS, HD))
-            fetched[ahead], scores[ahead] = (q, keys, values), []
-        if 0 <= here < n:
-            weights[here], peaks[here], totals[here] = [], [], []
-        acc = None
+            fetched[h, b] = view(q_refs, halves[h])[b * BS : (b + 1) * BS, :], keys, values
+            scores[h, b] = []
+        for block in here:
+            weights[block], peaks[block], totals[block] = [], [], []
+        for block in last:
+            products[block] = []
         for step in range(4):
-            if ahead < n:
-                q, keys, _ = fetched[ahead]
-                pair = jnp.concatenate(keys[2 * step : 2 * step + 2], axis=0)
-                scores[ahead].append(
-                    lax.dot_general(q, pair, (((1,), (1,)), ((), ())), preferred_element_type=F32)
-                )
-            if 0 <= here < n:
-                rows = slice(step * BS // 4, (step + 1) * BS // 4)
-                part = [s[rows] for s in scores[here]]
-                peak = jnp.max(functools.reduce(jnp.maximum, part), axis=1, keepdims=True)
-                w = [jnp.exp2((s - peak) * EXP2) for s in part]
-                totals[here].append(jnp.sum(functools.reduce(jnp.add, w), axis=1, keepdims=True))
-                peaks[here].append(peak)
-                weights[here].append([p.astype(BF) for p in w])
-            if 0 <= last < n:
-                w = jnp.concatenate([p[step] for p in weights[last]], axis=0)
-                pair = jnp.concatenate(fetched[last][2][2 * step : 2 * step + 2], axis=0)
-                product = jnp.dot(w, pair, preferred_element_type=F32)
-                acc = product if acc is None else acc + product
-        if 0 <= last < n:
-            h, b = blocks[last]
-            peak, total = jnp.concatenate(peaks[last], axis=0), jnp.concatenate(totals[last], axis=0)
-            outs[h][b * BS : (b + 1) * BS, :] = (acc * (1.0 / total)).astype(BF)
+            pair = slice(2 * step, 2 * step + 2)
+            rows = slice(step * BS // 4, (step + 1) * BS // 4)
+            for i in range(UNIT):
+                if i < len(ahead):
+                    q, keys, _ = fetched[ahead[i]]
+                    both = jnp.concatenate(keys[pair], axis=0)
+                    scores[ahead[i]].append(
+                        lax.dot_general(q, both, (((1,), (1,)), ((), ())), preferred_element_type=F32)
+                    )
+                if i < len(here):
+                    part = [s[rows] for s in scores[here[i]]]
+                    peak = jnp.max(functools.reduce(jnp.maximum, part), axis=1, keepdims=True)
+                    w = [jnp.exp2((s - peak) * EXP2) for s in part]
+                    totals[here[i]].append(jnp.sum(functools.reduce(jnp.add, w), axis=1, keepdims=True))
+                    peaks[here[i]].append(peak)
+                    weights[here[i]].append([p.astype(BF) for p in w])
+                if i < len(last):
+                    w = jnp.concatenate([p[step] for p in weights[last[i]]], axis=0)
+                    both = jnp.concatenate(fetched[last[i]][2][pair], axis=0)
+                    products[last[i]].append(jnp.dot(w, both, preferred_element_type=F32))
+        for block in last:
+            h, b = block
+            peak, total = jnp.concatenate(peaks[block], axis=0), jnp.concatenate(totals[block], axis=0)
+            o = functools.reduce(jnp.add, products[block]) * (1.0 / total)
+            outs[h][b * BS : (b + 1) * BS, :] = o.astype(BF)
             lse = peak * EXP2 + jnp.log2(total)
             lses[h].append(jnp.transpose(jnp.broadcast_to(lse, (BS, HD)))[0:1, :])
             if b == HALF - 1:
                 outs[h][ROWS:, :] = split3(jnp.concatenate(lses[h], axis=0))
-            fetched[last] = scores[last] = weights[last] = None
+            fetched[block] = scores[block] = weights[block] = products[block] = None
 
 
 def merge_halves(ins, out_ref, first, keep):
@@ -208,21 +210,23 @@
 
     k1, k3, k2 = (shift(k0, "x", dx) for dx in SHIFTS[1:])
     q1, q3 = shift(q0, "zh", 1), shift(q0, "zh", -1)
-    q2a, q2b = shift(q1[0], "zh", 1), shift(q3[1], "zh", -1)
-    k1, k3, k2, q2a, q2b = lax.optimization_barrier((k1, k3, k2, q2a, q2b))
+    k1, k3, k2, q1, q3 = lax.optimization_barrier((k1, k3, k2, q1, q3))
     near = jnp.stack([k0, k1, k3, k2])
     far = shift(near, "core", 1)
+    q2a, q2b = shift(q1[0], "zh", 1), shift(q3[1], "zh", -1)
     kvs = [near, far]
     slots = tuple((ref, n) for n in range(NX) for ref in range(NC))
 
+    four = ((0, 0), (0, 1), (1, 0), (1, 1))
+    o1, o3 = attend([q1, q3], four, [chunk_shape()] * 2, four, kvs, slots)
+    q2a, q2b, o1, o3 = lax.optimization_barrier((q2a, q2b, o1, o3))
     o2a, o2b = attend([q2a, q2b], ((0, None), (1, None)), [half_shape()] * 2, ((0, None), (1, None)), kvs, slots)
     via_a, via_b = shift(o2a, "zh", 1), shift(o2b, "zh", -1)
-    four = ((0, 0), (0, 1), (1, 0), (1, 1))
-    o1, o3 = attend([q1, q3], four, [chunk_shape()] * 2, four, kvs, slots)
+    q0, o2a, o2b = lax.optimization_barrier((q0, o2a, o2b))
+    (o0,) = attend([q0], four[:2], [chunk_shape()], four[:2], kvs, slots)
+    via_a, via_b, o0 = lax.optimization_barrier((via_a, via_b, o0))
     m1, m3 = call(pass_kernel, [chunk_shape()] * 2, [VMEM] * 4, o1, o3, via_a, via_b)
-    m1, m3, q0 = lax.optimization_barrier((m1, m3, q0))
     back1, back3 = shift(m1, "zh", -1), shift(m3, "zh", 1)
-    (o0,) = attend([q0], four[:2], [chunk_shape()], four[:2], kvs, slots)
     whole = call(final_kernel, jax.ShapeDtypeStruct((NU * TOK, HD), BF), [VMEM] * 3, o0, back1, back3)
     home = lax.all_to_all(whole.reshape(NU, TOK, HD), ("y", "zl"), split_axis=0, concat_axis=0, tiled=True)
     return call(unpack_kernel, jax.ShapeDtypeStruct((TOK, HEADS * HD), BF), [VMEM], home)

time: 139 us -> 139 us (level); the launches traced: 136 us -> 139 us
  waiting for transfers between devices: 23.9 us -> 26 us
    ppermute x12, waiting for transfers between devices: 23.9 us -> 26 us  [shift(): return lax.ppermute(field, axis, [(i, (i + by) % n) for i in range(n)])]
  transfers between devices with their start and end apart: 12 -> 12, of which waited for: 8 -> 7; matrix products, arithmetic and copies ran while one was open for 0% -> 0% of each run, Pallas kernels for 5% -> 5%
where the time goes in v9:
time: 139 us
  blocking collectives  51.3 us (37%)
  starting transfers between devices  47.2 us (34%)
  waiting for transfers between devices  26 us (19%)
  Pallas kernels  13.4 us (10%)
    ppermute x12, starting transfers between devices, shift(): return lax.ppermute(field, axis, [(i, (i + by) % n) for i in range(n)])  47.2 us
    all_to_all x1, blocking collectives, shards(): lax.all_to_all(packed, ('y', 'zl'), split_axis=0, concat_axis=0, tiled=True)  32.4 us
    ppermute x12, waiting for transfers between devices, shift(): return lax.ppermute(field, axis, [(i, (i + by) % n) for i in range(n)])  26 us
    all_to_all x1, blocking collectives, shards(): lax.all_to_all(whole.reshape(NU, TOK, HD), ('y', 'zl'), split_axis=0, con...  18.9 us
    pallas_call x7, Pallas kernels, call(): pl.pallas_call(kernel, out_shape=outs, in_specs=specs, out_specs=jax.tree...  13.4 us
  transfers between devices with their start and end apart: 12, of which 7 were waited for; matrix products, arithmetic and copies ran while one was open for 0% of the time, Pallas kernels for 5%

profile of v9, /device:TPU:6, one launch (start us, length us, event | category | flops | bytes accessed | tf_op | source)
XLA Modules:
  0.0 138.6 jit_solution(8100262060006753602)
XLA Ops:
  0.0 2.1 %shard_map.46 = (bf16[16,192,128]{2,1,0:T(8,128)(2,1)}, bf16[2,16,128]{2,1,0:T(8,128)(2,1)}) custom-call(bf16[64,1536]{1,0:T(8,128)(2,1)} %q_hbm.1, bf16[64,1536]{1,0:T(8,128)(2,1)} %k_hbm.1, bf16[64,1536]{1,0:T(8,128)(2,1)} %v_hbm.1, s32[12,8,256]{2,1,0:T(8,128)} %mask_hbm.1), custom_call_target="tpu_custom_call" | custom-call | bytes 262144 | tf_op jit(solution)/shard_map/pallas_call | solution.py:169
  2.1 0.0 copy-start
  2.1 32.4 %all_to_all.10 = bf16[16,192,128]{2,1,0:T(8,128)(2,1)S(1)} all-to-all(bf16[16,192,128]{2,1,0:T(8,128)(2,1)} %get-tuple-element.26), channel_id=1, replica_groups=mesh['x'=4,'zh'=4,'core'=2,'y'=8,'zl'=2] {'y','zl'}, dimensions={0} | all-to-all | bytes 1572864 | tf_op jit(solution)/shard_map/all_to_all | solution.py:207
  34.5 0.2 slice_bitcast_fusion.2
  34.7 2.4 %collective-permute-start = (bf16[16,128,128]{2,1,0:T(8,128)(2,1)S(1)}, bf16[16,128,128]{2,1,0:T(8,128)(2,1)S(1)}, u32[]{:S(2)}, u32[]{:S(2)}) collective-permute-start(bf16[16,128,128]{2,1,0:T(8,128)(2,1)S(1)} %get-tuple-element.48), channel_id=1, source_target_pairs={{0,128},{128,256},{256,384},{384,0},{1,129},{129,257},{257,385},{3... | collective-permute-start | bytes 1572872 | tf_op jit(solution)/shard_map/ppermute | solution.py:30
  37.1 3.5 %collective-permute-start.1 = (bf16[16,128,128]{2,1,0:T(8,128)(2,1)S(1)}, bf16[16,128,128]{2,1,0:T(8,128)(2,1)S(1)}, u32[]{:S(2)}, u32[]{:S(2)}) collective-permute-start(bf16[16,128,128]{2,1,0:T(8,128)(2,1)S(1)} %get-tuple-element.48), channel_id=1, source_target_pairs={{0,384},{128,0},{256,128},{384,256},{1,385},{129,1},{257,129},{385... | collective-permute-start | bytes 1572872 | tf_op jit(solution)/shard_map/ppermute | solution.py:30
  40.6 3.3 %collective-permute-start.2 = (bf16[16,128,128]{2,1,0:T(8,128)(2,1)S(1)}, bf16[16,128,128]{2,1,0:T(8,128)(2,1)S(1)}, u32[]{:S(2)}, u32[]{:S(2)}) collective-permute-start(bf16[16,128,128]{2,1,0:T(8,128)(2,1)S(1)} %get-tuple-element.48), channel_id=1, source_target_pairs={{0,256},{128,384},{256,0},{384,128},{1,257},{129,385},{257,1},{385... | collective-permute-start | bytes 1572872 | tf_op jit(solution)/shard_map/ppermute | solution.py:30
  44.0 6.1 %collective-permute-start.3 = (bf16[2,528,128]{2,1,0:T(8,128)(2,1)S(1)}, bf16[2,528,128]{2,1,0:T(8,128)(2,1)S(1)}, u32[]{:S(2)}, u32[]{:S(2)}) collective-permute-start(bf16[2,528,128]{2,1,0:T(8,128)(2,1)S(1)} %pad_maximum_fusion.1.refs_0_), channel_id=1, source_target_pairs={{0,32},{32,64},{64,96},{96,0},{1,33},{33,65},{65,97},{97,1},{2,34}... | collective-permute-start | bytes 811016 | tf_op jit(solution)/shard_map/ppermute | solution.py:30
  50.1 5.9 %collective-permute-start.4 = (bf16[2,528,128]{2,1,0:T(8,128)(2,1)S(1)}, bf16[2,528,128]{2,1,0:T(8,128)(2,1)S(1)}, u32[]{:S(2)}, u32[]{:S(2)}) collective-permute-start(bf16[2,528,128]{2,1,0:T(8,128)(2,1)S(1)} %pad_maximum_fusion.1.refs_0_), channel_id=1, source_target_pairs={{0,96},{32,0},{64,32},{96,64},{1,97},{33,1},{65,33},{97,65},{2,98}... | collective-permute-start | bytes 811016 | tf_op jit(solution)/shard_map/ppermute | solution.py:30
  55.9 7.8 %collective-permute-done.3.refs_0_ = bf16[2,528,128]{2,1,0:T(8,128)(2,1)S(1)} collective-permute-done((bf16[2,528,128]{2,1,0:T(8,128)(2,1)S(1)}, bf16[2,528,128]{2,1,0:T(8,128)(2,1)S(1)}, u32[]{:S(2)}, u32[]{:S(2)}) %collective-permute-start.3) | collective-permute-done | bytes 270368 | tf_op jit(solution)/shard_map/ppermute | solution.py:30
  63.8 1.9 %collective-permute-done.4.refs_1_ = bf16[2,528,128]{2,1,0:T(8,128)(2,1)S(1)} collective-permute-done((bf16[2,528,128]{2,1,0:T(8,128)(2,1)S(1)}, bf16[2,528,128]{2,1,0:T(8,128)(2,1)S(1)}, u32[]{:S(2)}, u32[]{:S(2)}) %collective-permute-start.4) | collective-permute-done | bytes 270368 | tf_op jit(solution)/shard_map/ppermute | solution.py:30
  65.7 0.3 pad_maximum_fusion.refs_2_.refs_1_
  65.9 1.9 %collective-permute-start.7 = (bf16[4,16,128,128]{3,2,1,0:T(8,128)(2,1)S(1)}, bf16[4,16,128,128]{3,2,1,0:T(8,128)(2,1)S(1)}, u32[]{:S(2)}, u32[]{:S(2)}) collective-permute-start(bf16[4,16,128,128]{3,2,1,0:T(8,128)(2,1)S(1)} %pad_maximum_fusion.refs_2_.refs_1_), channel_id=1, source_target_pairs={{0,16},{16,0},{1,17},{17,1},{2,18},{18,2},{3,19},{19,3},{4,20},{20... | collective-permute-start | bytes 6291464 | tf_op jit(solution)/shard_map/ppermute | solution.py:30
  67.9 5.7 %collective-permute-start.5 = (bf16[528,128]{1,0:T(8,128)(2,1)S(1)}, bf16[528,128]{1,0:T(8,128)(2,1)S(1)}, u32[]{:S(2)}, u32[]{:S(2)}) collective-permute-start(bf16[528,128]{1,0:T(8,128)(2,1)S(1)} %slice_bitcast_fusion.1), channel_id=1, source_target_pairs={{0,32},{32,64},{64,96},{96,0},{1,33},{33,65},{65,97},{97,1},{2,34}... | collective-permute-start | bytes 405512 | tf_op jit(solution)/shard_map/ppermute | solution.py:30
  73.6 3.8 %collective-permute-start.6 = (bf16[528,128]{1,0:T(8,128)(2,1)S(1)}, bf16[528,128]{1,0:T(8,128)(2,1)S(1)}, u32[]{:S(2)}, u32[]{:S(2)}) collective-permute-start(bf16[528,128]{1,0:T(8,128)(2,1)S(1)} %slice_bitcast_fusion), channel_id=1, source_target_pairs={{0,96},{32,0},{64,32},{96,64},{1,97},{33,1},{65,33},{97,65},{2,98}... | collective-permute-start | bytes 405512 | tf_op jit(solution)/shard_map/ppermute | solution.py:30
  77.4 0.0 collective-permute-done.7.refs_3_.refs_2_
  77.4 4.5 %shard_map.47 = (bf16[2,528,128]{2,1,0:T(8,128)(2,1)S(1)}, bf16[2,528,128]{2,1,0:T(8,128)(2,1)S(1)}) custom-call(bf16[2,528,128]{2,1,0:T(8,128)(2,1)S(1)} %collective-permute-done.3.refs_0_, bf16[2,528,128]{2,1,0:T(8,128)(2,1)S(1)} %collective-permute-done.4.refs_1_, bf16[4,16,128,128]{3,2,1,0:T(8,128)(2,1)S(1)} %pad_maximum_fusion.refs_2_.refs_1_, ...), custom_call_target="tpu_custom_call" | custom-call | flops 1073741824 | bytes 4194304 | tf_op jit(solution)/shard_map/pallas_call | solution.py:169
  81.9 0.7 collective-permute-done.5.refs_0_
  82.6 2.4 %collective-permute-done.6.refs_1_ = bf16[528,128]{1,0:T(8,128)(2,1)S(1)} collective-permute-done((bf16[528,128]{1,0:T(8,128)(2,1)S(1)}, bf16[528,128]{1,0:T(8,128)(2,1)S(1)}, u32[]{:S(2)}, u32[]{:S(2)}) %collective-permute-start.6) | collective-permute-done | bytes 135200 | tf_op jit(solution)/shard_map/ppermute | solution.py:30
  85.0 2.6 %shard_map.48 = (bf16[528,128]{1,0:T(8,128)(2,1)S(1)}, bf16[528,128]{1,0:T(8,128)(2,1)S(1)}) custom-call(bf16[528,128]{1,0:T(8,128)(2,1)S(1)} %collective-permute-done.5.refs_0_, bf16[528,128]{1,0:T(8,128)(2,1)S(1)} %collective-permute-done.6.refs_1_, bf16[4,16,128,128]{3,2,1,0:T(8,128)(2,1)S(1)} %pad_maximum_fusion.refs_2_.refs_1_, ...), custom_call_target="tpu_custom_call" | custom-call | flops 536870912 | bytes 4194304 | tf_op jit(solution)/shard_map/pallas_call | solution.py:169
  87.6 5.3 %collective-permute-start.8 = (bf16[528,128]{1,0:T(8,128)(2,1)S(1)}, bf16[528,128]{1,0:T(8,128)(2,1)S(1)}, u32[]{:S(2)}, u32[]{:S(2)}) collective-permute-start(bf16[528,128]{1,0:T(8,128)(2,1)S(1)} %get-tuple-element.37), channel_id=1, source_target_pairs={{0,32},{32,64},{64,96},{96,0},{1,33},{33,65},{65,97},{97,1},{2,34}... | collective-permute-start | bytes 405512 | tf_op jit(solution)/shard_map/ppermute | solution.py:30
  92.9 2.6 %collective-permute-start.9 = (bf16[528,128]{1,0:T(8,128)(2,1)S(1)}, bf16[528,128]{1,0:T(8,128)(2,1)S(1)}, u32[]{:S(2)}, u32[]{:S(2)}) collective-permute-start(bf16[528,128]{1,0:T(8,128)(2,1)S(1)} %get-tuple-element.38), channel_id=1, source_target_pairs={{0,96},{32,0},{64,32},{96,64},{1,97},{33,1},{65,33},{97,65},{2,98}... | collective-permute-start | bytes 405512 | tf_op jit(solution)/shard_map/ppermute | solution.py:30
  95.6 2.6 %shard_map.49.a_ref = bf16[2,528,128]{2,1,0:T(8,128)(2,1)S(1)} custom-call(bf16[2,528,128]{2,1,0:T(8,128)(2,1)S(1)} %pad_maximum_fusion.1.refs_0_, bf16[4,16,128,128]{3,2,1,0:T(8,128)(2,1)S(1)} %pad_maximum_fusion.refs_2_.refs_1_, bf16[4,16,128,128]{3,2,1,0:T(8,128)(2,1)S(1)} %collective-permute-done.7.refs_3_.refs_2_), custom_call_target="tpu_custom_call" | custom-call | flops 536870912 | bytes 4194304 | tf_op jit(solution)/shard_map/pallas_call | solution.py:169
  98.2 3.4 %collective-permute-done.9.via_b_ref = bf16[528,128]{1,0:T(8,128)(2,1)S(1)} collective-permute-done((bf16[528,128]{1,0:T(8,128)(2,1)S(1)}, bf16[528,128]{1,0:T(8,128)(2,1)S(1)}, u32[]{:S(2)}, u32[]{:S(2)}) %collective-permute-start.9) | collective-permute-done | bytes 135200 | tf_op jit(solution)/shard_map/ppermute | solution.py:30
  101.6 0.4 shard_map.50
  102.0 3.8 %collective-permute-start.10 = (bf16[2,528,128]{2,1,0:T(8,128)(2,1)S(1)}, bf16[2,528,128]{2,1,0:T(8,128)(2,1)S(1)}, u32[]{:S(2)}, u32[]{:S(2)}) collective-permute-start(bf16[2,528,128]{2,1,0:T(8,128)(2,1)S(1)} %get-tuple-element.45), channel_id=1, source_target_pairs={{0,96},{32,0},{64,32},{96,64},{1,97},{33,1},{65,33},{97,65},{2,98}... | collective-permute-start | bytes 811016 | tf_op jit(solution)/shard_map/ppermute | solution.py:30
  105.8 2.9 %collective-permute-start.11 = (bf16[2,528,128]{2,1,0:T(8,128)(2,1)S(1)}, bf16[2,528,128]{2,1,0:T(8,128)(2,1)S(1)}, u32[]{:S(2)}, u32[]{:S(2)}) collective-permute-start(bf16[2,528,128]{2,1,0:T(8,128)(2,1)S(1)} %get-tuple-element.46), channel_id=1, source_target_pairs={{0,32},{32,64},{64,96},{96,0},{1,33},{33,65},{65,97},{97,1},{2,34}... | collective-permute-start | bytes 811016 | tf_op jit(solution)/shard_map/ppermute | solution.py:30
  108.8 6.3 %collective-permute-done.10.b_ref = bf16[2,528,128]{2,1,0:T(8,128)(2,1)S(1)} collective-permute-done((bf16[2,528,128]{2,1,0:T(8,128)(2,1)S(1)}, bf16[2,528,128]{2,1,0:T(8,128)(2,1)S(1)}, u32[]{:S(2)}, u32[]{:S(2)}) %collective-permute-start.10) | collective-permute-done | bytes 270368 | tf_op jit(solution)/shard_map/ppermute | solution.py:30
  115.1 3.4 %collective-permute-done.11.c_ref = bf16[2,528,128]{2,1,0:T(8,128)(2,1)S(1)} collective-permute-done((bf16[2,528,128]{2,1,0:T(8,128)(2,1)S(1)}, bf16[2,528,128]{2,1,0:T(8,128)(2,1)S(1)}, u32[]{:S(2)}, u32[]{:S(2)}) %collective-permute-start.11) | collective-permute-done | bytes 270368 | tf_op jit(solution)/shard_map/ppermute | solution.py:30
  118.5 0.5 shard_map.51
  119.0 18.9 %all_to_all.11.in_ref = bf16[16,64,128]{2,1,0:T(8,128)(2,1)S(1)} all-to-all(bf16[16,64,128]{2,1,0:T(8,128)(2,1)S(1)} %bitcast.11), channel_id=1, replica_groups=mesh['x'=4,'zh'=4,'core'=2,'y'=8,'zl'=2] {'y','zl'}, dimensions={0} | all-to-all | bytes 524288 | tf_op jit(solution)/shard_map/all_to_all | solution.py:231
  137.9 0.7 shard_map.52
  (9 shorter events, 0.1 us)
Async XLA Ops:
  2.1 41.8 %copy-start = (bf16[2,16,128]{2,1,0:T(8,128)(2,1)S(1)}, bf16[2,16,128]{2,1,0:T(8,128)(2,1)}, u32[]{:S(2)}) copy-start(bf16[2,16,128]{2,1,0:T(8,128)(2,1)} %get-tuple-element.27) | copy-start | bytes 24580
  34.7 30.9 %collective-permute-start = (bf16[16,128,128]{2,1,0:T(8,128)(2,1)S(1)}, bf16[16,128,128]{2,1,0:T(8,128)(2,1)S(1)}, u32[]{:S(2)}, u32[]{:S(2)}) collective-permute-start(bf16[16,128,128]{2,1,0:T(8,128)(2,1)S(1)} %get-tuple-element.48), channel_id=1, source_target_pairs={{0,128},{128,256},{256,384},{384,0},{1,129},{129,257},{257,385},{3... | collective-permute-start | bytes 1572872 | tf_op jit(solution)/shard_map/ppermute | solution.py:30
  37.1 28.5 %collective-permute-start.1 = (bf16[16,128,128]{2,1,0:T(8,128)(2,1)S(1)}, bf16[16,128,128]{2,1,0:T(8,128)(2,1)S(1)}, u32[]{:S(2)}, u32[]{:S(2)}) collective-permute-start(bf16[16,128,128]{2,1,0:T(8,128)(2,1)S(1)} %get-tuple-element.48), channel_id=1, source_target_pairs={{0,384},{128,0},{256,128},{384,256},{1,385},{129,1},{257,129},{385... | collective-permute-start | bytes 1572872 | tf_op jit(solution)/shard_map/ppermute | solution.py:30
  40.6 25.1 %collective-permute-start.2 = (bf16[16,128,128]{2,1,0:T(8,128)(2,1)S(1)}, bf16[16,128,128]{2,1,0:T(8,128)(2,1)S(1)}, u32[]{:S(2)}, u32[]{:S(2)}) collective-permute-start(bf16[16,128,128]{2,1,0:T(8,128)(2,1)S(1)} %get-tuple-element.48), channel_id=1, source_target_pairs={{0,256},{128,384},{256,0},{384,128},{1,257},{129,385},{257,1},{385... | collective-permute-start | bytes 1572872 | tf_op jit(solution)/shard_map/ppermute | solution.py:30
  44.0 19.8 %collective-permute-start.3 = (bf16[2,528,128]{2,1,0:T(8,128)(2,1)S(1)}, bf16[2,528,128]{2,1,0:T(8,128)(2,1)S(1)}, u32[]{:S(2)}, u32[]{:S(2)}) collective-permute-start(bf16[2,528,128]{2,1,0:T(8,128)(2,1)S(1)} %pad_maximum_fusion.1.refs_0_), channel_id=1, source_target_pairs={{0,32},{32,64},{64,96},{96,0},{1,33},{33,65},{65,97},{97,1},{2,34}... | collective-permute-start | bytes 811016 | tf_op jit(solution)/shard_map/ppermute | solution.py:30
  50.1 15.6 %collective-permute-start.4 = (bf16[2,528,128]{2,1,0:T(8,128)(2,1)S(1)}, bf16[2,528,128]{2,1,0:T(8,128)(2,1)S(1)}, u32[]{:S(2)}, u32[]{:S(2)}) collective-permute-start(bf16[2,528,128]{2,1,0:T(8,128)(2,1)S(1)} %pad_maximum_fusion.1.refs_0_), channel_id=1, source_target_pairs={{0,96},{32,0},{64,32},{96,64},{1,97},{33,1},{65,33},{97,65},{2,98}... | collective-permute-start | bytes 811016 | tf_op jit(solution)/shard_map/ppermute | solution.py:30
  65.9 11.4 %collective-permute-start.7 = (bf16[4,16,128,128]{3,2,1,0:T(8,128)(2,1)S(1)}, bf16[4,16,128,128]{3,2,1,0:T(8,128)(2,1)S(1)}, u32[]{:S(2)}, u32[]{:S(2)}) collective-permute-start(bf16[4,16,128,128]{3,2,1,0:T(8,128)(2,1)S(1)} %pad_maximum_fusion.refs_2_.refs_1_), channel_id=1, source_target_pairs={{0,16},{16,0},{1,17},{17,1},{2,18},{18,2},{3,19},{19,3},{4,20},{20... | collective-permute-start | bytes 6291464 | tf_op jit(solution)/shard_map/ppermute | solution.py:30
  67.9 14.7 %collective-permute-start.5 = (bf16[528,128]{1,0:T(8,128)(2,1)S(1)}, bf16[528,128]{1,0:T(8,128)(2,1)S(1)}, u32[]{:S(2)}, u32[]{:S(2)}) collective-permute-start(bf16[528,128]{1,0:T(8,128)(2,1)S(1)} %slice_bitcast_fusion.1), channel_id=1, source_target_pairs={{0,32},{32,64},{64,96},{96,0},{1,33},{33,65},{65,97},{97,1},{2,34}... | collective-permute-start | bytes 405512 | tf_op jit(solution)/shard_map/ppermute | solution.py:30
  73.6 11.4 %collective-permute-start.6 = (bf16[528,128]{1,0:T(8,128)(2,1)S(1)}, bf16[528,128]{1,0:T(8,128)(2,1)S(1)}, u32[]{:S(2)}, u32[]{:S(2)}) collective-permute-start(bf16[528,128]{1,0:T(8,128)(2,1)S(1)} %slice_bitcast_fusion), channel_id=1, source_target_pairs={{0,96},{32,0},{64,32},{96,64},{1,97},{33,1},{65,33},{97,65},{2,98}... | collective-permute-start | bytes 405512 | tf_op jit(solution)/shard_map/ppermute | solution.py:30
  87.6 10.6 %collective-permute-start.8 = (bf16[528,128]{1,0:T(8,128)(2,1)S(1)}, bf16[528,128]{1,0:T(8,128)(2,1)S(1)}, u32[]{:S(2)}, u32[]{:S(2)}) collective-permute-start(bf16[528,128]{1,0:T(8,128)(2,1)S(1)} %get-tuple-element.37), channel_id=1, source_target_pairs={{0,32},{32,64},{64,96},{96,0},{1,33},{33,65},{65,97},{97,1},{2,34}... | collective-permute-start | bytes 405512 | tf_op jit(solution)/shard_map/ppermute | solution.py:30
  92.9 8.7 %collective-permute-start.9 = (bf16[528,128]{1,0:T(8,128)(2,1)S(1)}, bf16[528,128]{1,0:T(8,128)(2,1)S(1)}, u32[]{:S(2)}, u32[]{:S(2)}) collective-permute-start(bf16[528,128]{1,0:T(8,128)(2,1)S(1)} %get-tuple-element.38), channel_id=1, source_target_pairs={{0,96},{32,0},{64,32},{96,64},{1,97},{33,1},{65,33},{97,65},{2,98}... | collective-permute-start | bytes 405512 | tf_op jit(solution)/shard_map/ppermute | solution.py:30
  102.0 13.1 %collective-permute-start.10 = (bf16[2,528,128]{2,1,0:T(8,128)(2,1)S(1)}, bf16[2,528,128]{2,1,0:T(8,128)(2,1)S(1)}, u32[]{:S(2)}, u32[]{:S(2)}) collective-permute-start(bf16[2,528,128]{2,1,0:T(8,128)(2,1)S(1)} %get-tuple-element.45), channel_id=1, source_target_pairs={{0,96},{32,0},{64,32},{96,64},{1,97},{33,1},{65,33},{97,65},{2,98}... | collective-permute-start | bytes 811016 | tf_op jit(solution)/shard_map/ppermute | solution.py:30
  105.8 12.7 %collective-permute-start.11 = (bf16[2,528,128]{2,1,0:T(8,128)(2,1)S(1)}, bf16[2,528,128]{2,1,0:T(8,128)(2,1)S(1)}, u32[]{:S(2)}, u32[]{:S(2)}) collective-permute-start(bf16[2,528,128]{2,1,0:T(8,128)(2,1)S(1)} %get-tuple-element.46), channel_id=1, source_target_pairs={{0,32},{32,64},{64,96},{96,0},{1,33},{33,65},{65,97},{97,1},{2,34}... | collective-permute-start | bytes 811016 | tf_op jit(solution)/shard_map/ppermute | solution.py:30

commit v10 on v8

--- a/solution.py
+++ b/solution.py
@@ -69,14 +69,12 @@
     q_refs, (near_ref, far_ref), rest = refs[:chunks], refs[chunks : chunks + 2], refs[chunks + 2 :]
     old_refs = () if opening else rest[:chunks]
     rest = rest[len(old_refs) :]
-    out_refs, (flat_ref, picks_ref, sem) = rest[:-3], rest[-3:]
+    out_refs, (flat_ref, picks_ref, sem) = rest[:chunks], rest[chunks:]
     for n, q_ref in enumerate(q_refs):
         flat_ref[n * SEGB : (n + 1) * SEGB, :] = q_ref[ROWS:, :].astype(F32)[:SEGB].astype(jnp.int32)
     fetch = pltpu.make_async_copy(flat_ref, picks_ref, sem)
     fetch.start()
     x, z, c = lax.axis_index("x"), lax.axis_index("zh"), lax.axis_index("core")
-    if not opening:
-        out_refs = [out_refs[0].at[(x + NX - n) % NX] for n in range(chunks)]
     columns = [(x * NZ + (z + NZ - dz) % NZ) * NC + cc for dz in shifts for cc in (c, 1 - c)]
     groups = [ref.at[n] for n in range(len(shifts)) for ref in (near_ref, far_ref)]
     fetch.wait()
@@ -140,8 +138,8 @@
             fetched[block] = scores[block] = weights[block] = products[block] = None
 
 
-def merge_kernel(in_ref, out_ref):
-    ins = [in_ref.at[n] for n in range(NX)]
+def merge_kernel(keep, *refs):
+    ins, out_ref = refs[:-1], refs[-1]
     lses = [join3(r[ROWS:, :]) for r in ins]
     top = functools.reduce(jnp.maximum, lses)
     parts = [jnp.exp2(s - top) for s in lses]
@@ -152,7 +150,9 @@
         acc = jnp.zeros((BS, HD), F32)
         for r, p in zip(ins, parts):
             acc = acc + jnp.transpose(jnp.broadcast_to(p[b : b + 1, :], (BS, HD))) * r[rows, :].astype(F32)
-        out_ref[rows, :] = acc.astype(BF)
+        out_ref[rows, :] = acc.astype(out_ref.dtype)
+    if keep:
+        out_ref[ROWS:, :] = split3(top + jnp.log2(total))
 
 
 def unpack_kernel(in_ref, out_ref):
@@ -178,7 +178,7 @@
         outs = [jax.ShapeDtypeStruct((2, ROWS, HD), F32)] * n
         unit = 4
     else:
-        outs = jax.ShapeDtypeStruct((n, ROWS + LSE, HD), BF)
+        outs = [jax.ShapeDtypeStruct((ROWS + LSE, HD), BF)] * n
         unit = 8
     ins = [*queries, near, far, *(old or [])]
     return call(
@@ -187,6 +187,11 @@
         scratch=[pltpu.VMEM((n * SEGB, HD), jnp.int32), pltpu.SMEM((n * SEGB, HD), jnp.int32), pltpu.SemaphoreType.DMA],
         flops=n * len(shifts) * (1 << 27), moved=2 << 20,
     )
+
+
+def merge(keep, flops, *ins):
+    out = jax.ShapeDtypeStruct((ROWS + LSE if keep else ROWS, HD), BF)
+    return call(functools.partial(merge_kernel, keep), out, [VMEM] * len(ins), *ins, flops=flops)
 
 
 def shards(queries, keys, values, block_mask):
@@ -213,9 +218,15 @@
     k2a, k2b, *old = lax.optimization_barrier((k2a, k2b, *old))
     near = jnp.concatenate([k2a, k2b], axis=0)[None]
     far = shift(near, "core", 1)
-    parts = attend([q0, q1, q2, q3], (2,), near, far, old)
-    parts = exchange(parts, "x")
-    whole = call(merge_kernel, jax.ShapeDtypeStruct((ROWS, HD), BF), [VMEM], parts)
+    (o2,) = attend([q2], (2,), near, far, [old[2]])
+    o2, far = lax.optimization_barrier((o2, far))
+    back2 = shift(o2, "x", -2)
+    o1, o3 = attend([q1, q3], (2,), near, far, [old[1], old[3]])
+    o1, o3, far = lax.optimization_barrier((o1, o3, far))
+    back1, back3 = shift(o1, "x", -1), shift(o3, "x", -3)
+    (o0,) = attend([q0], (2,), near, far, [old[0]])
+    first = merge(True, 1 << 33, o0, back2)
+    whole = merge(False, 0, first, back1, back3)
     home = exchange(whole.reshape(NU, TOK, HD), ("y", "zl"))
     return call(unpack_kernel, jax.ShapeDtypeStruct((TOK, HEADS * HD), BF), [VMEM], home)
 

time: 143 us -> 137 us (0.958)
  the two profiles are of different devices: /device:TPU:6 before, /device:TPU:8 now
where the time goes in v10:
time: 137 us
  blocking collectives  45.3 us (33%)
  starting transfers between devices  43.5 us (32%)
  waiting for transfers between devices  28.9 us (21%)
  Pallas kernels  18.3 us (13%)
    all_to_all x2, blocking collectives, exchange(): return lax.all_to_all(field, axes, split_axis=0, concat_axis=0, tiled=True)  45.3 us
    ppermute x12, starting transfers between devices, shift(): return lax.ppermute(field, axis, [(i, (i + by) % n) for i in range(n)])  43.5 us
    ppermute x12, waiting for transfers between devices, shift(): return lax.ppermute(field, axis, [(i, (i + by) % n) for i in range(n)])  28.9 us
    pallas_call x8, Pallas kernels, call(): pl.pallas_call(kernel, out_shape=outs, in_specs=specs, out_specs=jax.tree...  18.3 us
  transfers between devices with their start and end apart: 12, of which 9 were waited for; matrix products, arithmetic and copies ran while one was open for 0% of the time, Pallas kernels for 9%

profile of v10, /device:TPU:8, one launch (start us, length us, event | category | flops | bytes accessed | tf_op | source)
XLA Modules:
  0.0 136.7 jit_solution(3528495251545931621)
XLA Ops:
  0.0 2.1 %shard_map.46 = (bf16[16,192,128]{2,1,0:T(8,128)(2,1)}, bf16[16,128]{1,0:T(8,128)(2,1)}) custom-call(bf16[64,1536]{1,0:T(8,128)(2,1)} %q_hbm.1, bf16[64,1536]{1,0:T(8,128)(2,1)} %k_hbm.1, bf16[64,1536]{1,0:T(8,128)(2,1)} %v_hbm.1, s32[12,8,256]{2,1,0:T(8,128)} %mask_hbm.1), custom_call_target="tpu_custom_call" | custom-call | bytes 262144 | tf_op jit(solution)/shard_map/pallas_call | solution.py:164
  2.1 31.0 %all_to_all.10 = bf16[16,192,128]{2,1,0:T(8,128)(2,1)S(1)} all-to-all(bf16[16,192,128]{2,1,0:T(8,128)(2,1)} %get-tuple-element.29), channel_id=1, replica_groups=mesh['x'=4,'zh'=4,'core'=2,'y'=8,'zl'=2] {'y','zl'}, dimensions={0} | all-to-all | bytes 1572864 | tf_op jit(solution)/shard_map/all_to_all | solution.py:32
  33.3 10.0 %collective-permute-start.1 = (bf16[16,128,128]{2,1,0:T(8,128)(2,1)S(1)}, bf16[16,128,128]{2,1,0:T(8,128)(2,1)S(1)}, u32[]{:S(2)}, u32[]{:S(2)}) collective-permute-start(bf16[16,128,128]{2,1,0:T(8,128)(2,1)S(1)} %get-tuple-element.54), channel_id=1, source_target_pairs={{0,96},{32,0},{64,32},{96,64},{1,97},{33,1},{65,33},{97,65},{2,98}... | collective-permute-start | bytes 1572872 | tf_op jit(solution)/shard_map/ppermute | solution.py:28
  43.3 1.9 %collective-permute-start = (bf16[16,128,128]{2,1,0:T(8,128)(2,1)S(1)}, bf16[16,128,128]{2,1,0:T(8,128)(2,1)S(1)}, u32[]{:S(2)}, u32[]{:S(2)}) collective-permute-start(bf16[16,128,128]{2,1,0:T(8,128)(2,1)S(1)} %get-tuple-element.54), channel_id=1, source_target_pairs={{0,32},{32,64},{64,96},{96,0},{1,33},{33,65},{65,97},{97,1},{2,34}... | collective-permute-start | bytes 1572872 | tf_op jit(solution)/shard_map/ppermute | solution.py:28
  45.3 4.7 %collective-permute-start.4 = (bf16[1040,128]{1,0:T(8,128)(2,1)S(1)}, bf16[1040,128]{1,0:T(8,128)(2,1)S(1)}, u32[]{:S(2)}, u32[]{:S(2)}) collective-permute-start(bf16[1040,128]{1,0:T(8,128)(2,1)S(1)} %pad_maximum_fusion.1.refs_0_), channel_id=1, source_target_pairs={{0,384},{128,0},{256,128},{384,256},{1,385},{129,1},{257,129},{385... | collective-permute-start | bytes 798728 | tf_op jit(solution)/shard_map/ppermute | solution.py:28
  50.0 2.7 %collective-permute-start.3 = (bf16[1040,128]{1,0:T(8,128)(2,1)S(1)}, bf16[1040,128]{1,0:T(8,128)(2,1)S(1)}, u32[]{:S(2)}, u32[]{:S(2)}) collective-permute-start(bf16[1040,128]{1,0:T(8,128)(2,1)S(1)} %pad_maximum_fusion.1.refs_0_), channel_id=1, source_target_pairs={{0,256},{128,384},{256,0},{384,128},{1,257},{129,385},{257,1},{385... | collective-permute-start | bytes 798728 | tf_op jit(solution)/shard_map/ppermute | solution.py:28
  52.7 2.8 %collective-permute-start.2 = (bf16[1040,128]{1,0:T(8,128)(2,1)S(1)}, bf16[1040,128]{1,0:T(8,128)(2,1)S(1)}, u32[]{:S(2)}, u32[]{:S(2)}) collective-permute-start(bf16[1040,128]{1,0:T(8,128)(2,1)S(1)} %pad_maximum_fusion.1.refs_0_), channel_id=1, source_target_pairs={{0,128},{128,256},{256,384},{384,0},{1,129},{129,257},{257,385},{3... | collective-permute-start | bytes 798728 | tf_op jit(solution)/shard_map/ppermute | solution.py:28
  55.5 5.1 %collective-permute-done.4.refs_3_.refs_1_ = bf16[1040,128]{1,0:T(8,128)(2,1)S(1)} collective-permute-done((bf16[1040,128]{1,0:T(8,128)(2,1)S(1)}, bf16[1040,128]{1,0:T(8,128)(2,1)S(1)}, u32[]{:S(2)}, u32[]{:S(2)}) %collective-permute-start.4) | collective-permute-done | bytes 266272 | tf_op jit(solution)/shard_map/ppermute | solution.py:28
  60.6 2.1 %collective-permute-done.3.refs_2_.refs_0_ = bf16[1040,128]{1,0:T(8,128)(2,1)S(1)} collective-permute-done((bf16[1040,128]{1,0:T(8,128)(2,1)S(1)}, bf16[1040,128]{1,0:T(8,128)(2,1)S(1)}, u32[]{:S(2)}, u32[]{:S(2)}) %collective-permute-start.3) | collective-permute-done | bytes 266272 | tf_op jit(solution)/shard_map/ppermute | solution.py:28
  62.7 3.5 %collective-permute-done.2.refs_1_.refs_0_ = bf16[1040,128]{1,0:T(8,128)(2,1)S(1)} collective-permute-done((bf16[1040,128]{1,0:T(8,128)(2,1)S(1)}, bf16[1040,128]{1,0:T(8,128)(2,1)S(1)}, u32[]{:S(2)}, u32[]{:S(2)}) %collective-permute-start.2) | collective-permute-done | bytes 266272 | tf_op jit(solution)/shard_map/ppermute | solution.py:28
  66.2 3.5 %collective-permute-done = bf16[16,128,128]{2,1,0:T(8,128)(2,1)S(1)} collective-permute-done((bf16[16,128,128]{2,1,0:T(8,128)(2,1)S(1)}, bf16[16,128,128]{2,1,0:T(8,128)(2,1)S(1)}, u32[]{:S(2)}, u32[]{:S(2)}) %collective-permute-start) | collective-permute-done | bytes 524320 | tf_op jit(solution)/shard_map/ppermute | solution.py:28
  69.7 0.2 pad_maximum_fusion.refs_4_
  69.9 1.9 %collective-permute-start.7 = (bf16[3,16,128,128]{3,2,1,0:T(8,128)(2,1)S(1)}, bf16[3,16,128,128]{3,2,1,0:T(8,128)(2,1)S(1)}, u32[]{:S(2)}, u32[]{:S(2)}) collective-permute-start(bf16[3,16,128,128]{3,2,1,0:T(8,128)(2,1)S(1)} %pad_maximum_fusion.refs_4_), channel_id=1, source_target_pairs={{0,16},{16,0},{1,17},{17,1},{2,18},{18,2},{3,19},{19,3},{4,20},{20... | collective-permute-start | bytes 4718600 | tf_op jit(solution)/shard_map/ppermute | solution.py:28
  71.9 3.2 %collective-permute-start.6 = (bf16[8,128,128]{2,1,0:T(8,128)(2,1)S(1)}, bf16[8,128,128]{2,1,0:T(8,128)(2,1)S(1)}, u32[]{:S(2)}, u32[]{:S(2)}) collective-permute-start(bf16[8,128,128]{2,1,0:T(8,128)(2,1)S(1)} %slice.15), channel_id=1, source_target_pairs={{0,96},{32,0},{64,32},{96,64},{1,97},{33,1},{65,33},{97,65},{2,98}... | collective-permute-start | bytes 786440 | tf_op jit(solution)/shard_map/ppermute | solution.py:28
  75.1 3.6 %collective-permute-start.5 = (bf16[8,128,128]{2,1,0:T(8,128)(2,1)S(1)}, bf16[8,128,128]{2,1,0:T(8,128)(2,1)S(1)}, u32[]{:S(2)}, u32[]{:S(2)}) collective-permute-start(bf16[8,128,128]{2,1,0:T(8,128)(2,1)S(1)} %slice.14), channel_id=1, source_target_pairs={{0,32},{32,64},{64,96},{96,0},{1,33},{33,65},{65,97},{97,1},{2,34}... | collective-permute-start | bytes 786440 | tf_op jit(solution)/shard_map/ppermute | solution.py:28
  78.6 7.4 %shard_map.47 = (f32[2,1024,128]{2,1,0:T(8,128)S(1)}, f32[2,1024,128]{2,1,0:T(8,128)S(1)}, f32[2,1024,128]{2,1,0:T(8,128)S(1)}, f32[2,1024,128]{2,1,0:T(8,128)S(1)}) custom-call(bf16[1040,128]{1,0:T(8,128)(2,1)S(1)} %pad_maximum_fusion.1.refs_0_, bf16[1040,128]{1,0:T(8,128)(2,1)S(1)} %collective-permute-done.2.refs_1_.refs_0_, ...), custom_call_target="tpu_custom_call" | custom-call | flops 1610612736 | bytes 2097152 | tf_op jit(solution)/shard_map/pallas_call | solution.py:164
  86.1 3.0 %collective-permute-done.6 = bf16[8,128,128]{2,1,0:T(8,128)(2,1)S(1)} collective-permute-done((bf16[8,128,128]{2,1,0:T(8,128)(2,1)S(1)}, bf16[8,128,128]{2,1,0:T(8,128)(2,1)S(1)}, u32[]{:S(2)}, u32[]{:S(2)}) %collective-permute-start.6) | collective-permute-done | bytes 262176 | tf_op jit(solution)/shard_map/ppermute | solution.py:28
  89.0 4.0 %collective-permute-done.5 = bf16[8,128,128]{2,1,0:T(8,128)(2,1)S(1)} collective-permute-done((bf16[8,128,128]{2,1,0:T(8,128)(2,1)S(1)}, bf16[8,128,128]{2,1,0:T(8,128)(2,1)S(1)}, u32[]{:S(2)}, u32[]{:S(2)}) %collective-permute-start.5) | collective-permute-done | bytes 262176 | tf_op jit(solution)/shard_map/ppermute | solution.py:28
  93.1 1.9 %collective-permute-start.8 = (bf16[1,16,128,128]{3,2,1,0:T(8,128)(2,1)S(1)}, bf16[1,16,128,128]{3,2,1,0:T(8,128)(2,1)S(1)}, u32[]{:S(2)}, u32[]{:S(2)}) collective-permute-start(bf16[1,16,128,128]{3,2,1,0:T(8,128)(2,1)S(1)} %maximum_bitcast_fusion.refs_1_.refs_2_), channel_id=1, source_target_pairs={{0,16},{16,0},{1,17},{17,1},{2,18},{18,2},{3,19},{19,3},{4,20},{20... | collective-permute-start | bytes 1572872 | tf_op jit(solution)/shard_map/ppermute | solution.py:28
  95.0 1.9 %collective-permute-done.8.refs_2_.refs_3_ = bf16[1,16,128,128]{3,2,1,0:T(8,128)(2,1)S(1)} collective-permute-done((bf16[1,16,128,128]{3,2,1,0:T(8,128)(2,1)S(1)}, bf16[1,16,128,128]{3,2,1,0:T(8,128)(2,1)S(1)}, u32[]{:S(2)}, u32[]{:S(2)}) %collective-permute-start.8) | collective-permute-done | bytes 524320 | tf_op jit(solution)/shard_map/ppermute | solution.py:28
  96.9 2.0 %shard_map.48 = bf16[1056,128]{1,0:T(8,128)(2,1)S(1)} custom-call(bf16[1040,128]{1,0:T(8,128)(2,1)S(1)} %collective-permute-done.3.refs_2_.refs_0_, bf16[1,16,128,128]{3,2,1,0:T(8,128)(2,1)S(1)} %maximum_bitcast_fusion.refs_1_.refs_2_, bf16[1,16,128,128]{3,2,1,0:T(8,128)(2,1)S(1)} %collective-permute-done.8.refs_2_.refs_3_, ...), custom_call_target="tpu_custom_call" | custom-call | flops 134217728 | bytes 2097152 | tf_op jit(solution)/shard_map/pallas_call | solution.py:164
  99.0 4.9 %collective-permute-start.9 = (bf16[1056,128]{1,0:T(8,128)(2,1)S(1)}, bf16[1056,128]{1,0:T(8,128)(2,1)S(1)}, u32[]{:S(2)}, u32[]{:S(2)}) collective-permute-start(bf16[1056,128]{1,0:T(8,128)(2,1)S(1)} %shard_map.48), channel_id=1, source_target_pairs={{0,256},{128,384},{256,0},{384,128},{1,257},{129,385},{257,1},{385... | collective-permute-start | bytes 811016 | tf_op jit(solution)/shard_map/ppermute | solution.py:28
  103.9 3.1 %shard_map.49 = (bf16[1056,128]{1,0:T(8,128)(2,1)S(1)}, bf16[1056,128]{1,0:T(8,128)(2,1)S(1)}) custom-call(bf16[1040,128]{1,0:T(8,128)(2,1)S(1)} %collective-permute-done.2.refs_1_.refs_0_, bf16[1040,128]{1,0:T(8,128)(2,1)S(1)} %collective-permute-done.4.refs_3_.refs_1_, bf16[1,16,128,128]{3,2,1,0:T(8,128)(2,1)S(1)} %maximum_bitcast_fusion.refs_1_.refs_2_, ...), custom_call_target="tpu_custom_call" | custom-call | flops 268435456 | bytes 2097152 | tf_op jit(solution)/shard_map/pallas_call | solution.py:164
  107.0 3.0 %collective-permute-start.10 = (bf16[1056,128]{1,0:T(8,128)(2,1)S(1)}, bf16[1056,128]{1,0:T(8,128)(2,1)S(1)}, u32[]{:S(2)}, u32[]{:S(2)}) collective-permute-start(bf16[1056,128]{1,0:T(8,128)(2,1)S(1)} %get-tuple-element.51), channel_id=1, source_target_pairs={{0,384},{128,0},{256,128},{384,256},{1,385},{129,1},{257,129},{385... | collective-permute-start | bytes 811016 | tf_op jit(solution)/shard_map/ppermute | solution.py:28
  110.1 2.8 %collective-permute-start.11 = (bf16[1056,128]{1,0:T(8,128)(2,1)S(1)}, bf16[1056,128]{1,0:T(8,128)(2,1)S(1)}, u32[]{:S(2)}, u32[]{:S(2)}) collective-permute-start(bf16[1056,128]{1,0:T(8,128)(2,1)S(1)} %get-tuple-element.52), channel_id=1, source_target_pairs={{0,128},{128,256},{256,384},{384,0},{1,129},{129,257},{257,385},{3... | collective-permute-start | bytes 811016 | tf_op jit(solution)/shard_map/ppermute | solution.py:28
  112.9 2.0 %shard_map.50.refs_0_ = bf16[1056,128]{1,0:T(8,128)(2,1)S(1)} custom-call(bf16[1040,128]{1,0:T(8,128)(2,1)S(1)} %pad_maximum_fusion.1.refs_0_, bf16[1,16,128,128]{3,2,1,0:T(8,128)(2,1)S(1)} %maximum_bitcast_fusion.refs_1_.refs_2_, bf16[1,16,128,128]{3,2,1,0:T(8,128)(2,1)S(1)} %collective-permute-done.8.refs_2_.refs_3_, ...), custom_call_target="tpu_custom_call" | custom-call | flops 134217728 | bytes 2097152 | tf_op jit(solution)/shard_map/pallas_call | solution.py:164
  114.9 0.4 shard_map.51.refs_0_
  115.3 1.8 %collective-permute-done.10.refs_1_ = bf16[1056,128]{1,0:T(8,128)(2,1)S(1)} collective-permute-done((bf16[1056,128]{1,0:T(8,128)(2,1)S(1)}, bf16[1056,128]{1,0:T(8,128)(2,1)S(1)}, u32[]{:S(2)}, u32[]{:S(2)}) %collective-permute-start.10) | collective-permute-done | bytes 270368 | tf_op jit(solution)/shard_map/ppermute | solution.py:28
  117.1 4.0 %collective-permute-done.11.refs_2_ = bf16[1056,128]{1,0:T(8,128)(2,1)S(1)} collective-permute-done((bf16[1056,128]{1,0:T(8,128)(2,1)S(1)}, bf16[1056,128]{1,0:T(8,128)(2,1)S(1)}, u32[]{:S(2)}, u32[]{:S(2)}) %collective-permute-start.11) | collective-permute-done | bytes 270368 | tf_op jit(solution)/shard_map/ppermute | solution.py:28
  121.1 0.5 shard_map.52
  121.6 14.3 %all_to_all.11.in_ref = bf16[16,64,128]{2,1,0:T(8,128)(2,1)S(1)} all-to-all(bf16[16,64,128]{2,1,0:T(8,128)(2,1)S(1)} %bitcast.8), channel_id=1, replica_groups=mesh['x'=4,'zh'=4,'core'=2,'y'=8,'zl'=2] {'y','zl'}, dimensions={0} | all-to-all | bytes 524288 | tf_op jit(solution)/shard_map/all_to_all | solution.py:32
  135.9 0.7 shard_map.53
  (11 shorter events, 0.3 us)
Async XLA Ops:
  2.1 43.2 %copy-start = (bf16[16,128]{1,0:T(8,128)(2,1)S(1)}, bf16[16,128]{1,0:T(8,128)(2,1)}, u32[]{:S(2)}) copy-start(bf16[16,128]{1,0:T(8,128)(2,1)} %get-tuple-element.30) | copy-start | bytes 12292
  33.3 32.9 %collective-permute-start.1 = (bf16[16,128,128]{2,1,0:T(8,128)(2,1)S(1)}, bf16[16,128,128]{2,1,0:T(8,128)(2,1)S(1)}, u32[]{:S(2)}, u32[]{:S(2)}) collective-permute-start(bf16[16,128,128]{2,1,0:T(8,128)(2,1)S(1)} %get-tuple-element.54), channel_id=1, source_target_pairs={{0,96},{32,0},{64,32},{96,64},{1,97},{33,1},{65,33},{97,65},{2,98}... | collective-permute-start | bytes 1572872 | tf_op jit(solution)/shard_map/ppermute | solution.py:28
  43.3 26.4 %collective-permute-start = (bf16[16,128,128]{2,1,0:T(8,128)(2,1)S(1)}, bf16[16,128,128]{2,1,0:T(8,128)(2,1)S(1)}, u32[]{:S(2)}, u32[]{:S(2)}) collective-permute-start(bf16[16,128,128]{2,1,0:T(8,128)(2,1)S(1)} %get-tuple-element.54), channel_id=1, source_target_pairs={{0,32},{32,64},{64,96},{96,0},{1,33},{33,65},{65,97},{97,1},{2,34}... | collective-permute-start | bytes 1572872 | tf_op jit(solution)/shard_map/ppermute | solution.py:28
  45.3 15.3 %collective-permute-start.4 = (bf16[1040,128]{1,0:T(8,128)(2,1)S(1)}, bf16[1040,128]{1,0:T(8,128)(2,1)S(1)}, u32[]{:S(2)}, u32[]{:S(2)}) collective-permute-start(bf16[1040,128]{1,0:T(8,128)(2,1)S(1)} %pad_maximum_fusion.1.refs_0_), channel_id=1, source_target_pairs={{0,384},{128,0},{256,128},{384,256},{1,385},{129,1},{257,129},{385... | collective-permute-start | bytes 798728 | tf_op jit(solution)/shard_map/ppermute | solution.py:28
  50.0 12.7 %collective-permute-start.3 = (bf16[1040,128]{1,0:T(8,128)(2,1)S(1)}, bf16[1040,128]{1,0:T(8,128)(2,1)S(1)}, u32[]{:S(2)}, u32[]{:S(2)}) collective-permute-start(bf16[1040,128]{1,0:T(8,128)(2,1)S(1)} %pad_maximum_fusion.1.refs_0_), channel_id=1, source_target_pairs={{0,256},{128,384},{256,0},{384,128},{1,257},{129,385},{257,1},{385... | collective-permute-start | bytes 798728 | tf_op jit(solution)/shard_map/ppermute | solution.py:28
  52.7 13.5 %collective-permute-start.2 = (bf16[1040,128]{1,0:T(8,128)(2,1)S(1)}, bf16[1040,128]{1,0:T(8,128)(2,1)S(1)}, u32[]{:S(2)}, u32[]{:S(2)}) collective-permute-start(bf16[1040,128]{1,0:T(8,128)(2,1)S(1)} %pad_maximum_fusion.1.refs_0_), channel_id=1, source_target_pairs={{0,128},{128,256},{256,384},{384,0},{1,129},{129,257},{257,385},{3... | collective-permute-start | bytes 798728 | tf_op jit(solution)/shard_map/ppermute | solution.py:28
  69.9 8.7 %collective-permute-start.7 = (bf16[3,16,128,128]{3,2,1,0:T(8,128)(2,1)S(1)}, bf16[3,16,128,128]{3,2,1,0:T(8,128)(2,1)S(1)}, u32[]{:S(2)}, u32[]{:S(2)}) collective-permute-start(bf16[3,16,128,128]{3,2,1,0:T(8,128)(2,1)S(1)} %pad_maximum_fusion.refs_4_), channel_id=1, source_target_pairs={{0,16},{16,0},{1,17},{17,1},{2,18},{18,2},{3,19},{19,3},{4,20},{20... | collective-permute-start | bytes 4718600 | tf_op jit(solution)/shard_map/ppermute | solution.py:28
  71.9 17.2 %collective-permute-start.6 = (bf16[8,128,128]{2,1,0:T(8,128)(2,1)S(1)}, bf16[8,128,128]{2,1,0:T(8,128)(2,1)S(1)}, u32[]{:S(2)}, u32[]{:S(2)}) collective-permute-start(bf16[8,128,128]{2,1,0:T(8,128)(2,1)S(1)} %slice.15), channel_id=1, source_target_pairs={{0,96},{32,0},{64,32},{96,64},{1,97},{33,1},{65,33},{97,65},{2,98}... | collective-permute-start | bytes 786440 | tf_op jit(solution)/shard_map/ppermute | solution.py:28
  75.1 18.0 %collective-permute-start.5 = (bf16[8,128,128]{2,1,0:T(8,128)(2,1)S(1)}, bf16[8,128,128]{2,1,0:T(8,128)(2,1)S(1)}, u32[]{:S(2)}, u32[]{:S(2)}) collective-permute-start(bf16[8,128,128]{2,1,0:T(8,128)(2,1)S(1)} %slice.14), channel_id=1, source_target_pairs={{0,32},{32,64},{64,96},{96,0},{1,33},{33,65},{65,97},{97,1},{2,34}... | collective-permute-start | bytes 786440 | tf_op jit(solution)/shard_map/ppermute | solution.py:28
  93.1 3.8 %collective-permute-start.8 = (bf16[1,16,128,128]{3,2,1,0:T(8,128)(2,1)S(1)}, bf16[1,16,128,128]{3,2,1,0:T(8,128)(2,1)S(1)}, u32[]{:S(2)}, u32[]{:S(2)}) collective-permute-start(bf16[1,16,128,128]{3,2,1,0:T(8,128)(2,1)S(1)} %maximum_bitcast_fusion.refs_1_.refs_2_), channel_id=1, source_target_pairs={{0,16},{16,0},{1,17},{17,1},{2,18},{18,2},{3,19},{19,3},{4,20},{20... | collective-permute-start | bytes 1572872 | tf_op jit(solution)/shard_map/ppermute | solution.py:28
  99.0 16.0 %collective-permute-start.9 = (bf16[1056,128]{1,0:T(8,128)(2,1)S(1)}, bf16[1056,128]{1,0:T(8,128)(2,1)S(1)}, u32[]{:S(2)}, u32[]{:S(2)}) collective-permute-start(bf16[1056,128]{1,0:T(8,128)(2,1)S(1)} %shard_map.48), channel_id=1, source_target_pairs={{0,256},{128,384},{256,0},{384,128},{1,257},{129,385},{257,1},{385... | collective-permute-start | bytes 811016 | tf_op jit(solution)/shard_map/ppermute | solution.py:28
  107.0 10.1 %collective-permute-start.10 = (bf16[1056,128]{1,0:T(8,128)(2,1)S(1)}, bf16[1056,128]{1,0:T(8,128)(2,1)S(1)}, u32[]{:S(2)}, u32[]{:S(2)}) collective-permute-start(bf16[1056,128]{1,0:T(8,128)(2,1)S(1)} %get-tuple-element.51), channel_id=1, source_target_pairs={{0,384},{128,0},{256,128},{384,256},{1,385},{129,1},{257,129},{385... | collective-permute-start | bytes 811016 | tf_op jit(solution)/shard_map/ppermute | solution.py:28
  110.1 11.1 %collective-permute-start.11 = (bf16[1056,128]{1,0:T(8,128)(2,1)S(1)}, bf16[1056,128]{1,0:T(8,128)(2,1)S(1)}, u32[]{:S(2)}, u32[]{:S(2)}) collective-permute-start(bf16[1056,128]{1,0:T(8,128)(2,1)S(1)} %get-tuple-element.52), channel_id=1, source_target_pairs={{0,128},{128,256},{256,384},{384,0},{1,129},{129,257},{257,385},{3... | collective-permute-start | bytes 811016 | tf_op jit(solution)/shard_map/ppermute | solution.py:28

commit v11 on v10

--- a/solution.py
+++ b/solution.py
@@ -26,6 +26,11 @@
 def shift(field, axis, by):
     n = lax.axis_size(axis)
     return lax.ppermute(field, axis, [(i, (i + by) % n) for i in range(n)])
+
+
+def ring_step(field):
+    pairs = [(z * NC + c, (z + (1, -1)[c]) % NZ * NC + c) for z in range(NZ) for c in range(NC)]
+    return lax.ppermute(field, ("zh", "core"), pairs)
 
 
 def exchange(field, axes):
@@ -65,8 +70,9 @@
     return rows[0:SEGB] + rows[SEGB : 2 * SEGB] + rows[2 * SEGB : 3 * SEGB]
 
 
-def attend_kernel(chunks, shifts, unit, opening, *refs):
-    q_refs, (near_ref, far_ref), rest = refs[:chunks], refs[chunks : chunks + 2], refs[chunks + 2 :]
+def attend_kernel(chunks, unit, opening, *refs):
+    n_kv = 3 if opening else 1
+    q_refs, kv_refs, rest = refs[:chunks], refs[chunks : chunks + n_kv], refs[chunks + n_kv :]
     old_refs = () if opening else rest[:chunks]
     rest = rest[len(old_refs) :]
     out_refs, (flat_ref, picks_ref, sem) = rest[:chunks], rest[chunks:]
@@ -75,8 +81,22 @@
     fetch = pltpu.make_async_copy(flat_ref, picks_ref, sem)
     fetch.start()
     x, z, c = lax.axis_index("x"), lax.axis_index("zh"), lax.axis_index("core")
-    columns = [(x * NZ + (z + NZ - dz) % NZ) * NC + cc for dz in shifts for cc in (c, 1 - c)]
-    groups = [ref.at[n] for n in range(len(shifts)) for ref in (near_ref, far_ref)]
+    if opening:
+        own, near, far = kv_refs
+        before, after = z + NZ - 1 + 2 * c, z + NZ + 1 - 2 * c
+        groups = [(own, 0, z, c), (own, 1, z, 1 - c), (near, 0, before, c), (near, 1, before, 1 - c)]
+        groups += [(far, 0, after, 1 - c), (far, 1, after, c)]
+    else:
+        groups = [(kv_refs[0], 0, z + 2, c), (kv_refs[0], 1, z + 2, 1 - c)]
+    columns = [(x * NZ + lax.rem(zz, NZ)) * NC + cc for _, _, zz, cc in groups]
+    pairs = len(groups) // 2
+
+    def pick(group, j):
+        ref, n = group[:2]
+        if opening:
+            return ref[n, pl.ds(2 * j, 2)]
+        return ref[jnp.where(j // (SEGB // 2) == c, n, 3 - n), pl.ds(2 * lax.rem(j, SEGB // 2), 2)]
+
     fetch.wait()
     blocks = [(n, b) for n in range(chunks) for b in range(SEGB)]
     units = [blocks[i : i + unit] for i in range(0, len(blocks), unit)]
@@ -87,7 +107,7 @@
         for n, b in ahead:
             keys, values = [], []
             for group, column in zip(groups, columns):
-                both = group[pl.ds(2 * picks_ref[n * SEGB + b, column], 2)]
+                both = pick(group, picks_ref[n * SEGB + b, column])
                 keys.append(both[:, :TOK, :].reshape(BS, HD))
                 values.append(both[:, TOK:, :].reshape(BS, HD))
             fetched[n, b] = q_refs[n][b * BS : (b + 1) * BS, :], keys, values
@@ -100,7 +120,7 @@
             pair = slice(2 * step, 2 * step + 2)
             rows = slice(step * BS // STEPS, (step + 1) * BS // STEPS)
             for i in range(unit):
-                if i < len(ahead) and step < len(shifts):
+                if i < len(ahead) and step < pairs:
                     q, keys, _ = fetched[ahead[i]]
                     both = jnp.concatenate(keys[pair], axis=0)
                     scores[ahead[i]].append(
@@ -113,7 +133,7 @@
                     totals[here[i]].append(jnp.sum(functools.reduce(jnp.add, w), axis=1, keepdims=True))
                     peaks[here[i]].append(peak)
                     weights[here[i]].append([p.astype(BF) for p in w])
-                if i < len(last) and step < len(shifts):
+                if i < len(last) and step < pairs:
                     w = jnp.concatenate([p[step] for p in weights[last[i]]], axis=0)
                     both = jnp.concatenate(fetched[last[i]][2][pair], axis=0)
                     products[last[i]].append(jnp.dot(w, both, preferred_element_type=F32))
@@ -172,7 +192,7 @@
     )(*args)
 
 
-def attend(queries, shifts, near, far, old=None):
+def attend(queries, kvs, old=None):
     n = len(queries)
     if old is None:
         outs = [jax.ShapeDtypeStruct((2, ROWS, HD), F32)] * n
@@ -180,12 +200,12 @@
     else:
         outs = [jax.ShapeDtypeStruct((ROWS + LSE, HD), BF)] * n
         unit = 8
-    ins = [*queries, near, far, *(old or [])]
+    ins = [*queries, *kvs, *(old or [])]
     return call(
-        functools.partial(attend_kernel, n, shifts, unit, old is None),
+        functools.partial(attend_kernel, n, unit, old is None),
         outs, [VMEM] * len(ins), *ins,
         scratch=[pltpu.VMEM((n * SEGB, HD), jnp.int32), pltpu.SMEM((n * SEGB, HD), jnp.int32), pltpu.SemaphoreType.DMA],
-        flops=n * len(shifts) * (1 << 27), moved=2 << 20,
+        flops=n * (3 if old is None else 1) * (1 << 27), moved=2 << 20,
     )
 
 
@@ -207,24 +227,24 @@
     k0 = got[:, TOK:]
     q0 = jnp.concatenate([got[:, :TOK].reshape(ROWS, HD), picks], axis=0)
 
-    k1, k3 = shift(k0, "zh", 1), shift(k0, "zh", -1)
+    own = jnp.stack([k0, shift(k0, "core", 1)])
+    near = ring_step(own)
     q1, q2, q3 = (shift(q0, "x", dx) for dx in (1, 2, 3))
-    k1, k3, q1, q2, q3 = lax.optimization_barrier((k1, k3, q1, q2, q3))
-    k2a, k2b = shift(k1[: NU // 2], "zh", 1), shift(k3[NU // 2 :], "zh", -1)
-    near = jnp.stack([k0, k1, k3])
+    near, q1, q2, q3 = lax.optimization_barrier((near, q1, q2, q3))
+    half = lax.dynamic_slice_in_dim(near, lax.axis_index("core") * (NU // 2), NU // 2, axis=1)
+    last = ring_step(half)
     far = shift(near, "core", 1)
-    old = attend([q0, q1, q2, q3], (0, 1, 3), near, far)
-
-    k2a, k2b, *old = lax.optimization_barrier((k2a, k2b, *old))
-    near = jnp.concatenate([k2a, k2b], axis=0)[None]
-    far = shift(near, "core", 1)
-    (o2,) = attend([q2], (2,), near, far, [old[2]])
-    o2, far = lax.optimization_barrier((o2, far))
+    old = attend([q0, q1, q2, q3], [own, near, far])
+
+    last, *old = lax.optimization_barrier((last, *old))
+    kvs = [jnp.concatenate([last, shift(last, "core", 1)], axis=0)]
+    (o2,) = attend([q2], kvs, [old[2]])
+    o2, *kvs = lax.optimization_barrier((o2, *kvs))
     back2 = shift(o2, "x", -2)
-    o1, o3 = attend([q1, q3], (2,), near, far, [old[1], old[3]])
-    o1, o3, far = lax.optimization_barrier((o1, o3, far))
+    o1, o3 = attend([q1, q3], kvs, [old[1], old[3]])
+    o1, o3, *kvs = lax.optimization_barrier((o1, o3, *kvs))
     back1, back3 = shift(o1, "x", -1), shift(o3, "x", -3)
-    (o0,) = attend([q0], (2,), near, far, [old[0]])
+    (o0,) = attend([q0], kvs, [old[0]])
     first = merge(True, 1 << 33, o0, back2)
     whole = merge(False, 0, first, back1, back3)
     home = exchange(whole.reshape(NU, TOK, HD), ("y", "zl"))

time: 137 us -> 135 us (0.985)
  the two profiles are of different devices: /device:TPU:8 before, /device:TPU:6 now
where the time goes in v11:
time: 135 us
  blocking collectives  46.9 us (35%)
  waiting for transfers between devices  35.7 us (26%)
  starting transfers between devices  31.6 us (23%)
  Pallas kernels  19.3 us (14%)
    all_to_all x2, blocking collectives, exchange(): return lax.all_to_all(field, axes, split_axis=0, concat_axis=0, tiled=True)  46.9 us
    ppermute x9, starting transfers between devices, shift(): return lax.ppermute(field, axis, [(i, (i + by) % n) for i in range(n)])  23.6 us
    ppermute x9, waiting for transfers between devices, shift(): return lax.ppermute(field, axis, [(i, (i + by) % n) for i in range(n)])  22.2 us
    pallas_call x8, Pallas kernels, call(): pl.pallas_call(kernel, out_shape=outs, in_specs=specs, out_specs=jax.tree...  19.3 us
    ppermute x2, waiting for transfers between devices, ring_step(): return lax.ppermute(field, ('zh', 'core'), pairs)  13.5 us
    ppermute x2, starting transfers between devices, ring_step(): return lax.ppermute(field, ('zh', 'core'), pairs)  8.01 us
  transfers between devices with their start and end apart: 11, of which 9 were waited for; matrix products, arithmetic and copies ran while one was open for 0% of the time, Pallas kernels for 10%

profile of v11, /device:TPU:6, one launch (start us, length us, event | category | flops | bytes accessed | tf_op | source)
XLA Modules:
  0.0 134.8 jit_solution(3621102388149350930)
XLA Ops:
  0.0 2.1 %shard_map.46 = (bf16[16,192,128]{2,1,0:T(8,128)(2,1)}, bf16[16,128]{1,0:T(8,128)(2,1)}) custom-call(bf16[64,1536]{1,0:T(8,128)(2,1)} %q_hbm.1, bf16[64,1536]{1,0:T(8,128)(2,1)} %k_hbm.1, bf16[64,1536]{1,0:T(8,128)(2,1)} %v_hbm.1, s32[12,8,256]{2,1,0:T(8,128)} %mask_hbm.1), custom_call_target="tpu_custom_call" | custom-call | bytes 262144 | tf_op jit(solution)/shard_map/pallas_call | solution.py:184
  2.1 32.4 %all_to_all.10 = bf16[16,192,128]{2,1,0:T(8,128)(2,1)S(1)} all-to-all(bf16[16,192,128]{2,1,0:T(8,128)(2,1)} %get-tuple-element.27), channel_id=1, replica_groups=mesh['x'=4,'zh'=4,'core'=2,'y'=8,'zl'=2] {'y','zl'}, dimensions={0} | all-to-all | bytes 1572864 | tf_op jit(solution)/shard_map/all_to_all | solution.py:37
  34.5 0.2 slice_bitcast_fusion
  34.7 1.9 %collective-permute-start = (bf16[16,128,128]{2,1,0:T(8,128)(2,1)S(1)}, bf16[16,128,128]{2,1,0:T(8,128)(2,1)S(1)}, u32[]{:S(2)}, u32[]{:S(2)}) collective-permute-start(bf16[16,128,128]{2,1,0:T(8,128)(2,1)S(1)} %get-tuple-element.50), channel_id=1, source_target_pairs={{0,16},{16,0},{1,17},{17,1},{2,18},{18,2},{3,19},{19,3},{4,20},{20... | collective-permute-start | bytes 1572872 | tf_op jit(solution)/shard_map/ppermute | solution.py:28
  36.7 1.9 %collective-permute-done = bf16[16,128,128]{2,1,0:T(8,128)(2,1)S(1)} collective-permute-done((bf16[16,128,128]{2,1,0:T(8,128)(2,1)S(1)}, bf16[16,128,128]{2,1,0:T(8,128)(2,1)S(1)}, u32[]{:S(2)}, u32[]{:S(2)}) %collective-permute-start) | collective-permute-done | bytes 524320 | tf_op jit(solution)/shard_map/ppermute | solution.py:28
  38.6 6.1 %collective-permute-start.1 = (bf16[2,16,128,128]{3,2,1,0:T(8,128)(2,1)S(1)}, bf16[2,16,128,128]{3,2,1,0:T(8,128)(2,1)S(1)}, u32[]{:S(2)}, u32[]{:S(2)}) collective-permute-start(bf16[2,16,128,128]{3,2,1,0:T(8,128)(2,1)S(1)} %pad_maximum_fusion.refs_4_), channel_id=1, source_target_pairs={{0,32},{16,112},{32,64},{48,16},{64,96},{80,48},{96,0},{112,80},{1... | collective-permute-start | bytes 3145736 | tf_op jit(solution)/shard_map/ppermute | solution.py:33
  44.8 0.7 copy-done
  45.4 2.4 %collective-permute-start.2 = (bf16[1040,128]{1,0:T(8,128)(2,1)S(1)}, bf16[1040,128]{1,0:T(8,128)(2,1)S(1)}, u32[]{:S(2)}, u32[]{:S(2)}) collective-permute-start(bf16[1040,128]{1,0:T(8,128)(2,1)S(1)} %pad_maximum_fusion.1.refs_0_), channel_id=1, source_target_pairs={{0,128},{128,256},{256,384},{384,0},{1,129},{129,257},{257,385},{3... | collective-permute-start | bytes 798728 | tf_op jit(solution)/shard_map/ppermute | solution.py:28
  47.8 4.3 %collective-permute-start.3 = (bf16[1040,128]{1,0:T(8,128)(2,1)S(1)}, bf16[1040,128]{1,0:T(8,128)(2,1)S(1)}, u32[]{:S(2)}, u32[]{:S(2)}) collective-permute-start(bf16[1040,128]{1,0:T(8,128)(2,1)S(1)} %pad_maximum_fusion.1.refs_0_), channel_id=1, source_target_pairs={{0,256},{128,384},{256,0},{384,128},{1,257},{129,385},{257,1},{385... | collective-permute-start | bytes 798728 | tf_op jit(solution)/shard_map/ppermute | solution.py:28
  52.2 1.9 %collective-permute-start.4 = (bf16[1040,128]{1,0:T(8,128)(2,1)S(1)}, bf16[1040,128]{1,0:T(8,128)(2,1)S(1)}, u32[]{:S(2)}, u32[]{:S(2)}) collective-permute-start(bf16[1040,128]{1,0:T(8,128)(2,1)S(1)} %pad_maximum_fusion.1.refs_0_), channel_id=1, source_target_pairs={{0,384},{128,0},{256,128},{384,256},{1,385},{129,1},{257,129},{385... | collective-permute-start | bytes 798728 | tf_op jit(solution)/shard_map/ppermute | solution.py:28
  54.1 3.8 %collective-permute-done.3.refs_2_.refs_0_ = bf16[1040,128]{1,0:T(8,128)(2,1)S(1)} collective-permute-done((bf16[1040,128]{1,0:T(8,128)(2,1)S(1)}, bf16[1040,128]{1,0:T(8,128)(2,1)S(1)}, u32[]{:S(2)}, u32[]{:S(2)}) %collective-permute-start.3) | collective-permute-done | bytes 266272 | tf_op jit(solution)/shard_map/ppermute | solution.py:28
  57.9 7.2 %collective-permute-done.4.refs_3_.refs_1_ = bf16[1040,128]{1,0:T(8,128)(2,1)S(1)} collective-permute-done((bf16[1040,128]{1,0:T(8,128)(2,1)S(1)}, bf16[1040,128]{1,0:T(8,128)(2,1)S(1)}, u32[]{:S(2)}, u32[]{:S(2)}) %collective-permute-start.4) | collective-permute-done | bytes 266272 | tf_op jit(solution)/shard_map/ppermute | solution.py:28
  65.0 7.7 %collective-permute-done.1.refs_5_ = bf16[2,16,128,128]{3,2,1,0:T(8,128)(2,1)S(1)} collective-permute-done((bf16[2,16,128,128]{3,2,1,0:T(8,128)(2,1)S(1)}, bf16[2,16,128,128]{3,2,1,0:T(8,128)(2,1)S(1)}, u32[]{:S(2)}, u32[]{:S(2)}) %collective-permute-start.1) | collective-permute-done | bytes 1048608 | tf_op jit(solution)/shard_map/ppermute | solution.py:33
  72.7 1.9 %collective-permute-start.6 = (bf16[2,16,128,128]{3,2,1,0:T(8,128)(2,1)S(1)}, bf16[2,16,128,128]{3,2,1,0:T(8,128)(2,1)}, u32[]{:S(2)}, u32[]{:S(2)}) collective-permute-start(bf16[2,16,128,128]{3,2,1,0:T(8,128)(2,1)S(1)} %collective-permute-done.1.refs_5_), channel_id=1, source_target_pairs={{0,16},{16,0},{1,17},{17,1},{2,18},{18,2},{3,19},{19,3},{4,20},{20... | collective-permute-start | bytes 3145736 | tf_op jit(solution)/shard_map/ppermute | solution.py:28
  74.7 1.9 %collective-permute-start.5 = (bf16[2,8,128,128]{3,2,1,0:T(8,128)(2,1)S(1)}, bf16[2,8,128,128]{3,2,1,0:T(8,128)(2,1)S(1)}, u32[]{:S(2)}, u32[]{:S(2)}) collective-permute-start(bf16[2,8,128,128]{3,2,1,0:T(8,128)(2,1)S(1)} %constant_dynamic-slice_fusion), channel_id=1, source_target_pairs={{0,32},{16,112},{32,64},{48,16},{64,96},{80,48},{96,0},{112,80},{1... | collective-permute-start | bytes 1572872 | tf_op jit(solution)/shard_map/ppermute | solution.py:33
  76.6 0.8 collective-permute-done.6.refs_6_
  77.4 8.6 %shard_map.47 = (f32[2,1024,128]{2,1,0:T(8,128)S(1)}, f32[2,1024,128]{2,1,0:T(8,128)S(1)}, f32[2,1024,128]{2,1,0:T(8,128)S(1)}, f32[2,1024,128]{2,1,0:T(8,128)S(1)}) custom-call(bf16[1040,128]{1,0:T(8,128)(2,1)S(1)} %pad_maximum_fusion.1.refs_0_, bf16[1040,128]{1,0:T(8,128)(2,1)S(1)} %collective-permute-done.2.refs_1_.refs_0_, ...), custom_call_target="tpu_custom_call" | custom-call | flops 1610612736 | bytes 2097152 | tf_op jit(solution)/shard_map/pallas_call | solution.py:184
  86.0 5.8 %collective-permute-done.5 = bf16[2,8,128,128]{3,2,1,0:T(8,128)(2,1)S(1)} collective-permute-done((bf16[2,8,128,128]{3,2,1,0:T(8,128)(2,1)S(1)}, bf16[2,8,128,128]{3,2,1,0:T(8,128)(2,1)S(1)}, u32[]{:S(2)}, u32[]{:S(2)}) %collective-permute-start.5) | collective-permute-done | bytes 524320 | tf_op jit(solution)/shard_map/ppermute | solution.py:33
  91.9 1.9 %collective-permute-start.7 = (bf16[2,8,128,128]{3,2,1,0:T(8,128)(2,1)S(1)}, bf16[2,8,128,128]{3,2,1,0:T(8,128)(2,1)S(1)}, u32[]{:S(2)}, u32[]{:S(2)}) collective-permute-start(bf16[2,8,128,128]{3,2,1,0:T(8,128)(2,1)S(1)} %collective-permute-done.5), channel_id=1, source_target_pairs={{0,16},{16,0},{1,17},{17,1},{2,18},{18,2},{3,19},{19,3},{4,20},{20... | collective-permute-start | bytes 1572872 | tf_op jit(solution)/shard_map/ppermute | solution.py:28
  93.8 1.8 %collective-permute-done.7 = bf16[2,8,128,128]{3,2,1,0:T(8,128)(2,1)S(1)} collective-permute-done((bf16[2,8,128,128]{3,2,1,0:T(8,128)(2,1)S(1)}, bf16[2,8,128,128]{3,2,1,0:T(8,128)(2,1)S(1)}, u32[]{:S(2)}, u32[]{:S(2)}) %collective-permute-start.7) | collective-permute-done | bytes 524320 | tf_op jit(solution)/shard_map/ppermute | solution.py:28
  95.7 2.0 %shard_map.48 = bf16[1056,128]{1,0:T(8,128)(2,1)S(1)} custom-call(bf16[1040,128]{1,0:T(8,128)(2,1)S(1)} %collective-permute-done.3.refs_2_.refs_0_, bf16[4,8,128,128]{3,2,1,0:T(8,128)(2,1)S(1)} %constant_dynamic-update-slice_fusion.refs_1_.refs_2_, f32[2,1024,128]{2,1,0:T(8,128)S(1)} %get-tuple-element.38.refs_2_), custom_call_target="tpu_custom_call" | custom-call | flops 134217728 | bytes 2097152 | tf_op jit(solution)/shard_map/pallas_call | solution.py:184
  97.8 3.3 %collective-permute-start.8 = (bf16[1056,128]{1,0:T(8,128)(2,1)S(1)}, bf16[1056,128]{1,0:T(8,128)(2,1)S(1)}, u32[]{:S(2)}, u32[]{:S(2)}) collective-permute-start(bf16[1056,128]{1,0:T(8,128)(2,1)S(1)} %shard_map.48), channel_id=1, source_target_pairs={{0,256},{128,384},{256,0},{384,128},{1,257},{129,385},{257,1},{385... | collective-permute-start | bytes 811016 | tf_op jit(solution)/shard_map/ppermute | solution.py:28
  101.1 3.0 %shard_map.49 = (bf16[1056,128]{1,0:T(8,128)(2,1)S(1)}, bf16[1056,128]{1,0:T(8,128)(2,1)S(1)}) custom-call(bf16[1040,128]{1,0:T(8,128)(2,1)S(1)} %collective-permute-done.2.refs_1_.refs_0_, bf16[1040,128]{1,0:T(8,128)(2,1)S(1)} %collective-permute-done.4.refs_3_.refs_1_, bf16[4,8,128,128]{3,2,1,0:T(8,128)(2,1)S(1)} %constant_dynamic-update-slice_fusion.refs_1_.refs_2_, ...), custom_call_target="tpu_custom_call" | custom-call | flops 268435456 | bytes 2097152 | tf_op jit(solution)/shard_map/pallas_call | solution.py:184
  104.1 4.0 %collective-permute-start.10 = (bf16[1056,128]{1,0:T(8,128)(2,1)S(1)}, bf16[1056,128]{1,0:T(8,128)(2,1)S(1)}, u32[]{:S(2)}, u32[]{:S(2)}) collective-permute-start(bf16[1056,128]{1,0:T(8,128)(2,1)S(1)} %get-tuple-element.48), channel_id=1, source_target_pairs={{0,128},{128,256},{256,384},{384,0},{1,129},{129,257},{257,385},{3... | collective-permute-start | bytes 811016 | tf_op jit(solution)/shard_map/ppermute | solution.py:28
  108.1 1.9 %collective-permute-start.9 = (bf16[1056,128]{1,0:T(8,128)(2,1)S(1)}, bf16[1056,128]{1,0:T(8,128)(2,1)S(1)}, u32[]{:S(2)}, u32[]{:S(2)}) collective-permute-start(bf16[1056,128]{1,0:T(8,128)(2,1)S(1)} %get-tuple-element.47), channel_id=1, source_target_pairs={{0,384},{128,0},{256,128},{384,256},{1,385},{129,1},{257,129},{385... | collective-permute-start | bytes 811016 | tf_op jit(solution)/shard_map/ppermute | solution.py:28
  110.0 2.0 %shard_map.50.refs_0_ = bf16[1056,128]{1,0:T(8,128)(2,1)S(1)} custom-call(bf16[1040,128]{1,0:T(8,128)(2,1)S(1)} %pad_maximum_fusion.1.refs_0_, bf16[4,8,128,128]{3,2,1,0:T(8,128)(2,1)S(1)} %constant_dynamic-update-slice_fusion.refs_1_.refs_2_, f32[2,1024,128]{2,1,0:T(8,128)S(1)} %get-tuple-element.45.refs_2_), custom_call_target="tpu_custom_call" | custom-call | flops 134217728 | bytes 2097152 | tf_op jit(solution)/shard_map/pallas_call | solution.py:184
  112.0 0.4 shard_map.51.refs_0_
  112.4 1.8 %collective-permute-done.10.refs_2_ = bf16[1056,128]{1,0:T(8,128)(2,1)S(1)} collective-permute-done((bf16[1056,128]{1,0:T(8,128)(2,1)S(1)}, bf16[1056,128]{1,0:T(8,128)(2,1)S(1)}, u32[]{:S(2)}, u32[]{:S(2)}) %collective-permute-start.10) | collective-permute-done | bytes 270368 | tf_op jit(solution)/shard_map/ppermute | solution.py:28
  114.2 4.9 %collective-permute-done.9.refs_1_ = bf16[1056,128]{1,0:T(8,128)(2,1)S(1)} collective-permute-done((bf16[1056,128]{1,0:T(8,128)(2,1)S(1)}, bf16[1056,128]{1,0:T(8,128)(2,1)S(1)}, u32[]{:S(2)}, u32[]{:S(2)}) %collective-permute-start.9) | collective-permute-done | bytes 270368 | tf_op jit(solution)/shard_map/ppermute | solution.py:28
  119.1 0.5 shard_map.52
  119.6 14.5 %all_to_all.11.in_ref = bf16[16,64,128]{2,1,0:T(8,128)(2,1)S(1)} all-to-all(bf16[16,64,128]{2,1,0:T(8,128)(2,1)S(1)} %bitcast.5), channel_id=1, replica_groups=mesh['x'=4,'zh'=4,'core'=2,'y'=8,'zl'=2] {'y','zl'}, dimensions={0} | all-to-all | bytes 524288 | tf_op jit(solution)/shard_map/all_to_all | solution.py:37
  134.1 0.7 shard_map.53
  (9 shorter events, 0.3 us)
Async XLA Ops:
  34.7 3.8 %collective-permute-start = (bf16[16,128,128]{2,1,0:T(8,128)(2,1)S(1)}, bf16[16,128,128]{2,1,0:T(8,128)(2,1)S(1)}, u32[]{:S(2)}, u32[]{:S(2)}) collective-permute-start(bf16[16,128,128]{2,1,0:T(8,128)(2,1)S(1)} %get-tuple-element.50), channel_id=1, source_target_pairs={{0,16},{16,0},{1,17},{17,1},{2,18},{18,2},{3,19},{19,3},{4,20},{20... | collective-permute-start | bytes 1572872 | tf_op jit(solution)/shard_map/ppermute | solution.py:28
  38.6 34.1 %collective-permute-start.1 = (bf16[2,16,128,128]{3,2,1,0:T(8,128)(2,1)S(1)}, bf16[2,16,128,128]{3,2,1,0:T(8,128)(2,1)S(1)}, u32[]{:S(2)}, u32[]{:S(2)}) collective-permute-start(bf16[2,16,128,128]{3,2,1,0:T(8,128)(2,1)S(1)} %pad_maximum_fusion.refs_4_), channel_id=1, source_target_pairs={{0,32},{16,112},{32,64},{48,16},{64,96},{80,48},{96,0},{112,80},{1... | collective-permute-start | bytes 3145736 | tf_op jit(solution)/shard_map/ppermute | solution.py:33
  44.7 0.7 copy-start
  45.4 8.7 %collective-permute-start.2 = (bf16[1040,128]{1,0:T(8,128)(2,1)S(1)}, bf16[1040,128]{1,0:T(8,128)(2,1)S(1)}, u32[]{:S(2)}, u32[]{:S(2)}) collective-permute-start(bf16[1040,128]{1,0:T(8,128)(2,1)S(1)} %pad_maximum_fusion.1.refs_0_), channel_id=1, source_target_pairs={{0,128},{128,256},{256,384},{384,0},{1,129},{129,257},{257,385},{3... | collective-permute-start | bytes 798728 | tf_op jit(solution)/shard_map/ppermute | solution.py:28
  47.8 10.0 %collective-permute-start.3 = (bf16[1040,128]{1,0:T(8,128)(2,1)S(1)}, bf16[1040,128]{1,0:T(8,128)(2,1)S(1)}, u32[]{:S(2)}, u32[]{:S(2)}) collective-permute-start(bf16[1040,128]{1,0:T(8,128)(2,1)S(1)} %pad_maximum_fusion.1.refs_0_), channel_id=1, source_target_pairs={{0,256},{128,384},{256,0},{384,128},{1,257},{129,385},{257,1},{385... | collective-permute-start | bytes 798728 | tf_op jit(solution)/shard_map/ppermute | solution.py:28
  52.2 12.9 %collective-permute-start.4 = (bf16[1040,128]{1,0:T(8,128)(2,1)S(1)}, bf16[1040,128]{1,0:T(8,128)(2,1)S(1)}, u32[]{:S(2)}, u32[]{:S(2)}) collective-permute-start(bf16[1040,128]{1,0:T(8,128)(2,1)S(1)} %pad_maximum_fusion.1.refs_0_), channel_id=1, source_target_pairs={{0,384},{128,0},{256,128},{384,256},{1,385},{129,1},{257,129},{385... | collective-permute-start | bytes 798728 | tf_op jit(solution)/shard_map/ppermute | solution.py:28
  72.7 4.7 %collective-permute-start.6 = (bf16[2,16,128,128]{3,2,1,0:T(8,128)(2,1)S(1)}, bf16[2,16,128,128]{3,2,1,0:T(8,128)(2,1)}, u32[]{:S(2)}, u32[]{:S(2)}) collective-permute-start(bf16[2,16,128,128]{3,2,1,0:T(8,128)(2,1)S(1)} %collective-permute-done.1.refs_5_), channel_id=1, source_target_pairs={{0,16},{16,0},{1,17},{17,1},{2,18},{18,2},{3,19},{19,3},{4,20},{20... | collective-permute-start | bytes 3145736 | tf_op jit(solution)/shard_map/ppermute | solution.py:28
  74.7 17.2 %collective-permute-start.5 = (bf16[2,8,128,128]{3,2,1,0:T(8,128)(2,1)S(1)}, bf16[2,8,128,128]{3,2,1,0:T(8,128)(2,1)S(1)}, u32[]{:S(2)}, u32[]{:S(2)}) collective-permute-start(bf16[2,8,128,128]{3,2,1,0:T(8,128)(2,1)S(1)} %constant_dynamic-slice_fusion), channel_id=1, source_target_pairs={{0,32},{16,112},{32,64},{48,16},{64,96},{80,48},{96,0},{112,80},{1... | collective-permute-start | bytes 1572872 | tf_op jit(solution)/shard_map/ppermute | solution.py:33
  91.9 3.8 %collective-permute-start.7 = (bf16[2,8,128,128]{3,2,1,0:T(8,128)(2,1)S(1)}, bf16[2,8,128,128]{3,2,1,0:T(8,128)(2,1)S(1)}, u32[]{:S(2)}, u32[]{:S(2)}) collective-permute-start(bf16[2,8,128,128]{3,2,1,0:T(8,128)(2,1)S(1)} %collective-permute-done.5), channel_id=1, source_target_pairs={{0,16},{16,0},{1,17},{17,1},{2,18},{18,2},{3,19},{19,3},{4,20},{20... | collective-permute-start | bytes 1572872 | tf_op jit(solution)/shard_map/ppermute | solution.py:28
  97.8 14.3 %collective-permute-start.8 = (bf16[1056,128]{1,0:T(8,128)(2,1)S(1)}, bf16[1056,128]{1,0:T(8,128)(2,1)S(1)}, u32[]{:S(2)}, u32[]{:S(2)}) collective-permute-start(bf16[1056,128]{1,0:T(8,128)(2,1)S(1)} %shard_map.48), channel_id=1, source_target_pairs={{0,256},{128,384},{256,0},{384,128},{1,257},{129,385},{257,1},{385... | collective-permute-start | bytes 811016 | tf_op jit(solution)/shard_map/ppermute | solution.py:28
  104.1 10.1 %collective-permute-start.10 = (bf16[1056,128]{1,0:T(8,128)(2,1)S(1)}, bf16[1056,128]{1,0:T(8,128)(2,1)S(1)}, u32[]{:S(2)}, u32[]{:S(2)}) collective-permute-start(bf16[1056,128]{1,0:T(8,128)(2,1)S(1)} %get-tuple-element.48), channel_id=1, source_target_pairs={{0,128},{128,256},{256,384},{384,0},{1,129},{129,257},{257,385},{3... | collective-permute-start | bytes 811016 | tf_op jit(solution)/shard_map/ppermute | solution.py:28
  108.1 11.1 %collective-permute-start.9 = (bf16[1056,128]{1,0:T(8,128)(2,1)S(1)}, bf16[1056,128]{1,0:T(8,128)(2,1)S(1)}, u32[]{:S(2)}, u32[]{:S(2)}) collective-permute-start(bf16[1056,128]{1,0:T(8,128)(2,1)S(1)} %get-tuple-element.47), channel_id=1, source_target_pairs={{0,384},{128,0},{256,128},{384,256},{1,385},{129,1},{257,129},{385... | collective-permute-start | bytes 811016 | tf_op jit(solution)/shard_map/ppermute | solution.py:28

commit v12 on v11

--- a/solution.py
+++ b/solution.py
@@ -31,6 +31,10 @@
 def ring_step(field):
     pairs = [(z * NC + c, (z + (1, -1)[c]) % NZ * NC + c) for z in range(NZ) for c in range(NC)]
     return lax.ppermute(field, ("zh", "core"), pairs)
+
+
+def half(field):
+    return lax.dynamic_slice_in_dim(field, lax.axis_index("core") * (NU // 2), NU // 2, axis=0)
 
 
 def exchange(field, axes):
@@ -227,16 +231,19 @@
     k0 = got[:, TOK:]
     q0 = jnp.concatenate([got[:, :TOK].reshape(ROWS, HD), picks], axis=0)
 
-    own = jnp.stack([k0, shift(k0, "core", 1)])
-    near = ring_step(own)
+    near0 = ring_step(k0)
+    other = shift(k0, "core", 1)
+    near1 = ring_step(other)
     q1, q2, q3 = (shift(q0, "x", dx) for dx in (1, 2, 3))
-    near, q1, q2, q3 = lax.optimization_barrier((near, q1, q2, q3))
-    half = lax.dynamic_slice_in_dim(near, lax.axis_index("core") * (NU // 2), NU // 2, axis=1)
-    last = ring_step(half)
+    near0, q1, q2, q3 = lax.optimization_barrier((near0, q1, q2, q3))
+    last0, last1 = ring_step(half(near0)), ring_step(half(near1))
+    near0, near1, last0 = lax.optimization_barrier((near0, near1, last0))
+    own, near = jnp.stack([k0, other]), jnp.stack([near0, near1])
     far = shift(near, "core", 1)
     old = attend([q0, q1, q2, q3], [own, near, far])
 
-    last, *old = lax.optimization_barrier((last, *old))
+    last0, last1, *old = lax.optimization_barrier((last0, last1, *old))
+    last = jnp.stack([last0, last1])
     kvs = [jnp.concatenate([last, shift(last, "core", 1)], axis=0)]
     (o2,) = attend([q2], kvs, [old[2]])
     o2, *kvs = lax.optimization_barrier((o2, *kvs))

time: 135 us -> 138 us (1.022); the launches traced: 135 us -> 135 us
  starting transfers between devices: 31.6 us -> 45.9 us
  waiting for transfers between devices: 35.7 us -> 21.8 us
    ppermute x9, waiting for transfers between devices: 22.2 us -> 8.13 us  [shift(): return lax.ppermute(field, axis, [(i, (i + by) % n) for i in range(n)])]
    ppermute x2 -> x4, starting transfers between devices: 8.01 us -> 18.7 us  [ring_step(): return lax.ppermute(field, ('zh', 'core'), pairs)]
    ppermute x9, starting transfers between devices: 23.6 us -> 27.1 us  [shift(): return lax.ppermute(field, axis, [(i, (i + by) % n) for i in range(n)])]
    ppermute x2 -> x4, waiting for transfers between devices: 13.5 us -> 13.7 us  [ring_step(): return lax.ppermute(field, ('zh', 'core'), pairs)]
  transfers between devices with their start and end apart: 11 -> 13, of which waited for: 9 -> 5; matrix products, arithmetic and copies ran while one was open for 0% -> 1% of each run, Pallas kernels for 10% -> 9%
where the time goes in v12:
time: 138 us; the launch traced here: 135 us
  blocking collectives  46.8 us (34%)
  starting transfers between devices  45.9 us (33%)
  waiting for transfers between devices  21.8 us (16%)
  Pallas kernels  18 us (13%)
  other arithmetic  1.41 us (1%)
    all_to_all x2, blocking collectives, exchange(): return lax.all_to_all(field, axes, split_axis=0, concat_axis=0, tiled=True)  46.8 us
    ppermute x9, starting transfers between devices, shift(): return lax.ppermute(field, axis, [(i, (i + by) % n) for i in range(n)])  27.1 us
    ppermute x4, starting transfers between devices, ring_step(): return lax.ppermute(field, ('zh', 'core'), pairs)  18.7 us
    pallas_call x8, Pallas kernels, call(): pl.pallas_call(kernel, out_shape=outs, in_specs=specs, out_specs=jax.tree...  18 us
    ppermute x4, waiting for transfers between devices, ring_step(): return lax.ppermute(field, ('zh', 'core'), pairs)  13.7 us
    ppermute x9, waiting for transfers between devices, shift(): return lax.ppermute(field, axis, [(i, (i + by) % n) for i in range(n)])  8.13 us
  transfers between devices with their start and end apart: 13, of which 5 were waited for; matrix products, arithmetic and copies ran while one was open for 1% of the time, Pallas kernels for 9%

profile of v12, /device:TPU:6, one launch (start us, length us, event | category | flops | bytes accessed | tf_op | source)
XLA Modules:
  0.0 135.1 jit_solution(9575595498315243903)
XLA Ops:
  0.0 2.1 %shard_map.46 = (bf16[16,192,128]{2,1,0:T(8,128)(2,1)}, bf16[16,128]{1,0:T(8,128)(2,1)}) custom-call(bf16[64,1536]{1,0:T(8,128)(2,1)} %q_hbm.1, bf16[64,1536]{1,0:T(8,128)(2,1)} %k_hbm.1, bf16[64,1536]{1,0:T(8,128)(2,1)} %v_hbm.1, s32[12,8,256]{2,1,0:T(8,128)} %mask_hbm.1), custom_call_target="tpu_custom_call" | custom-call | bytes 262144 | tf_op jit(solution)/shard_map/pallas_call | solution.py:188
  2.1 32.4 %all_to_all.10 = bf16[16,192,128]{2,1,0:T(8,128)(2,1)S(1)} all-to-all(bf16[16,192,128]{2,1,0:T(8,128)(2,1)} %get-tuple-element.31), channel_id=1, replica_groups=mesh['x'=4,'zh'=4,'core'=2,'y'=8,'zl'=2] {'y','zl'}, dimensions={0} | all-to-all | bytes 1572864 | tf_op jit(solution)/shard_map/all_to_all | solution.py:41
  34.5 0.3 slice_bitcast_fusion
  34.7 1.9 %collective-permute-start.4 = (bf16[16,128,128]{2,1,0:T(8,128)(2,1)S(1)}, bf16[16,128,128]{2,1,0:T(8,128)(2,1)}, u32[]{:S(2)}, u32[]{:S(2)}) collective-permute-start(bf16[16,128,128]{2,1,0:T(8,128)(2,1)S(1)} %get-tuple-element.58), channel_id=1, source_target_pairs={{0,16},{16,0},{1,17},{17,1},{2,18},{18,2},{3,19},{19,3},{4,20},{20... | collective-permute-start | bytes 1572872 | tf_op jit(solution)/shard_map/ppermute | solution.py:28
  36.7 6.1 %collective-permute-start = (bf16[16,128,128]{2,1,0:T(8,128)(2,1)S(1)}, bf16[16,128,128]{2,1,0:T(8,128)(2,1)S(1)}, u32[]{:S(2)}, u32[]{:S(2)}) collective-permute-start(bf16[16,128,128]{2,1,0:T(8,128)(2,1)S(1)} %get-tuple-element.58), channel_id=1, source_target_pairs={{0,32},{16,112},{32,64},{48,16},{64,96},{80,48},{96,0},{112,80},{1... | collective-permute-start | bytes 1572872 | tf_op jit(solution)/shard_map/ppermute | solution.py:33
  42.8 0.7 copy-done
  43.5 2.7 %collective-permute-start.3 = (bf16[1040,128]{1,0:T(8,128)(2,1)S(1)}, bf16[1040,128]{1,0:T(8,128)(2,1)S(1)}, u32[]{:S(2)}, u32[]{:S(2)}) collective-permute-start(bf16[1040,128]{1,0:T(8,128)(2,1)S(1)} %pad_maximum_fusion.4.refs_0_), channel_id=1, source_target_pairs={{0,384},{128,0},{256,128},{384,256},{1,385},{129,1},{257,129},{385... | collective-permute-start | bytes 798728 | tf_op jit(solution)/shard_map/ppermute | solution.py:28
  46.2 3.0 %collective-permute-start.2 = (bf16[1040,128]{1,0:T(8,128)(2,1)S(1)}, bf16[1040,128]{1,0:T(8,128)(2,1)S(1)}, u32[]{:S(2)}, u32[]{:S(2)}) collective-permute-start(bf16[1040,128]{1,0:T(8,128)(2,1)S(1)} %pad_maximum_fusion.4.refs_0_), channel_id=1, source_target_pairs={{0,256},{128,384},{256,0},{384,128},{1,257},{129,385},{257,1},{385... | collective-permute-start | bytes 798728 | tf_op jit(solution)/shard_map/ppermute | solution.py:28
  49.3 4.0 %collective-permute-start.1 = (bf16[1040,128]{1,0:T(8,128)(2,1)S(1)}, bf16[1040,128]{1,0:T(8,128)(2,1)S(1)}, u32[]{:S(2)}, u32[]{:S(2)}) collective-permute-start(bf16[1040,128]{1,0:T(8,128)(2,1)S(1)} %pad_maximum_fusion.4.refs_0_), channel_id=1, source_target_pairs={{0,128},{128,256},{256,384},{384,0},{1,129},{129,257},{257,385},{3... | collective-permute-start | bytes 798728 | tf_op jit(solution)/shard_map/ppermute | solution.py:28
  53.3 6.4 %collective-permute-start.5 = (bf16[16,128,128]{2,1,0:T(8,128)(2,1)}, bf16[16,128,128]{2,1,0:T(8,128)(2,1)S(1)}, u32[]{:S(2)}, u32[]{:S(2)}) collective-permute-start(bf16[16,128,128]{2,1,0:T(8,128)(2,1)} %collective-permute-done.4), channel_id=1, source_target_pairs={{0,32},{16,112},{32,64},{48,16},{64,96},{80,48},{96,0},{112,80},{1... | collective-permute-start | bytes 1572872 | tf_op jit(solution)/shard_map/ppermute | solution.py:33
  59.7 2.4 %collective-permute-done.1.refs_1_.refs_0_ = bf16[1040,128]{1,0:T(8,128)(2,1)S(1)} collective-permute-done((bf16[1040,128]{1,0:T(8,128)(2,1)S(1)}, bf16[1040,128]{1,0:T(8,128)(2,1)S(1)}, u32[]{:S(2)}, u32[]{:S(2)}) %collective-permute-start.1) | collective-permute-done | bytes 266272 | tf_op jit(solution)/shard_map/ppermute | solution.py:28
  62.1 3.4 %collective-permute-start.6 = (bf16[8,128,128]{2,1,0:T(8,128)(2,1)S(1)}, bf16[8,128,128]{2,1,0:T(8,128)(2,1)S(1)}, u32[]{:S(2)}, u32[]{:S(2)}) collective-permute-start(bf16[8,128,128]{2,1,0:T(8,128)(2,1)S(1)} %constant_dynamic-slice_fusion.1), channel_id=1, source_target_pairs={{0,32},{16,112},{32,64},{48,16},{64,96},{80,48},{96,0},{112,80},{1... | collective-permute-start | bytes 786440 | tf_op jit(solution)/shard_map/ppermute | solution.py:33
  65.5 13.7 %collective-permute-done.6 = bf16[8,128,128]{2,1,0:T(8,128)(2,1)S(1)} collective-permute-done((bf16[8,128,128]{2,1,0:T(8,128)(2,1)S(1)}, bf16[8,128,128]{2,1,0:T(8,128)(2,1)S(1)}, u32[]{:S(2)}, u32[]{:S(2)}) %collective-permute-start.6) | collective-permute-done | bytes 262176 | tf_op jit(solution)/shard_map/ppermute | solution.py:33
  79.3 1.9 %collective-permute-start.8 = (bf16[2,16,128,128]{3,2,1,0:T(8,128)(2,1)S(1)}, bf16[2,16,128,128]{3,2,1,0:T(8,128)(2,1)S(1)}, u32[]{:S(2)}, u32[]{:S(2)}) collective-permute-start(bf16[2,16,128,128]{3,2,1,0:T(8,128)(2,1)S(1)} %pad_maximum_fusion.1.refs_5_), channel_id=1, source_target_pairs={{0,16},{16,0},{1,17},{17,1},{2,18},{18,2},{3,19},{19,3},{4,20},{20... | collective-permute-start | bytes 3145736 | tf_op jit(solution)/shard_map/ppermute | solution.py:28
  81.3 2.8 %collective-permute-start.7 = (bf16[8,128,128]{2,1,0:T(8,128)(2,1)S(1)}, bf16[8,128,128]{2,1,0:T(8,128)(2,1)S(1)}, u32[]{:S(2)}, u32[]{:S(2)}) collective-permute-start(bf16[8,128,128]{2,1,0:T(8,128)(2,1)S(1)} %constant_dynamic-slice_fusion), channel_id=1, source_target_pairs={{0,32},{16,112},{32,64},{48,16},{64,96},{80,48},{96,0},{112,80},{1... | collective-permute-start | bytes 786440 | tf_op jit(solution)/shard_map/ppermute | solution.py:33
  84.1 1.1 pad_maximum_fusion.refs_4_
  85.3 7.3 %shard_map.47 = (f32[2,1024,128]{2,1,0:T(8,128)S(1)}, f32[2,1024,128]{2,1,0:T(8,128)S(1)}, f32[2,1024,128]{2,1,0:T(8,128)S(1)}, f32[2,1024,128]{2,1,0:T(8,128)S(1)}) custom-call(bf16[1040,128]{1,0:T(8,128)(2,1)S(1)} %pad_maximum_fusion.4.refs_0_, bf16[1040,128]{1,0:T(8,128)(2,1)S(1)} %collective-permute-done.1.refs_1_.refs_0_, ...), custom_call_target="tpu_custom_call" | custom-call | flops 1610612736 | bytes 2097152 | tf_op jit(solution)/shard_map/pallas_call | solution.py:188
  92.6 3.4 %collective-permute-start.9 = (bf16[2,8,128,128]{3,2,1,0:T(8,128)(2,1)S(1)}, bf16[2,8,128,128]{3,2,1,0:T(8,128)(2,1)S(1)}, u32[]{:S(2)}, u32[]{:S(2)}) collective-permute-start(bf16[2,8,128,128]{3,2,1,0:T(8,128)(2,1)S(1)} %pad_maximum_fusion.3), channel_id=1, source_target_pairs={{0,16},{16,0},{1,17},{17,1},{2,18},{18,2},{3,19},{19,3},{4,20},{20... | collective-permute-start | bytes 1572872 | tf_op jit(solution)/shard_map/ppermute | solution.py:28
  96.0 1.5 %collective-permute-done.9 = bf16[2,8,128,128]{3,2,1,0:T(8,128)(2,1)S(1)} collective-permute-done((bf16[2,8,128,128]{3,2,1,0:T(8,128)(2,1)S(1)}, bf16[2,8,128,128]{3,2,1,0:T(8,128)(2,1)S(1)}, u32[]{:S(2)}, u32[]{:S(2)}) %collective-permute-start.9) | collective-permute-done | bytes 524320 | tf_op jit(solution)/shard_map/ppermute | solution.py:28
  97.5 0.1 pad_maximum_fusion.2.refs_1_.refs_2_
  97.6 2.0 %shard_map.48 = bf16[1056,128]{1,0:T(8,128)(2,1)S(1)} custom-call(bf16[1040,128]{1,0:T(8,128)(2,1)S(1)} %collective-permute-done.2.refs_2_.refs_0_, bf16[4,8,128,128]{3,2,1,0:T(8,128)(2,1)S(1)} %pad_maximum_fusion.2.refs_1_.refs_2_, f32[2,1024,128]{2,1,0:T(8,128)S(1)} %get-tuple-element.46.refs_2_), custom_call_target="tpu_custom_call" | custom-call | flops 134217728 | bytes 2097152 | tf_op jit(solution)/shard_map/pallas_call | solution.py:188
  99.7 3.1 %collective-permute-start.10 = (bf16[1056,128]{1,0:T(8,128)(2,1)S(1)}, bf16[1056,128]{1,0:T(8,128)(2,1)S(1)}, u32[]{:S(2)}, u32[]{:S(2)}) collective-permute-start(bf16[1056,128]{1,0:T(8,128)(2,1)S(1)} %shard_map.48), channel_id=1, source_target_pairs={{0,256},{128,384},{256,0},{384,128},{1,257},{129,385},{257,1},{385... | collective-permute-start | bytes 811016 | tf_op jit(solution)/shard_map/ppermute | solution.py:28
  102.8 3.0 %shard_map.49 = (bf16[1056,128]{1,0:T(8,128)(2,1)S(1)}, bf16[1056,128]{1,0:T(8,128)(2,1)S(1)}) custom-call(bf16[1040,128]{1,0:T(8,128)(2,1)S(1)} %collective-permute-done.1.refs_1_.refs_0_, bf16[1040,128]{1,0:T(8,128)(2,1)S(1)} %collective-permute-done.3.refs_3_.refs_1_, bf16[4,8,128,128]{3,2,1,0:T(8,128)(2,1)S(1)} %pad_maximum_fusion.2.refs_1_.refs_2_, ...), custom_call_target="tpu_custom_call" | custom-call | flops 268435456 | bytes 2097152 | tf_op jit(solution)/shard_map/pallas_call | solution.py:188
  105.8 3.6 %collective-permute-start.11 = (bf16[1056,128]{1,0:T(8,128)(2,1)S(1)}, bf16[1056,128]{1,0:T(8,128)(2,1)S(1)}, u32[]{:S(2)}, u32[]{:S(2)}) collective-permute-start(bf16[1056,128]{1,0:T(8,128)(2,1)S(1)} %get-tuple-element.55), channel_id=1, source_target_pairs={{0,384},{128,0},{256,128},{384,256},{1,385},{129,1},{257,129},{385... | collective-permute-start | bytes 811016 | tf_op jit(solution)/shard_map/ppermute | solution.py:28
  109.4 3.4 %collective-permute-start.12 = (bf16[1056,128]{1,0:T(8,128)(2,1)S(1)}, bf16[1056,128]{1,0:T(8,128)(2,1)S(1)}, u32[]{:S(2)}, u32[]{:S(2)}) collective-permute-start(bf16[1056,128]{1,0:T(8,128)(2,1)S(1)} %get-tuple-element.56), channel_id=1, source_target_pairs={{0,128},{128,256},{256,384},{384,0},{1,129},{129,257},{257,385},{3... | collective-permute-start | bytes 811016 | tf_op jit(solution)/shard_map/ppermute | solution.py:28
  112.9 2.0 %shard_map.50.refs_0_ = bf16[1056,128]{1,0:T(8,128)(2,1)S(1)} custom-call(bf16[1040,128]{1,0:T(8,128)(2,1)S(1)} %pad_maximum_fusion.4.refs_0_, bf16[4,8,128,128]{3,2,1,0:T(8,128)(2,1)S(1)} %pad_maximum_fusion.2.refs_1_.refs_2_, f32[2,1024,128]{2,1,0:T(8,128)S(1)} %get-tuple-element.53.refs_2_), custom_call_target="tpu_custom_call" | custom-call | flops 134217728 | bytes 2097152 | tf_op jit(solution)/shard_map/pallas_call | solution.py:188
  114.9 0.4 shard_map.51.refs_0_
  115.3 2.4 %collective-permute-done.11.refs_1_ = bf16[1056,128]{1,0:T(8,128)(2,1)S(1)} collective-permute-done((bf16[1056,128]{1,0:T(8,128)(2,1)S(1)}, bf16[1056,128]{1,0:T(8,128)(2,1)S(1)}, u32[]{:S(2)}, u32[]{:S(2)}) %collective-permute-start.11) | collective-permute-done | bytes 270368 | tf_op jit(solution)/shard_map/ppermute | solution.py:28
  117.6 1.8 %collective-permute-done.12.refs_2_ = bf16[1056,128]{1,0:T(8,128)(2,1)S(1)} collective-permute-done((bf16[1056,128]{1,0:T(8,128)(2,1)S(1)}, bf16[1056,128]{1,0:T(8,128)(2,1)S(1)}, u32[]{:S(2)}, u32[]{:S(2)}) %collective-permute-start.12) | collective-permute-done | bytes 270368 | tf_op jit(solution)/shard_map/ppermute | solution.py:28
  119.5 0.5 shard_map.52
  120.0 14.4 %all_to_all.11.in_ref = bf16[16,64,128]{2,1,0:T(8,128)(2,1)S(1)} all-to-all(bf16[16,64,128]{2,1,0:T(8,128)(2,1)S(1)} %bitcast.9), channel_id=1, replica_groups=mesh['x'=4,'zh'=4,'core'=2,'y'=8,'zl'=2] {'y','zl'}, dimensions={0} | all-to-all | bytes 524288 | tf_op jit(solution)/shard_map/all_to_all | solution.py:41
  134.4 0.7 shard_map.53
  (15 shorter events, 0.3 us)
Async XLA Ops:
  34.7 18.5 %collective-permute-start.4 = (bf16[16,128,128]{2,1,0:T(8,128)(2,1)S(1)}, bf16[16,128,128]{2,1,0:T(8,128)(2,1)}, u32[]{:S(2)}, u32[]{:S(2)}) collective-permute-start(bf16[16,128,128]{2,1,0:T(8,128)(2,1)S(1)} %get-tuple-element.58), channel_id=1, source_target_pairs={{0,16},{16,0},{1,17},{17,1},{2,18},{18,2},{3,19},{19,3},{4,20},{20... | collective-permute-start | bytes 1572872 | tf_op jit(solution)/shard_map/ppermute | solution.py:28
  36.7 25.4 %collective-permute-start = (bf16[16,128,128]{2,1,0:T(8,128)(2,1)S(1)}, bf16[16,128,128]{2,1,0:T(8,128)(2,1)S(1)}, u32[]{:S(2)}, u32[]{:S(2)}) collective-permute-start(bf16[16,128,128]{2,1,0:T(8,128)(2,1)S(1)} %get-tuple-element.58), channel_id=1, source_target_pairs={{0,32},{16,112},{32,64},{48,16},{64,96},{80,48},{96,0},{112,80},{1... | collective-permute-start | bytes 1572872 | tf_op jit(solution)/shard_map/ppermute | solution.py:33
  42.8 0.7 copy-start
  43.5 16.2 %collective-permute-start.3 = (bf16[1040,128]{1,0:T(8,128)(2,1)S(1)}, bf16[1040,128]{1,0:T(8,128)(2,1)S(1)}, u32[]{:S(2)}, u32[]{:S(2)}) collective-permute-start(bf16[1040,128]{1,0:T(8,128)(2,1)S(1)} %pad_maximum_fusion.4.refs_0_), channel_id=1, source_target_pairs={{0,384},{128,0},{256,128},{384,256},{1,385},{129,1},{257,129},{385... | collective-permute-start | bytes 798728 | tf_op jit(solution)/shard_map/ppermute | solution.py:28
  46.2 13.5 %collective-permute-start.2 = (bf16[1040,128]{1,0:T(8,128)(2,1)S(1)}, bf16[1040,128]{1,0:T(8,128)(2,1)S(1)}, u32[]{:S(2)}, u32[]{:S(2)}) collective-permute-start(bf16[1040,128]{1,0:T(8,128)(2,1)S(1)} %pad_maximum_fusion.4.refs_0_), channel_id=1, source_target_pairs={{0,256},{128,384},{256,0},{384,128},{1,257},{129,385},{257,1},{385... | collective-permute-start | bytes 798728 | tf_op jit(solution)/shard_map/ppermute | solution.py:28
  49.3 12.8 %collective-permute-start.1 = (bf16[1040,128]{1,0:T(8,128)(2,1)S(1)}, bf16[1040,128]{1,0:T(8,128)(2,1)S(1)}, u32[]{:S(2)}, u32[]{:S(2)}) collective-permute-start(bf16[1040,128]{1,0:T(8,128)(2,1)S(1)} %pad_maximum_fusion.4.refs_0_), channel_id=1, source_target_pairs={{0,128},{128,256},{256,384},{384,0},{1,129},{129,257},{257,385},{3... | collective-permute-start | bytes 798728 | tf_op jit(solution)/shard_map/ppermute | solution.py:28
  53.3 25.9 %collective-permute-start.5 = (bf16[16,128,128]{2,1,0:T(8,128)(2,1)}, bf16[16,128,128]{2,1,0:T(8,128)(2,1)S(1)}, u32[]{:S(2)}, u32[]{:S(2)}) collective-permute-start(bf16[16,128,128]{2,1,0:T(8,128)(2,1)} %collective-permute-done.4), channel_id=1, source_target_pairs={{0,32},{16,112},{32,64},{48,16},{64,96},{80,48},{96,0},{112,80},{1... | collective-permute-start | bytes 1572872 | tf_op jit(solution)/shard_map/ppermute | solution.py:33
  62.1 17.1 %collective-permute-start.6 = (bf16[8,128,128]{2,1,0:T(8,128)(2,1)S(1)}, bf16[8,128,128]{2,1,0:T(8,128)(2,1)S(1)}, u32[]{:S(2)}, u32[]{:S(2)}) collective-permute-start(bf16[8,128,128]{2,1,0:T(8,128)(2,1)S(1)} %constant_dynamic-slice_fusion.1), channel_id=1, source_target_pairs={{0,32},{16,112},{32,64},{48,16},{64,96},{80,48},{96,0},{112,80},{1... | collective-permute-start | bytes 786440 | tf_op jit(solution)/shard_map/ppermute | solution.py:33
  79.3 5.9 %collective-permute-start.8 = (bf16[2,16,128,128]{3,2,1,0:T(8,128)(2,1)S(1)}, bf16[2,16,128,128]{3,2,1,0:T(8,128)(2,1)S(1)}, u32[]{:S(2)}, u32[]{:S(2)}) collective-permute-start(bf16[2,16,128,128]{3,2,1,0:T(8,128)(2,1)S(1)} %pad_maximum_fusion.1.refs_5_), channel_id=1, source_target_pairs={{0,16},{16,0},{1,17},{17,1},{2,18},{18,2},{3,19},{19,3},{4,20},{20... | collective-permute-start | bytes 3145736 | tf_op jit(solution)/shard_map/ppermute | solution.py:28
  81.3 11.3 %collective-permute-start.7 = (bf16[8,128,128]{2,1,0:T(8,128)(2,1)S(1)}, bf16[8,128,128]{2,1,0:T(8,128)(2,1)S(1)}, u32[]{:S(2)}, u32[]{:S(2)}) collective-permute-start(bf16[8,128,128]{2,1,0:T(8,128)(2,1)S(1)} %constant_dynamic-slice_fusion), channel_id=1, source_target_pairs={{0,32},{16,112},{32,64},{48,16},{64,96},{80,48},{96,0},{112,80},{1... | collective-permute-start | bytes 786440 | tf_op jit(solution)/shard_map/ppermute | solution.py:33
  92.6 4.9 %collective-permute-start.9 = (bf16[2,8,128,128]{3,2,1,0:T(8,128)(2,1)S(1)}, bf16[2,8,128,128]{3,2,1,0:T(8,128)(2,1)S(1)}, u32[]{:S(2)}, u32[]{:S(2)}) collective-permute-start(bf16[2,8,128,128]{3,2,1,0:T(8,128)(2,1)S(1)} %pad_maximum_fusion.3), channel_id=1, source_target_pairs={{0,16},{16,0},{1,17},{17,1},{2,18},{18,2},{3,19},{19,3},{4,20},{20... | collective-permute-start | bytes 1572872 | tf_op jit(solution)/shard_map/ppermute | solution.py:28
  99.7 15.2 %collective-permute-start.10 = (bf16[1056,128]{1,0:T(8,128)(2,1)S(1)}, bf16[1056,128]{1,0:T(8,128)(2,1)S(1)}, u32[]{:S(2)}, u32[]{:S(2)}) collective-permute-start(bf16[1056,128]{1,0:T(8,128)(2,1)S(1)} %shard_map.48), channel_id=1, source_target_pairs={{0,256},{128,384},{256,0},{384,128},{1,257},{129,385},{257,1},{385... | collective-permute-start | bytes 811016 | tf_op jit(solution)/shard_map/ppermute | solution.py:28
  105.8 11.8 %collective-permute-start.11 = (bf16[1056,128]{1,0:T(8,128)(2,1)S(1)}, bf16[1056,128]{1,0:T(8,128)(2,1)S(1)}, u32[]{:S(2)}, u32[]{:S(2)}) collective-permute-start(bf16[1056,128]{1,0:T(8,128)(2,1)S(1)} %get-tuple-element.55), channel_id=1, source_target_pairs={{0,384},{128,0},{256,128},{384,256},{1,385},{129,1},{257,129},{385... | collective-permute-start | bytes 811016 | tf_op jit(solution)/shard_map/ppermute | solution.py:28
  109.4 10.1 %collective-permute-start.12 = (bf16[1056,128]{1,0:T(8,128)(2,1)S(1)}, bf16[1056,128]{1,0:T(8,128)(2,1)S(1)}, u32[]{:S(2)}, u32[]{:S(2)}) collective-permute-start(bf16[1056,128]{1,0:T(8,128)(2,1)S(1)} %get-tuple-element.56), channel_id=1, source_target_pairs={{0,128},{128,256},{256,384},{384,0},{1,129},{129,257},{257,385},{3... | collective-permute-start | bytes 811016 | tf_op jit(solution)/shard_map/ppermute | solution.py:28

commit v13 on v11

--- a/solution.py
+++ b/solution.py
@@ -71,7 +71,7 @@
 
 
 def attend_kernel(chunks, unit, opening, *refs):
-    n_kv = 3 if opening else 1
+    n_kv = 2
     q_refs, kv_refs, rest = refs[:chunks], refs[chunks : chunks + n_kv], refs[chunks + n_kv :]
     old_refs = () if opening else rest[:chunks]
     rest = rest[len(old_refs) :]
@@ -81,19 +81,18 @@
     fetch = pltpu.make_async_copy(flat_ref, picks_ref, sem)
     fetch.start()
     x, z, c = lax.axis_index("x"), lax.axis_index("zh"), lax.axis_index("core")
+    before, after = z + NZ - 1 + 2 * c, z + NZ + 1 - 2 * c
+    first, second = kv_refs
     if opening:
-        own, near, far = kv_refs
-        before, after = z + NZ - 1 + 2 * c, z + NZ + 1 - 2 * c
-        groups = [(own, 0, z, c), (own, 1, z, 1 - c), (near, 0, before, c), (near, 1, before, 1 - c)]
-        groups += [(far, 0, after, 1 - c), (far, 1, after, c)]
+        groups = [(first, 0, z, c), (first, 1, z, 1 - c), (second, 0, before, c), (second, 1, before, 1 - c)]
     else:
-        groups = [(kv_refs[0], 0, z + 2, c), (kv_refs[0], 1, z + 2, 1 - c)]
+        groups = [(first, 0, after, 1 - c), (first, 1, after, c), (second, 0, z + 2, c), (second, 1, z + 2, 1 - c)]
     columns = [(x * NZ + lax.rem(zz, NZ)) * NC + cc for _, _, zz, cc in groups]
     pairs = len(groups) // 2
 
     def pick(group, j):
         ref, n = group[:2]
-        if opening:
+        if opening or ref is first:
             return ref[n, pl.ds(2 * j, 2)]
         return ref[jnp.where(j // (SEGB // 2) == c, n, 3 - n), pl.ds(2 * lax.rem(j, SEGB // 2), 2)]
 
@@ -205,7 +204,7 @@
         functools.partial(attend_kernel, n, unit, old is None),
         outs, [VMEM] * len(ins), *ins,
         scratch=[pltpu.VMEM((n * SEGB, HD), jnp.int32), pltpu.SMEM((n * SEGB, HD), jnp.int32), pltpu.SemaphoreType.DMA],
-        flops=n * (3 if old is None else 1) * (1 << 27), moved=2 << 20,
+        flops=n * (1 << 28), moved=2 << 20,
     )
 
 
@@ -233,11 +232,11 @@
     near, q1, q2, q3 = lax.optimization_barrier((near, q1, q2, q3))
     half = lax.dynamic_slice_in_dim(near, lax.axis_index("core") * (NU // 2), NU // 2, axis=1)
     last = ring_step(half)
-    far = shift(near, "core", 1)
-    old = attend([q0, q1, q2, q3], [own, near, far])
-
-    last, *old = lax.optimization_barrier((last, *old))
-    kvs = [jnp.concatenate([last, shift(last, "core", 1)], axis=0)]
+    old = attend([q0, q1, q2, q3], [own, near])
+
+    near, last, *old = lax.optimization_barrier((near, last, *old))
+    far = shift(jnp.concatenate([near, last], axis=1), "core", 1)
+    kvs = [far, jnp.concatenate([last, far[:, NU:]], axis=0)]
     (o2,) = attend([q2], kvs, [old[2]])
     o2, *kvs = lax.optimization_barrier((o2, *kvs))
     back2 = shift(o2, "x", -2)

time: 135 us -> 136 us (level)
  the two profiles are of different devices: /device:TPU:6 before, /device:TPU:8 now
where the time goes in v13:
time: 136 us
  blocking collectives  45.4 us (33%)
  starting transfers between devices  37.9 us (28%)
  waiting for transfers between devices  30.4 us (22%)
  Pallas kernels  21.2 us (16%)
    all_to_all x2, blocking collectives, exchange(): return lax.all_to_all(field, axes, split_axis=0, concat_axis=0, tiled=True)  45.4 us
    ppermute x8, starting transfers between devices, shift(): return lax.ppermute(field, axis, [(i, (i + by) % n) for i in range(n)])  25 us
    ppermute x8, waiting for transfers between devices, shift(): return lax.ppermute(field, axis, [(i, (i + by) % n) for i in range(n)])  22.7 us
    pallas_call x8, Pallas kernels, call(): pl.pallas_call(kernel, out_shape=outs, in_specs=specs, out_specs=jax.tree...  21.2 us
    ppermute x2, starting transfers between devices, ring_step(): return lax.ppermute(field, ('zh', 'core'), pairs)  12.9 us
    ppermute x2, waiting for transfers between devices, ring_step(): return lax.ppermute(field, ('zh', 'core'), pairs)  7.77 us
  transfers between devices with their start and end apart: 10, of which 8 were waited for; matrix products, arithmetic and copies ran while one was open for 0% of the time, Pallas kernels for 11%

profile of v13, /device:TPU:8, one launch (start us, length us, event | category | flops | bytes accessed | tf_op | source)
XLA Modules:
  0.0 135.8 jit_solution(15554866068419283571)
XLA Ops:
  0.0 2.1 %shard_map.46 = (bf16[16,192,128]{2,1,0:T(8,128)(2,1)}, bf16[16,128]{1,0:T(8,128)(2,1)}) custom-call(bf16[64,1536]{1,0:T(8,128)(2,1)} %q_hbm.1, bf16[64,1536]{1,0:T(8,128)(2,1)} %k_hbm.1, bf16[64,1536]{1,0:T(8,128)(2,1)} %v_hbm.1, s32[12,8,256]{2,1,0:T(8,128)} %mask_hbm.1), custom_call_target="tpu_custom_call" | custom-call | bytes 262144 | tf_op jit(solution)/shard_map/pallas_call | solution.py:183
  2.1 31.0 %all_to_all.10 = bf16[16,192,128]{2,1,0:T(8,128)(2,1)S(1)} all-to-all(bf16[16,192,128]{2,1,0:T(8,128)(2,1)} %get-tuple-element.30), channel_id=1, replica_groups=mesh['x'=4,'zh'=4,'core'=2,'y'=8,'zl'=2] {'y','zl'}, dimensions={0} | all-to-all | bytes 1572864 | tf_op jit(solution)/shard_map/all_to_all | solution.py:37
  33.1 0.3 slice_bitcast_fusion
  33.4 1.9 %collective-permute-start = (bf16[16,128,128]{2,1,0:T(8,128)(2,1)S(1)}, bf16[16,128,128]{2,1,0:T(8,128)(2,1)S(1)}, u32[]{:S(2)}, u32[]{:S(2)}) collective-permute-start(bf16[16,128,128]{2,1,0:T(8,128)(2,1)S(1)} %get-tuple-element.56), channel_id=1, source_target_pairs={{0,16},{16,0},{1,17},{17,1},{2,18},{18,2},{3,19},{19,3},{4,20},{20... | collective-permute-start | bytes 1572872 | tf_op jit(solution)/shard_map/ppermute | solution.py:28
  35.3 1.9 %collective-permute-done = bf16[16,128,128]{2,1,0:T(8,128)(2,1)S(1)} collective-permute-done((bf16[16,128,128]{2,1,0:T(8,128)(2,1)S(1)}, bf16[16,128,128]{2,1,0:T(8,128)(2,1)S(1)}, u32[]{:S(2)}, u32[]{:S(2)}) %collective-permute-start) | collective-permute-done | bytes 524320 | tf_op jit(solution)/shard_map/ppermute | solution.py:28
  37.2 0.1 pad_maximum_fusion.1.refs_4_
  37.3 6.1 %collective-permute-start.1 = (bf16[2,16,128,128]{3,2,1,0:T(8,128)(2,1)S(1)}, bf16[2,16,128,128]{3,2,1,0:T(8,128)(2,1)S(1)}, u32[]{:S(2)}, u32[]{:S(2)}) collective-permute-start(bf16[2,16,128,128]{3,2,1,0:T(8,128)(2,1)S(1)} %pad_maximum_fusion.1.refs_4_), channel_id=1, source_target_pairs={{0,32},{16,112},{32,64},{48,16},{64,96},{80,48},{96,0},{112,80},{1... | collective-permute-start | bytes 3145736 | tf_op jit(solution)/shard_map/ppermute | solution.py:33
  43.5 4.7 %collective-permute-start.4 = (bf16[1040,128]{1,0:T(8,128)(2,1)S(1)}, bf16[1040,128]{1,0:T(8,128)(2,1)S(1)}, u32[]{:S(2)}, u32[]{:S(2)}) collective-permute-start(bf16[1040,128]{1,0:T(8,128)(2,1)S(1)} %pad_maximum_fusion.3.refs_0_), channel_id=1, source_target_pairs={{0,384},{128,0},{256,128},{384,256},{1,385},{129,1},{257,129},{385... | collective-permute-start | bytes 798728 | tf_op jit(solution)/shard_map/ppermute | solution.py:28
  48.1 2.7 %collective-permute-start.3 = (bf16[1040,128]{1,0:T(8,128)(2,1)S(1)}, bf16[1040,128]{1,0:T(8,128)(2,1)S(1)}, u32[]{:S(2)}, u32[]{:S(2)}) collective-permute-start(bf16[1040,128]{1,0:T(8,128)(2,1)S(1)} %pad_maximum_fusion.3.refs_0_), channel_id=1, source_target_pairs={{0,256},{128,384},{256,0},{384,128},{1,257},{129,385},{257,1},{385... | collective-permute-start | bytes 798728 | tf_op jit(solution)/shard_map/ppermute | solution.py:28
  50.9 2.8 %collective-permute-start.2 = (bf16[1040,128]{1,0:T(8,128)(2,1)S(1)}, bf16[1040,128]{1,0:T(8,128)(2,1)S(1)}, u32[]{:S(2)}, u32[]{:S(2)}) collective-permute-start(bf16[1040,128]{1,0:T(8,128)(2,1)S(1)} %pad_maximum_fusion.3.refs_0_), channel_id=1, source_target_pairs={{0,128},{128,256},{256,384},{384,0},{1,129},{129,257},{257,385},{3... | collective-permute-start | bytes 798728 | tf_op jit(solution)/shard_map/ppermute | solution.py:28
  53.7 4.6 %collective-permute-done.3.refs_2_.refs_0_ = bf16[1040,128]{1,0:T(8,128)(2,1)S(1)} collective-permute-done((bf16[1040,128]{1,0:T(8,128)(2,1)S(1)}, bf16[1040,128]{1,0:T(8,128)(2,1)S(1)}, u32[]{:S(2)}, u32[]{:S(2)}) %collective-permute-start.3) | collective-permute-done | bytes 266272 | tf_op jit(solution)/shard_map/ppermute | solution.py:28
  58.3 7.4 %collective-permute-done.2.refs_1_.refs_0_ = bf16[1040,128]{1,0:T(8,128)(2,1)S(1)} collective-permute-done((bf16[1040,128]{1,0:T(8,128)(2,1)S(1)}, bf16[1040,128]{1,0:T(8,128)(2,1)S(1)}, u32[]{:S(2)}, u32[]{:S(2)}) %collective-permute-start.2) | collective-permute-done | bytes 266272 | tf_op jit(solution)/shard_map/ppermute | solution.py:28
  65.6 0.3 collective-permute-done.1.refs_5_
  66.0 6.8 %collective-permute-start.5 = (bf16[2,8,128,128]{3,2,1,0:T(8,128)(2,1)S(1)}, bf16[2,8,128,128]{3,2,1,0:T(8,128)(2,1)S(1)}, u32[]{:S(2)}, u32[]{:S(2)}) collective-permute-start(bf16[2,8,128,128]{3,2,1,0:T(8,128)(2,1)S(1)} %constant_dynamic-slice_fusion), channel_id=1, source_target_pairs={{0,32},{16,112},{32,64},{48,16},{64,96},{80,48},{96,0},{112,80},{1... | collective-permute-start | bytes 1572872 | tf_op jit(solution)/shard_map/ppermute | solution.py:33
  72.8 9.0 %shard_map.47 = (f32[2,1024,128]{2,1,0:T(8,128)S(1)}, f32[2,1024,128]{2,1,0:T(8,128)S(1)}, f32[2,1024,128]{2,1,0:T(8,128)S(1)}, f32[2,1024,128]{2,1,0:T(8,128)S(1)}) custom-call(bf16[1040,128]{1,0:T(8,128)(2,1)S(1)} %pad_maximum_fusion.3.refs_0_, bf16[1040,128]{1,0:T(8,128)(2,1)S(1)} %collective-permute-done.2.refs_1_.refs_0_, ...), custom_call_target="tpu_custom_call" | custom-call | flops 1073741824 | bytes 2097152 | tf_op jit(solution)/shard_map/pallas_call | solution.py:183
  81.8 7.5 %collective-permute-done.5 = bf16[2,8,128,128]{3,2,1,0:T(8,128)(2,1)S(1)} collective-permute-done((bf16[2,8,128,128]{3,2,1,0:T(8,128)(2,1)S(1)}, bf16[2,8,128,128]{3,2,1,0:T(8,128)(2,1)S(1)}, u32[]{:S(2)}, u32[]{:S(2)}) %collective-permute-start.5) | collective-permute-done | bytes 524320 | tf_op jit(solution)/shard_map/ppermute | solution.py:33
  89.3 0.1 pad_maximum_fusion
  89.4 1.9 %collective-permute-start.6 = (bf16[2,24,128,128]{3,2,1,0:T(8,128)(2,1)S(1)}, bf16[2,24,128,128]{3,2,1,0:T(8,128)(2,1)S(1)}, u32[]{:S(2)}, u32[]{:S(2)}) collective-permute-start(bf16[2,24,128,128]{3,2,1,0:T(8,128)(2,1)S(1)} %pad_maximum_fusion), channel_id=1, source_target_pairs={{0,16},{16,0},{1,17},{17,1},{2,18},{18,2},{3,19},{19,3},{4,20},{20... | collective-permute-start | bytes 4718600 | tf_op jit(solution)/shard_map/ppermute | solution.py:28
  91.4 3.4 %collective-permute-done.6.refs_1_.refs_2_ = bf16[2,24,128,128]{3,2,1,0:T(8,128)(2,1)S(1)} collective-permute-done((bf16[2,24,128,128]{3,2,1,0:T(8,128)(2,1)S(1)}, bf16[2,24,128,128]{3,2,1,0:T(8,128)(2,1)S(1)}, u32[]{:S(2)}, u32[]{:S(2)}) %collective-permute-start.6) | collective-permute-done | bytes 1572896 | tf_op jit(solution)/shard_map/ppermute | solution.py:28
  94.8 0.1 pad_maximum_fusion.2.refs_2_.refs_3_
  94.9 2.5 %shard_map.48 = bf16[1056,128]{1,0:T(8,128)(2,1)S(1)} custom-call(bf16[1040,128]{1,0:T(8,128)(2,1)S(1)} %collective-permute-done.3.refs_2_.refs_0_, bf16[2,24,128,128]{3,2,1,0:T(8,128)(2,1)S(1)} %collective-permute-done.6.refs_1_.refs_2_, bf16[4,8,128,128]{3,2,1,0:T(8,128)(2,1)S(1)} %pad_maximum_fusion.2.refs_2_.refs_3_, ...), custom_call_target="tpu_custom_call" | custom-call | flops 268435456 | bytes 2097152 | tf_op jit(solution)/shard_map/pallas_call | solution.py:183
  97.3 5.1 %collective-permute-start.7 = (bf16[1056,128]{1,0:T(8,128)(2,1)S(1)}, bf16[1056,128]{1,0:T(8,128)(2,1)S(1)}, u32[]{:S(2)}, u32[]{:S(2)}) collective-permute-start(bf16[1056,128]{1,0:T(8,128)(2,1)S(1)} %shard_map.48), channel_id=1, source_target_pairs={{0,256},{128,384},{256,0},{384,128},{1,257},{129,385},{257,1},{385... | collective-permute-start | bytes 811016 | tf_op jit(solution)/shard_map/ppermute | solution.py:28
  102.5 3.7 %shard_map.49 = (bf16[1056,128]{1,0:T(8,128)(2,1)S(1)}, bf16[1056,128]{1,0:T(8,128)(2,1)S(1)}) custom-call(bf16[1040,128]{1,0:T(8,128)(2,1)S(1)} %collective-permute-done.2.refs_1_.refs_0_, bf16[1040,128]{1,0:T(8,128)(2,1)S(1)} %collective-permute-done.4.refs_3_.refs_1_, bf16[2,24,128,128]{3,2,1,0:T(8,128)(2,1)S(1)} %collective-permute-done.6.refs_1_.refs_2_, ...), custom_call_target="tpu_custom_call" | custom-call | flops 536870912 | bytes 2097152 | tf_op jit(solution)/shard_map/pallas_call | solution.py:183
  106.1 3.0 %collective-permute-start.8 = (bf16[1056,128]{1,0:T(8,128)(2,1)S(1)}, bf16[1056,128]{1,0:T(8,128)(2,1)S(1)}, u32[]{:S(2)}, u32[]{:S(2)}) collective-permute-start(bf16[1056,128]{1,0:T(8,128)(2,1)S(1)} %get-tuple-element.53), channel_id=1, source_target_pairs={{0,384},{128,0},{256,128},{384,256},{1,385},{129,1},{257,129},{385... | collective-permute-start | bytes 811016 | tf_op jit(solution)/shard_map/ppermute | solution.py:28
  109.2 2.8 %collective-permute-start.9 = (bf16[1056,128]{1,0:T(8,128)(2,1)S(1)}, bf16[1056,128]{1,0:T(8,128)(2,1)S(1)}, u32[]{:S(2)}, u32[]{:S(2)}) collective-permute-start(bf16[1056,128]{1,0:T(8,128)(2,1)S(1)} %get-tuple-element.54), channel_id=1, source_target_pairs={{0,128},{128,256},{256,384},{384,0},{1,129},{129,257},{257,385},{3... | collective-permute-start | bytes 811016 | tf_op jit(solution)/shard_map/ppermute | solution.py:28
  112.0 2.5 %shard_map.50.refs_0_ = bf16[1056,128]{1,0:T(8,128)(2,1)S(1)} custom-call(bf16[1040,128]{1,0:T(8,128)(2,1)S(1)} %pad_maximum_fusion.3.refs_0_, bf16[2,24,128,128]{3,2,1,0:T(8,128)(2,1)S(1)} %collective-permute-done.6.refs_1_.refs_2_, bf16[4,8,128,128]{3,2,1,0:T(8,128)(2,1)S(1)} %pad_maximum_fusion.2.refs_2_.refs_3_, ...), custom_call_target="tpu_custom_call" | custom-call | flops 268435456 | bytes 2097152 | tf_op jit(solution)/shard_map/pallas_call | solution.py:183
  114.5 0.4 shard_map.51.refs_0_
  114.8 1.4 %collective-permute-done.8.refs_1_ = bf16[1056,128]{1,0:T(8,128)(2,1)S(1)} collective-permute-done((bf16[1056,128]{1,0:T(8,128)(2,1)S(1)}, bf16[1056,128]{1,0:T(8,128)(2,1)S(1)}, u32[]{:S(2)}, u32[]{:S(2)}) %collective-permute-start.8) | collective-permute-done | bytes 270368 | tf_op jit(solution)/shard_map/ppermute | solution.py:28
  116.3 4.0 %collective-permute-done.9.refs_2_ = bf16[1056,128]{1,0:T(8,128)(2,1)S(1)} collective-permute-done((bf16[1056,128]{1,0:T(8,128)(2,1)S(1)}, bf16[1056,128]{1,0:T(8,128)(2,1)S(1)}, u32[]{:S(2)}, u32[]{:S(2)}) %collective-permute-start.9) | collective-permute-done | bytes 270368 | tf_op jit(solution)/shard_map/ppermute | solution.py:28
  120.3 0.5 shard_map.52
  120.8 14.4 %all_to_all.11.in_ref = bf16[16,64,128]{2,1,0:T(8,128)(2,1)S(1)} all-to-all(bf16[16,64,128]{2,1,0:T(8,128)(2,1)S(1)} %bitcast.5), channel_id=1, replica_groups=mesh['x'=4,'zh'=4,'core'=2,'y'=8,'zl'=2] {'y','zl'}, dimensions={0} | all-to-all | bytes 524288 | tf_op jit(solution)/shard_map/all_to_all | solution.py:37
  135.1 0.7 shard_map.53
  (8 shorter events, 0.1 us)
Async XLA Ops:
  33.4 10.0 %copy-start = (bf16[16,128]{1,0:T(8,128)(2,1)S(1)}, bf16[16,128]{1,0:T(8,128)(2,1)}, u32[]{:S(2)}) copy-start(bf16[16,128]{1,0:T(8,128)(2,1)} %get-tuple-element.31) | copy-start | bytes 12292
  33.4 3.8 %collective-permute-start = (bf16[16,128,128]{2,1,0:T(8,128)(2,1)S(1)}, bf16[16,128,128]{2,1,0:T(8,128)(2,1)S(1)}, u32[]{:S(2)}, u32[]{:S(2)}) collective-permute-start(bf16[16,128,128]{2,1,0:T(8,128)(2,1)S(1)} %get-tuple-element.56), channel_id=1, source_target_pairs={{0,16},{16,0},{1,17},{17,1},{2,18},{18,2},{3,19},{19,3},{4,20},{20... | collective-permute-start | bytes 1572872 | tf_op jit(solution)/shard_map/ppermute | solution.py:28
  37.3 28.6 %collective-permute-start.1 = (bf16[2,16,128,128]{3,2,1,0:T(8,128)(2,1)S(1)}, bf16[2,16,128,128]{3,2,1,0:T(8,128)(2,1)S(1)}, u32[]{:S(2)}, u32[]{:S(2)}) collective-permute-start(bf16[2,16,128,128]{3,2,1,0:T(8,128)(2,1)S(1)} %pad_maximum_fusion.1.refs_4_), channel_id=1, source_target_pairs={{0,32},{16,112},{32,64},{48,16},{64,96},{80,48},{96,0},{112,80},{1... | collective-permute-start | bytes 3145736 | tf_op jit(solution)/shard_map/ppermute | solution.py:33
  43.5 10.2 %collective-permute-start.4 = (bf16[1040,128]{1,0:T(8,128)(2,1)S(1)}, bf16[1040,128]{1,0:T(8,128)(2,1)S(1)}, u32[]{:S(2)}, u32[]{:S(2)}) collective-permute-start(bf16[1040,128]{1,0:T(8,128)(2,1)S(1)} %pad_maximum_fusion.3.refs_0_), channel_id=1, source_target_pairs={{0,384},{128,0},{256,128},{384,256},{1,385},{129,1},{257,129},{385... | collective-permute-start | bytes 798728 | tf_op jit(solution)/shard_map/ppermute | solution.py:28
  48.1 10.1 %collective-permute-start.3 = (bf16[1040,128]{1,0:T(8,128)(2,1)S(1)}, bf16[1040,128]{1,0:T(8,128)(2,1)S(1)}, u32[]{:S(2)}, u32[]{:S(2)}) collective-permute-start(bf16[1040,128]{1,0:T(8,128)(2,1)S(1)} %pad_maximum_fusion.3.refs_0_), channel_id=1, source_target_pairs={{0,256},{128,384},{256,0},{384,128},{1,257},{129,385},{257,1},{385... | collective-permute-start | bytes 798728 | tf_op jit(solution)/shard_map/ppermute | solution.py:28
  50.9 14.8 %collective-permute-start.2 = (bf16[1040,128]{1,0:T(8,128)(2,1)S(1)}, bf16[1040,128]{1,0:T(8,128)(2,1)S(1)}, u32[]{:S(2)}, u32[]{:S(2)}) collective-permute-start(bf16[1040,128]{1,0:T(8,128)(2,1)S(1)} %pad_maximum_fusion.3.refs_0_), channel_id=1, source_target_pairs={{0,128},{128,256},{256,384},{384,0},{1,129},{129,257},{257,385},{3... | collective-permute-start | bytes 798728 | tf_op jit(solution)/shard_map/ppermute | solution.py:28
  66.0 23.3 %collective-permute-start.5 = (bf16[2,8,128,128]{3,2,1,0:T(8,128)(2,1)S(1)}, bf16[2,8,128,128]{3,2,1,0:T(8,128)(2,1)S(1)}, u32[]{:S(2)}, u32[]{:S(2)}) collective-permute-start(bf16[2,8,128,128]{3,2,1,0:T(8,128)(2,1)S(1)} %constant_dynamic-slice_fusion), channel_id=1, source_target_pairs={{0,32},{16,112},{32,64},{48,16},{64,96},{80,48},{96,0},{112,80},{1... | collective-permute-start | bytes 1572872 | tf_op jit(solution)/shard_map/ppermute | solution.py:33
  89.4 5.3 %collective-permute-start.6 = (bf16[2,24,128,128]{3,2,1,0:T(8,128)(2,1)S(1)}, bf16[2,24,128,128]{3,2,1,0:T(8,128)(2,1)S(1)}, u32[]{:S(2)}, u32[]{:S(2)}) collective-permute-start(bf16[2,24,128,128]{3,2,1,0:T(8,128)(2,1)S(1)} %pad_maximum_fusion), channel_id=1, source_target_pairs={{0,16},{16,0},{1,17},{17,1},{2,18},{18,2},{3,19},{19,3},{4,20},{20... | collective-permute-start | bytes 4718600 | tf_op jit(solution)/shard_map/ppermute | solution.py:28
  97.3 17.1 %collective-permute-start.7 = (bf16[1056,128]{1,0:T(8,128)(2,1)S(1)}, bf16[1056,128]{1,0:T(8,128)(2,1)S(1)}, u32[]{:S(2)}, u32[]{:S(2)}) collective-permute-start(bf16[1056,128]{1,0:T(8,128)(2,1)S(1)} %shard_map.48), channel_id=1, source_target_pairs={{0,256},{128,384},{256,0},{384,128},{1,257},{129,385},{257,1},{385... | collective-permute-start | bytes 811016 | tf_op jit(solution)/shard_map/ppermute | solution.py:28
  106.1 10.1 %collective-permute-start.8 = (bf16[1056,128]{1,0:T(8,128)(2,1)S(1)}, bf16[1056,128]{1,0:T(8,128)(2,1)S(1)}, u32[]{:S(2)}, u32[]{:S(2)}) collective-permute-start(bf16[1056,128]{1,0:T(8,128)(2,1)S(1)} %get-tuple-element.53), channel_id=1, source_target_pairs={{0,384},{128,0},{256,128},{384,256},{1,385},{129,1},{257,129},{385... | collective-permute-start | bytes 811016 | tf_op jit(solution)/shard_map/ppermute | solution.py:28
  109.2 11.1 %collective-permute-start.9 = (bf16[1056,128]{1,0:T(8,128)(2,1)S(1)}, bf16[1056,128]{1,0:T(8,128)(2,1)S(1)}, u32[]{:S(2)}, u32[]{:S(2)}) collective-permute-start(bf16[1056,128]{1,0:T(8,128)(2,1)S(1)} %get-tuple-element.54), channel_id=1, source_target_pairs={{0,128},{128,256},{256,384},{384,0},{1,129},{129,257},{257,385},{3... | collective-permute-start | bytes 811016 | tf_op jit(solution)/shard_map/ppermute | solution.py:28

commit v14 on v11

--- a/solution.py
+++ b/solution.py
@@ -180,7 +180,7 @@
         out_ref[:, h * HD : (h + 1) * HD] = in_ref[h]
 
 
-def call(kernel, outs, specs, *args, scratch=(), flops=0, moved=1 << 18, vmem=24):
+def call(kernel, outs, specs, *args, scratch=(), flops=0, moved=1 << 18, vmem=14):
     return pl.pallas_call(
         kernel,
         out_shape=outs,

time: 135 us -> 135 us (level)
  no operation moved by 1% of the time
where the time goes in v14:
time: 135 us
  blocking collectives  46.9 us (35%)
  waiting for transfers between devices  35.7 us (26%)
  starting transfers between devices  31.6 us (23%)
  Pallas kernels  19.3 us (14%)
    all_to_all x2, blocking collectives, exchange(): return lax.all_to_all(field, axes, split_axis=0, concat_axis=0, tiled=True)  46.9 us
    ppermute x9, starting transfers between devices, shift(): return lax.ppermute(field, axis, [(i, (i + by) % n) for i in range(n)])  23.6 us
    ppermute x9, waiting for transfers between devices, shift(): return lax.ppermute(field, axis, [(i, (i + by) % n) for i in range(n)])  22.2 us
    pallas_call x8, Pallas kernels, call(): pl.pallas_call(kernel, out_shape=outs, in_specs=specs, out_specs=jax.tree...  19.3 us
    ppermute x2, waiting for transfers between devices, ring_step(): return lax.ppermute(field, ('zh', 'core'), pairs)  13.5 us
    ppermute x2, starting transfers between devices, ring_step(): return lax.ppermute(field, ('zh', 'core'), pairs)  8.01 us
  transfers between devices with their start and end apart: 11, of which 9 were waited for; matrix products, arithmetic and copies ran while one was open for 0% of the time, Pallas kernels for 10%

profile of v14, /device:TPU:6, one launch (start us, length us, event | category | flops | bytes accessed | tf_op | source)
XLA Modules:
  0.0 134.8 jit_solution(15324019994284514763)
XLA Ops:
  0.0 2.1 %shard_map.46 = (bf16[16,192,128]{2,1,0:T(8,128)(2,1)}, bf16[16,128]{1,0:T(8,128)(2,1)}) custom-call(bf16[64,1536]{1,0:T(8,128)(2,1)} %q_hbm.1, bf16[64,1536]{1,0:T(8,128)(2,1)} %k_hbm.1, bf16[64,1536]{1,0:T(8,128)(2,1)} %v_hbm.1, s32[12,8,256]{2,1,0:T(8,128)} %mask_hbm.1), custom_call_target="tpu_custom_call" | custom-call | bytes 262144 | tf_op jit(solution)/shard_map/pallas_call | solution.py:184
  2.1 32.4 %all_to_all.10 = bf16[16,192,128]{2,1,0:T(8,128)(2,1)S(1)} all-to-all(bf16[16,192,128]{2,1,0:T(8,128)(2,1)} %get-tuple-element.27), channel_id=1, replica_groups=mesh['x'=4,'zh'=4,'core'=2,'y'=8,'zl'=2] {'y','zl'}, dimensions={0} | all-to-all | bytes 1572864 | tf_op jit(solution)/shard_map/all_to_all | solution.py:37
  34.5 0.2 slice_bitcast_fusion
  34.7 1.9 %collective-permute-start = (bf16[16,128,128]{2,1,0:T(8,128)(2,1)S(1)}, bf16[16,128,128]{2,1,0:T(8,128)(2,1)S(1)}, u32[]{:S(2)}, u32[]{:S(2)}) collective-permute-start(bf16[16,128,128]{2,1,0:T(8,128)(2,1)S(1)} %get-tuple-element.50), channel_id=1, source_target_pairs={{0,16},{16,0},{1,17},{17,1},{2,18},{18,2},{3,19},{19,3},{4,20},{20... | collective-permute-start | bytes 1572872 | tf_op jit(solution)/shard_map/ppermute | solution.py:28
  36.7 1.9 %collective-permute-done = bf16[16,128,128]{2,1,0:T(8,128)(2,1)S(1)} collective-permute-done((bf16[16,128,128]{2,1,0:T(8,128)(2,1)S(1)}, bf16[16,128,128]{2,1,0:T(8,128)(2,1)S(1)}, u32[]{:S(2)}, u32[]{:S(2)}) %collective-permute-start) | collective-permute-done | bytes 524320 | tf_op jit(solution)/shard_map/ppermute | solution.py:28
  38.6 6.1 %collective-permute-start.1 = (bf16[2,16,128,128]{3,2,1,0:T(8,128)(2,1)S(1)}, bf16[2,16,128,128]{3,2,1,0:T(8,128)(2,1)S(1)}, u32[]{:S(2)}, u32[]{:S(2)}) collective-permute-start(bf16[2,16,128,128]{3,2,1,0:T(8,128)(2,1)S(1)} %pad_maximum_fusion.refs_4_), channel_id=1, source_target_pairs={{0,32},{16,112},{32,64},{48,16},{64,96},{80,48},{96,0},{112,80},{1... | collective-permute-start | bytes 3145736 | tf_op jit(solution)/shard_map/ppermute | solution.py:33
  44.8 0.7 copy-done
  45.4 2.4 %collective-permute-start.2 = (bf16[1040,128]{1,0:T(8,128)(2,1)S(1)}, bf16[1040,128]{1,0:T(8,128)(2,1)S(1)}, u32[]{:S(2)}, u32[]{:S(2)}) collective-permute-start(bf16[1040,128]{1,0:T(8,128)(2,1)S(1)} %pad_maximum_fusion.1.refs_0_), channel_id=1, source_target_pairs={{0,128},{128,256},{256,384},{384,0},{1,129},{129,257},{257,385},{3... | collective-permute-start | bytes 798728 | tf_op jit(solution)/shard_map/ppermute | solution.py:28
  47.8 4.3 %collective-permute-start.3 = (bf16[1040,128]{1,0:T(8,128)(2,1)S(1)}, bf16[1040,128]{1,0:T(8,128)(2,1)S(1)}, u32[]{:S(2)}, u32[]{:S(2)}) collective-permute-start(bf16[1040,128]{1,0:T(8,128)(2,1)S(1)} %pad_maximum_fusion.1.refs_0_), channel_id=1, source_target_pairs={{0,256},{128,384},{256,0},{384,128},{1,257},{129,385},{257,1},{385... | collective-permute-start | bytes 798728 | tf_op jit(solution)/shard_map/ppermute | solution.py:28
  52.2 1.9 %collective-permute-start.4 = (bf16[1040,128]{1,0:T(8,128)(2,1)S(1)}, bf16[1040,128]{1,0:T(8,128)(2,1)S(1)}, u32[]{:S(2)}, u32[]{:S(2)}) collective-permute-start(bf16[1040,128]{1,0:T(8,128)(2,1)S(1)} %pad_maximum_fusion.1.refs_0_), channel_id=1, source_target_pairs={{0,384},{128,0},{256,128},{384,256},{1,385},{129,1},{257,129},{385... | collective-permute-start | bytes 798728 | tf_op jit(solution)/shard_map/ppermute | solution.py:28
  54.1 3.8 %collective-permute-done.3.refs_2_.refs_0_ = bf16[1040,128]{1,0:T(8,128)(2,1)S(1)} collective-permute-done((bf16[1040,128]{1,0:T(8,128)(2,1)S(1)}, bf16[1040,128]{1,0:T(8,128)(2,1)S(1)}, u32[]{:S(2)}, u32[]{:S(2)}) %collective-permute-start.3) | collective-permute-done | bytes 266272 | tf_op jit(solution)/shard_map/ppermute | solution.py:28
  57.9 7.2 %collective-permute-done.4.refs_3_.refs_1_ = bf16[1040,128]{1,0:T(8,128)(2,1)S(1)} collective-permute-done((bf16[1040,128]{1,0:T(8,128)(2,1)S(1)}, bf16[1040,128]{1,0:T(8,128)(2,1)S(1)}, u32[]{:S(2)}, u32[]{:S(2)}) %collective-permute-start.4) | collective-permute-done | bytes 266272 | tf_op jit(solution)/shard_map/ppermute | solution.py:28
  65.0 7.7 %collective-permute-done.1.refs_5_ = bf16[2,16,128,128]{3,2,1,0:T(8,128)(2,1)S(1)} collective-permute-done((bf16[2,16,128,128]{3,2,1,0:T(8,128)(2,1)S(1)}, bf16[2,16,128,128]{3,2,1,0:T(8,128)(2,1)S(1)}, u32[]{:S(2)}, u32[]{:S(2)}) %collective-permute-start.1) | collective-permute-done | bytes 1048608 | tf_op jit(solution)/shard_map/ppermute | solution.py:33
  72.7 1.9 %collective-permute-start.6 = (bf16[2,16,128,128]{3,2,1,0:T(8,128)(2,1)S(1)}, bf16[2,16,128,128]{3,2,1,0:T(8,128)(2,1)}, u32[]{:S(2)}, u32[]{:S(2)}) collective-permute-start(bf16[2,16,128,128]{3,2,1,0:T(8,128)(2,1)S(1)} %collective-permute-done.1.refs_5_), channel_id=1, source_target_pairs={{0,16},{16,0},{1,17},{17,1},{2,18},{18,2},{3,19},{19,3},{4,20},{20... | collective-permute-start | bytes 3145736 | tf_op jit(solution)/shard_map/ppermute | solution.py:28
  74.7 1.9 %collective-permute-start.5 = (bf16[2,8,128,128]{3,2,1,0:T(8,128)(2,1)S(1)}, bf16[2,8,128,128]{3,2,1,0:T(8,128)(2,1)S(1)}, u32[]{:S(2)}, u32[]{:S(2)}) collective-permute-start(bf16[2,8,128,128]{3,2,1,0:T(8,128)(2,1)S(1)} %constant_dynamic-slice_fusion), channel_id=1, source_target_pairs={{0,32},{16,112},{32,64},{48,16},{64,96},{80,48},{96,0},{112,80},{1... | collective-permute-start | bytes 1572872 | tf_op jit(solution)/shard_map/ppermute | solution.py:33
  76.6 0.8 collective-permute-done.6.refs_6_
  77.4 8.6 %shard_map.47 = (f32[2,1024,128]{2,1,0:T(8,128)S(1)}, f32[2,1024,128]{2,1,0:T(8,128)S(1)}, f32[2,1024,128]{2,1,0:T(8,128)S(1)}, f32[2,1024,128]{2,1,0:T(8,128)S(1)}) custom-call(bf16[1040,128]{1,0:T(8,128)(2,1)S(1)} %pad_maximum_fusion.1.refs_0_, bf16[1040,128]{1,0:T(8,128)(2,1)S(1)} %collective-permute-done.2.refs_1_.refs_0_, ...), custom_call_target="tpu_custom_call" | custom-call | flops 1610612736 | bytes 2097152 | tf_op jit(solution)/shard_map/pallas_call | solution.py:184
  86.0 5.8 %collective-permute-done.5 = bf16[2,8,128,128]{3,2,1,0:T(8,128)(2,1)S(1)} collective-permute-done((bf16[2,8,128,128]{3,2,1,0:T(8,128)(2,1)S(1)}, bf16[2,8,128,128]{3,2,1,0:T(8,128)(2,1)S(1)}, u32[]{:S(2)}, u32[]{:S(2)}) %collective-permute-start.5) | collective-permute-done | bytes 524320 | tf_op jit(solution)/shard_map/ppermute | solution.py:33
  91.9 1.9 %collective-permute-start.7 = (bf16[2,8,128,128]{3,2,1,0:T(8,128)(2,1)S(1)}, bf16[2,8,128,128]{3,2,1,0:T(8,128)(2,1)S(1)}, u32[]{:S(2)}, u32[]{:S(2)}) collective-permute-start(bf16[2,8,128,128]{3,2,1,0:T(8,128)(2,1)S(1)} %collective-permute-done.5), channel_id=1, source_target_pairs={{0,16},{16,0},{1,17},{17,1},{2,18},{18,2},{3,19},{19,3},{4,20},{20... | collective-permute-start | bytes 1572872 | tf_op jit(solution)/shard_map/ppermute | solution.py:28
  93.8 1.8 %collective-permute-done.7 = bf16[2,8,128,128]{3,2,1,0:T(8,128)(2,1)S(1)} collective-permute-done((bf16[2,8,128,128]{3,2,1,0:T(8,128)(2,1)S(1)}, bf16[2,8,128,128]{3,2,1,0:T(8,128)(2,1)S(1)}, u32[]{:S(2)}, u32[]{:S(2)}) %collective-permute-start.7) | collective-permute-done | bytes 524320 | tf_op jit(solution)/shard_map/ppermute | solution.py:28
  95.7 2.0 %shard_map.48 = bf16[1056,128]{1,0:T(8,128)(2,1)S(1)} custom-call(bf16[1040,128]{1,0:T(8,128)(2,1)S(1)} %collective-permute-done.3.refs_2_.refs_0_, bf16[4,8,128,128]{3,2,1,0:T(8,128)(2,1)S(1)} %constant_dynamic-update-slice_fusion.refs_1_.refs_2_, f32[2,1024,128]{2,1,0:T(8,128)S(1)} %get-tuple-element.38.refs_2_), custom_call_target="tpu_custom_call" | custom-call | flops 134217728 | bytes 2097152 | tf_op jit(solution)/shard_map/pallas_call | solution.py:184
  97.8 3.3 %collective-permute-start.8 = (bf16[1056,128]{1,0:T(8,128)(2,1)S(1)}, bf16[1056,128]{1,0:T(8,128)(2,1)S(1)}, u32[]{:S(2)}, u32[]{:S(2)}) collective-permute-start(bf16[1056,128]{1,0:T(8,128)(2,1)S(1)} %shard_map.48), channel_id=1, source_target_pairs={{0,256},{128,384},{256,0},{384,128},{1,257},{129,385},{257,1},{385... | collective-permute-start | bytes 811016 | tf_op jit(solution)/shard_map/ppermute | solution.py:28
  101.1 3.0 %shard_map.49 = (bf16[1056,128]{1,0:T(8,128)(2,1)S(1)}, bf16[1056,128]{1,0:T(8,128)(2,1)S(1)}) custom-call(bf16[1040,128]{1,0:T(8,128)(2,1)S(1)} %collective-permute-done.2.refs_1_.refs_0_, bf16[1040,128]{1,0:T(8,128)(2,1)S(1)} %collective-permute-done.4.refs_3_.refs_1_, bf16[4,8,128,128]{3,2,1,0:T(8,128)(2,1)S(1)} %constant_dynamic-update-slice_fusion.refs_1_.refs_2_, ...), custom_call_target="tpu_custom_call" | custom-call | flops 268435456 | bytes 2097152 | tf_op jit(solution)/shard_map/pallas_call | solution.py:184
  104.1 4.0 %collective-permute-start.10 = (bf16[1056,128]{1,0:T(8,128)(2,1)S(1)}, bf16[1056,128]{1,0:T(8,128)(2,1)S(1)}, u32[]{:S(2)}, u32[]{:S(2)}) collective-permute-start(bf16[1056,128]{1,0:T(8,128)(2,1)S(1)} %get-tuple-element.48), channel_id=1, source_target_pairs={{0,128},{128,256},{256,384},{384,0},{1,129},{129,257},{257,385},{3... | collective-permute-start | bytes 811016 | tf_op jit(solution)/shard_map/ppermute | solution.py:28
  108.1 1.9 %collective-permute-start.9 = (bf16[1056,128]{1,0:T(8,128)(2,1)S(1)}, bf16[1056,128]{1,0:T(8,128)(2,1)S(1)}, u32[]{:S(2)}, u32[]{:S(2)}) collective-permute-start(bf16[1056,128]{1,0:T(8,128)(2,1)S(1)} %get-tuple-element.47), channel_id=1, source_target_pairs={{0,384},{128,0},{256,128},{384,256},{1,385},{129,1},{257,129},{385... | collective-permute-start | bytes 811016 | tf_op jit(solution)/shard_map/ppermute | solution.py:28
  110.0 2.0 %shard_map.50.refs_0_ = bf16[1056,128]{1,0:T(8,128)(2,1)S(1)} custom-call(bf16[1040,128]{1,0:T(8,128)(2,1)S(1)} %pad_maximum_fusion.1.refs_0_, bf16[4,8,128,128]{3,2,1,0:T(8,128)(2,1)S(1)} %constant_dynamic-update-slice_fusion.refs_1_.refs_2_, f32[2,1024,128]{2,1,0:T(8,128)S(1)} %get-tuple-element.45.refs_2_), custom_call_target="tpu_custom_call" | custom-call | flops 134217728 | bytes 2097152 | tf_op jit(solution)/shard_map/pallas_call | solution.py:184
  112.0 0.4 shard_map.51.refs_0_
  112.4 1.8 %collective-permute-done.10.refs_2_ = bf16[1056,128]{1,0:T(8,128)(2,1)S(1)} collective-permute-done((bf16[1056,128]{1,0:T(8,128)(2,1)S(1)}, bf16[1056,128]{1,0:T(8,128)(2,1)S(1)}, u32[]{:S(2)}, u32[]{:S(2)}) %collective-permute-start.10) | collective-permute-done | bytes 270368 | tf_op jit(solution)/shard_map/ppermute | solution.py:28
  114.2 4.9 %collective-permute-done.9.refs_1_ = bf16[1056,128]{1,0:T(8,128)(2,1)S(1)} collective-permute-done((bf16[1056,128]{1,0:T(8,128)(2,1)S(1)}, bf16[1056,128]{1,0:T(8,128)(2,1)S(1)}, u32[]{:S(2)}, u32[]{:S(2)}) %collective-permute-start.9) | collective-permute-done | bytes 270368 | tf_op jit(solution)/shard_map/ppermute | solution.py:28
  119.1 0.5 shard_map.52
  119.6 14.5 %all_to_all.11.in_ref = bf16[16,64,128]{2,1,0:T(8,128)(2,1)S(1)} all-to-all(bf16[16,64,128]{2,1,0:T(8,128)(2,1)S(1)} %bitcast.5), channel_id=1, replica_groups=mesh['x'=4,'zh'=4,'core'=2,'y'=8,'zl'=2] {'y','zl'}, dimensions={0} | all-to-all | bytes 524288 | tf_op jit(solution)/shard_map/all_to_all | solution.py:37
  134.1 0.7 shard_map.53
  (9 shorter events, 0.3 us)
Async XLA Ops:
  34.7 3.8 %collective-permute-start = (bf16[16,128,128]{2,1,0:T(8,128)(2,1)S(1)}, bf16[16,128,128]{2,1,0:T(8,128)(2,1)S(1)}, u32[]{:S(2)}, u32[]{:S(2)}) collective-permute-start(bf16[16,128,128]{2,1,0:T(8,128)(2,1)S(1)} %get-tuple-element.50), channel_id=1, source_target_pairs={{0,16},{16,0},{1,17},{17,1},{2,18},{18,2},{3,19},{19,3},{4,20},{20... | collective-permute-start | bytes 1572872 | tf_op jit(solution)/shard_map/ppermute | solution.py:28
  38.6 34.1 %collective-permute-start.1 = (bf16[2,16,128,128]{3,2,1,0:T(8,128)(2,1)S(1)}, bf16[2,16,128,128]{3,2,1,0:T(8,128)(2,1)S(1)}, u32[]{:S(2)}, u32[]{:S(2)}) collective-permute-start(bf16[2,16,128,128]{3,2,1,0:T(8,128)(2,1)S(1)} %pad_maximum_fusion.refs_4_), channel_id=1, source_target_pairs={{0,32},{16,112},{32,64},{48,16},{64,96},{80,48},{96,0},{112,80},{1... | collective-permute-start | bytes 3145736 | tf_op jit(solution)/shard_map/ppermute | solution.py:33
  44.7 0.7 copy-start
  45.4 8.7 %collective-permute-start.2 = (bf16[1040,128]{1,0:T(8,128)(2,1)S(1)}, bf16[1040,128]{1,0:T(8,128)(2,1)S(1)}, u32[]{:S(2)}, u32[]{:S(2)}) collective-permute-start(bf16[1040,128]{1,0:T(8,128)(2,1)S(1)} %pad_maximum_fusion.1.refs_0_), channel_id=1, source_target_pairs={{0,128},{128,256},{256,384},{384,0},{1,129},{129,257},{257,385},{3... | collective-permute-start | bytes 798728 | tf_op jit(solution)/shard_map/ppermute | solution.py:28
  47.8 10.0 %collective-permute-start.3 = (bf16[1040,128]{1,0:T(8,128)(2,1)S(1)}, bf16[1040,128]{1,0:T(8,128)(2,1)S(1)}, u32[]{:S(2)}, u32[]{:S(2)}) collective-permute-start(bf16[1040,128]{1,0:T(8,128)(2,1)S(1)} %pad_maximum_fusion.1.refs_0_), channel_id=1, source_target_pairs={{0,256},{128,384},{256,0},{384,128},{1,257},{129,385},{257,1},{385... | collective-permute-start | bytes 798728 | tf_op jit(solution)/shard_map/ppermute | solution.py:28
  52.2 12.9 %collective-permute-start.4 = (bf16[1040,128]{1,0:T(8,128)(2,1)S(1)}, bf16[1040,128]{1,0:T(8,128)(2,1)S(1)}, u32[]{:S(2)}, u32[]{:S(2)}) collective-permute-start(bf16[1040,128]{1,0:T(8,128)(2,1)S(1)} %pad_maximum_fusion.1.refs_0_), channel_id=1, source_target_pairs={{0,384},{128,0},{256,128},{384,256},{1,385},{129,1},{257,129},{385... | collective-permute-start | bytes 798728 | tf_op jit(solution)/shard_map/ppermute | solution.py:28
  72.7 4.7 %collective-permute-start.6 = (bf16[2,16,128,128]{3,2,1,0:T(8,128)(2,1)S(1)}, bf16[2,16,128,128]{3,2,1,0:T(8,128)(2,1)}, u32[]{:S(2)}, u32[]{:S(2)}) collective-permute-start(bf16[2,16,128,128]{3,2,1,0:T(8,128)(2,1)S(1)} %collective-permute-done.1.refs_5_), channel_id=1, source_target_pairs={{0,16},{16,0},{1,17},{17,1},{2,18},{18,2},{3,19},{19,3},{4,20},{20... | collective-permute-start | bytes 3145736 | tf_op jit(solution)/shard_map/ppermute | solution.py:28
  74.7 17.2 %collective-permute-start.5 = (bf16[2,8,128,128]{3,2,1,0:T(8,128)(2,1)S(1)}, bf16[2,8,128,128]{3,2,1,0:T(8,128)(2,1)S(1)}, u32[]{:S(2)}, u32[]{:S(2)}) collective-permute-start(bf16[2,8,128,128]{3,2,1,0:T(8,128)(2,1)S(1)} %constant_dynamic-slice_fusion), channel_id=1, source_target_pairs={{0,32},{16,112},{32,64},{48,16},{64,96},{80,48},{96,0},{112,80},{1... | collective-permute-start | bytes 1572872 | tf_op jit(solution)/shard_map/ppermute | solution.py:33
  91.9 3.8 %collective-permute-start.7 = (bf16[2,8,128,128]{3,2,1,0:T(8,128)(2,1)S(1)}, bf16[2,8,128,128]{3,2,1,0:T(8,128)(2,1)S(1)}, u32[]{:S(2)}, u32[]{:S(2)}) collective-permute-start(bf16[2,8,128,128]{3,2,1,0:T(8,128)(2,1)S(1)} %collective-permute-done.5), channel_id=1, source_target_pairs={{0,16},{16,0},{1,17},{17,1},{2,18},{18,2},{3,19},{19,3},{4,20},{20... | collective-permute-start | bytes 1572872 | tf_op jit(solution)/shard_map/ppermute | solution.py:28
  97.8 14.3 %collective-permute-start.8 = (bf16[1056,128]{1,0:T(8,128)(2,1)S(1)}, bf16[1056,128]{1,0:T(8,128)(2,1)S(1)}, u32[]{:S(2)}, u32[]{:S(2)}) collective-permute-start(bf16[1056,128]{1,0:T(8,128)(2,1)S(1)} %shard_map.48), channel_id=1, source_target_pairs={{0,256},{128,384},{256,0},{384,128},{1,257},{129,385},{257,1},{385... | collective-permute-start | bytes 811016 | tf_op jit(solution)/shard_map/ppermute | solution.py:28
  104.1 10.1 %collective-permute-start.10 = (bf16[1056,128]{1,0:T(8,128)(2,1)S(1)}, bf16[1056,128]{1,0:T(8,128)(2,1)S(1)}, u32[]{:S(2)}, u32[]{:S(2)}) collective-permute-start(bf16[1056,128]{1,0:T(8,128)(2,1)S(1)} %get-tuple-element.48), channel_id=1, source_target_pairs={{0,128},{128,256},{256,384},{384,0},{1,129},{129,257},{257,385},{3... | collective-permute-start | bytes 811016 | tf_op jit(solution)/shard_map/ppermute | solution.py:28
  108.1 11.1 %collective-permute-start.9 = (bf16[1056,128]{1,0:T(8,128)(2,1)S(1)}, bf16[1056,128]{1,0:T(8,128)(2,1)S(1)}, u32[]{:S(2)}, u32[]{:S(2)}) collective-permute-start(bf16[1056,128]{1,0:T(8,128)(2,1)S(1)} %get-tuple-element.47), channel_id=1, source_target_pairs={{0,384},{128,0},{256,128},{384,256},{1,385},{129,1},{257,129},{385... | collective-permute-start | bytes 811016 | tf_op jit(solution)/shard_map/ppermute | solution.py:28
